TPU v7x, 128 devices: a whole 4x4x4 slice. The times are simulated.
128 devices in a mesh: layer: 8 (over x_lo, y), plane: 16 (over z, x_hi, core).
Axes of the slice: x: 4 (x_hi: 2, x_lo: 2; x = x_hi * 2 + x_lo), y: 4, z: 4, core: 2. Of those that a mesh axis runs over, the one named last changes fastest.
Arguments:
- rhs: float32 [2, 8, 768, 32, 128], P(None, None, 'layer', 'plane'), may hold values from -6 to 6
- inverse_blocks: bfloat16 [8, 2, 32, 128, 2, 32, 128], P('layer', None, 'plane')
- mode_panel: bfloat16 [256, 32, 128], P(None, 'plane'), may hold values from -5 to 5
- mode_profile: bfloat16 [256, 768], P('plane', 'layer'), may hold values from -5 to 5
- generator: int32 [256], replicated, may hold values from 1 to 32767
- lattice_index: int32 [8], replicated, may hold values from 0 to 32767
- shift_index: int32 [8, 256], replicated, may hold values from 0 to 32767
Outputs:
- solution: float32 [2, 8, 768, 32, 128], P(None, None, 'layer', 'plane')
- residual: float32 [2, 8, 768, 32, 128], P(None, None, 'layer', 'plane')
All inputs are finite; a program needn't handle non-finite values.
Results may differ from a plain program's by a relative error of at most 0.0033.
Values may be sent and summed in bfloat16 or wider, within the bound.
No kernel may reach another device: no remote copies, remote signals or barrier semaphores. Data moves between devices by JAX's collectives and lax.ppermute only.
A program may use at most 128 MiB of HBM per device.

v0:
```python
import jax
import jax.numpy as jnp
from jax import lax
from jax.sharding import PartitionSpec as P

MODES = 256
NPTS = 32768


COUPLING = 0.8
ABSORB_RATE = 0.3
WAVE_SCALE = 0.8


def shifted(value, axis, by):
    size = lax.axis_size(axis)
    pairs = [(i, i + by) for i in range(size) if 0 <= i + by < size]
    return lax.ppermute(value, axis, pairs)


def with_halo(value, sides, width):
    for axis, dim in sides:
        size, length = (lax.axis_size(axis), value.shape[dim])
        up = [(i, (i + 1) % size) for i in range(size - 1)]
        down = [(j, i) for i, j in up]
        last = lax.slice_in_dim(value, length - width, length, axis=dim)
        leading = lax.slice_in_dim(value, 0, width, axis=dim)
        before = lax.ppermute(last, axis, up)
        after = lax.ppermute(leading, axis, down)
        value = jnp.concatenate([before, value, after], axis=dim)
    return value


def apply_front(blocks, piece):
    return jnp.einsum("axbcpq,crlpq->arlxb", blocks, piece, preferred_element_type=jnp.float32)


def shards(rhs, inverse_blocks, mode_panel, mode_profile, generator, lattice_index, shift_index):
    blocks = inverse_blocks[0]
    rounded = rhs.astype(jnp.bfloat16)

    def fold_rows(piece):
        return apply_front(blocks, piece)

    later = fold_rows(lax.all_gather(rounded[:, :, 1:], "plane", axis=3, tiled=True))
    first = fold_rows(lax.all_gather(rounded[:, :, :1], "plane", axis=3, tiled=True))
    fronts = jnp.concatenate([first, later], axis=2)
    base_front = fronts[:, :, :1]

    def sweep_step(step, interface):
        incoming = shifted(interface.astype(jnp.bfloat16), "layer", 1)
        coupled = fold_rows(lax.all_gather(incoming, "plane", axis=3, tiled=True))
        return base_front + COUPLING * coupled

    interface = lax.fori_loop(0, lax.axis_size("layer") - 1, sweep_step, base_front)
    solution = jnp.concatenate([interface, fronts[:, :, 1:]], axis=2)
    profile = lax.all_gather(mode_profile, "plane", axis=0, tiled=True)
    mixed = (lattice_index[:, None] * generator[None, :] + shift_index) % NPTS
    amplitude = 0.25 / jnp.sqrt(1.0 + jnp.arange(MODES, dtype=jnp.float32) / 8.0)
    coef = amplitude[None, :] * ((mixed.astype(jnp.float32) + 0.5) / NPTS - 0.5)
    weights = coef[:, :, None] * profile.astype(jnp.float32)[None, :, :]
    logc = jnp.einsum(
        "rkz,kxy->rzxy", weights, mode_panel.astype(jnp.float32), precision=lax.Precision.HIGHEST
    )
    wavenum = WAVE_SCALE * jnp.exp(-2.0 * logc)
    extended = with_halo(solution.astype(jnp.bfloat16), (("layer", 2), ("plane", 3)), 1).astype(
        solution.dtype
    )
    padded = jnp.pad(extended, ((0, 0), (0, 0), (0, 0), (0, 0), (1, 1)))
    beside = padded[:, :, 2:, 1:-1, 1:-1] + padded[:, :, :-2, 1:-1, 1:-1]
    beside = beside + padded[:, :, 1:-1, 2:, 1:-1] + padded[:, :, 1:-1, :-2, 1:-1]
    beside = beside + padded[:, :, 1:-1, 1:-1, 2:] + padded[:, :, 1:-1, 1:-1, :-2]
    lap = 6.0 * solution - beside
    real_part = solution[0]
    imag_part = solution[1]
    apply_real = lap[0] - wavenum * real_part + ABSORB_RATE * wavenum * imag_part
    apply_imag = lap[1] - wavenum * imag_part - ABSORB_RATE * wavenum * real_part
    residual = rhs - jnp.stack([apply_real, apply_imag])
    return (solution, residual)


def solution(mesh):
    return jax.shard_map(
        shards,
        mesh=mesh,
        in_specs=(
            P(None, None, "layer", "plane", None),
            P("layer", None, "plane", None, None, None, None),
            P(None, "plane", None),
            P("plane", "layer"),
            P(),
            P(),
            P(),
        ),
        out_specs=(P(None, None, "layer", "plane", None), P(None, None, "layer", "plane", None)),
        check_vma=False,
    )
```

profile of v0, /device:TPU:7, one launch (start us, length us, event | category | flops | bytes accessed | tf_op | source)
XLA Modules:
  0.0 422.1 jit_solution(12144929566058941278)
XLA Ops:
  7.2 0.0 copy-start
  7.2 0.0 all-gather.2.cloned.1.call-start
  7.2 2.0 slice.69
  9.3 1.0 copy.85
  10.3 0.0 all-gather.2.cloned.1.call-update
  10.4 12.0 %copy.83 = bf16[1,2,2,128,2,32,128]{6,3,5,4,2,1,0:T(8,128)(2,1)} copy(bf16[1,2,2,128,2,32,128]{6,5,4,3,2,1,0:T(8,128)(2,1)} %param.10) | data formatting | bytes 16777216 | tf_op args[1]
  22.3 23.1 %all_gather.12 = bf16[2,8,1,32,128]{4,1,3,0,2:T(8,128)(2,1)S(1)} all-gather(bf16[2,8,1,2,128]{4,1,3,0,2:T(8,128)(2,1)S(1)} %copy.84), channel_id=1, replica_groups=mesh['layer'=8,'plane'=16] {'plane'}, dimensions={3}, use_global_device_ids=true | all-gather | bytes 139264 | tf_op jit(solution)/shard_map/all_gather | solution.py:46
  45.4 11.6 %convolution_bitcast_fusion.1 = f32[2,8,1,2,128]{4,1,3,0,2:T(8,128)S(1)} fusion(bf16[2,8,1,32,128]{4,1,3,0,2:T(8,128)(2,1)S(1)} %all_gather.12, bf16[1,2,2,128,2,32,128]{6,5,4,3,2,1,0:T(8,128)(2,1)} %param.10), kind=kOutput, calls=%fused_computation.27 | convolution fusion | flops 67108864 | bytes 8536064 | tf_op jit(solution)/shard_map/axbcpq,crlpq->arlxb/dot_general | solution.py:35
  57.1 53.3 %all-gather.2.cloned.1.call-done = bf16[2,8,95,32,128]{4,1,3,0,2:T(8,128)(2,1)} async-done(((bf16[2,8,95,2,128]{4,1,3,0,2:T(8,128)(2,1)}), bf16[2,8,95,32,128]{4,1,3,0,2:T(8,128)(2,1)}) %all-gather.2.cloned.1.call-update) | async-done | bytes 12451856 | tf_op jit(solution)/shard_map/all_gather | solution.py:45
  110.4 10.9 %fusion.11 = f32[2,8,95,2,128]{4,1,3,0,2:T(8,128)S(1)} fusion(bf16[1,2,2,128,2,32,128]{6,5,4,3,2,1,0:T(8,128)(2,1)} %param.10, bf16[2,8,95,32,128]{4,1,3,0,2:T(8,128)(2,1)} %all-gather.2.cloned.1.call-done), kind=kOutput, calls=%fused_computation.23 | convolution fusion | flops 6375342080 | bytes 22396928 | tf_op jit(solution)/shard_map/axbcpq,crlpq->arlxb/dot_general | solution.py:35
  121.2 241.8 %while.10 = (s32[]{:T(128)}, f32[2,8,1,2,128]{4,1,3,0,2:T(8,128)S(1)}, bf16[2,2,128,2,32,128]{5,2,4,3,1,0:T(8,128)(2,1)}, f32[2,8,1,2,128]{4,1,3,0,2:T(8,128)S(1)}, s32[]{:T(128)}) while((s32[]{:T(128)}, f32[2,8,1,2,128]{4,1,3,0,2:T(8,128)S(1)}, bf16[2,2,128,2,32,128]{5,2,4,3,1,0:T(8,128)(2,1)}, f32[2,8,1,2,128]{4,1,3,0,2:T(8,128)S(1)}, ...), condition=%wide.region_1.0_spmd, body=%wide.region_0.0_spmd.sunk | while | flops 67121152 | bytes 8749157 | solution.py:55
  121.3 3.1 collective-permute-start
  124.4 3.4 collective-permute-done
  127.8 22.7 %all_gather.16 = bf16[2,8,1,32,128]{4,1,3,0,2:T(8,128)(2,1)S(1)} all-gather(bf16[2,8,1,2,128]{4,1,3,0,2:T(8,128)(2,1)S(1)} %collective-permute-done), channel_id=1, replica_groups=mesh['layer'=8,'plane'=16] {'plane'}, dimensions={3}, use_global_device_ids=true | all-gather | bytes 139264 | tf_op jit(solution)/shard_map/while/body/eval_jaxpr/all_gather | solution.py:52
  150.4 5.6 %fusion.51 = f32[2,8,1,2,128]{4,1,3,0,2:T(8,128)S(1)} fusion(f32[2,8,1,2,128]{4,1,3,0,2:T(8,128)S(1)} %get-tuple-element.85, bf16[2,2,128,2,32,128]{5,2,4,3,1,0:T(8,128)(2,1)} %get-tuple-element.84, bf16[2,8,1,32,128]{4,1,3,0,2:T(8,128)(2,1)S(1)} %all_gather.16), kind=kOutput, calls=%fused_computation.3.clone.1 | convolution fusion | flops 67117056 | bytes 8552448 | tf_op jit(solution)/shard_map/while/body/eval_jaxpr/axbcpq,crlpq->arlxb/dot_general | solution.py:35
  156.1 1.9 collective-permute-start
  158.0 4.6 %collective-permute-done = bf16[2,8,1,2,128]{4,1,3,0,2:T(8,128)(2,1)S(1)} collective-permute-done((bf16[2,8,1,2,128]{4,1,3,0,2:T(8,128)(2,1)S(1)}, bf16[2,8,1,2,128]{4,1,3,0,2:T(8,128)(2,1)S(1)}, u32[]{:S(2)}, u32[]{:S(2)}) %collective-permute-start) | collective-permute-done | bytes 8224 | tf_op jit(solution)/shard_map/while/body/eval_jaxpr/ppermute | solution.py:18
  162.6 22.2 %all_gather.16 = bf16[2,8,1,32,128]{4,1,3,0,2:T(8,128)(2,1)S(1)} all-gather(bf16[2,8,1,2,128]{4,1,3,0,2:T(8,128)(2,1)S(1)} %collective-permute-done), channel_id=1, replica_groups=mesh['layer'=8,'plane'=16] {'plane'}, dimensions={3}, use_global_device_ids=true | all-gather | bytes 139264 | tf_op jit(solution)/shard_map/while/body/eval_jaxpr/all_gather | solution.py:52
  184.8 5.6 %fusion.51 = f32[2,8,1,2,128]{4,1,3,0,2:T(8,128)S(1)} fusion(f32[2,8,1,2,128]{4,1,3,0,2:T(8,128)S(1)} %get-tuple-element.85, bf16[2,2,128,2,32,128]{5,2,4,3,1,0:T(8,128)(2,1)} %get-tuple-element.84, bf16[2,8,1,32,128]{4,1,3,0,2:T(8,128)(2,1)S(1)} %all_gather.16), kind=kOutput, calls=%fused_computation.3.clone.1 | convolution fusion | flops 67117056 | bytes 8552448 | tf_op jit(solution)/shard_map/while/body/eval_jaxpr/axbcpq,crlpq->arlxb/dot_general | solution.py:35
  190.5 1.9 collective-permute-start
  192.4 4.6 %collective-permute-done = bf16[2,8,1,2,128]{4,1,3,0,2:T(8,128)(2,1)S(1)} collective-permute-done((bf16[2,8,1,2,128]{4,1,3,0,2:T(8,128)(2,1)S(1)}, bf16[2,8,1,2,128]{4,1,3,0,2:T(8,128)(2,1)S(1)}, u32[]{:S(2)}, u32[]{:S(2)}) %collective-permute-start) | collective-permute-done | bytes 8224 | tf_op jit(solution)/shard_map/while/body/eval_jaxpr/ppermute | solution.py:18
  197.0 22.5 %all_gather.16 = bf16[2,8,1,32,128]{4,1,3,0,2:T(8,128)(2,1)S(1)} all-gather(bf16[2,8,1,2,128]{4,1,3,0,2:T(8,128)(2,1)S(1)} %collective-permute-done), channel_id=1, replica_groups=mesh['layer'=8,'plane'=16] {'plane'}, dimensions={3}, use_global_device_ids=true | all-gather | bytes 139264 | tf_op jit(solution)/shard_map/while/body/eval_jaxpr/all_gather | solution.py:52
  219.4 5.6 %fusion.51 = f32[2,8,1,2,128]{4,1,3,0,2:T(8,128)S(1)} fusion(f32[2,8,1,2,128]{4,1,3,0,2:T(8,128)S(1)} %get-tuple-element.85, bf16[2,2,128,2,32,128]{5,2,4,3,1,0:T(8,128)(2,1)} %get-tuple-element.84, bf16[2,8,1,32,128]{4,1,3,0,2:T(8,128)(2,1)S(1)} %all_gather.16), kind=kOutput, calls=%fused_computation.3.clone.1 | convolution fusion | flops 67117056 | bytes 8552448 | tf_op jit(solution)/shard_map/while/body/eval_jaxpr/axbcpq,crlpq->arlxb/dot_general | solution.py:35
  225.1 1.9 collective-permute-start
  227.0 4.6 %collective-permute-done = bf16[2,8,1,2,128]{4,1,3,0,2:T(8,128)(2,1)S(1)} collective-permute-done((bf16[2,8,1,2,128]{4,1,3,0,2:T(8,128)(2,1)S(1)}, bf16[2,8,1,2,128]{4,1,3,0,2:T(8,128)(2,1)S(1)}, u32[]{:S(2)}, u32[]{:S(2)}) %collective-permute-start) | collective-permute-done | bytes 8224 | tf_op jit(solution)/shard_map/while/body/eval_jaxpr/ppermute | solution.py:18
  231.6 22.2 %all_gather.16 = bf16[2,8,1,32,128]{4,1,3,0,2:T(8,128)(2,1)S(1)} all-gather(bf16[2,8,1,2,128]{4,1,3,0,2:T(8,128)(2,1)S(1)} %collective-permute-done), channel_id=1, replica_groups=mesh['layer'=8,'plane'=16] {'plane'}, dimensions={3}, use_global_device_ids=true | all-gather | bytes 139264 | tf_op jit(solution)/shard_map/while/body/eval_jaxpr/all_gather | solution.py:52
  253.8 5.6 %fusion.51 = f32[2,8,1,2,128]{4,1,3,0,2:T(8,128)S(1)} fusion(f32[2,8,1,2,128]{4,1,3,0,2:T(8,128)S(1)} %get-tuple-element.85, bf16[2,2,128,2,32,128]{5,2,4,3,1,0:T(8,128)(2,1)} %get-tuple-element.84, bf16[2,8,1,32,128]{4,1,3,0,2:T(8,128)(2,1)S(1)} %all_gather.16), kind=kOutput, calls=%fused_computation.3.clone.1 | convolution fusion | flops 67117056 | bytes 8552448 | tf_op jit(solution)/shard_map/while/body/eval_jaxpr/axbcpq,crlpq->arlxb/dot_general | solution.py:35
  259.4 1.9 collective-permute-start
  261.4 4.6 %collective-permute-done = bf16[2,8,1,2,128]{4,1,3,0,2:T(8,128)(2,1)S(1)} collective-permute-done((bf16[2,8,1,2,128]{4,1,3,0,2:T(8,128)(2,1)S(1)}, bf16[2,8,1,2,128]{4,1,3,0,2:T(8,128)(2,1)S(1)}, u32[]{:S(2)}, u32[]{:S(2)}) %collective-permute-start) | collective-permute-done | bytes 8224 | tf_op jit(solution)/shard_map/while/body/eval_jaxpr/ppermute | solution.py:18
  266.0 22.5 %all_gather.16 = bf16[2,8,1,32,128]{4,1,3,0,2:T(8,128)(2,1)S(1)} all-gather(bf16[2,8,1,2,128]{4,1,3,0,2:T(8,128)(2,1)S(1)} %collective-permute-done), channel_id=1, replica_groups=mesh['layer'=8,'plane'=16] {'plane'}, dimensions={3}, use_global_device_ids=true | all-gather | bytes 139264 | tf_op jit(solution)/shard_map/while/body/eval_jaxpr/all_gather | solution.py:52
  288.4 5.6 %fusion.51 = f32[2,8,1,2,128]{4,1,3,0,2:T(8,128)S(1)} fusion(f32[2,8,1,2,128]{4,1,3,0,2:T(8,128)S(1)} %get-tuple-element.85, bf16[2,2,128,2,32,128]{5,2,4,3,1,0:T(8,128)(2,1)} %get-tuple-element.84, bf16[2,8,1,32,128]{4,1,3,0,2:T(8,128)(2,1)S(1)} %all_gather.16), kind=kOutput, calls=%fused_computation.3.clone.1 | convolution fusion | flops 67117056 | bytes 8552448 | tf_op jit(solution)/shard_map/while/body/eval_jaxpr/axbcpq,crlpq->arlxb/dot_general | solution.py:35
  294.1 1.9 collective-permute-start
  296.0 4.6 %collective-permute-done = bf16[2,8,1,2,128]{4,1,3,0,2:T(8,128)(2,1)S(1)} collective-permute-done((bf16[2,8,1,2,128]{4,1,3,0,2:T(8,128)(2,1)S(1)}, bf16[2,8,1,2,128]{4,1,3,0,2:T(8,128)(2,1)S(1)}, u32[]{:S(2)}, u32[]{:S(2)}) %collective-permute-start) | collective-permute-done | bytes 8224 | tf_op jit(solution)/shard_map/while/body/eval_jaxpr/ppermute | solution.py:18
  300.6 22.2 %all_gather.16 = bf16[2,8,1,32,128]{4,1,3,0,2:T(8,128)(2,1)S(1)} all-gather(bf16[2,8,1,2,128]{4,1,3,0,2:T(8,128)(2,1)S(1)} %collective-permute-done), channel_id=1, replica_groups=mesh['layer'=8,'plane'=16] {'plane'}, dimensions={3}, use_global_device_ids=true | all-gather | bytes 139264 | tf_op jit(solution)/shard_map/while/body/eval_jaxpr/all_gather | solution.py:52
  322.8 5.6 %fusion.51 = f32[2,8,1,2,128]{4,1,3,0,2:T(8,128)S(1)} fusion(f32[2,8,1,2,128]{4,1,3,0,2:T(8,128)S(1)} %get-tuple-element.85, bf16[2,2,128,2,32,128]{5,2,4,3,1,0:T(8,128)(2,1)} %get-tuple-element.84, bf16[2,8,1,32,128]{4,1,3,0,2:T(8,128)(2,1)S(1)} %all_gather.16), kind=kOutput, calls=%fused_computation.3.clone.1 | convolution fusion | flops 67117056 | bytes 8552448 | tf_op jit(solution)/shard_map/while/body/eval_jaxpr/axbcpq,crlpq->arlxb/dot_general | solution.py:35
  328.4 1.9 collective-permute-start
  330.4 4.6 %collective-permute-done = bf16[2,8,1,2,128]{4,1,3,0,2:T(8,128)(2,1)S(1)} collective-permute-done((bf16[2,8,1,2,128]{4,1,3,0,2:T(8,128)(2,1)S(1)}, bf16[2,8,1,2,128]{4,1,3,0,2:T(8,128)(2,1)S(1)}, u32[]{:S(2)}, u32[]{:S(2)}) %collective-permute-start) | collective-permute-done | bytes 8224 | tf_op jit(solution)/shard_map/while/body/eval_jaxpr/ppermute | solution.py:18
  335.0 22.5 %all_gather.16 = bf16[2,8,1,32,128]{4,1,3,0,2:T(8,128)(2,1)S(1)} all-gather(bf16[2,8,1,2,128]{4,1,3,0,2:T(8,128)(2,1)S(1)} %collective-permute-done), channel_id=1, replica_groups=mesh['layer'=8,'plane'=16] {'plane'}, dimensions={3}, use_global_device_ids=true | all-gather | bytes 139264 | tf_op jit(solution)/shard_map/while/body/eval_jaxpr/all_gather | solution.py:52
  357.4 5.6 %fusion.51 = f32[2,8,1,2,128]{4,1,3,0,2:T(8,128)S(1)} fusion(f32[2,8,1,2,128]{4,1,3,0,2:T(8,128)S(1)} %get-tuple-element.85, bf16[2,2,128,2,32,128]{5,2,4,3,1,0:T(8,128)(2,1)} %get-tuple-element.84, bf16[2,8,1,32,128]{4,1,3,0,2:T(8,128)(2,1)S(1)} %all_gather.16), kind=kOutput, calls=%fused_computation.3.clone.1 | convolution fusion | flops 67117056 | bytes 8552448 | tf_op jit(solution)/shard_map/while/body/eval_jaxpr/axbcpq,crlpq->arlxb/dot_general | solution.py:35
  363.1 0.0 copy-start.7
  363.1 2.1 collective-permute-start.1
  365.2 5.5 %collective-permute-start.2 = (bf16[2,8,1,2,128]{4,1,3,2,0:T(8,128)(2,1)S(1)}, bf16[2,8,1,2,128]{4,1,3,2,0:T(8,128)(2,1)S(1)}, u32[]{:S(2)}, u32[]{:S(2)}) collective-permute-start(bf16[2,8,1,2,128]{4,1,3,2,0:T(8,128)(2,1)S(1)} %get-tuple-element.46), channel_id=1, source_target_pairs={{16,0},{32,16},{48,32},{64,48},{80,64},{96,80},{112,96},{17,1},{33... | collective-permute-start | bytes 24584 | tf_op jit(solution)/shard_map/ppermute | solution.py:29
  370.7 0.7 fusion.34
  371.3 0.0 collective-permute-done.1
  371.3 0.1 collective-permute-done.2
  371.4 0.6 copy-done.2
  372.0 0.1 pad_maximum_fusion.1
  372.1 0.9 fusion.36
  373.0 3.2 collective-permute-start.3
  376.2 1.9 collective-permute-start.4
  378.2 25.3 %all_gather.14 = bf16[256,96]{1,0:T(8,128)(2,1)} all-gather(bf16[16,96]{1,0:T(8,128)(2,1)S(1)} %copy-done.5), channel_id=1, replica_groups=mesh['layer'=8,'plane'=16] {'plane'}, dimensions={0}, use_global_device_ids=true | all-gather | bytes 52224 | tf_op jit(solution)/shard_map/all_gather | solution.py:57
  403.5 1.6 copy.37
  405.0 0.8 convert_element_type.25
  405.8 0.8 multiply_bitcast_fusion
  406.6 0.1 pad_maximum_fusion
  406.7 2.0 copy.42
  408.7 0.0 collective-permute-done.3
  408.7 0.0 collective-permute-done.4
  408.7 1.4 maximum_convert_fusion
  410.1 0.0 copy-start.1
  410.1 1.0 fusion.35
  411.1 1.2 fusion.24
  412.3 1.0 maximum_subtract_fusion
  413.3 2.0 copy.43
  (24 shorter events, 0.1 us)
Async XLA Ops:
  7.2 3.1 copy-start
  7.2 103.2 %all-gather.2.cloned.1.call-start = ((), (), s32[]{:S(2)}) async-start(), calls=%async_computation | async-start | bytes 13230080 | tf_op jit(solution)/shard_map/all_gather | solution.py:45
  121.3 6.5 %collective-permute-start = (bf16[2,8,1,2,128]{4,1,3,0,2:T(8,128)(2,1)S(1)}, bf16[2,8,1,2,128]{4,1,3,0,2:T(8,128)(2,1)S(1)}, u32[]{:S(2)}, u32[]{:S(2)}) collective-permute-start(bf16[2,8,1,2,128]{4,1,3,0,2:T(8,128)(2,1)S(1)} %convert_element_type.39), channel_id=1, source_target_pairs={{0,16},{16,32},{32,48},{48,64},{64,80},{80,96},{96,112},{1,17},{17... | collective-permute-start | bytes 24584 | tf_op jit(solution)/shard_map/while/body/eval_jaxpr/ppermute | solution.py:18
  156.1 6.5 %collective-permute-start = (bf16[2,8,1,2,128]{4,1,3,0,2:T(8,128)(2,1)S(1)}, bf16[2,8,1,2,128]{4,1,3,0,2:T(8,128)(2,1)S(1)}, u32[]{:S(2)}, u32[]{:S(2)}) collective-permute-start(bf16[2,8,1,2,128]{4,1,3,0,2:T(8,128)(2,1)S(1)} %convert_element_type.39), channel_id=1, source_target_pairs={{0,16},{16,32},{32,48},{48,64},{64,80},{80,96},{96,112},{1,17},{17... | collective-permute-start | bytes 24584 | tf_op jit(solution)/shard_map/while/body/eval_jaxpr/ppermute | solution.py:18
  190.5 6.5 %collective-permute-start = (bf16[2,8,1,2,128]{4,1,3,0,2:T(8,128)(2,1)S(1)}, bf16[2,8,1,2,128]{4,1,3,0,2:T(8,128)(2,1)S(1)}, u32[]{:S(2)}, u32[]{:S(2)}) collective-permute-start(bf16[2,8,1,2,128]{4,1,3,0,2:T(8,128)(2,1)S(1)} %convert_element_type.39), channel_id=1, source_target_pairs={{0,16},{16,32},{32,48},{48,64},{64,80},{80,96},{96,112},{1,17},{17... | collective-permute-start | bytes 24584 | tf_op jit(solution)/shard_map/while/body/eval_jaxpr/ppermute | solution.py:18
  225.1 6.5 %collective-permute-start = (bf16[2,8,1,2,128]{4,1,3,0,2:T(8,128)(2,1)S(1)}, bf16[2,8,1,2,128]{4,1,3,0,2:T(8,128)(2,1)S(1)}, u32[]{:S(2)}, u32[]{:S(2)}) collective-permute-start(bf16[2,8,1,2,128]{4,1,3,0,2:T(8,128)(2,1)S(1)} %convert_element_type.39), channel_id=1, source_target_pairs={{0,16},{16,32},{32,48},{48,64},{64,80},{80,96},{96,112},{1,17},{17... | collective-permute-start | bytes 24584 | tf_op jit(solution)/shard_map/while/body/eval_jaxpr/ppermute | solution.py:18
  259.4 6.5 %collective-permute-start = (bf16[2,8,1,2,128]{4,1,3,0,2:T(8,128)(2,1)S(1)}, bf16[2,8,1,2,128]{4,1,3,0,2:T(8,128)(2,1)S(1)}, u32[]{:S(2)}, u32[]{:S(2)}) collective-permute-start(bf16[2,8,1,2,128]{4,1,3,0,2:T(8,128)(2,1)S(1)} %convert_element_type.39), channel_id=1, source_target_pairs={{0,16},{16,32},{32,48},{48,64},{64,80},{80,96},{96,112},{1,17},{17... | collective-permute-start | bytes 24584 | tf_op jit(solution)/shard_map/while/body/eval_jaxpr/ppermute | solution.py:18
  294.1 6.5 %collective-permute-start = (bf16[2,8,1,2,128]{4,1,3,0,2:T(8,128)(2,1)S(1)}, bf16[2,8,1,2,128]{4,1,3,0,2:T(8,128)(2,1)S(1)}, u32[]{:S(2)}, u32[]{:S(2)}) collective-permute-start(bf16[2,8,1,2,128]{4,1,3,0,2:T(8,128)(2,1)S(1)} %convert_element_type.39), channel_id=1, source_target_pairs={{0,16},{16,32},{32,48},{48,64},{64,80},{80,96},{96,112},{1,17},{17... | collective-permute-start | bytes 24584 | tf_op jit(solution)/shard_map/while/body/eval_jaxpr/ppermute | solution.py:18
  328.4 6.5 %collective-permute-start = (bf16[2,8,1,2,128]{4,1,3,0,2:T(8,128)(2,1)S(1)}, bf16[2,8,1,2,128]{4,1,3,0,2:T(8,128)(2,1)S(1)}, u32[]{:S(2)}, u32[]{:S(2)}) collective-permute-start(bf16[2,8,1,2,128]{4,1,3,0,2:T(8,128)(2,1)S(1)} %convert_element_type.39), channel_id=1, source_target_pairs={{0,16},{16,32},{32,48},{48,64},{64,80},{80,96},{96,112},{1,17},{17... | collective-permute-start | bytes 24584 | tf_op jit(solution)/shard_map/while/body/eval_jaxpr/ppermute | solution.py:18
  363.0 7.6 %copy-start.4 = (s32[8,256]{1,0:T(8,128)S(1)}, s32[8,256]{1,0:T(8,128)}, u32[]{:S(2)}) copy-start(s32[8,256]{1,0:T(8,128)} %param.15) | copy-start | bytes 24580
  363.0 7.6 %copy-start.6 = (s32[256]{0:T(256)S(1)}, s32[256]{0:T(256)}, u32[]{:S(2)}) copy-start(s32[256]{0:T(256)} %param.13) | copy-start | bytes 3076
  363.1 7.6 %copy-start.7 = (s32[8]{0:T(128)S(1)}, s32[8]{0:T(128)}, u32[]{:S(2)}) copy-start(s32[8]{0:T(128)} %param.14) | copy-start | bytes 100
  363.1 8.3 %collective-permute-start.1 = (bf16[2,8,1,2,128]{4,1,3,2,0:T(8,128)(2,1)S(1)}, bf16[2,8,1,2,128]{4,1,3,2,0:T(8,128)(2,1)S(1)}, u32[]{:S(2)}, u32[]{:S(2)}) collective-permute-start(bf16[2,8,1,2,128]{4,1,3,2,0:T(8,128)(2,1)S(1)} %get-tuple-element.45), channel_id=1, source_target_pairs={{0,16},{16,32},{32,48},{48,64},{64,80},{80,96},{96,112},{1,17},{17... | collective-permute-start | bytes 24584 | tf_op jit(solution)/shard_map/ppermute | solution.py:28
  365.2 6.3 %collective-permute-start.2 = (bf16[2,8,1,2,128]{4,1,3,2,0:T(8,128)(2,1)S(1)}, bf16[2,8,1,2,128]{4,1,3,2,0:T(8,128)(2,1)S(1)}, u32[]{:S(2)}, u32[]{:S(2)}) collective-permute-start(bf16[2,8,1,2,128]{4,1,3,2,0:T(8,128)(2,1)S(1)} %get-tuple-element.46), channel_id=1, source_target_pairs={{16,0},{32,16},{48,32},{64,48},{80,64},{96,80},{112,96},{17,1},{33... | collective-permute-start | bytes 24584 | tf_op jit(solution)/shard_map/ppermute | solution.py:29
  371.3 6.8 %copy-start.5 = (bf16[16,96]{1,0:T(8,128)(2,1)S(1)}, bf16[16,96]{1,0:T(8,128)(2,1)}, u32[]{:S(2)}) copy-start(bf16[16,96]{1,0:T(8,128)(2,1)} %param.12) | copy-start | bytes 9220
  371.4 0.6 copy-start.2
  373.0 35.7 %collective-permute-start.3 = (bf16[2,8,98,1,128]{4,1,3,2,0:T(8,128)(2,1)}, bf16[2,8,98,1,128]{4,1,3,2,0:T(8,128)(2,1)}, u32[]{:S(2)}, u32[]{:S(2)}) collective-permute-start(bf16[2,8,98,1,128]{4,1,3,2,0:T(8,128)(2,1)} %get-tuple-element.43), channel_id=1, source_target_pairs={{0,1},{1,2},{2,3},{3,4},{4,5},{5,6},{6,7},{7,8},{8,9},{9,10},{10,1... | collective-permute-start | bytes 1204232 | tf_op jit(solution)/shard_map/ppermute | solution.py:28
  376.2 32.4 %collective-permute-start.4 = (bf16[2,8,98,1,128]{4,1,3,2,0:T(8,128)(2,1)S(1)}, bf16[2,8,98,1,128]{4,1,3,2,0:T(8,128)(2,1)}, u32[]{:S(2)}, u32[]{:S(2)}) collective-permute-start(bf16[2,8,98,1,128]{4,1,3,2,0:T(8,128)(2,1)S(1)} %get-tuple-element.44), channel_id=1, source_target_pairs={{1,0},{2,1},{3,2},{4,3},{5,4},{6,5},{7,6},{8,7},{9,8},{10,9},{11,1... | collective-permute-start | bytes 1204232 | tf_op jit(solution)/shard_map/ppermute | solution.py:29
  406.7 2.0 copy-start.3
  410.1 1.0 copy-start.1
Sparse Core Ops, SparseCore 0:
  10.9 99.3 all-gather.1
where the time goes:
time: 426 us; the launch traced here: 422 us
  blocking collectives  205 us (48%)
  waiting for transfers between devices  84.2 us (20%)
  matrix products  63.1 us (15%)
  starting transfers between devices  27.4 us (6%)
  local copies, waits for them, and re-layouts  22 us (5%)
  between operations  14.2 us (3%)
  other arithmetic  5.9 us (1%)
    all_gather x7, blocking collectives, sweep_step(): coupled = fold_rows(lax.all_gather(incoming, 'plane', axis=3, tiled=True))  157 us
    dot_general x9, matrix products, apply_front(): jnp.einsum('axbcpq,crlpq->arlxb', blocks, piece, preferred_element_type=j...  61.9 us
    all_gather x1, waiting for transfers between devices, shards(): lax.all_gather(rounded[:, :, 1:], 'plane', axis=3, tiled=True)  53.3 us
    ppermute x7, waiting for transfers between devices, shifted(): return lax.ppermute(value, axis, pairs)  30.8 us
    all_gather x1, blocking collectives, shards(): profile = lax.all_gather(mode_profile, 'plane', axis=0, tiled=True)  25.3 us
    all_gather x1, blocking collectives, shards(): lax.all_gather(rounded[:, :, :1], 'plane', axis=3, tiled=True)  23.1 us
    unnamed x22, local copies, waits for them, and re-layouts  17.5 us
    ppermute x7, starting transfers between devices, shifted(): return lax.ppermute(value, axis, pairs)  14.7 us
  transfers between devices with their start and end apart: 12, of which 9 were waited for; matrix products, arithmetic and copies ran while one was open for 7% of the time, Pallas kernels for 0%

commit v1 on v0

v1 whole, which is shorter than its diff:
```python
import jax
import jax.numpy as jnp
from jax import lax
from jax.experimental import pallas as pl
from jax.experimental.pallas import tpu as pltpu
from jax.sharding import PartitionSpec as P

MODES = 256
NPTS = 32768
COUPLING = 0.8
ABSORB_RATE = 0.3
WAVE_SCALE = 0.8

G = 8
D = 16
LZ = 96
R = 8
K = 512
NY = 128

bf16 = jnp.bfloat16
f32 = jnp.float32
VMEM = pltpu.VMEM


def whole(space=VMEM):
    return pl.BlockSpec(memory_space=space)


def params(mib):
    return pltpu.CompilerParams(vmem_limit_bytes=mib * 2**20)


def dot_t(x, h):
    return lax.dot_general(x, h, (((1,), (1,)), ((), ())), preferred_element_type=f32)


def prepare_kernel(rhs_ref, profile_ref, x_ref, chunk_ref):
    chunk_ref[0] = jnp.zeros((32, K), bf16)
    for a in range(2):
        for x in range(2):
            cols = pl.ds(a * 256 + x * NY, NY)
            for r in range(R):
                x_ref[pl.ds(r * LZ, LZ), cols] = rhs_ref[a, r, pl.ds(x, LZ, stride=2), :].astype(bf16)
    head = jnp.concatenate([rhs_ref[a, :, x, :] for a in range(2) for x in range(2)], axis=1)
    profile = jnp.concatenate([profile_ref[...], jnp.zeros((16, K - LZ), bf16)], axis=1)
    chunk = jnp.concatenate([head, jnp.zeros((8, K), f32)], axis=0).astype(bf16)
    for i in range(D):
        chunk_ref[i, pl.ds(0, 16), :] = chunk
        chunk_ref[i, pl.ds(16, 16), :] = profile


def prepare(rhs, profile):
    return pl.pallas_call(
        prepare_kernel,
        out_shape=(jax.ShapeDtypeStruct((R * LZ, K), bf16), jax.ShapeDtypeStruct((D, 32, K), bf16)),
        in_specs=[whole(), whole()],
        out_specs=(whole(), whole()),
        compiler_params=params(8),
    )(rhs, profile)


def arrange_kernel(blocks_ref, out_ref):
    m = lax.broadcasted_iota(jnp.int32, (256, 256), 0)
    n = lax.broadcasted_iota(jnp.int32, (256, 256), 1)
    swap = ((m // 16 == n % 16) & (m % 16 == n // 16)).astype(f32).astype(bf16)

    def body(b_ref):
        base = pl.multiple_of(pl.program_id(0) * 32, 32)
        for s in range(2):
            for c in range(2):
                for half in range(2):
                    tile = b_ref[pl.ds(s * 16, 16), c, pl.ds(half * 16, 16), :].reshape(256, NY)
                    moved = jnp.dot(swap, tile, preferred_element_type=f32).astype(bf16)
                    for q in range(16):
                        p = half * 16 + q
                        out_ref[p // 2, pl.ds(base + s * 16, 16), pl.ds(c * 256 + (p % 2) * NY, NY)] = moved[
                            q * 16 : (q + 1) * 16
                        ]

    pltpu.emit_pipeline(
        body, grid=(K // 32,), in_specs=[pl.BlockSpec((32, 2, 32, NY), lambda i: (i, 0, 0, 0))]
    )(blocks_ref)


def arrange(blocks):
    return pl.pallas_call(
        arrange_kernel,
        out_shape=jax.ShapeDtypeStruct((D, K, K), bf16),
        in_specs=[whole(pl.ANY)],
        out_specs=whole(),
        compiler_params=params(14),
        cost_estimate=pl.CostEstimate(flops=2 * 10**9, bytes_accessed=17 * 10**6, transcendentals=0),
    )(blocks)


def first_kernel(h_ref, x_ref, v_ref, out_ref):
    acc = jnp.zeros((16, K), f32)
    for i in range(D):
        acc = acc + dot_t(x_ref[i, pl.ds(0, 16), :], h_ref[i])
    v = acc[:R]
    v_ref[...] = v
    for i in range(2 * D):
        out_ref[i] = v.astype(bf16)


def step_kernel(mine_ref, h_ref, x_ref, base_ref, old_ref, v_ref, out_ref):
    acc = jnp.zeros((R, K), f32)
    for i in range(D):
        acc = acc + dot_t(x_ref[i], h_ref[i])
    v = jnp.where(mine_ref[0] > 0, base_ref[...] + COUPLING * acc, old_ref[...])
    v_ref[...] = v
    for i in range(2 * D):
        out_ref[i] = v.astype(bf16)


MATVEC_OUT = (jax.ShapeDtypeStruct((R, K), f32), jax.ShapeDtypeStruct((2 * D, R, K), bf16))
MATVEC_COST = pl.CostEstimate(flops=10**8, bytes_accessed=8 * 10**6, transcendentals=0)


def first_product(h, x):
    return pl.pallas_call(
        first_kernel,
        out_shape=MATVEC_OUT,
        in_specs=[whole()] * 2,
        out_specs=(whole(), whole()),
        compiler_params=params(12),
        cost_estimate=MATVEC_COST,
    )(h, x)


def step_product(mine, h, x, base, old):
    return pl.pallas_call(
        step_kernel,
        out_shape=MATVEC_OUT,
        in_specs=[whole(pltpu.SMEM)] + [whole()] * 4,
        out_specs=(whole(), whole()),
        compiler_params=params(12),
        cost_estimate=MATVEC_COST,
    )(mine, h, x, base, old)


def fronts_kernel(x_ref, h_ref, y_ref, low_ref, high_ref, last_ref):
    acc = jnp.zeros((2 * LZ, K), f32)
    for i in range(D):
        acc = acc + dot_t(x_ref[i], h_ref[i])
    acc = acc.reshape(2, LZ, K)
    y_ref[...] = acc
    for r in range(2):
        for a in range(2):
            low_ref[r, a] = acc[r, :, a * 256 : a * 256 + NY].astype(bf16)
            high_ref[r, a] = acc[r, :, a * 256 + NY : a * 256 + 256].astype(bf16)
        last_ref[r] = acc[r, LZ - 16 :, :].astype(bf16)


def fronts_of(x, h, part):
    return pl.pallas_call(
        fronts_kernel,
        grid=(2,),
        out_shape=(
            jax.ShapeDtypeStruct((4, LZ, K), f32),
            jax.ShapeDtypeStruct((4, 2, LZ, NY), bf16),
            jax.ShapeDtypeStruct((4, 2, LZ, NY), bf16),
            jax.ShapeDtypeStruct((4, 16, K), bf16),
        ),
        in_specs=[pl.BlockSpec((D, 2 * LZ, K), lambda i: (0, 2 * part + i, 0)), whole()],
        out_specs=(
            pl.BlockSpec((2, LZ, K), lambda i: (i, 0, 0)),
            pl.BlockSpec((2, 2, LZ, NY), lambda i: (i, 0, 0, 0)),
            pl.BlockSpec((2, 2, LZ, NY), lambda i: (i, 0, 0, 0)),
            pl.BlockSpec((2, 16, K), lambda i: (i, 0, 0)),
        ),
        compiler_params=params(18),
        cost_estimate=pl.CostEstimate(flops=3 * 10**9, bytes_accessed=15 * 10**6, transcendentals=0),
    )(x, h)


def wave_kernel(x_ref, coef_ref, panel_ref, out_ref):
    profile = jnp.concatenate([x_ref[i, pl.ds(16, 16), :][:, :LZ] for i in range(D)], axis=0).astype(f32)
    panel = panel_ref[...]
    for r in range(R):
        weights = profile * coef_ref[:, r : r + 1]
        log = jnp.zeros((LZ, 256), f32)
        for _ in range(3):
            term = weights.astype(bf16)
            weights = weights - term.astype(f32)
            log = log + lax.dot_general(term, panel, (((0,), (0,)), ((), ())), preferred_element_type=f32)
        out_ref[r] = WAVE_SCALE * jnp.exp(-2.0 * log)


def wave(x, coef, panel):
    return pl.pallas_call(
        wave_kernel,
        out_shape=jax.ShapeDtypeStruct((R, LZ, 256), f32),
        in_specs=[whole()] * 3,
        out_specs=whole(),
        compiler_params=params(8),
        cost_estimate=pl.CostEstimate(flops=3 * 10**8, bytes_accessed=2 * 10**6, transcendentals=2 * 10**5),
    )(x, coef, panel)


def residual_kernel(ya, yb, rhs_ref, la, lb, ha, hb, pa, pb, v_ref, nl_ref, vl_ref, vh_ref, wave_ref, sol_ref, res_ref):
    row = lax.broadcasted_iota(jnp.int32, (LZ, NY), 0)
    lane = lax.broadcasted_iota(jnp.int32, (LZ, NY), 1)
    for r in range(R):
        y_ref, low_ref, high_ref, prev_ref = (ya, la, ha, pa) if r < 4 else (yb, lb, hb, pb)
        k = r % 4
        s = {}
        for a in range(2):
            for x in range(2):
                cols = slice(a * 256 + x * NY, a * 256 + (x + 1) * NY)
                s[a, x] = jnp.where(row == 0, v_ref[r : r + 1, cols], y_ref[k, :, cols])
        lap = {}
        for a in range(2):
            below = jnp.where(row == 0, vl_ref[r : r + 1, a * NY : (a + 1) * NY].astype(f32), low_ref[k, a].astype(f32))
            above = jnp.where(row == 0, vh_ref[r : r + 1, a * NY : (a + 1) * NY].astype(f32), high_ref[k, a].astype(f32))
            for x in range(2):
                cols = slice(a * 256 + x * NY, a * 256 + (x + 1) * NY)
                own = s[a, x]
                before = jnp.where(row == 0, prev_ref[k, :, cols][15:16].astype(f32), pltpu.roll(own, 1, 0))
                after = jnp.where(row == LZ - 1, nl_ref[r : r + 1, cols].astype(f32), pltpu.roll(own, LZ - 1, 0))
                left = jnp.where(lane == 0, 0.0, pltpu.roll(own, 1, 1))
                right = jnp.where(lane == NY - 1, 0.0, pltpu.roll(own, NY - 1, 1))
                beside = before + after + left + right
                beside = beside + (below if x == 0 else s[a, 0]) + (s[a, 1] if x == 0 else above)
                lap[a, x] = 6.0 * own - beside
        for x in range(2):
            w = wave_ref[r, :, x * NY : (x + 1) * NY]
            rows = pl.ds(x, LZ, stride=2)
            real = lap[0, x] - w * s[0, x] + ABSORB_RATE * w * s[1, x]
            imag = lap[1, x] - w * s[1, x] - ABSORB_RATE * w * s[0, x]
            sol_ref[0, r, rows, :] = s[0, x]
            sol_ref[1, r, rows, :] = s[1, x]
            res_ref[0, r, rows, :] = rhs_ref[0, r, rows, :] - real
            res_ref[1, r, rows, :] = rhs_ref[1, r, rows, :] - imag


def residual(*args):
    shape = jax.ShapeDtypeStruct((2, R, 2 * LZ, NY), f32)
    return pl.pallas_call(
        residual_kernel,
        out_shape=(shape, shape),
        in_specs=[whole()] * len(args),
        out_specs=(whole(), whole()),
        compiler_params=params(24),
    )(*args)


def pair_groups(step):
    groups = []
    for k in range(G // 2):
        first = (2 * k + step - 1) % G
        second = (first + 1) % G
        groups.append([first * D + i for i in range(D)] + [second * D + i for i in range(D)])
    return groups


def shift(value, axis, by):
    size = lax.axis_size(axis)
    return lax.ppermute(value, axis, [(i, i + by) for i in range(size) if 0 <= i + by < size])


def shards(rhs, inverse_blocks, mode_panel, mode_profile, generator, lattice_index, shift_index):
    group = lax.axis_index("layer")
    flat = rhs.reshape(2, R, 2 * LZ, NY)
    own, chunk = prepare(flat, mode_profile)
    gathered = lax.all_gather(own, "plane", axis=0)
    heads = lax.all_to_all(chunk, "plane", 0, 0)
    h = arrange(inverse_blocks.reshape(K, 2, 32, NY))

    mixed = (lattice_index[None, :] * generator[:, None] + shift_index.T) % NPTS
    amplitude = 0.25 / jnp.sqrt(1.0 + jnp.arange(MODES, dtype=f32) / 8.0)
    coef = amplitude[:, None] * ((mixed.astype(f32) + 0.5) / NPTS - 0.5)
    wavenum = wave(heads, coef, mode_panel.reshape(MODES, 256))

    base, out = first_product(h, heads)
    v = base
    for step in range(1, G):
        got = lax.all_to_all(out, ("layer", "plane"), 0, 0, axis_index_groups=pair_groups(step))
        mine = (group == step).astype(jnp.int32).reshape(1)
        v, out = step_product(mine, h, got, base, v)

    ya, sla, sha, ta = fronts_of(gathered, h, 0)
    yb, slb, shb, tb = fronts_of(gathered, h, 1)
    la, lb = shift(sha, "plane", 1), shift(shb, "plane", 1)
    ha, hb = shift(sla, "plane", -1), shift(slb, "plane", -1)
    pa, pb = shift(ta, "layer", 1), shift(tb, "layer", 1)
    vb = v.astype(bf16)
    nl = shift(vb, "layer", -1)
    vl = shift(jnp.concatenate([vb[:, NY : 2 * NY], vb[:, 3 * NY :]], axis=1), "plane", 1)
    vh = shift(jnp.concatenate([vb[:, :NY], vb[:, 2 * NY : 3 * NY]], axis=1), "plane", -1)
    sol, res = residual(ya, yb, flat, la, lb, ha, hb, pa, pb, v, nl, vl, vh, wavenum)
    return sol.reshape(rhs.shape), res.reshape(rhs.shape)


def solution(mesh):
    return jax.shard_map(
        shards,
        mesh=mesh,
        in_specs=(
            P(None, None, "layer", "plane", None),
            P("layer", None, "plane", None, None, None, None),
            P(None, "plane", None),
            P("plane", "layer"),
            P(),
            P(),
            P(),
        ),
        out_specs=(P(None, None, "layer", "plane", None), P(None, None, "layer", "plane", None)),
        check_vma=False,
    )
```

time: 426 us -> 268 us (0.63)
  blocking collectives: 205 us -> 0 us
  starting transfers between devices: 27.4 us -> 102 us
  matrix products: 63.1 us -> 0 us
  Pallas kernels: 0 us -> 48.9 us
  waiting for transfers between devices: 84.2 us -> 54.8 us
  local copies, waits for them, and re-layouts: 22 us -> 44 us
  other arithmetic: 5.9 us -> 0.18 us
    all_gather x9 -> x0, blocking collectives: 205 us -> none  [the longest x7 157 us: sweep_step(): coupled = fold_rows(lax.all_gather(incoming, 'plane', axis=3, tiled=True))]
    all_to_all x0 -> x8, starting transfers between devices: none -> 74.5 us  [the longest x7 65.9 us: shards(): lax.all_to_all(out, ('layer', 'plane'), 0, 0, axis_index_groups=pair_grou...]
    dot_general x10 -> x0, matrix products: 63.1 us -> none  [the longest x9 61.9 us: apply_front(): jnp.einsum('axbcpq,crlpq->arlxb', blocks, piece, preferred_element_type=j...]
    all_gather x1, waiting for transfers between devices: 53.3 us -> 0.02 us  [shards(): gathered = lax.all_gather(own, 'plane', axis=0)]
    all_to_all x0 -> x8, waiting for transfers between devices: none -> 51.9 us  [the longest x7 51.9 us: shards(): lax.all_to_all(out, ('layer', 'plane'), 0, 0, axis_index_groups=pair_grou...]
    pallas_call x0 -> x14, Pallas kernels: none -> 48.9 us  [the longest x7 20.9 us: step_product(): pl.pallas_call(step_kernel, out_shape=MATVEC_OUT, in_specs=[whole(pltpu.S...]
    ppermute x11 -> x9, waiting for transfers between devices: 30.9 us -> 2.84 us  [shift(): lax.ppermute(value, axis, [(i, i + by) for i in range(size) if 0 <= i + b...]
    unnamed x22 -> x40, local copies, waits for them, and re-layouts: 17.5 us -> 44 us
  transfers between devices with their start and end apart: 12 -> 18, of which waited for: 9 -> 9; matrix products, arithmetic and copies ran while one was open for 7% -> 0% of each run, Pallas kernels for 0% -> 17%
where the time goes in v1:
time: 268 us; the launch traced here: 265 us
  starting transfers between devices  102 us (38%)
  waiting for transfers between devices  54.8 us (20%)
  Pallas kernels  48.9 us (18%)
  local copies, waits for them, and re-layouts  44 us (16%)
  between operations  14.4 us (5%)
    all_to_all x7, starting transfers between devices, shards(): lax.all_to_all(out, ('layer', 'plane'), 0, 0, axis_index_groups=pair_grou...  65.9 us
    all_to_all x7, waiting for transfers between devices, shards(): lax.all_to_all(out, ('layer', 'plane'), 0, 0, axis_index_groups=pair_grou...  51.9 us
    unnamed x40, local copies, waits for them, and re-layouts  44 us
    ppermute x9, starting transfers between devices, shift(): lax.ppermute(value, axis, [(i, i + by) for i in range(size) if 0 <= i + b...  27.7 us
    pallas_call x7, Pallas kernels, step_product(): pl.pallas_call(step_kernel, out_shape=MATVEC_OUT, in_specs=[whole(pltpu.S...  20.9 us
    pallas_call x2, Pallas kernels, fronts_of(): pl.pallas_call(fronts_kernel, grid=(2,), out_shape=(jax.ShapeDtypeStruct(...  12.3 us
    all_to_all x1, starting transfers between devices, shards(): heads = lax.all_to_all(chunk, 'plane', 0, 0)  8.62 us
    pallas_call x1, Pallas kernels, arrange(): pl.pallas_call(arrange_kernel, out_shape=jax.ShapeDtypeStruct((D, K, K),...  7.46 us
  transfers between devices with their start and end apart: 18, of which 9 were waited for; matrix products, arithmetic and copies ran while one was open for 0% of the time, Pallas kernels for 17%

profile of v1, /device:TPU:7, one launch (start us, length us, event | category | flops | bytes accessed | tf_op | source)
XLA Modules:
  0.0 264.5 jit_solution(1362054790093347962)
XLA Ops:
  7.2 0.0 all-gather.3.cloned.1.call-start
  7.2 0.0 copy-start.12
  7.2 1.4 copy-done.12
  8.6 0.7 copy-done.14
  9.3 1.2 shard_map.86
  10.5 0.0 all-gather.3.cloned.1.call-update
  10.5 8.6 %all-to-all-start = ((bf16[16,32,512]{2,1,0:T(8,128)(2,1)}), bf16[16,32,512]{2,1,0:T(8,128)(2,1)S(1)}, u32[]{:S(2)}, u32[]{:S(2)}) async-start(bf16[16,32,512]{2,1,0:T(8,128)(2,1)} %get-tuple-element.38), calls=%async_computation | async-start | bytes 1048576 | tf_op jit(solution)/shard_map/all_to_all | solution.py:268
  19.2 3.4 %copy-done.11 = bf16[1,2,2,128,2,32,128]{6,5,4,3,2,1,0:T(8,128)(2,1)S(1)} copy-done((bf16[1,2,2,128,2,32,128]{6,5,4,3,2,1,0:T(8,128)(2,1)S(1)}, bf16[1,2,2,128,2,32,128]{6,5,4,3,2,1,0:T(8,128)(2,1)}, u32[]{:S(2)}) %copy-start.11) | copy-done | bytes 8388632
  22.5 7.5 %shard_map.87.h_ref = bf16[16,512,512]{2,1,0:T(8,128)(2,1)S(1)} custom-call(bf16[512,2,32,128]{3,2,1,0:T(8,128)(2,1)S(1)} %bitcast.24), custom_call_target="tpu_custom_call" | custom-call | flops 2000000000 | bytes 17000000 | tf_op jit(solution)/shard_map/pallas_call | solution.py:87
  30.0 3.2 %copy-done = bf16[16,512,512]{2,1,0:T(8,128)(2,1)} copy-done((bf16[16,512,512]{2,1,0:T(8,128)(2,1)}, bf16[16,512,512]{2,1,0:T(8,128)(2,1)S(1)}, u32[]{:S(2)}) %copy-start) | copy-done | bytes 8388632
  33.2 3.5 %copy-done.1 = bf16[16,512,512]{2,1,0:T(8,128)(2,1)S(1)} copy-done((bf16[16,512,512]{2,1,0:T(8,128)(2,1)S(1)}, bf16[16,512,512]{2,1,0:T(8,128)(2,1)}, u32[]{:S(2)}) %copy-start.1) | copy-done | bytes 8388632
  36.7 3.0 %shard_map.90 = (f32[8,512]{1,0:T(8,128)S(1)}, bf16[32,8,512]{2,1,0:T(8,128)(2,1)}) custom-call(bf16[16,512,512]{2,1,0:T(8,128)(2,1)S(1)} %copy-done.1, bf16[16,32,512]{2,1,0:T(8,128)(2,1)S(1)} %all-to-all-done.x_ref), custom_call_target="tpu_custom_call" | custom-call | flops 100000000 | bytes 8000000 | tf_op jit(solution)/shard_map/pallas_call | solution.py:122
  39.7 8.3 %all-to-all-start.1 = ((bf16[32,8,512]{2,1,0:T(8,128)(2,1)}), bf16[32,8,512]{2,1,0:T(8,128)(2,1)S(1)}, u32[]{:S(2)}, u32[]{:S(2)}) async-start(bf16[32,8,512]{2,1,0:T(8,128)(2,1)} %get-tuple-element.39), calls=%async_computation.1 | async-start | bytes 524288 | tf_op jit(solution)/shard_map/all_to_all | solution.py:279
  48.1 7.3 %all-to-all-done.1.x_ref = bf16[32,8,512]{2,1,0:T(8,128)(2,1)S(1)} async-done(((bf16[32,8,512]{2,1,0:T(8,128)(2,1)}), bf16[32,8,512]{2,1,0:T(8,128)(2,1)S(1)}, u32[]{:S(2)}, u32[]{:S(2)}) %all-to-all-start.1) | async-done | bytes 262176 | tf_op jit(solution)/shard_map/all_to_all | solution.py:279
  55.3 3.4 %copy-done.2 = bf16[16,512,512]{2,1,0:T(8,128)(2,1)S(1)} copy-done((bf16[16,512,512]{2,1,0:T(8,128)(2,1)S(1)}, bf16[16,512,512]{2,1,0:T(8,128)(2,1)}, u32[]{:S(2)}) %copy-start.2) | copy-done | bytes 8388632
  58.7 3.0 %shard_map.91 = (f32[8,512]{1,0:T(8,128)S(1)}, bf16[32,8,512]{2,1,0:T(8,128)(2,1)}) custom-call(s32[1]{0:T(128)} %bitcast.9.mine_ref, bf16[16,512,512]{2,1,0:T(8,128)(2,1)S(1)} %copy-done.2, bf16[32,8,512]{2,1,0:T(8,128)(2,1)S(1)} %all-to-all-done.1.x_ref, f32[8,512]{1,0:T(8,128)S(1)} %get-tuple-element.40.base_ref.old_ref, ...), custom_call_target="tpu_custom_call" | custom-call | flops 100000000 | bytes 8000000 | tf_op jit(solution)/shard_map/pallas_call | solution.py:133
  61.7 8.2 %all-to-all-start.2 = ((bf16[32,8,512]{2,1,0:T(8,128)(2,1)}), bf16[32,8,512]{2,1,0:T(8,128)(2,1)S(1)}, u32[]{:S(2)}, u32[]{:S(2)}) async-start(bf16[32,8,512]{2,1,0:T(8,128)(2,1)} %get-tuple-element.41), calls=%async_computation.2 | async-start | bytes 524288 | tf_op jit(solution)/shard_map/all_to_all | solution.py:279
  69.9 9.7 %all-to-all-done.2.x_ref = bf16[32,8,512]{2,1,0:T(8,128)(2,1)S(1)} async-done(((bf16[32,8,512]{2,1,0:T(8,128)(2,1)}), bf16[32,8,512]{2,1,0:T(8,128)(2,1)S(1)}, u32[]{:S(2)}, u32[]{:S(2)}) %all-to-all-start.2) | async-done | bytes 262176 | tf_op jit(solution)/shard_map/all_to_all | solution.py:279
  79.6 3.4 %copy-done.3 = bf16[16,512,512]{2,1,0:T(8,128)(2,1)S(1)} copy-done((bf16[16,512,512]{2,1,0:T(8,128)(2,1)S(1)}, bf16[16,512,512]{2,1,0:T(8,128)(2,1)}, u32[]{:S(2)}) %copy-start.3) | copy-done | bytes 8388632
  83.0 3.0 %shard_map.92 = (f32[8,512]{1,0:T(8,128)S(1)}, bf16[32,8,512]{2,1,0:T(8,128)(2,1)}) custom-call(s32[1]{0:T(128)} %bitcast.8.mine_ref, bf16[16,512,512]{2,1,0:T(8,128)(2,1)S(1)} %copy-done.3, bf16[32,8,512]{2,1,0:T(8,128)(2,1)S(1)} %all-to-all-done.2.x_ref, f32[8,512]{1,0:T(8,128)S(1)} %get-tuple-element.40.base_ref.old_ref, ...), custom_call_target="tpu_custom_call" | custom-call | flops 100000000 | bytes 8000000 | tf_op jit(solution)/shard_map/pallas_call | solution.py:133
  86.0 6.5 %all-to-all-start.3 = ((bf16[32,8,512]{2,1,0:T(8,128)(2,1)}), bf16[32,8,512]{2,1,0:T(8,128)(2,1)S(1)}, u32[]{:S(2)}, u32[]{:S(2)}) async-start(bf16[32,8,512]{2,1,0:T(8,128)(2,1)} %get-tuple-element.43), calls=%async_computation.3 | async-start | bytes 524288 | tf_op jit(solution)/shard_map/all_to_all | solution.py:279
  92.5 7.2 %all-to-all-done.3.x_ref = bf16[32,8,512]{2,1,0:T(8,128)(2,1)S(1)} async-done(((bf16[32,8,512]{2,1,0:T(8,128)(2,1)}), bf16[32,8,512]{2,1,0:T(8,128)(2,1)S(1)}, u32[]{:S(2)}, u32[]{:S(2)}) %all-to-all-start.3) | async-done | bytes 262176 | tf_op jit(solution)/shard_map/all_to_all | solution.py:279
  99.6 3.4 %copy-done.4 = bf16[16,512,512]{2,1,0:T(8,128)(2,1)S(1)} copy-done((bf16[16,512,512]{2,1,0:T(8,128)(2,1)S(1)}, bf16[16,512,512]{2,1,0:T(8,128)(2,1)}, u32[]{:S(2)}) %copy-start.4) | copy-done | bytes 8388632
  103.0 3.0 %shard_map.93 = (f32[8,512]{1,0:T(8,128)S(1)}, bf16[32,8,512]{2,1,0:T(8,128)(2,1)}) custom-call(s32[1]{0:T(128)} %bitcast.7.mine_ref, bf16[16,512,512]{2,1,0:T(8,128)(2,1)S(1)} %copy-done.4, bf16[32,8,512]{2,1,0:T(8,128)(2,1)S(1)} %all-to-all-done.3.x_ref, f32[8,512]{1,0:T(8,128)S(1)} %get-tuple-element.40.base_ref.old_ref, ...), custom_call_target="tpu_custom_call" | custom-call | flops 100000000 | bytes 8000000 | tf_op jit(solution)/shard_map/pallas_call | solution.py:133
  106.0 9.3 %all-to-all-start.4 = ((bf16[32,8,512]{2,1,0:T(8,128)(2,1)}), bf16[32,8,512]{2,1,0:T(8,128)(2,1)S(1)}, u32[]{:S(2)}, u32[]{:S(2)}) async-start(bf16[32,8,512]{2,1,0:T(8,128)(2,1)} %get-tuple-element.45), calls=%async_computation.4 | async-start | bytes 524288 | tf_op jit(solution)/shard_map/all_to_all | solution.py:279
  115.3 6.9 %all-to-all-done.4.x_ref = bf16[32,8,512]{2,1,0:T(8,128)(2,1)S(1)} async-done(((bf16[32,8,512]{2,1,0:T(8,128)(2,1)}), bf16[32,8,512]{2,1,0:T(8,128)(2,1)S(1)}, u32[]{:S(2)}, u32[]{:S(2)}) %all-to-all-start.4) | async-done | bytes 262176 | tf_op jit(solution)/shard_map/all_to_all | solution.py:279
  122.2 3.4 %copy-done.5 = bf16[16,512,512]{2,1,0:T(8,128)(2,1)S(1)} copy-done((bf16[16,512,512]{2,1,0:T(8,128)(2,1)S(1)}, bf16[16,512,512]{2,1,0:T(8,128)(2,1)}, u32[]{:S(2)}) %copy-start.5) | copy-done | bytes 8388632
  125.5 3.0 %shard_map.94 = (f32[8,512]{1,0:T(8,128)S(1)}, bf16[32,8,512]{2,1,0:T(8,128)(2,1)}) custom-call(s32[1]{0:T(128)} %bitcast.6.mine_ref, bf16[16,512,512]{2,1,0:T(8,128)(2,1)S(1)} %copy-done.5, bf16[32,8,512]{2,1,0:T(8,128)(2,1)S(1)} %all-to-all-done.4.x_ref, f32[8,512]{1,0:T(8,128)S(1)} %get-tuple-element.40.base_ref.old_ref, ...), custom_call_target="tpu_custom_call" | custom-call | flops 100000000 | bytes 8000000 | tf_op jit(solution)/shard_map/pallas_call | solution.py:133
  128.5 6.2 %all-to-all-start.5 = ((bf16[32,8,512]{2,1,0:T(8,128)(2,1)}), bf16[32,8,512]{2,1,0:T(8,128)(2,1)S(1)}, u32[]{:S(2)}, u32[]{:S(2)}) async-start(bf16[32,8,512]{2,1,0:T(8,128)(2,1)} %get-tuple-element.47), calls=%async_computation.5 | async-start | bytes 524288 | tf_op jit(solution)/shard_map/all_to_all | solution.py:279
  134.7 7.2 %all-to-all-done.5.x_ref = bf16[32,8,512]{2,1,0:T(8,128)(2,1)S(1)} async-done(((bf16[32,8,512]{2,1,0:T(8,128)(2,1)}), bf16[32,8,512]{2,1,0:T(8,128)(2,1)S(1)}, u32[]{:S(2)}, u32[]{:S(2)}) %all-to-all-start.5) | async-done | bytes 262176 | tf_op jit(solution)/shard_map/all_to_all | solution.py:279
  141.9 3.4 %copy-done.6 = bf16[16,512,512]{2,1,0:T(8,128)(2,1)S(1)} copy-done((bf16[16,512,512]{2,1,0:T(8,128)(2,1)S(1)}, bf16[16,512,512]{2,1,0:T(8,128)(2,1)}, u32[]{:S(2)}) %copy-start.6) | copy-done | bytes 8388632
  145.3 3.0 %shard_map.95 = (f32[8,512]{1,0:T(8,128)S(1)}, bf16[32,8,512]{2,1,0:T(8,128)(2,1)}) custom-call(s32[1]{0:T(128)} %bitcast.5.mine_ref, bf16[16,512,512]{2,1,0:T(8,128)(2,1)S(1)} %copy-done.6, bf16[32,8,512]{2,1,0:T(8,128)(2,1)S(1)} %all-to-all-done.5.x_ref, f32[8,512]{1,0:T(8,128)S(1)} %get-tuple-element.40.base_ref.old_ref, ...), custom_call_target="tpu_custom_call" | custom-call | flops 100000000 | bytes 8000000 | tf_op jit(solution)/shard_map/pallas_call | solution.py:133
  148.3 19.1 %all-to-all-start.6 = ((bf16[32,8,512]{2,1,0:T(8,128)(2,1)}), bf16[32,8,512]{2,1,0:T(8,128)(2,1)S(1)}, u32[]{:S(2)}, u32[]{:S(2)}) async-start(bf16[32,8,512]{2,1,0:T(8,128)(2,1)} %get-tuple-element.49), calls=%async_computation.6 | async-start | bytes 524288 | tf_op jit(solution)/shard_map/all_to_all | solution.py:279
  167.4 6.8 %all-to-all-done.6.x_ref = bf16[32,8,512]{2,1,0:T(8,128)(2,1)S(1)} async-done(((bf16[32,8,512]{2,1,0:T(8,128)(2,1)}), bf16[32,8,512]{2,1,0:T(8,128)(2,1)S(1)}, u32[]{:S(2)}, u32[]{:S(2)}) %all-to-all-start.6) | async-done | bytes 262176 | tf_op jit(solution)/shard_map/all_to_all | solution.py:279
  174.2 3.4 %copy-done.7 = bf16[16,512,512]{2,1,0:T(8,128)(2,1)S(1)} copy-done((bf16[16,512,512]{2,1,0:T(8,128)(2,1)S(1)}, bf16[16,512,512]{2,1,0:T(8,128)(2,1)}, u32[]{:S(2)}) %copy-start.7) | copy-done | bytes 8388632
  177.6 3.0 %shard_map.96 = (f32[8,512]{1,0:T(8,128)S(1)}, bf16[32,8,512]{2,1,0:T(8,128)(2,1)}) custom-call(s32[1]{0:T(128)} %bitcast.4.mine_ref, bf16[16,512,512]{2,1,0:T(8,128)(2,1)S(1)} %copy-done.7, bf16[32,8,512]{2,1,0:T(8,128)(2,1)S(1)} %all-to-all-done.6.x_ref, f32[8,512]{1,0:T(8,128)S(1)} %get-tuple-element.40.base_ref.old_ref, ...), custom_call_target="tpu_custom_call" | custom-call | flops 100000000 | bytes 8000000 | tf_op jit(solution)/shard_map/pallas_call | solution.py:133
  180.5 8.3 %all-to-all-start.7 = ((bf16[32,8,512]{2,1,0:T(8,128)(2,1)}), bf16[32,8,512]{2,1,0:T(8,128)(2,1)S(1)}, u32[]{:S(2)}, u32[]{:S(2)}) async-start(bf16[32,8,512]{2,1,0:T(8,128)(2,1)} %get-tuple-element.51), calls=%async_computation.7 | async-start | bytes 524288 | tf_op jit(solution)/shard_map/all_to_all | solution.py:279
  188.8 0.1 copy.10
  189.0 7.0 %all-to-all-done.7.x_ref = bf16[32,8,512]{2,1,0:T(8,128)(2,1)S(1)} async-done(((bf16[32,8,512]{2,1,0:T(8,128)(2,1)}), bf16[32,8,512]{2,1,0:T(8,128)(2,1)S(1)}, u32[]{:S(2)}, u32[]{:S(2)}) %all-to-all-start.7) | async-done | bytes 262176 | tf_op jit(solution)/shard_map/all_to_all | solution.py:279
  196.0 3.4 %copy-done.8 = bf16[16,512,512]{2,1,0:T(8,128)(2,1)S(1)} copy-done((bf16[16,512,512]{2,1,0:T(8,128)(2,1)S(1)}, bf16[16,512,512]{2,1,0:T(8,128)(2,1)}, u32[]{:S(2)}) %copy-start.8) | copy-done | bytes 8388632
  199.4 3.0 %shard_map.97 = (f32[8,512]{1,0:T(8,128)S(1)}, bf16[32,8,512]{2,1,0:T(8,128)(2,1)}) custom-call(s32[1]{0:T(128)} %bitcast.3.mine_ref, bf16[16,512,512]{2,1,0:T(8,128)(2,1)S(1)} %copy-done.8, bf16[32,8,512]{2,1,0:T(8,128)(2,1)S(1)} %all-to-all-done.7.x_ref, f32[8,512]{1,0:T(8,128)S(1)} %get-tuple-element.40.base_ref.old_ref, ...), custom_call_target="tpu_custom_call" | custom-call | flops 100000000 | bytes 8000000 | tf_op jit(solution)/shard_map/pallas_call | solution.py:133
  202.4 2.3 collective-permute-start.6
  204.7 5.7 %collective-permute-start.7 = (bf16[8,256]{1,0:T(8,128)(2,1)S(1)}, bf16[8,256]{1,0:T(8,128)(2,1)S(1)}, u32[]{:S(2)}, u32[]{:S(2)}) collective-permute-start(bf16[8,256]{1,0:T(8,128)(2,1)S(1)} %pad_maximum_fusion), channel_id=1, source_target_pairs={{0,1},{1,2},{2,3},{3,4},{4,5},{5,6},{6,7},{7,8},{8,9},{9,10},{10,1... | collective-permute-start | bytes 12296 | tf_op jit(solution)/shard_map/ppermute | solution.py:260
  210.4 1.9 collective-permute-start.8
  212.3 0.0 all-gather.3.cloned.1.call-done
  212.3 3.4 %copy-done.9 = bf16[16,512,512]{2,1,0:T(8,128)(2,1)S(1)} copy-done((bf16[16,512,512]{2,1,0:T(8,128)(2,1)S(1)}, bf16[16,512,512]{2,1,0:T(8,128)(2,1)}, u32[]{:S(2)}) %copy-start.9) | copy-done | bytes 8388632
  215.7 4.6 %copy-done.10 = bf16[12288,512]{1,0:T(8,128)(2,1)S(1)} copy-done((bf16[12288,512]{1,0:T(8,128)(2,1)S(1)}, bf16[12288,512]{1,0:T(8,128)(2,1)}, u32[]{:S(2)}) %copy-start.10) | copy-done | bytes 12582936
  220.3 6.2 %shard_map.88 = (f32[4,96,512]{2,1,0:T(8,128)S(1)}, bf16[4,2,96,128]{3,2,1,0:T(8,128)(2,1)S(1)}, bf16[4,2,96,128]{3,2,1,0:T(8,128)(2,1)S(1)}, bf16[4,16,512]{2,1,0:T(8,128)(2,1)S(1)}) custom-call(bf16[16,768,512]{2,1,0:T(8,128)(2,1)S(1)} %bitcast.22, bf16[16,512,512]{2,1,0:T(8,128)(2,1)S(1)} %copy-done.9), custom_call_target="tpu_custom_call" | custom-call | flops 3000000000 | bytes 15000000 | tf_op jit(solution)/shard_map/pallas_call | solution.py:157
  226.4 0.0 copy-start.17
  226.4 0.0 copy-start.18
  226.5 0.0 copy-start.15
  226.5 0.0 copy-start.13
  226.5 2.2 collective-permute-start.4
  228.7 6.2 %shard_map.89 = (f32[4,96,512]{2,1,0:T(8,128)S(1)}, bf16[4,2,96,128]{3,2,1,0:T(8,128)(2,1)S(1)}, bf16[4,2,96,128]{3,2,1,0:T(8,128)(2,1)S(1)}, bf16[4,16,512]{2,1,0:T(8,128)(2,1)S(1)}) custom-call(bf16[16,768,512]{2,1,0:T(8,128)(2,1)S(1)} %bitcast.23, bf16[16,512,512]{2,1,0:T(8,128)(2,1)S(1)} %copy-done.9), custom_call_target="tpu_custom_call" | custom-call | flops 3000000000 | bytes 15000000 | tf_op jit(solution)/shard_map/pallas_call | solution.py:157
  234.9 6.3 %collective-permute-start = (bf16[4,2,96,128]{3,2,1,0:T(8,128)(2,1)S(1)}, bf16[4,2,96,128]{3,2,1,0:T(8,128)(2,1)S(1)}, u32[]{:S(2)}, u32[]{:S(2)}) collective-permute-start(bf16[4,2,96,128]{3,2,1,0:T(8,128)(2,1)S(1)} %get-tuple-element.32), channel_id=1, source_target_pairs={{0,1},{1,2},{2,3},{3,4},{4,5},{5,6},{6,7},{7,8},{8,9},{9,10},{10,1... | collective-permute-start | bytes 589832 | tf_op jit(solution)/shard_map/ppermute | solution.py:260
  241.2 1.9 collective-permute-start.1
  243.2 2.4 collective-permute-start.2
  245.6 2.1 collective-permute-start.3
  247.6 2.9 %collective-permute-start.5 = (bf16[4,16,512]{2,1,0:T(8,128)(2,1)S(1)}, bf16[4,16,512]{2,1,0:T(8,128)(2,1)S(1)}, u32[]{:S(2)}, u32[]{:S(2)}) collective-permute-start(bf16[4,16,512]{2,1,0:T(8,128)(2,1)S(1)} %get-tuple-element.37), channel_id=1, source_target_pairs={{0,16},{16,32},{32,48},{48,64},{64,80},{80,96},{96,112},{1,17},{17... | collective-permute-start | bytes 196616 | tf_op jit(solution)/shard_map/ppermute | solution.py:260
  250.6 0.2 fusion.5.coef_ref
  250.8 1.3 shard_map.98.wave_ref
  252.1 2.6 collective-permute-done.5.pb
  254.8 0.2 collective-permute-done.3.hb
  255.0 2.7 %shard_map.99 = (f32[2,8,192,128]{3,2,1,0:T(8,128)}, f32[2,8,192,128]{3,2,1,0:T(8,128)}) custom-call(f32[4,96,512]{2,1,0:T(8,128)S(1)} %get-tuple-element.30.ya, f32[4,96,512]{2,1,0:T(8,128)S(1)} %get-tuple-element.31.yb, f32[2,8,192,128]{3,2,1,0:T(8,128)S(1)} %bitcast.26, bf16[4,2,96,128]{3,2,1,0:T(8,128)(2,1)S(1)} %collective-permute-done.la, ...), custom_call_target="tpu_custom_call" | custom-call | tf_op jit(solution)/shard_map/pallas_call | solution.py:240
  (33 shorter events, 0.1 us)
Async XLA Ops:
  7.2 205.1 %all-gather.3.cloned.1.call-start = ((), (), s32[]{:S(2)}) async-start(), calls=%async_computation.8 | async-start | bytes 13369344 | tf_op jit(solution)/shard_map/all_gather | solution.py:267
  7.2 1.4 copy-start.12
  8.6 0.7 copy-start.14
  10.5 22.7 %all-to-all-start = ((bf16[16,32,512]{2,1,0:T(8,128)(2,1)}), bf16[16,32,512]{2,1,0:T(8,128)(2,1)S(1)}, u32[]{:S(2)}, u32[]{:S(2)}) async-start(bf16[16,32,512]{2,1,0:T(8,128)(2,1)} %get-tuple-element.38), calls=%async_computation | async-start | bytes 1048576 | tf_op jit(solution)/shard_map/all_to_all | solution.py:268
  19.2 3.4 %copy-start.11 = (bf16[1,2,2,128,2,32,128]{6,5,4,3,2,1,0:T(8,128)(2,1)S(1)}, bf16[1,2,2,128,2,32,128]{6,5,4,3,2,1,0:T(8,128)(2,1)}, u32[]{:S(2)}) copy-start(bf16[1,2,2,128,2,32,128]{6,5,4,3,2,1,0:T(8,128)(2,1)} %param.8) | copy-start | bytes 25165828
  30.0 3.2 %copy-start = (bf16[16,512,512]{2,1,0:T(8,128)(2,1)}, bf16[16,512,512]{2,1,0:T(8,128)(2,1)S(1)}, u32[]{:S(2)}) copy-start(bf16[16,512,512]{2,1,0:T(8,128)(2,1)S(1)} %shard_map.87.h_ref) | copy-start | bytes 25165828
  33.2 3.5 %copy-start.1 = (bf16[16,512,512]{2,1,0:T(8,128)(2,1)S(1)}, bf16[16,512,512]{2,1,0:T(8,128)(2,1)}, u32[]{:S(2)}) copy-start(bf16[16,512,512]{2,1,0:T(8,128)(2,1)} %copy-done) | copy-start | bytes 25165828
  39.7 15.6 %all-to-all-start.1 = ((bf16[32,8,512]{2,1,0:T(8,128)(2,1)}), bf16[32,8,512]{2,1,0:T(8,128)(2,1)S(1)}, u32[]{:S(2)}, u32[]{:S(2)}) async-start(bf16[32,8,512]{2,1,0:T(8,128)(2,1)} %get-tuple-element.39), calls=%async_computation.1 | async-start | bytes 524288 | tf_op jit(solution)/shard_map/all_to_all | solution.py:279
  55.3 3.4 %copy-start.2 = (bf16[16,512,512]{2,1,0:T(8,128)(2,1)S(1)}, bf16[16,512,512]{2,1,0:T(8,128)(2,1)}, u32[]{:S(2)}) copy-start(bf16[16,512,512]{2,1,0:T(8,128)(2,1)} %copy-done) | copy-start | bytes 25165828
  61.7 17.9 %all-to-all-start.2 = ((bf16[32,8,512]{2,1,0:T(8,128)(2,1)}), bf16[32,8,512]{2,1,0:T(8,128)(2,1)S(1)}, u32[]{:S(2)}, u32[]{:S(2)}) async-start(bf16[32,8,512]{2,1,0:T(8,128)(2,1)} %get-tuple-element.41), calls=%async_computation.2 | async-start | bytes 524288 | tf_op jit(solution)/shard_map/all_to_all | solution.py:279
  79.6 3.4 %copy-start.3 = (bf16[16,512,512]{2,1,0:T(8,128)(2,1)S(1)}, bf16[16,512,512]{2,1,0:T(8,128)(2,1)}, u32[]{:S(2)}) copy-start(bf16[16,512,512]{2,1,0:T(8,128)(2,1)} %copy-done) | copy-start | bytes 25165828
  86.0 13.7 %all-to-all-start.3 = ((bf16[32,8,512]{2,1,0:T(8,128)(2,1)}), bf16[32,8,512]{2,1,0:T(8,128)(2,1)S(1)}, u32[]{:S(2)}, u32[]{:S(2)}) async-start(bf16[32,8,512]{2,1,0:T(8,128)(2,1)} %get-tuple-element.43), calls=%async_computation.3 | async-start | bytes 524288 | tf_op jit(solution)/shard_map/all_to_all | solution.py:279
  99.6 3.4 %copy-start.4 = (bf16[16,512,512]{2,1,0:T(8,128)(2,1)S(1)}, bf16[16,512,512]{2,1,0:T(8,128)(2,1)}, u32[]{:S(2)}) copy-start(bf16[16,512,512]{2,1,0:T(8,128)(2,1)} %copy-done) | copy-start | bytes 25165828
  106.0 16.1 %all-to-all-start.4 = ((bf16[32,8,512]{2,1,0:T(8,128)(2,1)}), bf16[32,8,512]{2,1,0:T(8,128)(2,1)S(1)}, u32[]{:S(2)}, u32[]{:S(2)}) async-start(bf16[32,8,512]{2,1,0:T(8,128)(2,1)} %get-tuple-element.45), calls=%async_computation.4 | async-start | bytes 524288 | tf_op jit(solution)/shard_map/all_to_all | solution.py:279
  122.2 3.4 %copy-start.5 = (bf16[16,512,512]{2,1,0:T(8,128)(2,1)S(1)}, bf16[16,512,512]{2,1,0:T(8,128)(2,1)}, u32[]{:S(2)}) copy-start(bf16[16,512,512]{2,1,0:T(8,128)(2,1)} %copy-done) | copy-start | bytes 25165828
  128.5 13.4 %all-to-all-start.5 = ((bf16[32,8,512]{2,1,0:T(8,128)(2,1)}), bf16[32,8,512]{2,1,0:T(8,128)(2,1)S(1)}, u32[]{:S(2)}, u32[]{:S(2)}) async-start(bf16[32,8,512]{2,1,0:T(8,128)(2,1)} %get-tuple-element.47), calls=%async_computation.5 | async-start | bytes 524288 | tf_op jit(solution)/shard_map/all_to_all | solution.py:279
  141.9 3.4 %copy-start.6 = (bf16[16,512,512]{2,1,0:T(8,128)(2,1)S(1)}, bf16[16,512,512]{2,1,0:T(8,128)(2,1)}, u32[]{:S(2)}) copy-start(bf16[16,512,512]{2,1,0:T(8,128)(2,1)} %copy-done) | copy-start | bytes 25165828
  145.3 43.6 %copy-start.16 = (s32[8,256]{1,0:T(8,128)S(1)}, s32[8,256]{1,0:T(8,128)}, u32[]{:S(2)}) copy-start(s32[8,256]{1,0:T(8,128)} %param.13) | copy-start | bytes 24580
  148.3 25.9 %all-to-all-start.6 = ((bf16[32,8,512]{2,1,0:T(8,128)(2,1)}), bf16[32,8,512]{2,1,0:T(8,128)(2,1)S(1)}, u32[]{:S(2)}, u32[]{:S(2)}) async-start(bf16[32,8,512]{2,1,0:T(8,128)(2,1)} %get-tuple-element.49), calls=%async_computation.6 | async-start | bytes 524288 | tf_op jit(solution)/shard_map/all_to_all | solution.py:279
  174.2 3.4 %copy-start.7 = (bf16[16,512,512]{2,1,0:T(8,128)(2,1)S(1)}, bf16[16,512,512]{2,1,0:T(8,128)(2,1)}, u32[]{:S(2)}) copy-start(bf16[16,512,512]{2,1,0:T(8,128)(2,1)} %copy-done) | copy-start | bytes 25165828
  180.5 15.4 %all-to-all-start.7 = ((bf16[32,8,512]{2,1,0:T(8,128)(2,1)}), bf16[32,8,512]{2,1,0:T(8,128)(2,1)S(1)}, u32[]{:S(2)}, u32[]{:S(2)}) async-start(bf16[32,8,512]{2,1,0:T(8,128)(2,1)} %get-tuple-element.51), calls=%async_computation.7 | async-start | bytes 524288 | tf_op jit(solution)/shard_map/all_to_all | solution.py:279
  196.0 3.4 %copy-start.8 = (bf16[16,512,512]{2,1,0:T(8,128)(2,1)S(1)}, bf16[16,512,512]{2,1,0:T(8,128)(2,1)}, u32[]{:S(2)}) copy-start(bf16[16,512,512]{2,1,0:T(8,128)(2,1)} %copy-done) | copy-start | bytes 25165828
  202.4 43.2 %collective-permute-start.6 = (bf16[8,512]{1,0:T(8,128)(2,1)S(1)}, bf16[8,512]{1,0:T(8,128)(2,1)S(1)}, u32[]{:S(2)}, u32[]{:S(2)}) collective-permute-start(bf16[8,512]{1,0:T(8,128)(2,1)S(1)} %convert_element_type.4), channel_id=1, source_target_pairs={{16,0},{32,16},{48,32},{64,48},{80,64},{96,80},{112,96},{17,1},{33... | collective-permute-start | bytes 24584 | tf_op jit(solution)/shard_map/ppermute | solution.py:260
  204.7 36.5 %collective-permute-start.7 = (bf16[8,256]{1,0:T(8,128)(2,1)S(1)}, bf16[8,256]{1,0:T(8,128)(2,1)S(1)}, u32[]{:S(2)}, u32[]{:S(2)}) collective-permute-start(bf16[8,256]{1,0:T(8,128)(2,1)S(1)} %pad_maximum_fusion), channel_id=1, source_target_pairs={{0,1},{1,2},{2,3},{3,4},{4,5},{5,6},{6,7},{7,8},{8,9},{9,10},{10,1... | collective-permute-start | bytes 12296 | tf_op jit(solution)/shard_map/ppermute | solution.py:260
  210.4 32.8 %collective-permute-start.8 = (bf16[8,256]{1,0:T(8,128)(2,1)S(1)}, bf16[8,256]{1,0:T(8,128)(2,1)S(1)}, u32[]{:S(2)}, u32[]{:S(2)}) collective-permute-start(bf16[8,256]{1,0:T(8,128)(2,1)S(1)} %pad_maximum_fusion.1), channel_id=1, source_target_pairs={{1,0},{2,1},{3,2},{4,3},{5,4},{6,5},{7,6},{8,7},{9,8},{10,9},{11,1... | collective-permute-start | bytes 12296 | tf_op jit(solution)/shard_map/ppermute | solution.py:260
  212.3 3.4 %copy-start.9 = (bf16[16,512,512]{2,1,0:T(8,128)(2,1)S(1)}, bf16[16,512,512]{2,1,0:T(8,128)(2,1)}, u32[]{:S(2)}) copy-start(bf16[16,512,512]{2,1,0:T(8,128)(2,1)} %copy-done) | copy-start | bytes 25165828
  215.7 4.6 %copy-start.10 = (bf16[12288,512]{1,0:T(8,128)(2,1)S(1)}, bf16[12288,512]{1,0:T(8,128)(2,1)}, u32[]{:S(2)}) copy-start(bf16[12288,512]{1,0:T(8,128)(2,1)} %all-gather.3.cloned.1.call-done) | copy-start | bytes 37748740
  226.4 24.2 %copy-start.17 = (s32[256]{0:T(256)S(1)}, s32[256]{0:T(256)}, u32[]{:S(2)}) copy-start(s32[256]{0:T(256)} %param.11) | copy-start | bytes 3076
  226.4 24.2 %copy-start.18 = (s32[8]{0:T(128)S(1)}, s32[8]{0:T(128)}, u32[]{:S(2)}) copy-start(s32[8]{0:T(128)} %param.12) | copy-start | bytes 100
  226.5 24.3 %copy-start.15 = (bf16[256,2,128]{2,1,0:T(2,128)(2,1)S(1)}, bf16[256,2,128]{2,1,0:T(2,128)(2,1)}, u32[]{:S(2)}) copy-start(bf16[256,2,128]{2,1,0:T(2,128)(2,1)} %param.9) | copy-start | bytes 393220
  226.5 28.5 %copy-start.13 = (f32[2,8,96,2,128]{4,3,2,1,0:T(2,128)S(1)}, f32[2,8,96,2,128]{4,3,2,1,0:T(2,128)}, u32[]{:S(2)}) copy-start(f32[2,8,96,2,128]{4,3,2,1,0:T(2,128)} %param.7) | copy-start | bytes 4718596
  226.5 21.2 %collective-permute-start.4 = (bf16[4,16,512]{2,1,0:T(8,128)(2,1)S(1)}, bf16[4,16,512]{2,1,0:T(8,128)(2,1)S(1)}, u32[]{:S(2)}, u32[]{:S(2)}) collective-permute-start(bf16[4,16,512]{2,1,0:T(8,128)(2,1)S(1)} %get-tuple-element.36), channel_id=1, source_target_pairs={{0,16},{16,32},{32,48},{48,64},{64,80},{80,96},{96,112},{1,17},{17... | collective-permute-start | bytes 196616 | tf_op jit(solution)/shard_map/ppermute | solution.py:260
  234.9 19.9 %collective-permute-start = (bf16[4,2,96,128]{3,2,1,0:T(8,128)(2,1)S(1)}, bf16[4,2,96,128]{3,2,1,0:T(8,128)(2,1)S(1)}, u32[]{:S(2)}, u32[]{:S(2)}) collective-permute-start(bf16[4,2,96,128]{3,2,1,0:T(8,128)(2,1)S(1)} %get-tuple-element.32), channel_id=1, source_target_pairs={{0,1},{1,2},{2,3},{3,4},{4,5},{5,6},{6,7},{7,8},{8,9},{9,10},{10,1... | collective-permute-start | bytes 589832 | tf_op jit(solution)/shard_map/ppermute | solution.py:260
  241.2 13.6 %collective-permute-start.1 = (bf16[4,2,96,128]{3,2,1,0:T(8,128)(2,1)S(1)}, bf16[4,2,96,128]{3,2,1,0:T(8,128)(2,1)S(1)}, u32[]{:S(2)}, u32[]{:S(2)}) collective-permute-start(bf16[4,2,96,128]{3,2,1,0:T(8,128)(2,1)S(1)} %get-tuple-element.33), channel_id=1, source_target_pairs={{0,1},{1,2},{2,3},{3,4},{4,5},{5,6},{6,7},{7,8},{8,9},{9,10},{10,1... | collective-permute-start | bytes 589832 | tf_op jit(solution)/shard_map/ppermute | solution.py:260
  243.2 11.6 %collective-permute-start.2 = (bf16[4,2,96,128]{3,2,1,0:T(8,128)(2,1)S(1)}, bf16[4,2,96,128]{3,2,1,0:T(8,128)(2,1)S(1)}, u32[]{:S(2)}, u32[]{:S(2)}) collective-permute-start(bf16[4,2,96,128]{3,2,1,0:T(8,128)(2,1)S(1)} %get-tuple-element.34), channel_id=1, source_target_pairs={{1,0},{2,1},{3,2},{4,3},{5,4},{6,5},{7,6},{8,7},{9,8},{10,9},{11,1... | collective-permute-start | bytes 589832 | tf_op jit(solution)/shard_map/ppermute | solution.py:260
  245.6 9.4 %collective-permute-start.3 = (bf16[4,2,96,128]{3,2,1,0:T(8,128)(2,1)S(1)}, bf16[4,2,96,128]{3,2,1,0:T(8,128)(2,1)S(1)}, u32[]{:S(2)}, u32[]{:S(2)}) collective-permute-start(bf16[4,2,96,128]{3,2,1,0:T(8,128)(2,1)S(1)} %get-tuple-element.35), channel_id=1, source_target_pairs={{1,0},{2,1},{3,2},{4,3},{5,4},{6,5},{7,6},{8,7},{9,8},{10,9},{11,1... | collective-permute-start | bytes 589832 | tf_op jit(solution)/shard_map/ppermute | solution.py:260
  247.6 7.1 %collective-permute-start.5 = (bf16[4,16,512]{2,1,0:T(8,128)(2,1)S(1)}, bf16[4,16,512]{2,1,0:T(8,128)(2,1)S(1)}, u32[]{:S(2)}, u32[]{:S(2)}) collective-permute-start(bf16[4,16,512]{2,1,0:T(8,128)(2,1)S(1)} %get-tuple-element.37), channel_id=1, source_target_pairs={{0,16},{16,32},{32,48},{48,64},{64,80},{80,96},{96,112},{1,17},{17... | collective-permute-start | bytes 196616 | tf_op jit(solution)/shard_map/ppermute | solution.py:260
Sparse Core Ops, SparseCore 0:
  11.0 97.9 all-gather.2

commit v2 on v1

v2 whole, which is shorter than its diff:
```python
import jax
import jax.numpy as jnp
from jax import lax
from jax.experimental import pallas as pl
from jax.experimental.pallas import tpu as pltpu
from jax.sharding import PartitionSpec as P

MODES = 256
NPTS = 32768
COUPLING = 0.8
ABSORB_RATE = 0.3
WAVE_SCALE = 0.8

G = 8
D = 16
C = 8
LZ = 96
R = 8
K = 512
NY = 128

bf16 = jnp.bfloat16
f32 = jnp.float32
VMEM = pltpu.VMEM


def whole(space=VMEM):
    return pl.BlockSpec(memory_space=space)


def params(mib):
    return pltpu.CompilerParams(vmem_limit_bytes=mib * 2**20)


def dot_t(x, h):
    return lax.dot_general(x, h, (((1,), (1,)), ((), ())), preferred_element_type=f32)


def prepare_kernel(rhs_ref, profile_ref, x_ref, chunk_ref):
    chunk_ref[0] = jnp.zeros((32, K), bf16)
    for a in range(2):
        for x in range(2):
            cols = pl.ds(a * 256 + x * NY, NY)
            for r in range(R):
                x_ref[pl.ds(r * LZ, LZ), cols] = rhs_ref[a, r, pl.ds(x, LZ, stride=2), :].astype(bf16)
    head = jnp.concatenate([rhs_ref[a, :, x, :] for a in range(2) for x in range(2)], axis=1)
    profile = jnp.concatenate([profile_ref[...], jnp.zeros((16, K - LZ), bf16)], axis=1)
    chunk = jnp.concatenate([head, jnp.zeros((8, K), f32)], axis=0).astype(bf16)
    for i in range(D):
        chunk_ref[i, pl.ds(0, 16), :] = chunk
        chunk_ref[i, pl.ds(16, 16), :] = profile


def prepare(rhs, profile):
    return pl.pallas_call(
        prepare_kernel,
        out_shape=(jax.ShapeDtypeStruct((R * LZ, K), bf16), jax.ShapeDtypeStruct((D, 32, K), bf16)),
        in_specs=[whole(), whole()],
        out_specs=(whole(), whole()),
        compiler_params=params(8),
    )(rhs, profile)


def arrange_kernel(blocks_ref, h_ref):
    m = lax.broadcasted_iota(jnp.int32, (256, 256), 0)
    n = lax.broadcasted_iota(jnp.int32, (256, 256), 1)
    swap = ((m // 16 == n % 16) & (m % 16 == n // 16)).astype(f32).astype(bf16)

    def body(b_ref, out_ref):
        for s in range(2):
            for c in range(2):
                for half in range(2):
                    tile = b_ref[pl.ds(s * 16, 16), c, pl.ds(half * 16, 16), :].reshape(256, NY)
                    moved = jnp.dot(swap, tile, preferred_element_type=f32).astype(bf16)
                    for q in range(16):
                        p = half * 16 + q
                        source = p // 2
                        out_ref[source % 2, source // 2, pl.ds(s * 16, 16), pl.ds(c * 256 + (p % 2) * NY, NY)] = moved[
                            q * 16 : (q + 1) * 16
                        ]

    pltpu.emit_pipeline(
        body,
        grid=(K // 32,),
        in_specs=[pl.BlockSpec((32, 2, 32, NY), lambda i: (i, 0, 0, 0))],
        out_specs=[pl.BlockSpec((2, C, 32, K), lambda i: (0, 0, i, 0))],
    )(blocks_ref, h_ref)


def arrange(blocks):
    return pl.pallas_call(
        arrange_kernel,
        out_shape=jax.ShapeDtypeStruct((2, C, K, K), bf16),
        in_specs=[whole(pltpu.HBM)],
        out_specs=whole(pltpu.HBM),
        compiler_params=params(50),
        cost_estimate=pl.CostEstimate(flops=2 * 10**9, bytes_accessed=17 * 10**6, transcendentals=0),
    )(blocks)


COST = pl.CostEstimate(flops=10**8, bytes_accessed=5 * 10**6, transcendentals=0)
CHUNK = 2


def stream(h_ref, acc_ref, core, operand):
    def body(b_ref):
        first = pl.program_id(0) * CHUNK
        for j in range(CHUNK):
            acc_ref[...] += dot_t(operand(first + j), b_ref[j])

    pltpu.emit_pipeline(
        body, grid=(C // CHUNK,), in_specs=[pl.BlockSpec((None, CHUNK, K, K), lambda k: (core, k, 0, 0))]
    )(h_ref)


def first_kernel(h_ref, x_ref, v_ref, out_ref, acc_ref):
    acc_ref[...] = jnp.zeros((16, K), f32)
    for core in range(2):
        stream(h_ref, acc_ref, core, lambda k: x_ref[2 * k + core, pl.ds(0, 16), :])
    v = acc_ref[pl.ds(0, R), :]
    v_ref[...] = v
    for i in range(D):
        out_ref[i] = v.astype(bf16)


def first_product(h, x):
    return pl.pallas_call(
        first_kernel,
        out_shape=MATVEC_OUT,
        in_specs=[whole(pltpu.HBM), whole()],
        out_specs=(whole(), whole()),
        scratch_shapes=[VMEM((16, K), f32)],
        compiler_params=params(50),
        cost_estimate=COST,
    )(h, x)


def own_kernel(core_ref, h_ref, x_ref, behind_ref, acc_ref):
    acc_ref[...] = jnp.zeros((R, K), f32)
    stream(h_ref, acc_ref, core_ref[0], lambda k: x_ref[k])


def own_half(core, h, x, behind):
    return pl.pallas_call(
        own_kernel,
        out_shape=jax.ShapeDtypeStruct((R, K), f32),
        in_specs=[whole(pltpu.SMEM), whole(pltpu.HBM), whole(), whole(pl.ANY)],
        out_specs=whole(),
        compiler_params=params(50),
        cost_estimate=COST,
    )(core, h, x, behind)


def other_kernel(core_ref, mine_ref, h_ref, x_ref, half_ref, base_ref, old_ref, v_ref, out_ref, acc_ref):
    acc_ref[...] = half_ref[...]
    stream(h_ref, acc_ref, 1 - core_ref[0], lambda k: x_ref[k])
    v = jnp.where(mine_ref[0] > 0, base_ref[...] + COUPLING * acc_ref[...], old_ref[...])
    v_ref[...] = v
    for i in range(D):
        out_ref[i] = v.astype(bf16)


MATVEC_OUT = (jax.ShapeDtypeStruct((R, K), f32), jax.ShapeDtypeStruct((D, R, K), bf16))


def other_half(core, mine, h, x, half, base, old):
    return pl.pallas_call(
        other_kernel,
        out_shape=MATVEC_OUT,
        in_specs=[whole(pltpu.SMEM)] * 2 + [whole(pltpu.HBM)] + [whole()] * 4,
        out_specs=(whole(), whole()),
        scratch_shapes=[VMEM((R, K), f32)],
        compiler_params=params(50),
        cost_estimate=COST,
    )(core, mine, h, x, half, base, old)


def fronts_kernel(x_ref, h_ref, behind_ref, y_ref, low_ref, high_ref, last_ref):
    def body(x_block, h_block):
        @pl.when(pl.program_id(0) == 0)
        def _():
            y_ref[...] = jnp.zeros((R, LZ, K), f32)

        for part in range(4):
            rows = pl.ds(part * 2 * LZ, 2 * LZ)
            y_ref[pl.ds(2 * part, 2)] += dot_t(x_block[rows, :], h_block[...]).reshape(2, LZ, K)

    pltpu.emit_pipeline(
        body,
        grid=(D,),
        in_specs=[
            pl.BlockSpec((None, R * LZ, K), lambda i: (i, 0, 0)),
            pl.BlockSpec((None, None, K, K), lambda i: (lax.rem(i, 2), lax.div(i, 2), 0, 0)),
        ],
    )(x_ref, h_ref)
    for r in range(R):
        for a in range(2):
            low_ref[r, a] = y_ref[r, :, a * 256 : a * 256 + NY].astype(bf16)
            high_ref[r, a] = y_ref[r, :, a * 256 + NY : a * 256 + 256].astype(bf16)
    last_ref[...] = jnp.concatenate([y_ref[r, LZ - 1 : LZ, :] for r in range(R)], axis=0).astype(bf16)


def fronts_of(x, h, behind):
    halo = jax.ShapeDtypeStruct((R, 2, LZ, NY), bf16)
    return pl.pallas_call(
        fronts_kernel,
        out_shape=(jax.ShapeDtypeStruct((R, LZ, K), f32), halo, halo, jax.ShapeDtypeStruct((R, K), bf16)),
        in_specs=[whole(pltpu.HBM), whole(pltpu.HBM), whole(pl.ANY)],
        out_specs=(whole(),) * 4,
        compiler_params=params(50),
        cost_estimate=pl.CostEstimate(flops=6 * 10**9, bytes_accessed=23 * 10**6, transcendentals=0),
    )(x, h, behind)


def wave_kernel(x_ref, coef_ref, panel_ref, behind_ref, out_ref):
    profile = jnp.concatenate([x_ref[i, pl.ds(16, 16), :][:, :LZ] for i in range(D)], axis=0).astype(f32)
    panel = panel_ref[...]
    for r in range(R):
        weights = profile * coef_ref[:, r : r + 1]
        log = jnp.zeros((LZ, 256), f32)
        for _ in range(3):
            term = weights.astype(bf16)
            weights = weights - term.astype(f32)
            log = log + lax.dot_general(term, panel, (((0,), (0,)), ((), ())), preferred_element_type=f32)
        out_ref[r] = WAVE_SCALE * jnp.exp(-2.0 * log)


def wave(x, coef, panel, behind):
    return pl.pallas_call(
        wave_kernel,
        out_shape=jax.ShapeDtypeStruct((R, LZ, 256), f32),
        in_specs=[whole()] * 3 + [whole(pl.ANY)],
        out_specs=whole(),
        compiler_params=params(8),
        cost_estimate=pl.CostEstimate(flops=3 * 10**8, bytes_accessed=2 * 10**6, transcendentals=2 * 10**5),
    )(x, coef, panel, behind)


def residual_kernel(y_ref, rhs_ref, low_ref, high_ref, prev_ref, v_ref, nl_ref, vl_ref, vh_ref, wave_ref, sol_ref, res_ref):
    row = lax.broadcasted_iota(jnp.int32, (LZ, NY), 0)
    lane = lax.broadcasted_iota(jnp.int32, (LZ, NY), 1)
    for r in range(R):
        s = {}
        for a in range(2):
            for x in range(2):
                cols = slice(a * 256 + x * NY, a * 256 + (x + 1) * NY)
                s[a, x] = jnp.where(row == 0, v_ref[r : r + 1, cols], y_ref[r, :, cols])
        lap = {}
        for a in range(2):
            below = jnp.where(row == 0, vl_ref[r : r + 1, a * NY : (a + 1) * NY].astype(f32), low_ref[r, a].astype(f32))
            above = jnp.where(row == 0, vh_ref[r : r + 1, a * NY : (a + 1) * NY].astype(f32), high_ref[r, a].astype(f32))
            for x in range(2):
                cols = slice(a * 256 + x * NY, a * 256 + (x + 1) * NY)
                own = s[a, x]
                before = jnp.where(row == 0, prev_ref[r : r + 1, cols].astype(f32), pltpu.roll(own, 1, 0))
                after = jnp.where(row == LZ - 1, nl_ref[r : r + 1, cols].astype(f32), pltpu.roll(own, LZ - 1, 0))
                left = jnp.where(lane == 0, 0.0, pltpu.roll(own, 1, 1))
                right = jnp.where(lane == NY - 1, 0.0, pltpu.roll(own, NY - 1, 1))
                beside = before + after + left + right
                beside = beside + (below if x == 0 else s[a, 0]) + (s[a, 1] if x == 0 else above)
                lap[a, x] = 6.0 * own - beside
        for x in range(2):
            w = wave_ref[r, :, x * NY : (x + 1) * NY]
            rows = pl.ds(x, LZ, stride=2)
            real = lap[0, x] - w * s[0, x] + ABSORB_RATE * w * s[1, x]
            imag = lap[1, x] - w * s[1, x] - ABSORB_RATE * w * s[0, x]
            sol_ref[0, r, rows, :] = s[0, x]
            sol_ref[1, r, rows, :] = s[1, x]
            res_ref[0, r, rows, :] = rhs_ref[0, r, rows, :] - real
            res_ref[1, r, rows, :] = rhs_ref[1, r, rows, :] - imag


def residual(*args):
    shape = jax.ShapeDtypeStruct((2, R, 2 * LZ, NY), f32)
    return pl.pallas_call(
        residual_kernel,
        out_shape=(shape, shape),
        in_specs=[whole()] * len(args),
        out_specs=(whole(), whole()),
        compiler_params=params(24),
    )(*args)


def pair_groups(step):
    groups = []
    for k in range(G // 2):
        first = (2 * k + step - 1) % G
        second = (first + 1) % G
        for core in range(2):
            groups.append([g * D + 2 * i + core for g in (first, second) for i in range(C)])
    return groups


def shift(value, axis, by):
    size = lax.axis_size(axis)
    return lax.ppermute(value, axis, [(i, i + by) for i in range(size) if 0 <= i + by < size])


def shards(rhs, inverse_blocks, mode_panel, mode_profile, generator, lattice_index, shift_index):
    group = lax.axis_index("layer")
    flat = rhs.reshape(2, R, 2 * LZ, NY)
    own, chunk = prepare(flat, mode_profile)
    gathered = lax.all_gather(own, "plane", axis=0)
    heads = lax.all_to_all(chunk, "plane", 0, 0)
    h = arrange(inverse_blocks.reshape(K, 2, 32, NY))

    mixed = (lattice_index[None, :] * generator[:, None] + shift_index.T) % NPTS
    amplitude = 0.25 / jnp.sqrt(1.0 + jnp.arange(MODES, dtype=f32) / 8.0)
    coef = amplitude[:, None] * ((mixed.astype(f32) + 0.5) / NPTS - 0.5)
    core = lax.rem(lax.axis_index("plane"), 2).astype(jnp.int32).reshape(1)
    twin = [(i, i ^ 1) for i in range(D)]

    base, out = first_product(h, heads)
    v = base
    for step in range(1, G):
        got = lax.all_to_all(out, ("layer", "plane"), 0, 0, axis_index_groups=pair_groups(step))
        other = lax.ppermute(got, "plane", twin)
        behind = v
        if step == 2:
            behind = wavenum = wave(heads, coef, mode_panel.reshape(MODES, 256), v)
        if step == 5:
            y, low, high, last = fronts_of(gathered, h, v)
            behind = last
        if step == 6:
            low, high, last, _ = lax.optimization_barrier((low, high, last, v))
            before = shift(high, "plane", 1)
            after = shift(low, "plane", -1)
            below = shift(last, "layer", 1)
        half = own_half(core, h, got, behind)
        mine = (group == step).astype(jnp.int32).reshape(1)
        v, out = other_half(core, mine, h, other, half, base, v)

    vb = v.astype(bf16)
    nl = shift(vb, "layer", -1)
    vl = shift(jnp.concatenate([vb[:, NY : 2 * NY], vb[:, 3 * NY :]], axis=1), "plane", 1)
    vh = shift(jnp.concatenate([vb[:, :NY], vb[:, 2 * NY : 3 * NY]], axis=1), "plane", -1)
    sol, res = residual(y, flat, before, after, below, v, nl, vl, vh, wavenum)
    return sol.reshape(rhs.shape), res.reshape(rhs.shape)


def solution(mesh):
    return jax.shard_map(
        shards,
        mesh=mesh,
        in_specs=(
            P(None, None, "layer", "plane", None),
            P("layer", None, "plane", None, None, None, None),
            P(None, "plane", None),
            P("plane", "layer"),
            P(),
            P(),
            P(),
        ),
        out_specs=(P(None, None, "layer", "plane", None), P(None, None, "layer", "plane", None)),
        check_vma=False,
    )
```

time: 268 us -> 258 us (0.963)
  blocking collectives: 0 us -> 72.2 us
  Pallas kernels: 48.9 us -> 100 us
  starting transfers between devices: 102 us -> 51.4 us
  local copies, waits for them, and re-layouts: 44 us -> 2.27 us
  waiting for transfers between devices: 54.8 us -> 13.7 us
    all_to_all x0 -> x5, blocking collectives: none -> 72.2 us  [shards(): lax.all_to_all(out, ('layer', 'plane'), 0, 0, axis_index_groups=pair_grou...]
    all_to_all x7 -> x2, starting transfers between devices: 65.9 us -> 12.6 us  [shards(): lax.all_to_all(out, ('layer', 'plane'), 0, 0, axis_index_groups=pair_grou...]
    pallas_call x11 -> x17, Pallas kernels: 43.7 us -> 95 us  [the longest x7 28.2 us: other_half(): pl.pallas_call(other_kernel, out_shape=MATVEC_OUT, in_specs=[whole(pltpu....]
    unnamed x40 -> x16, local copies, waits for them, and re-layouts: 44 us -> 2.27 us
    all_to_all x7 -> x2, waiting for transfers between devices: 51.9 us -> 12.9 us  [shards(): lax.all_to_all(out, ('layer', 'plane'), 0, 0, axis_index_groups=pair_grou...]
    ppermute x0 -> x7, starting transfers between devices: none -> 8.14 us  [shards(): other = lax.ppermute(got, 'plane', twin)]
    ppermute x9 -> x6, starting transfers between devices: 27.7 us -> 22.1 us  [shift(): lax.ppermute(value, axis, [(i, i + by) for i in range(size) if 0 <= i + b...]
  transfers between devices with their start and end apart: 18 -> 17, of which waited for: 9 -> 3; matrix products, arithmetic and copies ran while one was open for 0% -> 0% of each run, Pallas kernels for 17% -> 35%
where the time goes in v2:
time: 258 us; the launch traced here: 254 us
  Pallas kernels  100 us (39%)
  blocking collectives  72.2 us (28%)
  starting transfers between devices  51.4 us (20%)
  between operations  14.3 us (6%)
  waiting for transfers between devices  13.7 us (5%)
    all_to_all x5, blocking collectives, shards(): lax.all_to_all(out, ('layer', 'plane'), 0, 0, axis_index_groups=pair_grou...  72.2 us
    pallas_call x7, Pallas kernels, other_half(): pl.pallas_call(other_kernel, out_shape=MATVEC_OUT, in_specs=[whole(pltpu....  28.2 us
    pallas_call x7, Pallas kernels, own_half(): pl.pallas_call(own_kernel, out_shape=jax.ShapeDtypeStruct((R, K), f32), i...  25.8 us
    ppermute x6, starting transfers between devices, shift(): lax.ppermute(value, axis, [(i, i + by) for i in range(size) if 0 <= i + b...  22.1 us
    pallas_call x1, Pallas kernels, fronts_of(): pl.pallas_call(fronts_kernel, out_shape=(jax.ShapeDtypeStruct((R, LZ, K),...  18.5 us
    pallas_call x1, Pallas kernels, arrange(): pl.pallas_call(arrange_kernel, out_shape=jax.ShapeDtypeStruct((2, C, K, K...  15.1 us
    all_to_all x2, waiting for transfers between devices, shards(): lax.all_to_all(out, ('layer', 'plane'), 0, 0, axis_index_groups=pair_grou...  12.9 us
    all_to_all x2, starting transfers between devices, shards(): lax.all_to_all(out, ('layer', 'plane'), 0, 0, axis_index_groups=pair_grou...  12.6 us
  transfers between devices with their start and end apart: 17, of which 3 were waited for; matrix products, arithmetic and copies ran while one was open for 0% of the time, Pallas kernels for 35%

profile of v2, /device:TPU:7, one launch (start us, length us, event | category | flops | bytes accessed | tf_op | source)
XLA Modules:
  0.0 254.4 jit_solution(14944327896013684960)
XLA Ops:
  7.2 0.0 all-gather.3.cloned.1.call-start
  7.2 0.0 copy-start
  7.2 1.4 copy-done
  8.6 0.7 copy-done.2
  9.3 1.2 shard_map.86
  10.5 0.0 all-gather.3.cloned.1.call-update
  10.5 8.6 %all-to-all-start = ((bf16[16,32,512]{2,1,0:T(8,128)(2,1)}), bf16[16,32,512]{2,1,0:T(8,128)(2,1)S(1)}, u32[]{:S(2)}, u32[]{:S(2)}) async-start(bf16[16,32,512]{2,1,0:T(8,128)(2,1)} %get-tuple-element.29), calls=%async_computation | async-start | bytes 1048576 | tf_op jit(solution)/shard_map/all_to_all | solution.py:304
  19.2 15.1 %shard_map.87.h_ref = bf16[2,8,512,512]{3,2,1,0:T(8,128)(2,1)} custom-call(bf16[512,2,32,128]{3,2,1,0:T(8,128)(2,1)} %bitcast.26), custom_call_target="tpu_custom_call" | custom-call | flops 2000000000 | bytes 17000000 | tf_op jit(solution)/shard_map/pallas_call | solution.py:91
  34.2 0.0 all-to-all-done.x_ref
  34.2 7.4 %shard_map.88 = (f32[8,512]{1,0:T(8,128)S(1)}, bf16[16,8,512]{2,1,0:T(8,128)(2,1)S(1)}) custom-call(bf16[2,8,512,512]{3,2,1,0:T(8,128)(2,1)} %shard_map.87.h_ref, bf16[16,32,512]{2,1,0:T(8,128)(2,1)S(1)} %all-to-all-done.x_ref), custom_call_target="tpu_custom_call" | custom-call | flops 100000000 | bytes 5000000 | tf_op jit(solution)/shard_map/pallas_call | solution.py:127
  41.6 12.9 %all_to_all.40.x_ref = bf16[16,8,512]{2,1,0:T(8,128)(2,1)S(1)} all-to-all(bf16[16,8,512]{2,1,0:T(8,128)(2,1)S(1)} %get-tuple-element.30), channel_id=1, replica_groups={{0,2,4,6,8,10,12,14,16,18,20,22,24,26,28,30},{1,3,5,7,9,11,13,15,17,19,..., dimensions={0} | all-to-all | bytes 262144 | tf_op jit(solution)/shard_map/all_to_all | solution.py:316
  54.5 1.6 collective-permute-start
  56.1 3.7 %shard_map.89.half_ref = f32[8,512]{1,0:T(8,128)S(1)} custom-call(s32[1]{0:T(128)} %bitcast.3.core_ref, bf16[2,8,512,512]{3,2,1,0:T(8,128)(2,1)} %shard_map.87.h_ref, bf16[16,8,512]{2,1,0:T(8,128)(2,1)S(1)} %all_to_all.40.x_ref, f32[8,512]{1,0:T(8,128)S(1)} %get-tuple-element.31.behind_ref.base_ref.old_ref), custom_call_target="tpu_custom_call" | custom-call | flops 100000000 | bytes 5000000 | tf_op jit(solution)/shard_map/pallas_call | solution.py:144
  59.8 0.0 collective-permute-done.x_ref
  59.8 0.0 copy-start.5
  59.8 0.0 copy-start.6
  59.8 0.0 copy-start.3
  59.8 4.4 %shard_map.90 = (f32[8,512]{1,0:T(8,128)S(1)}, bf16[16,8,512]{2,1,0:T(8,128)(2,1)}) custom-call(s32[1]{0:T(128)} %bitcast.3.core_ref, s32[1]{0:T(128)} %bitcast.7.mine_ref, bf16[2,8,512,512]{3,2,1,0:T(8,128)(2,1)} %shard_map.87.h_ref, bf16[16,8,512]{2,1,0:T(8,128)(2,1)S(1)} %collective-permute-done.x_ref, f32[8,512]{1,0:T(8,128)S(1)} %shard_map.89.half_ref, ...), custom_call_target="tpu_custom_call" | custom-call | flops 100000000 | bytes 5000000 | tf_op jit(solution)/shard_map/pallas_call | solution.py:167
  64.2 7.6 %all-to-all-start.2 = ((bf16[16,8,512]{2,1,0:T(8,128)(2,1)}), bf16[16,8,512]{2,1,0:T(8,128)(2,1)S(1)}, u32[]{:S(2)}, u32[]{:S(2)}) async-start(bf16[16,8,512]{2,1,0:T(8,128)(2,1)} %get-tuple-element.32), calls=%async_computation.2 | async-start | bytes 262144 | tf_op jit(solution)/shard_map/all_to_all | solution.py:316
  71.8 0.1 copy.10
  72.0 6.9 %all-to-all-done.2.x_ref = bf16[16,8,512]{2,1,0:T(8,128)(2,1)S(1)} async-done(((bf16[16,8,512]{2,1,0:T(8,128)(2,1)}), bf16[16,8,512]{2,1,0:T(8,128)(2,1)S(1)}, u32[]{:S(2)}, u32[]{:S(2)}) %all-to-all-start.2) | async-done | bytes 131104 | tf_op jit(solution)/shard_map/all_to_all | solution.py:316
  78.8 1.3 collective-permute-start.1
  80.1 0.2 fusion.5.coef_ref
  80.3 1.3 shard_map.91.behind_ref.wave_ref
  81.6 3.8 %shard_map.92.half_ref = f32[8,512]{1,0:T(8,128)S(1)} custom-call(s32[1]{0:T(128)} %bitcast.3.core_ref, bf16[2,8,512,512]{3,2,1,0:T(8,128)(2,1)} %shard_map.87.h_ref, bf16[16,8,512]{2,1,0:T(8,128)(2,1)S(1)} %all-to-all-done.2.x_ref, f32[8,96,256]{2,1,0:T(8,128)S(1)} %shard_map.91.behind_ref.wave_ref), custom_call_target="tpu_custom_call" | custom-call | flops 100000000 | bytes 5000000 | tf_op jit(solution)/shard_map/pallas_call | solution.py:144
  85.4 0.0 collective-permute-done.1.x_ref
  85.4 3.7 %shard_map.93 = (f32[8,512]{1,0:T(8,128)S(1)}, bf16[16,8,512]{2,1,0:T(8,128)(2,1)S(1)}) custom-call(s32[1]{0:T(128)} %bitcast.3.core_ref, s32[1]{0:T(128)} %bitcast.6.mine_ref, bf16[2,8,512,512]{3,2,1,0:T(8,128)(2,1)} %shard_map.87.h_ref, bf16[16,8,512]{2,1,0:T(8,128)(2,1)S(1)} %collective-permute-done.1.x_ref, f32[8,512]{1,0:T(8,128)S(1)} %shard_map.92.half_ref, ...), custom_call_target="tpu_custom_call" | custom-call | flops 100000000 | bytes 5000000 | tf_op jit(solution)/shard_map/pallas_call | solution.py:167
  89.1 10.1 %all_to_all.41.x_ref = bf16[16,8,512]{2,1,0:T(8,128)(2,1)S(1)} all-to-all(bf16[16,8,512]{2,1,0:T(8,128)(2,1)S(1)} %get-tuple-element.34), channel_id=1, replica_groups={{32,34,36,38,40,42,44,46,48,50,52,54,56,58,60,62},{33,35,37,39,41,43,45..., dimensions={0} | all-to-all | bytes 262144 | tf_op jit(solution)/shard_map/all_to_all | solution.py:316
  99.2 1.1 collective-permute-start.2
  100.3 3.7 %shard_map.94.half_ref = f32[8,512]{1,0:T(8,128)S(1)} custom-call(s32[1]{0:T(128)} %bitcast.3.core_ref, bf16[2,8,512,512]{3,2,1,0:T(8,128)(2,1)} %shard_map.87.h_ref, bf16[16,8,512]{2,1,0:T(8,128)(2,1)S(1)} %all_to_all.41.x_ref, f32[8,512]{1,0:T(8,128)S(1)} %get-tuple-element.35.behind_ref.old_ref), custom_call_target="tpu_custom_call" | custom-call | flops 100000000 | bytes 5000000 | tf_op jit(solution)/shard_map/pallas_call | solution.py:144
  104.0 0.0 collective-permute-done.2.x_ref
  104.0 3.7 %shard_map.95 = (f32[8,512]{1,0:T(8,128)S(1)}, bf16[16,8,512]{2,1,0:T(8,128)(2,1)S(1)}) custom-call(s32[1]{0:T(128)} %bitcast.3.core_ref, s32[1]{0:T(128)} %bitcast.5.mine_ref, bf16[2,8,512,512]{3,2,1,0:T(8,128)(2,1)} %shard_map.87.h_ref, bf16[16,8,512]{2,1,0:T(8,128)(2,1)S(1)} %collective-permute-done.2.x_ref, f32[8,512]{1,0:T(8,128)S(1)} %shard_map.94.half_ref, ...), custom_call_target="tpu_custom_call" | custom-call | flops 100000000 | bytes 5000000 | tf_op jit(solution)/shard_map/pallas_call | solution.py:167
  107.7 24.8 %all_to_all.42.x_ref = bf16[16,8,512]{2,1,0:T(8,128)(2,1)S(1)} all-to-all(bf16[16,8,512]{2,1,0:T(8,128)(2,1)S(1)} %get-tuple-element.36), channel_id=1, replica_groups={{48,50,52,54,56,58,60,62,64,66,68,70,72,74,76,78},{49,51,53,55,57,59,61..., dimensions={0} | all-to-all | bytes 262144 | tf_op jit(solution)/shard_map/all_to_all | solution.py:316
  132.5 1.2 collective-permute-start.3
  133.7 3.7 %shard_map.96.half_ref = f32[8,512]{1,0:T(8,128)S(1)} custom-call(s32[1]{0:T(128)} %bitcast.3.core_ref, bf16[2,8,512,512]{3,2,1,0:T(8,128)(2,1)} %shard_map.87.h_ref, bf16[16,8,512]{2,1,0:T(8,128)(2,1)S(1)} %all_to_all.42.x_ref, f32[8,512]{1,0:T(8,128)S(1)} %get-tuple-element.37.behind_ref.old_ref), custom_call_target="tpu_custom_call" | custom-call | flops 100000000 | bytes 5000000 | tf_op jit(solution)/shard_map/pallas_call | solution.py:144
  137.4 0.0 collective-permute-done.3.x_ref
  137.4 4.4 %shard_map.97 = (f32[8,512]{1,0:T(8,128)S(1)}, bf16[16,8,512]{2,1,0:T(8,128)(2,1)}) custom-call(s32[1]{0:T(128)} %bitcast.3.core_ref, s32[1]{0:T(128)} %bitcast.4.mine_ref, bf16[2,8,512,512]{3,2,1,0:T(8,128)(2,1)} %shard_map.87.h_ref, bf16[16,8,512]{2,1,0:T(8,128)(2,1)S(1)} %collective-permute-done.3.x_ref, f32[8,512]{1,0:T(8,128)S(1)} %shard_map.96.half_ref, ...), custom_call_target="tpu_custom_call" | custom-call | flops 100000000 | bytes 5000000 | tf_op jit(solution)/shard_map/pallas_call | solution.py:167
  141.7 5.0 %all-to-all-start.5 = ((bf16[16,8,512]{2,1,0:T(8,128)(2,1)}), bf16[16,8,512]{2,1,0:T(8,128)(2,1)S(1)}, u32[]{:S(2)}, u32[]{:S(2)}) async-start(bf16[16,8,512]{2,1,0:T(8,128)(2,1)} %get-tuple-element.43), calls=%async_computation.5 | async-start | bytes 262144 | tf_op jit(solution)/shard_map/all_to_all | solution.py:316
  146.7 6.1 %all-to-all-done.5.x_ref = bf16[16,8,512]{2,1,0:T(8,128)(2,1)S(1)} async-done(((bf16[16,8,512]{2,1,0:T(8,128)(2,1)}), bf16[16,8,512]{2,1,0:T(8,128)(2,1)S(1)}, u32[]{:S(2)}, u32[]{:S(2)}) %all-to-all-start.5) | async-done | bytes 131104 | tf_op jit(solution)/shard_map/all_to_all | solution.py:316
  152.8 0.6 collective-permute-start.4
  153.4 18.5 %shard_map.98 = (f32[8,96,512]{2,1,0:T(8,128)S(1)}, bf16[8,2,96,128]{3,2,1,0:T(8,128)(2,1)S(1)}, bf16[8,2,96,128]{3,2,1,0:T(8,128)(2,1)S(1)}, bf16[8,512]{1,0:T(8,128)(2,1)S(1)}) custom-call(bf16[16,768,512]{2,1,0:T(8,128)(2,1)} %bitcast.28, bf16[2,8,512,512]{3,2,1,0:T(8,128)(2,1)} %shard_map.87.h_ref, f32[8,512]{1,0:T(8,128)S(1)} %get-tuple-element.38.behind_ref.old_ref), custom_call_target="tpu_custom_call" | custom-call | flops 6000000000 | bytes 23000000 | tf_op jit(solution)/shard_map/pallas_call | solution.py:205
  171.9 3.7 %shard_map.99.half_ref = f32[8,512]{1,0:T(8,128)S(1)} custom-call(s32[1]{0:T(128)} %bitcast.3.core_ref, bf16[2,8,512,512]{3,2,1,0:T(8,128)(2,1)} %shard_map.87.h_ref, bf16[16,8,512]{2,1,0:T(8,128)(2,1)S(1)} %all-to-all-done.5.x_ref, bf16[8,512]{1,0:T(8,128)(2,1)S(1)} %get-tuple-element.47.behind_ref), custom_call_target="tpu_custom_call" | custom-call | flops 100000000 | bytes 5000000 | tf_op jit(solution)/shard_map/pallas_call | solution.py:144
  175.6 0.0 collective-permute-done.4.x_ref
  175.6 3.7 %shard_map.100 = (f32[8,512]{1,0:T(8,128)S(1)}, bf16[16,8,512]{2,1,0:T(8,128)(2,1)S(1)}) custom-call(s32[1]{0:T(128)} %bitcast.3.core_ref, s32[1]{0:T(128)} %bitcast.9.mine_ref, bf16[2,8,512,512]{3,2,1,0:T(8,128)(2,1)} %shard_map.87.h_ref, bf16[16,8,512]{2,1,0:T(8,128)(2,1)S(1)} %collective-permute-done.4.x_ref, f32[8,512]{1,0:T(8,128)S(1)} %shard_map.99.half_ref, ...), custom_call_target="tpu_custom_call" | custom-call | flops 100000000 | bytes 5000000 | tf_op jit(solution)/shard_map/pallas_call | solution.py:167
  179.3 12.3 %all_to_all.43.x_ref = bf16[16,8,512]{2,1,0:T(8,128)(2,1)S(1)} all-to-all(bf16[16,8,512]{2,1,0:T(8,128)(2,1)S(1)} %get-tuple-element.48), channel_id=1, replica_groups={{80,82,84,86,88,90,92,94,96,98,100,102,104,106,108,110},{81,83,85,87,89..., dimensions={0} | all-to-all | bytes 262144 | tf_op jit(solution)/shard_map/all_to_all | solution.py:316
  191.7 1.3 collective-permute-start.8
  193.0 3.7 %shard_map.101.half_ref = f32[8,512]{1,0:T(8,128)S(1)} custom-call(s32[1]{0:T(128)} %bitcast.3.core_ref, bf16[2,8,512,512]{3,2,1,0:T(8,128)(2,1)} %shard_map.87.h_ref, bf16[16,8,512]{2,1,0:T(8,128)(2,1)S(1)} %all_to_all.43.x_ref, f32[8,512]{1,0:T(8,128)S(1)} %get-tuple-element.44.behind_ref.old_ref), custom_call_target="tpu_custom_call" | custom-call | flops 100000000 | bytes 5000000 | tf_op jit(solution)/shard_map/pallas_call | solution.py:144
  196.7 0.0 collective-permute-done.8.x_ref
  196.7 3.7 %shard_map.102 = (f32[8,512]{1,0:T(8,128)S(1)}, bf16[16,8,512]{2,1,0:T(8,128)(2,1)S(1)}) custom-call(s32[1]{0:T(128)} %bitcast.3.core_ref, s32[1]{0:T(128)} %bitcast.11.mine_ref, bf16[2,8,512,512]{3,2,1,0:T(8,128)(2,1)} %shard_map.87.h_ref, bf16[16,8,512]{2,1,0:T(8,128)(2,1)S(1)} %collective-permute-done.8.x_ref, f32[8,512]{1,0:T(8,128)S(1)} %shard_map.101.half_ref, ...), custom_call_target="tpu_custom_call" | custom-call | flops 100000000 | bytes 5000000 | tf_op jit(solution)/shard_map/pallas_call | solution.py:167
  200.4 12.1 %all_to_all.44.x_ref = bf16[16,8,512]{2,1,0:T(8,128)(2,1)S(1)} all-to-all(bf16[16,8,512]{2,1,0:T(8,128)(2,1)S(1)} %get-tuple-element.49), channel_id=1, replica_groups={{96,98,100,102,104,106,108,110,112,114,116,118,120,122,124,126},{97,99,..., dimensions={0} | all-to-all | bytes 262144 | tf_op jit(solution)/shard_map/all_to_all | solution.py:316
  212.5 1.1 collective-permute-start.9
  213.6 4.2 %collective-permute-start.5 = (bf16[8,2,96,128]{3,2,1,0:T(8,128)(2,1)S(1)}, bf16[8,2,96,128]{3,2,1,0:T(8,128)(2,1)S(1)}, u32[]{:S(2)}, u32[]{:S(2)}) collective-permute-start(bf16[8,2,96,128]{3,2,1,0:T(8,128)(2,1)S(1)} %get-tuple-element.45), channel_id=1, source_target_pairs={{0,1},{1,2},{2,3},{3,4},{4,5},{5,6},{6,7},{7,8},{8,9},{9,10},{10,1... | collective-permute-start | bytes 1179656 | tf_op jit(solution)/shard_map/ppermute | solution.py:296
  217.9 1.9 collective-permute-start.6
  219.8 2.5 collective-permute-start.7
  222.4 3.7 %shard_map.103.half_ref = f32[8,512]{1,0:T(8,128)S(1)} custom-call(s32[1]{0:T(128)} %bitcast.3.core_ref, bf16[2,8,512,512]{3,2,1,0:T(8,128)(2,1)} %shard_map.87.h_ref, bf16[16,8,512]{2,1,0:T(8,128)(2,1)S(1)} %all_to_all.44.x_ref, f32[8,512]{1,0:T(8,128)S(1)} %get-tuple-element.50.behind_ref.old_ref), custom_call_target="tpu_custom_call" | custom-call | flops 100000000 | bytes 5000000 | tf_op jit(solution)/shard_map/pallas_call | solution.py:144
  226.1 0.0 collective-permute-done.9.x_ref
  226.1 4.5 %shard_map.104 = (f32[8,512]{1,0:T(8,128)S(1)}, bf16[16,8,512]{2,1,0:T(8,128)(2,1)}) custom-call(s32[1]{0:T(128)} %bitcast.3.core_ref, s32[1]{0:T(128)} %bitcast.10.mine_ref, bf16[2,8,512,512]{3,2,1,0:T(8,128)(2,1)} %shard_map.87.h_ref, bf16[16,8,512]{2,1,0:T(8,128)(2,1)S(1)} %collective-permute-done.9.x_ref, f32[8,512]{1,0:T(8,128)S(1)} %shard_map.103.half_ref, ...), custom_call_target="tpu_custom_call" | custom-call | flops 100000000 | bytes 5000000 | tf_op jit(solution)/shard_map/pallas_call | solution.py:167
  230.6 4.8 %collective-permute-start.10 = (bf16[8,512]{1,0:T(8,128)(2,1)S(1)}, bf16[8,512]{1,0:T(8,128)(2,1)S(1)}, u32[]{:S(2)}, u32[]{:S(2)}) collective-permute-start(bf16[8,512]{1,0:T(8,128)(2,1)S(1)} %convert_element_type.5), channel_id=1, source_target_pairs={{16,0},{32,16},{48,32},{64,48},{80,64},{96,80},{112,96},{17,1},{33... | collective-permute-start | bytes 24584 | tf_op jit(solution)/shard_map/ppermute | solution.py:296
  235.4 3.4 %collective-permute-start.12 = (bf16[8,256]{1,0:T(8,128)(2,1)S(1)}, bf16[8,256]{1,0:T(8,128)(2,1)S(1)}, u32[]{:S(2)}, u32[]{:S(2)}) collective-permute-start(bf16[8,256]{1,0:T(8,128)(2,1)S(1)} %pad_maximum_fusion.1), channel_id=1, source_target_pairs={{1,0},{2,1},{3,2},{4,3},{5,4},{6,5},{7,6},{8,7},{9,8},{10,9},{11,1... | collective-permute-start | bytes 12296 | tf_op jit(solution)/shard_map/ppermute | solution.py:296
  238.8 5.2 %collective-permute-start.11 = (bf16[8,256]{1,0:T(8,128)(2,1)S(1)}, bf16[8,256]{1,0:T(8,128)(2,1)S(1)}, u32[]{:S(2)}, u32[]{:S(2)}) collective-permute-start(bf16[8,256]{1,0:T(8,128)(2,1)S(1)} %pad_maximum_fusion), channel_id=1, source_target_pairs={{0,1},{1,2},{2,3},{3,4},{4,5},{5,6},{6,7},{7,8},{8,9},{9,10},{10,1... | collective-permute-start | bytes 12296 | tf_op jit(solution)/shard_map/ppermute | solution.py:296
  244.0 0.0 collective-permute-done.6.high_ref
  244.0 0.0 collective-permute-done.12.vh_ref
  244.0 0.7 collective-permute-done.11.vl_ref
  244.7 2.8 %shard_map.105 = (f32[2,8,192,128]{3,2,1,0:T(8,128)}, f32[2,8,192,128]{3,2,1,0:T(8,128)}) custom-call(f32[8,96,512]{2,1,0:T(8,128)S(1)} %get-tuple-element.39.y_ref, f32[2,8,192,128]{3,2,1,0:T(8,128)S(1)} %bitcast.24, bf16[8,2,96,128]{3,2,1,0:T(8,128)(2,1)S(1)} %collective-permute-done.5.low_ref, ...), custom_call_target="tpu_custom_call" | custom-call | tf_op jit(solution)/shard_map/pallas_call | solution.py:275
  (18 shorter events, 0.1 us)
Async XLA Ops:
  7.2 146.2 %all-gather.3.cloned.1.call-start = ((), (), s32[]{:S(2)}) async-start(), calls=%async_computation.8 | async-start | bytes 13369344 | tf_op jit(solution)/shard_map/all_gather | solution.py:303
  7.2 1.4 copy-start
  8.6 0.7 copy-start.2
  10.5 23.7 %all-to-all-start = ((bf16[16,32,512]{2,1,0:T(8,128)(2,1)}), bf16[16,32,512]{2,1,0:T(8,128)(2,1)S(1)}, u32[]{:S(2)}, u32[]{:S(2)}) async-start(bf16[16,32,512]{2,1,0:T(8,128)(2,1)} %get-tuple-element.29), calls=%async_computation | async-start | bytes 1048576 | tf_op jit(solution)/shard_map/all_to_all | solution.py:304
  54.5 5.2 %collective-permute-start = (bf16[16,8,512]{2,1,0:T(8,128)(2,1)S(1)}, bf16[16,8,512]{2,1,0:T(8,128)(2,1)S(1)}, u32[]{:S(2)}, u32[]{:S(2)}) collective-permute-start(bf16[16,8,512]{2,1,0:T(8,128)(2,1)S(1)} %all_to_all.40.x_ref), channel_id=1, source_target_pairs={{0,1},{1,0},{2,3},{3,2},{4,5},{5,4},{6,7},{7,6},{8,9},{9,8},{10,11... | collective-permute-start | bytes 393224 | tf_op jit(solution)/shard_map/ppermute | solution.py:317
  59.8 12.0 %copy-start.4 = (s32[8,256]{1,0:T(8,128)S(1)}, s32[8,256]{1,0:T(8,128)}, u32[]{:S(2)}) copy-start(s32[8,256]{1,0:T(8,128)} %param.13) | copy-start | bytes 24580
  59.8 20.3 %copy-start.5 = (s32[256]{0:T(256)S(1)}, s32[256]{0:T(256)}, u32[]{:S(2)}) copy-start(s32[256]{0:T(256)} %param.11) | copy-start | bytes 3076
  59.8 20.3 %copy-start.6 = (s32[8]{0:T(128)S(1)}, s32[8]{0:T(128)}, u32[]{:S(2)}) copy-start(s32[8]{0:T(128)} %param.12) | copy-start | bytes 100
  59.8 20.5 %copy-start.3 = (bf16[256,2,128]{2,1,0:T(2,128)(2,1)S(1)}, bf16[256,2,128]{2,1,0:T(2,128)(2,1)}, u32[]{:S(2)}) copy-start(bf16[256,2,128]{2,1,0:T(2,128)(2,1)} %param.9) | copy-start | bytes 393220
  64.2 14.6 %all-to-all-start.2 = ((bf16[16,8,512]{2,1,0:T(8,128)(2,1)}), bf16[16,8,512]{2,1,0:T(8,128)(2,1)S(1)}, u32[]{:S(2)}, u32[]{:S(2)}) async-start(bf16[16,8,512]{2,1,0:T(8,128)(2,1)} %get-tuple-element.32), calls=%async_computation.2 | async-start | bytes 262144 | tf_op jit(solution)/shard_map/all_to_all | solution.py:316
  78.8 6.5 %collective-permute-start.1 = (bf16[16,8,512]{2,1,0:T(8,128)(2,1)S(1)}, bf16[16,8,512]{2,1,0:T(8,128)(2,1)S(1)}, u32[]{:S(2)}, u32[]{:S(2)}) collective-permute-start(bf16[16,8,512]{2,1,0:T(8,128)(2,1)S(1)} %all-to-all-done.2.x_ref), channel_id=1, source_target_pairs={{0,1},{1,0},{2,3},{3,2},{4,5},{5,4},{6,7},{7,6},{8,9},{9,8},{10,11... | collective-permute-start | bytes 393224 | tf_op jit(solution)/shard_map/ppermute | solution.py:317
  99.2 4.8 %collective-permute-start.2 = (bf16[16,8,512]{2,1,0:T(8,128)(2,1)S(1)}, bf16[16,8,512]{2,1,0:T(8,128)(2,1)S(1)}, u32[]{:S(2)}, u32[]{:S(2)}) collective-permute-start(bf16[16,8,512]{2,1,0:T(8,128)(2,1)S(1)} %all_to_all.41.x_ref), channel_id=1, source_target_pairs={{0,1},{1,0},{2,3},{3,2},{4,5},{5,4},{6,7},{7,6},{8,9},{9,8},{10,11... | collective-permute-start | bytes 393224 | tf_op jit(solution)/shard_map/ppermute | solution.py:317
  132.5 4.8 %collective-permute-start.3 = (bf16[16,8,512]{2,1,0:T(8,128)(2,1)S(1)}, bf16[16,8,512]{2,1,0:T(8,128)(2,1)S(1)}, u32[]{:S(2)}, u32[]{:S(2)}) collective-permute-start(bf16[16,8,512]{2,1,0:T(8,128)(2,1)S(1)} %all_to_all.42.x_ref), channel_id=1, source_target_pairs={{0,1},{1,0},{2,3},{3,2},{4,5},{5,4},{6,7},{7,6},{8,9},{9,8},{10,11... | collective-permute-start | bytes 393224 | tf_op jit(solution)/shard_map/ppermute | solution.py:317
  141.7 11.1 %all-to-all-start.5 = ((bf16[16,8,512]{2,1,0:T(8,128)(2,1)}), bf16[16,8,512]{2,1,0:T(8,128)(2,1)S(1)}, u32[]{:S(2)}, u32[]{:S(2)}) async-start(bf16[16,8,512]{2,1,0:T(8,128)(2,1)} %get-tuple-element.43), calls=%async_computation.5 | async-start | bytes 262144 | tf_op jit(solution)/shard_map/all_to_all | solution.py:316
  152.8 22.8 %collective-permute-start.4 = (bf16[16,8,512]{2,1,0:T(8,128)(2,1)S(1)}, bf16[16,8,512]{2,1,0:T(8,128)(2,1)S(1)}, u32[]{:S(2)}, u32[]{:S(2)}) collective-permute-start(bf16[16,8,512]{2,1,0:T(8,128)(2,1)S(1)} %all-to-all-done.5.x_ref), channel_id=1, source_target_pairs={{0,1},{1,0},{2,3},{3,2},{4,5},{5,4},{6,7},{7,6},{8,9},{9,8},{10,11... | collective-permute-start | bytes 393224 | tf_op jit(solution)/shard_map/ppermute | solution.py:317
  191.7 5.0 %collective-permute-start.8 = (bf16[16,8,512]{2,1,0:T(8,128)(2,1)S(1)}, bf16[16,8,512]{2,1,0:T(8,128)(2,1)S(1)}, u32[]{:S(2)}, u32[]{:S(2)}) collective-permute-start(bf16[16,8,512]{2,1,0:T(8,128)(2,1)S(1)} %all_to_all.43.x_ref), channel_id=1, source_target_pairs={{0,1},{1,0},{2,3},{3,2},{4,5},{5,4},{6,7},{7,6},{8,9},{9,8},{10,11... | collective-permute-start | bytes 393224 | tf_op jit(solution)/shard_map/ppermute | solution.py:317
  212.5 13.5 %collective-permute-start.9 = (bf16[16,8,512]{2,1,0:T(8,128)(2,1)S(1)}, bf16[16,8,512]{2,1,0:T(8,128)(2,1)S(1)}, u32[]{:S(2)}, u32[]{:S(2)}) collective-permute-start(bf16[16,8,512]{2,1,0:T(8,128)(2,1)S(1)} %all_to_all.44.x_ref), channel_id=1, source_target_pairs={{0,1},{1,0},{2,3},{3,2},{4,5},{5,4},{6,7},{7,6},{8,9},{9,8},{10,11... | collective-permute-start | bytes 393224 | tf_op jit(solution)/shard_map/ppermute | solution.py:317
  213.6 30.4 %collective-permute-start.5 = (bf16[8,2,96,128]{3,2,1,0:T(8,128)(2,1)S(1)}, bf16[8,2,96,128]{3,2,1,0:T(8,128)(2,1)S(1)}, u32[]{:S(2)}, u32[]{:S(2)}) collective-permute-start(bf16[8,2,96,128]{3,2,1,0:T(8,128)(2,1)S(1)} %get-tuple-element.45), channel_id=1, source_target_pairs={{0,1},{1,2},{2,3},{3,4},{4,5},{5,6},{6,7},{7,8},{8,9},{9,10},{10,1... | collective-permute-start | bytes 1179656 | tf_op jit(solution)/shard_map/ppermute | solution.py:296
  217.9 26.1 %collective-permute-start.6 = (bf16[8,2,96,128]{3,2,1,0:T(8,128)(2,1)S(1)}, bf16[8,2,96,128]{3,2,1,0:T(8,128)(2,1)S(1)}, u32[]{:S(2)}, u32[]{:S(2)}) collective-permute-start(bf16[8,2,96,128]{3,2,1,0:T(8,128)(2,1)S(1)} %get-tuple-element.46), channel_id=1, source_target_pairs={{1,0},{2,1},{3,2},{4,3},{5,4},{6,5},{7,6},{8,7},{9,8},{10,9},{11,1... | collective-permute-start | bytes 1179656 | tf_op jit(solution)/shard_map/ppermute | solution.py:296
  219.8 19.0 %collective-permute-start.7 = (bf16[8,512]{1,0:T(8,128)(2,1)S(1)}, bf16[8,512]{1,0:T(8,128)(2,1)S(1)}, u32[]{:S(2)}, u32[]{:S(2)}) collective-permute-start(bf16[8,512]{1,0:T(8,128)(2,1)S(1)} %get-tuple-element.47.behind_ref), channel_id=1, source_target_pairs={{0,16},{16,32},{32,48},{48,64},{64,80},{80,96},{96,112},{1,17},{17... | collective-permute-start | bytes 24584 | tf_op jit(solution)/shard_map/ppermute | solution.py:296
  226.1 18.7 %copy-start.1 = (f32[2,8,96,2,128]{4,3,2,1,0:T(2,128)S(1)}, f32[2,8,96,2,128]{4,3,2,1,0:T(2,128)}, u32[]{:S(2)}) copy-start(f32[2,8,96,2,128]{4,3,2,1,0:T(2,128)} %param.7) | copy-start | bytes 4718596
  230.6 14.2 %collective-permute-start.10 = (bf16[8,512]{1,0:T(8,128)(2,1)S(1)}, bf16[8,512]{1,0:T(8,128)(2,1)S(1)}, u32[]{:S(2)}, u32[]{:S(2)}) collective-permute-start(bf16[8,512]{1,0:T(8,128)(2,1)S(1)} %convert_element_type.5), channel_id=1, source_target_pairs={{16,0},{32,16},{48,32},{64,48},{80,64},{96,80},{112,96},{17,1},{33... | collective-permute-start | bytes 24584 | tf_op jit(solution)/shard_map/ppermute | solution.py:296
  235.4 8.6 %collective-permute-start.12 = (bf16[8,256]{1,0:T(8,128)(2,1)S(1)}, bf16[8,256]{1,0:T(8,128)(2,1)S(1)}, u32[]{:S(2)}, u32[]{:S(2)}) collective-permute-start(bf16[8,256]{1,0:T(8,128)(2,1)S(1)} %pad_maximum_fusion.1), channel_id=1, source_target_pairs={{1,0},{2,1},{3,2},{4,3},{5,4},{6,5},{7,6},{8,7},{9,8},{10,9},{11,1... | collective-permute-start | bytes 12296 | tf_op jit(solution)/shard_map/ppermute | solution.py:296
  238.8 5.9 %collective-permute-start.11 = (bf16[8,256]{1,0:T(8,128)(2,1)S(1)}, bf16[8,256]{1,0:T(8,128)(2,1)S(1)}, u32[]{:S(2)}, u32[]{:S(2)}) collective-permute-start(bf16[8,256]{1,0:T(8,128)(2,1)S(1)} %pad_maximum_fusion), channel_id=1, source_target_pairs={{0,1},{1,2},{2,3},{3,4},{4,5},{5,6},{6,7},{7,8},{8,9},{9,10},{10,1... | collective-permute-start | bytes 12296 | tf_op jit(solution)/shard_map/ppermute | solution.py:296
Sparse Core Ops, SparseCore 0:
  11.0 95.1 all-gather.2

commit v3 on v2

--- a/solution.py
+++ b/solution.py
@@ -61,30 +61,44 @@
     )(rhs, profile)
 
 
-def arrange_kernel(blocks_ref, h_ref):
+def arrange_kernel(blocks_ref, h_ref, in_buf, out_buf, in_sem, out_sem):
     m = lax.broadcasted_iota(jnp.int32, (256, 256), 0)
     n = lax.broadcasted_iota(jnp.int32, (256, 256), 1)
     swap = ((m // 16 == n % 16) & (m % 16 == n // 16)).astype(f32).astype(bf16)
 
-    def body(b_ref, out_ref):
+    def rows(i):
+        return pl.ds(pl.multiple_of(i * 32, 32), 32)
+
+    def load(i):
+        return pltpu.make_async_copy(blocks_ref.at[rows(i)], in_buf.at[i], in_sem.at[i])
+
+    def store(i):
+        return pltpu.make_async_copy(out_buf.at[:, :, rows(i)], h_ref.at[:, :, rows(i)], out_sem.at[i])
+
+    for i in range(K // 32):
+        load(i).start()
+
+    @pl.loop(0, K // 32)
+    def _(i):
+        load(i).wait()
         for s in range(2):
-            for c in range(2):
-                for half in range(2):
-                    tile = b_ref[pl.ds(s * 16, 16), c, pl.ds(half * 16, 16), :].reshape(256, NY)
-                    moved = jnp.dot(swap, tile, preferred_element_type=f32).astype(bf16)
-                    for q in range(16):
-                        p = half * 16 + q
-                        source = p // 2
-                        out_ref[source % 2, source // 2, pl.ds(s * 16, 16), pl.ds(c * 256 + (p % 2) * NY, NY)] = moved[
-                            q * 16 : (q + 1) * 16
+            for half in range(2):
+                tile = jnp.concatenate(
+                    [in_buf[i, pl.ds(s * 16, 16), c, pl.ds(half * 16, 16), :].reshape(256, NY) for c in range(2)], axis=1
+                )
+                moved = jnp.dot(swap, tile, preferred_element_type=f32).astype(bf16)
+                for q in range(16):
+                    p = half * 16 + q
+                    source = p // 2
+                    into = pl.ds(pl.multiple_of(i * 32 + s * 16, 16), 16)
+                    for c in range(2):
+                        out_buf[source % 2, source // 2, into, pl.ds(c * 256 + (p % 2) * NY, NY)] = moved[
+                            q * 16 : (q + 1) * 16, c * NY : (c + 1) * NY
                         ]
-
-    pltpu.emit_pipeline(
-        body,
-        grid=(K // 32,),
-        in_specs=[pl.BlockSpec((32, 2, 32, NY), lambda i: (i, 0, 0, 0))],
-        out_specs=[pl.BlockSpec((2, C, 32, K), lambda i: (0, 0, i, 0))],
-    )(blocks_ref, h_ref)
+        store(i).start()
+
+    for i in range(K // 32):
+        store(i).wait()
 
 
 def arrange(blocks):
@@ -93,34 +107,43 @@
         out_shape=jax.ShapeDtypeStruct((2, C, K, K), bf16),
         in_specs=[whole(pltpu.HBM)],
         out_specs=whole(pltpu.HBM),
-        compiler_params=params(50),
-        cost_estimate=pl.CostEstimate(flops=2 * 10**9, bytes_accessed=17 * 10**6, transcendentals=0),
+        scratch_shapes=[
+            VMEM((K // 32, 32, 2, 32, NY), bf16),
+            VMEM((2, C, K, K), bf16),
+            pltpu.SemaphoreType.DMA((K // 32,)),
+            pltpu.SemaphoreType.DMA((K // 32,)),
+        ],
+        compiler_params=params(50),
+        cost_estimate=pl.CostEstimate(flops=4 * 10**9, bytes_accessed=17 * 10**6, transcendentals=0),
     )(blocks)
 
 
 COST = pl.CostEstimate(flops=10**8, bytes_accessed=5 * 10**6, transcendentals=0)
-CHUNK = 2
-
-
-def stream(h_ref, acc_ref, core, operand):
-    def body(b_ref):
-        first = pl.program_id(0) * CHUNK
-        for j in range(CHUNK):
-            acc_ref[...] += dot_t(operand(first + j), b_ref[j])
-
-    pltpu.emit_pipeline(
-        body, grid=(C // CHUNK,), in_specs=[pl.BlockSpec((None, CHUNK, K, K), lambda k: (core, k, 0, 0))]
-    )(h_ref)
-
-
-def first_kernel(h_ref, x_ref, v_ref, out_ref, acc_ref):
-    acc_ref[...] = jnp.zeros((16, K), f32)
+
+
+def fetch(h_ref, buf, sem, core):
+    copies = [pltpu.make_async_copy(h_ref.at[core, k], buf.at[k], sem.at[k]) for k in range(C)]
+    for copy in copies:
+        copy.start()
+    return copies
+
+
+def first_kernel(h_ref, x_ref, v_ref, out_ref, even, odd, even_sem, odd_sem):
+    bufs = (even, odd)
+    copies = [fetch(h_ref, bufs[core], (even_sem, odd_sem)[core], core) for core in range(2)]
+    acc = jnp.zeros((16, K), f32)
     for core in range(2):
-        stream(h_ref, acc_ref, core, lambda k: x_ref[2 * k + core, pl.ds(0, 16), :])
-    v = acc_ref[pl.ds(0, R), :]
+        for k in range(C):
+            copies[core][k].wait()
+            acc = acc + dot_t(x_ref[2 * k + core, pl.ds(0, 16), :], bufs[core][k])
+    v = acc[:R]
     v_ref[...] = v
     for i in range(D):
         out_ref[i] = v.astype(bf16)
+
+
+HALF = [VMEM((C, K, K), bf16)]
+SEMS = [pltpu.SemaphoreType.DMA((C,))]
 
 
 def first_product(h, x):
@@ -129,32 +152,38 @@
         out_shape=MATVEC_OUT,
         in_specs=[whole(pltpu.HBM), whole()],
         out_specs=(whole(), whole()),
-        scratch_shapes=[VMEM((16, K), f32)],
+        scratch_shapes=HALF * 2 + SEMS * 2,
         compiler_params=params(50),
         cost_estimate=COST,
     )(h, x)
 
 
-def own_kernel(core_ref, h_ref, x_ref, behind_ref, acc_ref):
-    acc_ref[...] = jnp.zeros((R, K), f32)
-    stream(h_ref, acc_ref, core_ref[0], lambda k: x_ref[k])
-
-
-def own_half(core, h, x, behind):
+def own_kernel(core_ref, h_ref, x_ref, acc_ref, buf, sem):
+    acc = jnp.zeros((R, K), f32)
+    for k, copy in enumerate(fetch(h_ref, buf, sem, core_ref[0])):
+        copy.wait()
+        acc = acc + dot_t(x_ref[k], buf[k])
+    acc_ref[...] = acc
+
+
+def own_half(core, h, x):
     return pl.pallas_call(
         own_kernel,
         out_shape=jax.ShapeDtypeStruct((R, K), f32),
-        in_specs=[whole(pltpu.SMEM), whole(pltpu.HBM), whole(), whole(pl.ANY)],
+        in_specs=[whole(pltpu.SMEM), whole(pltpu.HBM), whole()],
         out_specs=whole(),
+        scratch_shapes=HALF + SEMS,
         compiler_params=params(50),
         cost_estimate=COST,
-    )(core, h, x, behind)
-
-
-def other_kernel(core_ref, mine_ref, h_ref, x_ref, half_ref, base_ref, old_ref, v_ref, out_ref, acc_ref):
-    acc_ref[...] = half_ref[...]
-    stream(h_ref, acc_ref, 1 - core_ref[0], lambda k: x_ref[k])
-    v = jnp.where(mine_ref[0] > 0, base_ref[...] + COUPLING * acc_ref[...], old_ref[...])
+    )(core, h, x)
+
+
+def other_kernel(core_ref, mine_ref, h_ref, x_ref, half_ref, base_ref, old_ref, v_ref, out_ref, buf, sem):
+    acc = half_ref[...]
+    for k, copy in enumerate(fetch(h_ref, buf, sem, 1 - core_ref[0])):
+        copy.wait()
+        acc = acc + dot_t(x_ref[k], buf[k])
+    v = jnp.where(mine_ref[0] > 0, base_ref[...] + COUPLING * acc, old_ref[...])
     v_ref[...] = v
     for i in range(D):
         out_ref[i] = v.astype(bf16)
@@ -169,30 +198,34 @@
         out_shape=MATVEC_OUT,
         in_specs=[whole(pltpu.SMEM)] * 2 + [whole(pltpu.HBM)] + [whole()] * 4,
         out_specs=(whole(), whole()),
-        scratch_shapes=[VMEM((R, K), f32)],
+        scratch_shapes=HALF + SEMS,
         compiler_params=params(50),
         cost_estimate=COST,
     )(core, mine, h, x, half, base, old)
 
 
-def fronts_kernel(x_ref, h_ref, behind_ref, y_ref, low_ref, high_ref, last_ref):
-    def body(x_block, h_block):
-        @pl.when(pl.program_id(0) == 0)
-        def _():
-            y_ref[...] = jnp.zeros((R, LZ, K), f32)
-
+def fronts_kernel(x_ref, h_ref, behind_ref, y_ref, low_ref, high_ref, last_ref, x_buf, h_buf, x_sem, h_sem):
+    def loads(i):
+        return (
+            pltpu.make_async_copy(x_ref.at[i], x_buf.at[i], x_sem.at[i]),
+            pltpu.make_async_copy(h_ref.at[lax.rem(i, 2), lax.div(i, 2)], h_buf.at[i], h_sem.at[i]),
+        )
+
+    @pl.loop(0, D)
+    def _(i):
+        for copy in loads(i):
+            copy.start()
+
+    y_ref[...] = jnp.zeros((R, LZ, K), f32)
+
+    @pl.loop(0, D)
+    def _(i):
+        for copy in loads(i):
+            copy.wait()
         for part in range(4):
             rows = pl.ds(part * 2 * LZ, 2 * LZ)
-            y_ref[pl.ds(2 * part, 2)] += dot_t(x_block[rows, :], h_block[...]).reshape(2, LZ, K)
-
-    pltpu.emit_pipeline(
-        body,
-        grid=(D,),
-        in_specs=[
-            pl.BlockSpec((None, R * LZ, K), lambda i: (i, 0, 0)),
-            pl.BlockSpec((None, None, K, K), lambda i: (lax.rem(i, 2), lax.div(i, 2), 0, 0)),
-        ],
-    )(x_ref, h_ref)
+            y_ref[pl.ds(2 * part, 2)] += dot_t(x_buf[i, rows, :], h_buf[i]).reshape(2, LZ, K)
+
     for r in range(R):
         for a in range(2):
             low_ref[r, a] = y_ref[r, :, a * 256 : a * 256 + NY].astype(bf16)
@@ -207,6 +240,12 @@
         out_shape=(jax.ShapeDtypeStruct((R, LZ, K), f32), halo, halo, jax.ShapeDtypeStruct((R, K), bf16)),
         in_specs=[whole(pltpu.HBM), whole(pltpu.HBM), whole(pl.ANY)],
         out_specs=(whole(),) * 4,
+        scratch_shapes=[
+            VMEM((D, R * LZ, K), bf16),
+            VMEM((D, K, K), bf16),
+            pltpu.SemaphoreType.DMA((D,)),
+            pltpu.SemaphoreType.DMA((D,)),
+        ],
         compiler_params=params(50),
         cost_estimate=pl.CostEstimate(flops=6 * 10**9, bytes_accessed=23 * 10**6, transcendentals=0),
     )(x, h, behind)
@@ -314,19 +353,20 @@
     v = base
     for step in range(1, G):
         got = lax.all_to_all(out, ("layer", "plane"), 0, 0, axis_index_groups=pair_groups(step))
-        other = lax.ppermute(got, "plane", twin)
-        behind = v
         if step == 2:
-            behind = wavenum = wave(heads, coef, mode_panel.reshape(MODES, 256), v)
+            wavenum = wave(heads, coef, mode_panel.reshape(MODES, 256), v)
+            got, wavenum = lax.optimization_barrier((got, wavenum))
         if step == 5:
             y, low, high, last = fronts_of(gathered, h, v)
-            behind = last
+            got, low, high, last = lax.optimization_barrier((got, low, high, last))
         if step == 6:
-            low, high, last, _ = lax.optimization_barrier((low, high, last, v))
+            low, high, last, v = lax.optimization_barrier((low, high, last, v))
             before = shift(high, "plane", 1)
             after = shift(low, "plane", -1)
             below = shift(last, "layer", 1)
-        half = own_half(core, h, got, behind)
+            got, before, after, below = lax.optimization_barrier((got, before, after, below))
+        other = lax.ppermute(got, "plane", twin)
+        half = own_half(core, h, got)
         mine = (group == step).astype(jnp.int32).reshape(1)
         v, out = other_half(core, mine, h, other, half, base, v)
 

time: 258 us -> 235 us (0.911)
  Pallas kernels: 100 us -> 70.6 us
  starting transfers between devices: 51.4 us -> 58.6 us
    all_to_all x2 -> x3, starting transfers between devices: 12.6 us -> 21.5 us  [shards(): lax.all_to_all(out, ('layer', 'plane'), 0, 0, axis_index_groups=pair_grou...]
    pallas_call x7, Pallas kernels: 25.8 us -> 17.4 us  [own_half(): pl.pallas_call(own_kernel, out_shape=jax.ShapeDtypeStruct((R, K), f32), i...]
    pallas_call x7, Pallas kernels: 28.2 us -> 20.1 us  [other_half(): pl.pallas_call(other_kernel, out_shape=MATVEC_OUT, in_specs=[whole(pltpu....]
    pallas_call x1, Pallas kernels: 15.1 us -> 7.07 us  [arrange(): pl.pallas_call(arrange_kernel, out_shape=jax.ShapeDtypeStruct((2, C, K, K...]
    all_to_all x2 -> x3, waiting for transfers between devices: 12.9 us -> 5.51 us  [shards(): lax.all_to_all(out, ('layer', 'plane'), 0, 0, axis_index_groups=pair_grou...]
    ppermute x6, starting transfers between devices: 22.1 us -> 16.8 us  [shift(): lax.ppermute(value, axis, [(i, i + by) for i in range(size) if 0 <= i + b...]
    ppermute x6, waiting for transfers between devices: 0.71 us -> 5.6 us  [shift(): lax.ppermute(value, axis, [(i, i + by) for i in range(size) if 0 <= i + b...]
    ppermute x7, starting transfers between devices: 8.14 us -> 11.7 us  [shards(): other = lax.ppermute(got, 'plane', twin)]
  transfers between devices with their start and end apart: 17 -> 18, of which waited for: 3 -> 4; matrix products, arithmetic and copies ran while one was open for 0% -> 0% of each run, Pallas kernels for 35% -> 25%
where the time goes in v3:
time: 235 us; the launch traced here: 232 us
  blocking collectives  71.4 us (30%)
  Pallas kernels  70.6 us (30%)
  starting transfers between devices  58.6 us (25%)
  between operations  14.4 us (6%)
  waiting for transfers between devices  14.2 us (6%)
    all_to_all x4, blocking collectives, shards(): lax.all_to_all(out, ('layer', 'plane'), 0, 0, axis_index_groups=pair_grou...  71.4 us
    all_to_all x3, starting transfers between devices, shards(): lax.all_to_all(out, ('layer', 'plane'), 0, 0, axis_index_groups=pair_grou...  21.5 us
    pallas_call x7, Pallas kernels, other_half(): pl.pallas_call(other_kernel, out_shape=MATVEC_OUT, in_specs=[whole(pltpu....  20.1 us
    pallas_call x7, Pallas kernels, own_half(): pl.pallas_call(own_kernel, out_shape=jax.ShapeDtypeStruct((R, K), f32), i...  17.4 us
    ppermute x6, starting transfers between devices, shift(): lax.ppermute(value, axis, [(i, i + by) for i in range(size) if 0 <= i + b...  16.8 us
    pallas_call x1, Pallas kernels, fronts_of(): pl.pallas_call(fronts_kernel, out_shape=(jax.ShapeDtypeStruct((R, LZ, K),...  16 us
    ppermute x7, starting transfers between devices, shards(): other = lax.ppermute(got, 'plane', twin)  11.7 us
    all_to_all x1, starting transfers between devices, shards(): heads = lax.all_to_all(chunk, 'plane', 0, 0)  8.62 us
  transfers between devices with their start and end apart: 18, of which 4 were waited for; matrix products, arithmetic and copies ran while one was open for 0% of the time, Pallas kernels for 25%

profile of v3, /device:TPU:7, one launch (start us, length us, event | category | flops | bytes accessed | tf_op | source)
XLA Modules:
  0.0 231.7 jit_solution(8255778434510124247)
XLA Ops:
  7.2 0.0 all-gather.3.cloned.1.call-start
  7.2 0.0 copy-start
  7.2 1.4 copy-done
  8.6 0.7 copy-done.2
  9.3 1.2 shard_map.86
  10.5 0.0 all-gather.3.cloned.1.call-update
  10.5 8.6 %all-to-all-start = ((bf16[16,32,512]{2,1,0:T(8,128)(2,1)}), bf16[16,32,512]{2,1,0:T(8,128)(2,1)S(1)}, u32[]{:S(2)}, u32[]{:S(2)}) async-start(bf16[16,32,512]{2,1,0:T(8,128)(2,1)} %get-tuple-element.40), calls=%async_computation | async-start | bytes 1048576 | tf_op jit(solution)/shard_map/all_to_all | solution.py:343
  19.2 7.1 %shard_map.87.h_ref = bf16[2,8,512,512]{3,2,1,0:T(8,128)(2,1)} custom-call(bf16[512,2,32,128]{3,2,1,0:T(8,128)(2,1)} %bitcast.26), custom_call_target="tpu_custom_call" | custom-call | flops 4000000000 | bytes 17000000 | tf_op jit(solution)/shard_map/pallas_call | solution.py:105
  26.2 0.0 copy-start.4
  26.2 3.0 %all-to-all-done.x_ref = bf16[16,32,512]{2,1,0:T(8,128)(2,1)S(1)} async-done(((bf16[16,32,512]{2,1,0:T(8,128)(2,1)}), bf16[16,32,512]{2,1,0:T(8,128)(2,1)S(1)}, u32[]{:S(2)}, u32[]{:S(2)}) %all-to-all-start) | async-done | bytes 524320 | tf_op jit(solution)/shard_map/all_to_all | solution.py:343
  29.3 4.8 %shard_map.88 = (f32[8,512]{1,0:T(8,128)S(1)}, bf16[16,8,512]{2,1,0:T(8,128)(2,1)S(1)}) custom-call(bf16[2,8,512,512]{3,2,1,0:T(8,128)(2,1)} %shard_map.87.h_ref, bf16[16,32,512]{2,1,0:T(8,128)(2,1)S(1)} %all-to-all-done.x_ref), custom_call_target="tpu_custom_call" | custom-call | flops 100000000 | bytes 5000000 | tf_op jit(solution)/shard_map/pallas_call | solution.py:150
  34.0 10.9 %all_to_all.40.x_ref = bf16[16,8,512]{2,1,0:T(8,128)(2,1)S(1)} all-to-all(bf16[16,8,512]{2,1,0:T(8,128)(2,1)S(1)} %get-tuple-element.41), channel_id=1, replica_groups={{0,2,4,6,8,10,12,14,16,18,20,22,24,26,28,30},{1,3,5,7,9,11,13,15,17,19,..., dimensions={0} | all-to-all | bytes 262144 | tf_op jit(solution)/shard_map/all_to_all | solution.py:355
  44.9 2.1 collective-permute-start
  47.0 0.1 copy.10
  47.2 2.5 %shard_map.89.half_ref = f32[8,512]{1,0:T(8,128)S(1)} custom-call(s32[1]{0:T(128)} %bitcast.3.core_ref, bf16[2,8,512,512]{3,2,1,0:T(8,128)(2,1)} %shard_map.87.h_ref, bf16[16,8,512]{2,1,0:T(8,128)(2,1)S(1)} %all_to_all.40.x_ref), custom_call_target="tpu_custom_call" | custom-call | flops 100000000 | bytes 5000000 | tf_op jit(solution)/shard_map/pallas_call | solution.py:170
  49.7 0.0 copy-start.5
  49.7 0.0 copy-start.6
  49.7 0.0 copy-start.3
  49.7 3.2 %shard_map.90 = (f32[8,512]{1,0:T(8,128)S(1)}, bf16[16,8,512]{2,1,0:T(8,128)(2,1)}) custom-call(s32[1]{0:T(128)} %bitcast.3.core_ref, s32[1]{0:T(128)} %bitcast.7.mine_ref, bf16[2,8,512,512]{3,2,1,0:T(8,128)(2,1)} %shard_map.87.h_ref, bf16[16,8,512]{2,1,0:T(8,128)(2,1)S(1)} %collective-permute-done.x_ref, f32[8,512]{1,0:T(8,128)S(1)} %shard_map.89.half_ref, ...), custom_call_target="tpu_custom_call" | custom-call | flops 100000000 | bytes 5000000 | tf_op jit(solution)/shard_map/pallas_call | solution.py:196
  52.9 7.7 %all-to-all-start.2 = ((bf16[16,8,512]{2,1,0:T(8,128)(2,1)}), bf16[16,8,512]{2,1,0:T(8,128)(2,1)S(1)}, u32[]{:S(2)}, u32[]{:S(2)}) async-start(bf16[16,8,512]{2,1,0:T(8,128)(2,1)} %get-tuple-element.43), calls=%async_computation.2 | async-start | bytes 262144 | tf_op jit(solution)/shard_map/all_to_all | solution.py:355
  60.6 0.2 fusion.5.coef_ref
  60.8 1.3 shard_map.91.wave_ref
  62.1 5.5 %all-to-all-done.2.x_ref = bf16[16,8,512]{2,1,0:T(8,128)(2,1)S(1)} async-done(((bf16[16,8,512]{2,1,0:T(8,128)(2,1)}), bf16[16,8,512]{2,1,0:T(8,128)(2,1)S(1)}, u32[]{:S(2)}, u32[]{:S(2)}) %all-to-all-start.2) | async-done | bytes 131104 | tf_op jit(solution)/shard_map/all_to_all | solution.py:355
  67.6 1.2 collective-permute-start.1
  68.9 2.5 %shard_map.92.half_ref = f32[8,512]{1,0:T(8,128)S(1)} custom-call(s32[1]{0:T(128)} %bitcast.3.core_ref, bf16[2,8,512,512]{3,2,1,0:T(8,128)(2,1)} %shard_map.87.h_ref, bf16[16,8,512]{2,1,0:T(8,128)(2,1)S(1)} %all-to-all-done.2.x_ref), custom_call_target="tpu_custom_call" | custom-call | flops 100000000 | bytes 5000000 | tf_op jit(solution)/shard_map/pallas_call | solution.py:170
  71.4 0.0 collective-permute-done.1.x_ref
  71.4 2.5 %shard_map.93 = (f32[8,512]{1,0:T(8,128)S(1)}, bf16[16,8,512]{2,1,0:T(8,128)(2,1)S(1)}) custom-call(s32[1]{0:T(128)} %bitcast.3.core_ref, s32[1]{0:T(128)} %bitcast.6.mine_ref, bf16[2,8,512,512]{3,2,1,0:T(8,128)(2,1)} %shard_map.87.h_ref, bf16[16,8,512]{2,1,0:T(8,128)(2,1)S(1)} %collective-permute-done.1.x_ref, f32[8,512]{1,0:T(8,128)S(1)} %shard_map.92.half_ref, ...), custom_call_target="tpu_custom_call" | custom-call | flops 100000000 | bytes 5000000 | tf_op jit(solution)/shard_map/pallas_call | solution.py:196
  73.9 10.8 %all_to_all.41.x_ref = bf16[16,8,512]{2,1,0:T(8,128)(2,1)S(1)} all-to-all(bf16[16,8,512]{2,1,0:T(8,128)(2,1)S(1)} %get-tuple-element.46), channel_id=1, replica_groups={{32,34,36,38,40,42,44,46,48,50,52,54,56,58,60,62},{33,35,37,39,41,43,45..., dimensions={0} | all-to-all | bytes 262144 | tf_op jit(solution)/shard_map/all_to_all | solution.py:355
  84.7 1.4 collective-permute-start.2
  86.1 2.5 %shard_map.94.half_ref = f32[8,512]{1,0:T(8,128)S(1)} custom-call(s32[1]{0:T(128)} %bitcast.3.core_ref, bf16[2,8,512,512]{3,2,1,0:T(8,128)(2,1)} %shard_map.87.h_ref, bf16[16,8,512]{2,1,0:T(8,128)(2,1)S(1)} %all_to_all.41.x_ref), custom_call_target="tpu_custom_call" | custom-call | flops 100000000 | bytes 5000000 | tf_op jit(solution)/shard_map/pallas_call | solution.py:170
  88.6 0.0 collective-permute-done.2.x_ref
  88.6 2.5 %shard_map.95 = (f32[8,512]{1,0:T(8,128)S(1)}, bf16[16,8,512]{2,1,0:T(8,128)(2,1)S(1)}) custom-call(s32[1]{0:T(128)} %bitcast.3.core_ref, s32[1]{0:T(128)} %bitcast.5.mine_ref, bf16[2,8,512,512]{3,2,1,0:T(8,128)(2,1)} %shard_map.87.h_ref, bf16[16,8,512]{2,1,0:T(8,128)(2,1)S(1)} %collective-permute-done.2.x_ref, f32[8,512]{1,0:T(8,128)S(1)} %shard_map.94.half_ref, ...), custom_call_target="tpu_custom_call" | custom-call | flops 100000000 | bytes 5000000 | tf_op jit(solution)/shard_map/pallas_call | solution.py:196
  91.1 37.8 %all_to_all.42.x_ref = bf16[16,8,512]{2,1,0:T(8,128)(2,1)S(1)} all-to-all(bf16[16,8,512]{2,1,0:T(8,128)(2,1)S(1)} %get-tuple-element.48), channel_id=1, replica_groups={{48,50,52,54,56,58,60,62,64,66,68,70,72,74,76,78},{49,51,53,55,57,59,61..., dimensions={0} | all-to-all | bytes 262144 | tf_op jit(solution)/shard_map/all_to_all | solution.py:355
  128.9 1.2 collective-permute-start.3
  130.0 2.5 %shard_map.96.half_ref = f32[8,512]{1,0:T(8,128)S(1)} custom-call(s32[1]{0:T(128)} %bitcast.3.core_ref, bf16[2,8,512,512]{3,2,1,0:T(8,128)(2,1)} %shard_map.87.h_ref, bf16[16,8,512]{2,1,0:T(8,128)(2,1)S(1)} %all_to_all.42.x_ref), custom_call_target="tpu_custom_call" | custom-call | flops 100000000 | bytes 5000000 | tf_op jit(solution)/shard_map/pallas_call | solution.py:170
  132.5 3.1 %shard_map.97 = (f32[8,512]{1,0:T(8,128)S(1)}, bf16[16,8,512]{2,1,0:T(8,128)(2,1)}) custom-call(s32[1]{0:T(128)} %bitcast.3.core_ref, s32[1]{0:T(128)} %bitcast.4.mine_ref, bf16[2,8,512,512]{3,2,1,0:T(8,128)(2,1)} %shard_map.87.h_ref, bf16[16,8,512]{2,1,0:T(8,128)(2,1)S(1)} %collective-permute-done.3.x_ref, f32[8,512]{1,0:T(8,128)S(1)} %shard_map.96.half_ref, ...), custom_call_target="tpu_custom_call" | custom-call | flops 100000000 | bytes 5000000 | tf_op jit(solution)/shard_map/pallas_call | solution.py:196
  135.7 5.0 %all-to-all-start.5 = ((bf16[16,8,512]{2,1,0:T(8,128)(2,1)}), bf16[16,8,512]{2,1,0:T(8,128)(2,1)S(1)}, u32[]{:S(2)}, u32[]{:S(2)}) async-start(bf16[16,8,512]{2,1,0:T(8,128)(2,1)} %get-tuple-element.52), calls=%async_computation.5 | async-start | bytes 262144 | tf_op jit(solution)/shard_map/all_to_all | solution.py:355
  140.7 0.0 all-gather.3.cloned.1.call-done
  140.7 16.0 %shard_map.98 = (f32[8,96,512]{2,1,0:T(8,128)S(1)}, bf16[8,2,96,128]{3,2,1,0:T(8,128)(2,1)}, bf16[8,2,96,128]{3,2,1,0:T(8,128)(2,1)}, bf16[8,512]{1,0:T(8,128)(2,1)S(1)}) custom-call(bf16[16,768,512]{2,1,0:T(8,128)(2,1)} %bitcast.28, bf16[2,8,512,512]{3,2,1,0:T(8,128)(2,1)} %shard_map.87.h_ref, f32[8,512]{1,0:T(8,128)S(1)} %get-tuple-element.50.behind_ref.old_ref), custom_call_target="tpu_custom_call" | custom-call | flops 6000000000 | bytes 23000000 | tf_op jit(solution)/shard_map/pallas_call | solution.py:238
  156.7 0.7 collective-permute-start.4
  157.4 2.5 %shard_map.99.half_ref = f32[8,512]{1,0:T(8,128)S(1)} custom-call(s32[1]{0:T(128)} %bitcast.3.core_ref, bf16[2,8,512,512]{3,2,1,0:T(8,128)(2,1)} %shard_map.87.h_ref, bf16[16,8,512]{2,1,0:T(8,128)(2,1)S(1)} %all-to-all-done.5.x_ref), custom_call_target="tpu_custom_call" | custom-call | flops 100000000 | bytes 5000000 | tf_op jit(solution)/shard_map/pallas_call | solution.py:170
  159.9 0.0 collective-permute-done.4.x_ref
  159.9 3.1 %shard_map.100 = (f32[8,512]{1,0:T(8,128)S(1)}, bf16[16,8,512]{2,1,0:T(8,128)(2,1)}) custom-call(s32[1]{0:T(128)} %bitcast.3.core_ref, s32[1]{0:T(128)} %bitcast.9.mine_ref, bf16[2,8,512,512]{3,2,1,0:T(8,128)(2,1)} %shard_map.87.h_ref, bf16[16,8,512]{2,1,0:T(8,128)(2,1)S(1)} %collective-permute-done.4.x_ref, f32[8,512]{1,0:T(8,128)S(1)} %shard_map.99.half_ref, ...), custom_call_target="tpu_custom_call" | custom-call | flops 100000000 | bytes 5000000 | tf_op jit(solution)/shard_map/pallas_call | solution.py:196
  163.0 3.1 %collective-permute-start.5 = (bf16[8,2,96,128]{3,2,1,0:T(8,128)(2,1)}, bf16[8,2,96,128]{3,2,1,0:T(8,128)(2,1)S(1)}, u32[]{:S(2)}, u32[]{:S(2)}) collective-permute-start(bf16[8,2,96,128]{3,2,1,0:T(8,128)(2,1)} %get-tuple-element.62), channel_id=1, source_target_pairs={{0,1},{1,2},{2,3},{3,4},{4,5},{5,6},{6,7},{7,8},{8,9},{9,10},{10,1... | collective-permute-start | bytes 1179656 | tf_op jit(solution)/shard_map/ppermute | solution.py:335
  166.1 1.9 collective-permute-start.6
  168.0 8.8 %all-to-all-start.6 = ((bf16[16,8,512]{2,1,0:T(8,128)(2,1)}), bf16[16,8,512]{2,1,0:T(8,128)(2,1)S(1)}, u32[]{:S(2)}, u32[]{:S(2)}) async-start(bf16[16,8,512]{2,1,0:T(8,128)(2,1)} %get-tuple-element.57), calls=%async_computation.6 | async-start | bytes 262144 | tf_op jit(solution)/shard_map/all_to_all | solution.py:355
  176.8 1.9 collective-permute-start.7
  178.7 4.9 %collective-permute-done.7.prev_ref = bf16[8,512]{1,0:T(8,128)(2,1)S(1)} collective-permute-done((bf16[8,512]{1,0:T(8,128)(2,1)S(1)}, bf16[8,512]{1,0:T(8,128)(2,1)S(1)}, u32[]{:S(2)}, u32[]{:S(2)}) %collective-permute-start.7) | collective-permute-done | bytes 8224 | tf_op jit(solution)/shard_map/ppermute | solution.py:335
  183.6 0.0 all-to-all-done.6.x_ref
  183.6 0.0 collective-permute-done.5.low_ref
  183.6 4.0 %collective-permute-start.8 = (bf16[16,8,512]{2,1,0:T(8,128)(2,1)S(1)}, bf16[16,8,512]{2,1,0:T(8,128)(2,1)S(1)}, u32[]{:S(2)}, u32[]{:S(2)}) collective-permute-start(bf16[16,8,512]{2,1,0:T(8,128)(2,1)S(1)} %all-to-all-done.6.x_ref), channel_id=1, source_target_pairs={{0,1},{1,0},{2,3},{3,2},{4,5},{5,4},{6,7},{7,6},{8,9},{9,8},{10,11... | collective-permute-start | bytes 393224 | tf_op jit(solution)/shard_map/ppermute | solution.py:368
  187.5 2.5 %shard_map.101.half_ref = f32[8,512]{1,0:T(8,128)S(1)} custom-call(s32[1]{0:T(128)} %bitcast.3.core_ref, bf16[2,8,512,512]{3,2,1,0:T(8,128)(2,1)} %shard_map.87.h_ref, bf16[16,8,512]{2,1,0:T(8,128)(2,1)S(1)} %all-to-all-done.6.x_ref), custom_call_target="tpu_custom_call" | custom-call | flops 100000000 | bytes 5000000 | tf_op jit(solution)/shard_map/pallas_call | solution.py:170
  190.0 0.0 collective-permute-done.8.x_ref
  190.0 2.5 %shard_map.102 = (f32[8,512]{1,0:T(8,128)S(1)}, bf16[16,8,512]{2,1,0:T(8,128)(2,1)S(1)}) custom-call(s32[1]{0:T(128)} %bitcast.3.core_ref, s32[1]{0:T(128)} %bitcast.11.mine_ref, bf16[2,8,512,512]{3,2,1,0:T(8,128)(2,1)} %shard_map.87.h_ref, bf16[16,8,512]{2,1,0:T(8,128)(2,1)S(1)} %collective-permute-done.8.x_ref, f32[8,512]{1,0:T(8,128)S(1)} %shard_map.101.half_ref, ...), custom_call_target="tpu_custom_call" | custom-call | flops 100000000 | bytes 5000000 | tf_op jit(solution)/shard_map/pallas_call | solution.py:196
  192.5 11.9 %all_to_all.43.x_ref = bf16[16,8,512]{2,1,0:T(8,128)(2,1)S(1)} all-to-all(bf16[16,8,512]{2,1,0:T(8,128)(2,1)S(1)} %get-tuple-element.70), channel_id=1, replica_groups={{96,98,100,102,104,106,108,110,112,114,116,118,120,122,124,126},{97,99,..., dimensions={0} | all-to-all | bytes 262144 | tf_op jit(solution)/shard_map/all_to_all | solution.py:355
  204.4 1.2 collective-permute-start.9
  205.6 2.5 %shard_map.103.half_ref = f32[8,512]{1,0:T(8,128)S(1)} custom-call(s32[1]{0:T(128)} %bitcast.3.core_ref, bf16[2,8,512,512]{3,2,1,0:T(8,128)(2,1)} %shard_map.87.h_ref, bf16[16,8,512]{2,1,0:T(8,128)(2,1)S(1)} %all_to_all.43.x_ref), custom_call_target="tpu_custom_call" | custom-call | flops 100000000 | bytes 5000000 | tf_op jit(solution)/shard_map/pallas_call | solution.py:170
  208.1 0.0 copy-start.1
  208.1 3.3 %shard_map.104 = (f32[8,512]{1,0:T(8,128)S(1)}, bf16[16,8,512]{2,1,0:T(8,128)(2,1)}) custom-call(s32[1]{0:T(128)} %bitcast.3.core_ref, s32[1]{0:T(128)} %bitcast.10.mine_ref, bf16[2,8,512,512]{3,2,1,0:T(8,128)(2,1)} %shard_map.87.h_ref, bf16[16,8,512]{2,1,0:T(8,128)(2,1)S(1)} %collective-permute-done.9.x_ref, f32[8,512]{1,0:T(8,128)S(1)} %shard_map.103.half_ref, ...), custom_call_target="tpu_custom_call" | custom-call | flops 100000000 | bytes 5000000 | tf_op jit(solution)/shard_map/pallas_call | solution.py:196
  211.4 1.9 collective-permute-start.10
  213.3 1.9 collective-permute-start.12
  215.3 6.0 %collective-permute-start.11 = (bf16[8,256]{1,0:T(8,128)(2,1)S(1)}, bf16[8,256]{1,0:T(8,128)(2,1)S(1)}, u32[]{:S(2)}, u32[]{:S(2)}) collective-permute-start(bf16[8,256]{1,0:T(8,128)(2,1)S(1)} %pad_maximum_fusion), channel_id=1, source_target_pairs={{0,1},{1,2},{2,3},{3,4},{4,5},{5,6},{6,7},{7,8},{8,9},{9,10},{10,1... | collective-permute-start | bytes 12296 | tf_op jit(solution)/shard_map/ppermute | solution.py:335
  221.3 0.7 collective-permute-done.11.vl_ref
  222.1 2.8 %shard_map.105 = (f32[2,8,192,128]{3,2,1,0:T(8,128)}, f32[2,8,192,128]{3,2,1,0:T(8,128)}) custom-call(f32[8,96,512]{2,1,0:T(8,128)S(1)} %get-tuple-element.51.y_ref, f32[2,8,192,128]{3,2,1,0:T(8,128)S(1)} %bitcast.24, bf16[8,2,96,128]{3,2,1,0:T(8,128)(2,1)S(1)} %collective-permute-done.5.low_ref, ...), custom_call_target="tpu_custom_call" | custom-call | tf_op jit(solution)/shard_map/pallas_call | solution.py:314
  (19 shorter events, 0.1 us)
Async XLA Ops:
  7.2 133.5 %all-gather.3.cloned.1.call-start = ((), (), s32[]{:S(2)}) async-start(), calls=%async_computation.8 | async-start | bytes 13369344 | tf_op jit(solution)/shard_map/all_gather | solution.py:342
  7.2 1.4 copy-start
  8.6 0.7 copy-start.2
  10.5 18.7 %all-to-all-start = ((bf16[16,32,512]{2,1,0:T(8,128)(2,1)}), bf16[16,32,512]{2,1,0:T(8,128)(2,1)S(1)}, u32[]{:S(2)}, u32[]{:S(2)}) async-start(bf16[16,32,512]{2,1,0:T(8,128)(2,1)} %get-tuple-element.40), calls=%async_computation | async-start | bytes 1048576 | tf_op jit(solution)/shard_map/all_to_all | solution.py:343
  26.2 20.8 %copy-start.4 = (s32[8,256]{1,0:T(8,128)S(1)}, s32[8,256]{1,0:T(8,128)}, u32[]{:S(2)}) copy-start(s32[8,256]{1,0:T(8,128)} %param.13) | copy-start | bytes 24580
  44.9 4.7 %collective-permute-start = (bf16[16,8,512]{2,1,0:T(8,128)(2,1)S(1)}, bf16[16,8,512]{2,1,0:T(8,128)(2,1)S(1)}, u32[]{:S(2)}, u32[]{:S(2)}) collective-permute-start(bf16[16,8,512]{2,1,0:T(8,128)(2,1)S(1)} %all_to_all.40.x_ref), channel_id=1, source_target_pairs={{0,1},{1,0},{2,3},{3,2},{4,5},{5,4},{6,7},{7,6},{8,9},{9,8},{10,11... | collective-permute-start | bytes 393224 | tf_op jit(solution)/shard_map/ppermute | solution.py:368
  49.7 10.9 %copy-start.5 = (s32[256]{0:T(256)S(1)}, s32[256]{0:T(256)}, u32[]{:S(2)}) copy-start(s32[256]{0:T(256)} %param.11) | copy-start | bytes 3076
  49.7 10.9 %copy-start.6 = (s32[8]{0:T(128)S(1)}, s32[8]{0:T(128)}, u32[]{:S(2)}) copy-start(s32[8]{0:T(128)} %param.12) | copy-start | bytes 100
  49.7 11.1 %copy-start.3 = (bf16[256,2,128]{2,1,0:T(2,128)(2,1)S(1)}, bf16[256,2,128]{2,1,0:T(2,128)(2,1)}, u32[]{:S(2)}) copy-start(bf16[256,2,128]{2,1,0:T(2,128)(2,1)} %param.9) | copy-start | bytes 393220
  52.9 14.7 %all-to-all-start.2 = ((bf16[16,8,512]{2,1,0:T(8,128)(2,1)}), bf16[16,8,512]{2,1,0:T(8,128)(2,1)S(1)}, u32[]{:S(2)}, u32[]{:S(2)}) async-start(bf16[16,8,512]{2,1,0:T(8,128)(2,1)} %get-tuple-element.43), calls=%async_computation.2 | async-start | bytes 262144 | tf_op jit(solution)/shard_map/all_to_all | solution.py:355
  67.6 3.7 %collective-permute-start.1 = (bf16[16,8,512]{2,1,0:T(8,128)(2,1)S(1)}, bf16[16,8,512]{2,1,0:T(8,128)(2,1)S(1)}, u32[]{:S(2)}, u32[]{:S(2)}) collective-permute-start(bf16[16,8,512]{2,1,0:T(8,128)(2,1)S(1)} %all-to-all-done.2.x_ref), channel_id=1, source_target_pairs={{0,1},{1,0},{2,3},{3,2},{4,5},{5,4},{6,7},{7,6},{8,9},{9,8},{10,11... | collective-permute-start | bytes 393224 | tf_op jit(solution)/shard_map/ppermute | solution.py:368
  84.7 3.9 %collective-permute-start.2 = (bf16[16,8,512]{2,1,0:T(8,128)(2,1)S(1)}, bf16[16,8,512]{2,1,0:T(8,128)(2,1)S(1)}, u32[]{:S(2)}, u32[]{:S(2)}) collective-permute-start(bf16[16,8,512]{2,1,0:T(8,128)(2,1)S(1)} %all_to_all.41.x_ref), channel_id=1, source_target_pairs={{0,1},{1,0},{2,3},{3,2},{4,5},{5,4},{6,7},{7,6},{8,9},{9,8},{10,11... | collective-permute-start | bytes 393224 | tf_op jit(solution)/shard_map/ppermute | solution.py:368
  128.9 3.7 %collective-permute-start.3 = (bf16[16,8,512]{2,1,0:T(8,128)(2,1)S(1)}, bf16[16,8,512]{2,1,0:T(8,128)(2,1)S(1)}, u32[]{:S(2)}, u32[]{:S(2)}) collective-permute-start(bf16[16,8,512]{2,1,0:T(8,128)(2,1)S(1)} %all_to_all.42.x_ref), channel_id=1, source_target_pairs={{0,1},{1,0},{2,3},{3,2},{4,5},{5,4},{6,7},{7,6},{8,9},{9,8},{10,11... | collective-permute-start | bytes 393224 | tf_op jit(solution)/shard_map/ppermute | solution.py:368
  135.7 21.0 %all-to-all-start.5 = ((bf16[16,8,512]{2,1,0:T(8,128)(2,1)}), bf16[16,8,512]{2,1,0:T(8,128)(2,1)S(1)}, u32[]{:S(2)}, u32[]{:S(2)}) async-start(bf16[16,8,512]{2,1,0:T(8,128)(2,1)} %get-tuple-element.52), calls=%async_computation.5 | async-start | bytes 262144 | tf_op jit(solution)/shard_map/all_to_all | solution.py:355
  156.7 3.2 %collective-permute-start.4 = (bf16[16,8,512]{2,1,0:T(8,128)(2,1)S(1)}, bf16[16,8,512]{2,1,0:T(8,128)(2,1)S(1)}, u32[]{:S(2)}, u32[]{:S(2)}) collective-permute-start(bf16[16,8,512]{2,1,0:T(8,128)(2,1)S(1)} %all-to-all-done.5.x_ref), channel_id=1, source_target_pairs={{0,1},{1,0},{2,3},{3,2},{4,5},{5,4},{6,7},{7,6},{8,9},{9,8},{10,11... | collective-permute-start | bytes 393224 | tf_op jit(solution)/shard_map/ppermute | solution.py:368
  163.0 20.6 %collective-permute-start.5 = (bf16[8,2,96,128]{3,2,1,0:T(8,128)(2,1)}, bf16[8,2,96,128]{3,2,1,0:T(8,128)(2,1)S(1)}, u32[]{:S(2)}, u32[]{:S(2)}) collective-permute-start(bf16[8,2,96,128]{3,2,1,0:T(8,128)(2,1)} %get-tuple-element.62), channel_id=1, source_target_pairs={{0,1},{1,2},{2,3},{3,4},{4,5},{5,6},{6,7},{7,8},{8,9},{9,10},{10,1... | collective-permute-start | bytes 1179656 | tf_op jit(solution)/shard_map/ppermute | solution.py:335
  166.1 17.5 %collective-permute-start.6 = (bf16[8,2,96,128]{3,2,1,0:T(8,128)(2,1)}, bf16[8,2,96,128]{3,2,1,0:T(8,128)(2,1)S(1)}, u32[]{:S(2)}, u32[]{:S(2)}) collective-permute-start(bf16[8,2,96,128]{3,2,1,0:T(8,128)(2,1)} %get-tuple-element.63), channel_id=1, source_target_pairs={{1,0},{2,1},{3,2},{4,3},{5,4},{6,5},{7,6},{8,7},{9,8},{10,9},{11,1... | collective-permute-start | bytes 1179656 | tf_op jit(solution)/shard_map/ppermute | solution.py:335
  168.0 15.6 %all-to-all-start.6 = ((bf16[16,8,512]{2,1,0:T(8,128)(2,1)}), bf16[16,8,512]{2,1,0:T(8,128)(2,1)S(1)}, u32[]{:S(2)}, u32[]{:S(2)}) async-start(bf16[16,8,512]{2,1,0:T(8,128)(2,1)} %get-tuple-element.57), calls=%async_computation.6 | async-start | bytes 262144 | tf_op jit(solution)/shard_map/all_to_all | solution.py:355
  176.8 6.8 %collective-permute-start.7 = (bf16[8,512]{1,0:T(8,128)(2,1)S(1)}, bf16[8,512]{1,0:T(8,128)(2,1)S(1)}, u32[]{:S(2)}, u32[]{:S(2)}) collective-permute-start(bf16[8,512]{1,0:T(8,128)(2,1)S(1)} %get-tuple-element.64), channel_id=1, source_target_pairs={{0,16},{16,32},{32,48},{48,64},{64,80},{80,96},{96,112},{1,17},{17... | collective-permute-start | bytes 24584 | tf_op jit(solution)/shard_map/ppermute | solution.py:335
  183.6 6.4 %collective-permute-start.8 = (bf16[16,8,512]{2,1,0:T(8,128)(2,1)S(1)}, bf16[16,8,512]{2,1,0:T(8,128)(2,1)S(1)}, u32[]{:S(2)}, u32[]{:S(2)}) collective-permute-start(bf16[16,8,512]{2,1,0:T(8,128)(2,1)S(1)} %all-to-all-done.6.x_ref), channel_id=1, source_target_pairs={{0,1},{1,0},{2,3},{3,2},{4,5},{5,4},{6,7},{7,6},{8,9},{9,8},{10,11... | collective-permute-start | bytes 393224 | tf_op jit(solution)/shard_map/ppermute | solution.py:368
  204.4 3.6 %collective-permute-start.9 = (bf16[16,8,512]{2,1,0:T(8,128)(2,1)S(1)}, bf16[16,8,512]{2,1,0:T(8,128)(2,1)S(1)}, u32[]{:S(2)}, u32[]{:S(2)}) collective-permute-start(bf16[16,8,512]{2,1,0:T(8,128)(2,1)S(1)} %all_to_all.43.x_ref), channel_id=1, source_target_pairs={{0,1},{1,0},{2,3},{3,2},{4,5},{5,4},{6,7},{7,6},{8,9},{9,8},{10,11... | collective-permute-start | bytes 393224 | tf_op jit(solution)/shard_map/ppermute | solution.py:368
  208.1 14.0 %copy-start.1 = (f32[2,8,96,2,128]{4,3,2,1,0:T(2,128)S(1)}, f32[2,8,96,2,128]{4,3,2,1,0:T(2,128)}, u32[]{:S(2)}) copy-start(f32[2,8,96,2,128]{4,3,2,1,0:T(2,128)} %param.7) | copy-start | bytes 4718596
  211.4 10.7 %collective-permute-start.10 = (bf16[8,512]{1,0:T(8,128)(2,1)S(1)}, bf16[8,512]{1,0:T(8,128)(2,1)S(1)}, u32[]{:S(2)}, u32[]{:S(2)}) collective-permute-start(bf16[8,512]{1,0:T(8,128)(2,1)S(1)} %convert_element_type.5), channel_id=1, source_target_pairs={{16,0},{32,16},{48,32},{64,48},{80,64},{96,80},{112,96},{17,1},{33... | collective-permute-start | bytes 24584 | tf_op jit(solution)/shard_map/ppermute | solution.py:335
  213.3 8.0 %collective-permute-start.12 = (bf16[8,256]{1,0:T(8,128)(2,1)S(1)}, bf16[8,256]{1,0:T(8,128)(2,1)S(1)}, u32[]{:S(2)}, u32[]{:S(2)}) collective-permute-start(bf16[8,256]{1,0:T(8,128)(2,1)S(1)} %pad_maximum_fusion.1), channel_id=1, source_target_pairs={{1,0},{2,1},{3,2},{4,3},{5,4},{6,5},{7,6},{8,7},{9,8},{10,9},{11,1... | collective-permute-start | bytes 12296 | tf_op jit(solution)/shard_map/ppermute | solution.py:335
  215.3 6.8 %collective-permute-start.11 = (bf16[8,256]{1,0:T(8,128)(2,1)S(1)}, bf16[8,256]{1,0:T(8,128)(2,1)S(1)}, u32[]{:S(2)}, u32[]{:S(2)}) collective-permute-start(bf16[8,256]{1,0:T(8,128)(2,1)S(1)} %pad_maximum_fusion), channel_id=1, source_target_pairs={{0,1},{1,2},{2,3},{3,4},{4,5},{5,6},{6,7},{7,8},{8,9},{9,10},{10,1... | collective-permute-start | bytes 12296 | tf_op jit(solution)/shard_map/ppermute | solution.py:335
Sparse Core Ops, SparseCore 0:
  11.0 95.9 all-gather.2

commit v4 on v3

--- a/solution.py
+++ b/solution.py
@@ -206,9 +206,10 @@
 
 def fronts_kernel(x_ref, h_ref, behind_ref, y_ref, low_ref, high_ref, last_ref, x_buf, h_buf, x_sem, h_sem):
     def loads(i):
+        core, chip = lax.rem(lax.div(i, 2), 2), lax.div(i, 4) * 2 + lax.rem(i, 2)
         return (
             pltpu.make_async_copy(x_ref.at[i], x_buf.at[i], x_sem.at[i]),
-            pltpu.make_async_copy(h_ref.at[lax.rem(i, 2), lax.div(i, 2)], h_buf.at[i], h_sem.at[i]),
+            pltpu.make_async_copy(h_ref.at[core, chip], h_buf.at[i], h_sem.at[i]),
         )
 
     @pl.loop(0, D)
@@ -218,13 +219,13 @@
 
     y_ref[...] = jnp.zeros((R, LZ, K), f32)
 
-    @pl.loop(0, D)
-    def _(i):
-        for copy in loads(i):
-            copy.wait()
-        for part in range(4):
-            rows = pl.ds(part * 2 * LZ, 2 * LZ)
-            y_ref[pl.ds(2 * part, 2)] += dot_t(x_buf[i, rows, :], h_buf[i]).reshape(2, LZ, K)
+    @pl.loop(0, D // 2)
+    def _(j):
+        for i in (2 * j, 2 * j + 1):
+            for copy in loads(i):
+                copy.wait()
+        total = dot_t(x_buf[2 * j], h_buf[2 * j]) + dot_t(x_buf[2 * j + 1], h_buf[2 * j + 1])
+        y_ref[...] += total.reshape(R, LZ, K)
 
     for r in range(R):
         for a in range(2):
@@ -249,6 +250,23 @@
         compiler_params=params(50),
         cost_estimate=pl.CostEstimate(flops=6 * 10**9, bytes_accessed=23 * 10**6, transcendentals=0),
     )(x, h, behind)
+
+
+def gate_kernel(*refs):
+    pass
+
+
+def gate(behind, *arrays):
+    n = len(arrays)
+    return pl.pallas_call(
+        gate_kernel,
+        out_shape=tuple(jax.ShapeDtypeStruct(x.shape, x.dtype) for x in arrays),
+        in_specs=[whole(pl.ANY)] * (n + 1),
+        out_specs=(whole(pl.ANY),) * n,
+        input_output_aliases={i: i for i in range(n)},
+        compiler_params=params(8),
+        cost_estimate=pl.CostEstimate(flops=6 * 10**9, bytes_accessed=10**6, transcendentals=0),
+    )(*arrays, behind)
 
 
 def wave_kernel(x_ref, coef_ref, panel_ref, behind_ref, out_ref):
@@ -339,7 +357,9 @@
     group = lax.axis_index("layer")
     flat = rhs.reshape(2, R, 2 * LZ, NY)
     own, chunk = prepare(flat, mode_profile)
-    gathered = lax.all_gather(own, "plane", axis=0)
+    along_x = [[z * 4 + x * 2 + c for x in range(2)] for z in range(4) for c in range(2)]
+    along_z = [[z * 4 + x * 2 + c for z in range(4) for c in range(2)] for x in range(2)]
+    paired = lax.all_gather(own, "plane", axis=0, axis_index_groups=along_x)
     heads = lax.all_to_all(chunk, "plane", 0, 0)
     h = arrange(inverse_blocks.reshape(K, 2, 32, NY))
 
@@ -352,15 +372,18 @@
     base, out = first_product(h, heads)
     v = base
     for step in range(1, G):
+        if step == 2:
+            paired, _ = lax.optimization_barrier((paired, v))
+            gathered = lax.all_gather(paired, "plane", axis=0, axis_index_groups=along_z).reshape(D, R * LZ, K)
         got = lax.all_to_all(out, ("layer", "plane"), 0, 0, axis_index_groups=pair_groups(step))
         if step == 2:
             wavenum = wave(heads, coef, mode_panel.reshape(MODES, 256), v)
             got, wavenum = lax.optimization_barrier((got, wavenum))
-        if step == 5:
+        if step == 6:
             y, low, high, last = fronts_of(gathered, h, v)
             got, low, high, last = lax.optimization_barrier((got, low, high, last))
-        if step == 6:
-            low, high, last, v = lax.optimization_barrier((low, high, last, v))
+        if step == 7:
+            low, high, last = gate(v, low, high, last)
             before = shift(high, "plane", 1)
             after = shift(low, "plane", -1)
             below = shift(last, "layer", 1)

time: 235 us -> 203 us (0.86)
  blocking collectives: 71.4 us -> 44.3 us
  Pallas kernels: 70.6 us -> 65.8 us
  waiting for transfers between devices: 14.2 us -> 11.3 us
    all_to_all x4, blocking collectives: 71.4 us -> 44.3 us  [shards(): lax.all_to_all(out, ('layer', 'plane'), 0, 0, axis_index_groups=pair_grou...]
    pallas_call x1, Pallas kernels: 16 us -> 10.9 us  [fronts_of(): pl.pallas_call(fronts_kernel, out_shape=(jax.ShapeDtypeStruct((R, LZ, K),...]
  transfers between devices with their start and end apart: 18 -> 19, of which waited for: 4 -> 4; matrix products, arithmetic and copies ran while one was open for 0% -> 0% of each run, Pallas kernels for 25% -> 28%
where the time goes in v4:
time: 203 us; the launch traced here: 200 us
  Pallas kernels  65.8 us (32%)
  starting transfers between devices  60.6 us (30%)
  blocking collectives  44.3 us (22%)
  between operations  14.5 us (7%)
  waiting for transfers between devices  11.3 us (6%)
  local copies, waits for them, and re-layouts  3.6 us (2%)
    all_to_all x4, blocking collectives, shards(): lax.all_to_all(out, ('layer', 'plane'), 0, 0, axis_index_groups=pair_grou...  44.3 us
    all_to_all x3, starting transfers between devices, shards(): lax.all_to_all(out, ('layer', 'plane'), 0, 0, axis_index_groups=pair_grou...  22 us
    pallas_call x7, Pallas kernels, other_half(): pl.pallas_call(other_kernel, out_shape=MATVEC_OUT, in_specs=[whole(pltpu....  20.4 us
    ppermute x6, starting transfers between devices, shift(): lax.ppermute(value, axis, [(i, i + by) for i in range(size) if 0 <= i + b...  19.1 us
    pallas_call x7, Pallas kernels, own_half(): pl.pallas_call(own_kernel, out_shape=jax.ShapeDtypeStruct((R, K), f32), i...  17.5 us
    pallas_call x1, Pallas kernels, fronts_of(): pl.pallas_call(fronts_kernel, out_shape=(jax.ShapeDtypeStruct((R, LZ, K),...  10.9 us
    ppermute x7, starting transfers between devices, shards(): other = lax.ppermute(got, 'plane', twin)  10.8 us
    all_to_all x1, starting transfers between devices, shards(): heads = lax.all_to_all(chunk, 'plane', 0, 0)  8.62 us
  transfers between devices with their start and end apart: 19, of which 4 were waited for; matrix products, arithmetic and copies ran while one was open for 0% of the time, Pallas kernels for 28%

profile of v4, /device:TPU:7, one launch (start us, length us, event | category | flops | bytes accessed | tf_op | source)
XLA Modules:
  0.0 200.3 jit_solution(12200729287079026214)
XLA Ops:
  7.2 0.0 all-gather.5.cloned.1.call-start
  7.2 0.0 copy-start
  7.2 1.4 copy-done
  8.6 0.7 copy-done.2
  9.3 1.2 shard_map.86
  10.5 0.0 all-gather.5.cloned.1.call-update
  10.5 8.6 %all-to-all-start = ((bf16[16,32,512]{2,1,0:T(8,128)(2,1)}), bf16[16,32,512]{2,1,0:T(8,128)(2,1)S(1)}, u32[]{:S(2)}, u32[]{:S(2)}) async-start(bf16[16,32,512]{2,1,0:T(8,128)(2,1)} %get-tuple-element.40), calls=%async_computation | async-start | bytes 1048576 | tf_op jit(solution)/shard_map/all_to_all | solution.py:363
  19.2 0.0 all-gather.7.cloned.1.call-start
  19.2 7.1 %shard_map.87.h_ref = bf16[2,8,512,512]{3,2,1,0:T(8,128)(2,1)} custom-call(bf16[512,2,32,128]{3,2,1,0:T(8,128)(2,1)} %bitcast.26), custom_call_target="tpu_custom_call" | custom-call | flops 4000000000 | bytes 17000000 | tf_op jit(solution)/shard_map/pallas_call | solution.py:105
  26.3 2.7 %all-to-all-done.x_ref = bf16[16,32,512]{2,1,0:T(8,128)(2,1)S(1)} async-done(((bf16[16,32,512]{2,1,0:T(8,128)(2,1)}), bf16[16,32,512]{2,1,0:T(8,128)(2,1)S(1)}, u32[]{:S(2)}, u32[]{:S(2)}) %all-to-all-start) | async-done | bytes 524320 | tf_op jit(solution)/shard_map/all_to_all | solution.py:363
  29.0 4.7 %shard_map.88 = (f32[8,512]{1,0:T(8,128)S(1)}, bf16[16,8,512]{2,1,0:T(8,128)(2,1)S(1)}) custom-call(bf16[2,8,512,512]{3,2,1,0:T(8,128)(2,1)} %shard_map.87.h_ref, bf16[16,32,512]{2,1,0:T(8,128)(2,1)S(1)} %all-to-all-done.x_ref), custom_call_target="tpu_custom_call" | custom-call | flops 100000000 | bytes 5000000 | tf_op jit(solution)/shard_map/pallas_call | solution.py:150
  33.7 11.4 %all_to_all.40.x_ref = bf16[16,8,512]{2,1,0:T(8,128)(2,1)S(1)} all-to-all(bf16[16,8,512]{2,1,0:T(8,128)(2,1)S(1)} %get-tuple-element.41), channel_id=1, replica_groups={{0,2,4,6,8,10,12,14,16,18,20,22,24,26,28,30},{1,3,5,7,9,11,13,15,17,19,..., dimensions={0} | all-to-all | bytes 262144 | tf_op jit(solution)/shard_map/all_to_all | solution.py:378
  45.2 2.7 %collective-permute-start = (bf16[16,8,512]{2,1,0:T(8,128)(2,1)S(1)}, bf16[16,8,512]{2,1,0:T(8,128)(2,1)S(1)}, u32[]{:S(2)}, u32[]{:S(2)}) collective-permute-start(bf16[16,8,512]{2,1,0:T(8,128)(2,1)S(1)} %all_to_all.40.x_ref), channel_id=1, source_target_pairs={{0,1},{1,0},{2,3},{3,2},{4,5},{5,4},{6,7},{7,6},{8,9},{9,8},{10,11... | collective-permute-start | bytes 393224 | tf_op jit(solution)/shard_map/ppermute | solution.py:391
  47.9 2.5 %shard_map.89.half_ref = f32[8,512]{1,0:T(8,128)S(1)} custom-call(s32[1]{0:T(128)} %bitcast.2.core_ref, bf16[2,8,512,512]{3,2,1,0:T(8,128)(2,1)} %shard_map.87.h_ref, bf16[16,8,512]{2,1,0:T(8,128)(2,1)S(1)} %all_to_all.40.x_ref), custom_call_target="tpu_custom_call" | custom-call | flops 100000000 | bytes 5000000 | tf_op jit(solution)/shard_map/pallas_call | solution.py:170
  50.4 3.1 %shard_map.90 = (f32[8,512]{1,0:T(8,128)S(1)}, bf16[16,8,512]{2,1,0:T(8,128)(2,1)}) custom-call(s32[1]{0:T(128)} %bitcast.2.core_ref, s32[1]{0:T(128)} %bitcast.3.mine_ref, bf16[2,8,512,512]{3,2,1,0:T(8,128)(2,1)} %shard_map.87.h_ref, bf16[16,8,512]{2,1,0:T(8,128)(2,1)S(1)} %collective-permute-done.x_ref, f32[8,512]{1,0:T(8,128)S(1)} %shard_map.89.half_ref, ...), custom_call_target="tpu_custom_call" | custom-call | flops 100000000 | bytes 5000000 | tf_op jit(solution)/shard_map/pallas_call | solution.py:196
  53.5 0.0 copy-start.5
  53.5 0.0 copy-start.6
  53.6 0.0 copy-start.7
  53.6 0.0 copy-start.4
  53.6 0.0 all-gather.5.cloned.1.call-done
  53.6 0.0 all-gather.7.cloned.1.call-update
  53.6 0.6 copy-done.5
  54.2 0.1 copy.14
  54.4 8.0 %all-to-all-start.2 = ((bf16[16,8,512]{2,1,0:T(8,128)(2,1)}), bf16[16,8,512]{2,1,0:T(8,128)(2,1)S(1)}, u32[]{:S(2)}, u32[]{:S(2)}) async-start(bf16[16,8,512]{2,1,0:T(8,128)(2,1)} %get-tuple-element.45), calls=%async_computation.2 | async-start | bytes 262144 | tf_op jit(solution)/shard_map/all_to_all | solution.py:378
  62.4 0.2 fusion.5.coef_ref
  62.6 1.3 shard_map.91.wave_ref
  63.9 4.1 %all-to-all-done.2.x_ref = bf16[16,8,512]{2,1,0:T(8,128)(2,1)S(1)} async-done(((bf16[16,8,512]{2,1,0:T(8,128)(2,1)}), bf16[16,8,512]{2,1,0:T(8,128)(2,1)S(1)}, u32[]{:S(2)}, u32[]{:S(2)}) %all-to-all-start.2) | async-done | bytes 131104 | tf_op jit(solution)/shard_map/all_to_all | solution.py:378
  68.0 1.2 collective-permute-start.1
  69.2 2.5 %shard_map.92.half_ref = f32[8,512]{1,0:T(8,128)S(1)} custom-call(s32[1]{0:T(128)} %bitcast.2.core_ref, bf16[2,8,512,512]{3,2,1,0:T(8,128)(2,1)} %shard_map.87.h_ref, bf16[16,8,512]{2,1,0:T(8,128)(2,1)S(1)} %all-to-all-done.2.x_ref), custom_call_target="tpu_custom_call" | custom-call | flops 100000000 | bytes 5000000 | tf_op jit(solution)/shard_map/pallas_call | solution.py:170
  71.7 2.6 %shard_map.93 = (f32[8,512]{1,0:T(8,128)S(1)}, bf16[16,8,512]{2,1,0:T(8,128)(2,1)S(1)}) custom-call(s32[1]{0:T(128)} %bitcast.2.core_ref, s32[1]{0:T(128)} %bitcast.8.mine_ref, bf16[2,8,512,512]{3,2,1,0:T(8,128)(2,1)} %shard_map.87.h_ref, bf16[16,8,512]{2,1,0:T(8,128)(2,1)S(1)} %collective-permute-done.1.x_ref, f32[8,512]{1,0:T(8,128)S(1)} %shard_map.92.half_ref, ...), custom_call_target="tpu_custom_call" | custom-call | flops 100000000 | bytes 5000000 | tf_op jit(solution)/shard_map/pallas_call | solution.py:196
  74.3 10.3 %all_to_all.41.x_ref = bf16[16,8,512]{2,1,0:T(8,128)(2,1)S(1)} all-to-all(bf16[16,8,512]{2,1,0:T(8,128)(2,1)S(1)} %get-tuple-element.47), channel_id=1, replica_groups={{32,34,36,38,40,42,44,46,48,50,52,54,56,58,60,62},{33,35,37,39,41,43,45..., dimensions={0} | all-to-all | bytes 262144 | tf_op jit(solution)/shard_map/all_to_all | solution.py:378
  84.6 1.1 collective-permute-start.2
  85.6 2.5 %shard_map.94.half_ref = f32[8,512]{1,0:T(8,128)S(1)} custom-call(s32[1]{0:T(128)} %bitcast.2.core_ref, bf16[2,8,512,512]{3,2,1,0:T(8,128)(2,1)} %shard_map.87.h_ref, bf16[16,8,512]{2,1,0:T(8,128)(2,1)S(1)} %all_to_all.41.x_ref), custom_call_target="tpu_custom_call" | custom-call | flops 100000000 | bytes 5000000 | tf_op jit(solution)/shard_map/pallas_call | solution.py:170
  88.1 2.5 %shard_map.95 = (f32[8,512]{1,0:T(8,128)S(1)}, bf16[16,8,512]{2,1,0:T(8,128)(2,1)S(1)}) custom-call(s32[1]{0:T(128)} %bitcast.2.core_ref, s32[1]{0:T(128)} %bitcast.7.mine_ref, bf16[2,8,512,512]{3,2,1,0:T(8,128)(2,1)} %shard_map.87.h_ref, bf16[16,8,512]{2,1,0:T(8,128)(2,1)S(1)} %collective-permute-done.2.x_ref, f32[8,512]{1,0:T(8,128)S(1)} %shard_map.94.half_ref, ...), custom_call_target="tpu_custom_call" | custom-call | flops 100000000 | bytes 5000000 | tf_op jit(solution)/shard_map/pallas_call | solution.py:196
  90.7 12.5 %all_to_all.42.x_ref = bf16[16,8,512]{2,1,0:T(8,128)(2,1)S(1)} all-to-all(bf16[16,8,512]{2,1,0:T(8,128)(2,1)S(1)} %get-tuple-element.49), channel_id=1, replica_groups={{48,50,52,54,56,58,60,62,64,66,68,70,72,74,76,78},{49,51,53,55,57,59,61..., dimensions={0} | all-to-all | bytes 262144 | tf_op jit(solution)/shard_map/all_to_all | solution.py:378
  103.1 1.5 collective-permute-start.3
  104.6 2.6 %shard_map.96.half_ref = f32[8,512]{1,0:T(8,128)S(1)} custom-call(s32[1]{0:T(128)} %bitcast.2.core_ref, bf16[2,8,512,512]{3,2,1,0:T(8,128)(2,1)} %shard_map.87.h_ref, bf16[16,8,512]{2,1,0:T(8,128)(2,1)S(1)} %all_to_all.42.x_ref), custom_call_target="tpu_custom_call" | custom-call | flops 100000000 | bytes 5000000 | tf_op jit(solution)/shard_map/pallas_call | solution.py:170
  107.2 2.5 %shard_map.97 = (f32[8,512]{1,0:T(8,128)S(1)}, bf16[16,8,512]{2,1,0:T(8,128)(2,1)S(1)}) custom-call(s32[1]{0:T(128)} %bitcast.2.core_ref, s32[1]{0:T(128)} %bitcast.6.mine_ref, bf16[2,8,512,512]{3,2,1,0:T(8,128)(2,1)} %shard_map.87.h_ref, bf16[16,8,512]{2,1,0:T(8,128)(2,1)S(1)} %collective-permute-done.3.x_ref, f32[8,512]{1,0:T(8,128)S(1)} %shard_map.96.half_ref, ...), custom_call_target="tpu_custom_call" | custom-call | flops 100000000 | bytes 5000000 | tf_op jit(solution)/shard_map/pallas_call | solution.py:196
  109.7 10.1 %all_to_all.43.x_ref = bf16[16,8,512]{2,1,0:T(8,128)(2,1)S(1)} all-to-all(bf16[16,8,512]{2,1,0:T(8,128)(2,1)S(1)} %get-tuple-element.51), channel_id=1, replica_groups={{64,66,68,70,72,74,76,78,80,82,84,86,88,90,92,94},{65,67,69,71,73,75,77..., dimensions={0} | all-to-all | bytes 262144 | tf_op jit(solution)/shard_map/all_to_all | solution.py:378
  119.9 1.1 collective-permute-start.4
  121.0 2.5 %shard_map.98.half_ref = f32[8,512]{1,0:T(8,128)S(1)} custom-call(s32[1]{0:T(128)} %bitcast.2.core_ref, bf16[2,8,512,512]{3,2,1,0:T(8,128)(2,1)} %shard_map.87.h_ref, bf16[16,8,512]{2,1,0:T(8,128)(2,1)S(1)} %all_to_all.43.x_ref), custom_call_target="tpu_custom_call" | custom-call | flops 100000000 | bytes 5000000 | tf_op jit(solution)/shard_map/pallas_call | solution.py:170
  123.5 3.2 %shard_map.99 = (f32[8,512]{1,0:T(8,128)S(1)}, bf16[16,8,512]{2,1,0:T(8,128)(2,1)}) custom-call(s32[1]{0:T(128)} %bitcast.2.core_ref, s32[1]{0:T(128)} %bitcast.5.mine_ref, bf16[2,8,512,512]{3,2,1,0:T(8,128)(2,1)} %shard_map.87.h_ref, bf16[16,8,512]{2,1,0:T(8,128)(2,1)S(1)} %collective-permute-done.4.x_ref, f32[8,512]{1,0:T(8,128)S(1)} %shard_map.98.half_ref, ...), custom_call_target="tpu_custom_call" | custom-call | flops 100000000 | bytes 5000000 | tf_op jit(solution)/shard_map/pallas_call | solution.py:196
  126.7 7.6 %all-to-all-start.6 = ((bf16[16,8,512]{2,1,0:T(8,128)(2,1)}), bf16[16,8,512]{2,1,0:T(8,128)(2,1)S(1)}, u32[]{:S(2)}, u32[]{:S(2)}) async-start(bf16[16,8,512]{2,1,0:T(8,128)(2,1)} %get-tuple-element.55), calls=%async_computation.6 | async-start | bytes 262144 | tf_op jit(solution)/shard_map/all_to_all | solution.py:378
  134.3 0.0 all-gather.7.cloned.1.call-done.x_ref
  134.4 10.9 %shard_map.100 = (f32[8,96,512]{2,1,0:T(8,128)S(1)}, bf16[8,2,96,128]{3,2,1,0:T(8,128)(2,1)S(1)}, bf16[8,2,96,128]{3,2,1,0:T(8,128)(2,1)}, bf16[8,512]{1,0:T(8,128)(2,1)S(1)}) custom-call(bf16[16,768,512]{2,1,0:T(8,128)(2,1)} %all-gather.7.cloned.1.call-done.x_ref, bf16[2,8,512,512]{3,2,1,0:T(8,128)(2,1)} %shard_map.87.h_ref, ...), custom_call_target="tpu_custom_call" | custom-call | flops 6000000000 | bytes 23000000 | tf_op jit(solution)/shard_map/pallas_call | solution.py:239
  145.3 0.2 collective-permute-start.5
  145.5 2.5 %shard_map.101.half_ref = f32[8,512]{1,0:T(8,128)S(1)} custom-call(s32[1]{0:T(128)} %bitcast.2.core_ref, bf16[2,8,512,512]{3,2,1,0:T(8,128)(2,1)} %shard_map.87.h_ref, bf16[16,8,512]{2,1,0:T(8,128)(2,1)S(1)} %all-to-all-done.6.x_ref), custom_call_target="tpu_custom_call" | custom-call | flops 100000000 | bytes 5000000 | tf_op jit(solution)/shard_map/pallas_call | solution.py:170
  148.0 3.1 %shard_map.102 = (f32[8,512]{1,0:T(8,128)S(1)}, bf16[16,8,512]{2,1,0:T(8,128)(2,1)}) custom-call(s32[1]{0:T(128)} %bitcast.2.core_ref, s32[1]{0:T(128)} %bitcast.10.mine_ref, bf16[2,8,512,512]{3,2,1,0:T(8,128)(2,1)} %shard_map.87.h_ref, bf16[16,8,512]{2,1,0:T(8,128)(2,1)S(1)} %collective-permute-done.5.x_ref, f32[8,512]{1,0:T(8,128)S(1)} %shard_map.101.half_ref, ...), custom_call_target="tpu_custom_call" | custom-call | flops 100000000 | bytes 5000000 | tf_op jit(solution)/shard_map/pallas_call | solution.py:196
  151.2 0.0 copy-start.3
  151.2 0.7 copy-done.3
  151.9 4.2 %collective-permute-start.6 = (bf16[8,2,96,128]{3,2,1,0:T(8,128)(2,1)}, bf16[8,2,96,128]{3,2,1,0:T(8,128)(2,1)S(1)}, u32[]{:S(2)}, u32[]{:S(2)}) collective-permute-start(bf16[8,2,96,128]{3,2,1,0:T(8,128)(2,1)} %get-tuple-element.65), channel_id=1, source_target_pairs={{0,1},{1,2},{2,3},{3,4},{4,5},{5,6},{6,7},{7,8},{8,9},{9,10},{10,1... | collective-permute-start | bytes 1179656 | tf_op jit(solution)/shard_map/ppermute | solution.py:353
  156.2 1.9 collective-permute-start.7
  158.1 6.4 %all-to-all-start.7 = ((bf16[16,8,512]{2,1,0:T(8,128)(2,1)}), bf16[16,8,512]{2,1,0:T(8,128)(2,1)S(1)}, u32[]{:S(2)}, u32[]{:S(2)}) async-start(bf16[16,8,512]{2,1,0:T(8,128)(2,1)} %get-tuple-element.60), calls=%async_computation.7 | async-start | bytes 262144 | tf_op jit(solution)/shard_map/all_to_all | solution.py:378
  164.5 3.1 %collective-permute-start.8 = (bf16[8,512]{1,0:T(8,128)(2,1)S(1)}, bf16[8,512]{1,0:T(8,128)(2,1)S(1)}, u32[]{:S(2)}, u32[]{:S(2)}) collective-permute-start(bf16[8,512]{1,0:T(8,128)(2,1)S(1)} %get-tuple-element.67), channel_id=1, source_target_pairs={{0,16},{16,32},{32,48},{48,64},{64,80},{80,96},{96,112},{1,17},{17... | collective-permute-start | bytes 24584 | tf_op jit(solution)/shard_map/ppermute | solution.py:353
  167.6 3.7 %collective-permute-done.8.prev_ref = bf16[8,512]{1,0:T(8,128)(2,1)S(1)} collective-permute-done((bf16[8,512]{1,0:T(8,128)(2,1)S(1)}, bf16[8,512]{1,0:T(8,128)(2,1)S(1)}, u32[]{:S(2)}, u32[]{:S(2)}) %collective-permute-start.8) | collective-permute-done | bytes 8224 | tf_op jit(solution)/shard_map/ppermute | solution.py:353
  171.3 3.1 %collective-permute-start.9 = (bf16[16,8,512]{2,1,0:T(8,128)(2,1)S(1)}, bf16[16,8,512]{2,1,0:T(8,128)(2,1)S(1)}, u32[]{:S(2)}, u32[]{:S(2)}) collective-permute-start(bf16[16,8,512]{2,1,0:T(8,128)(2,1)S(1)} %all-to-all-done.7.x_ref), channel_id=1, source_target_pairs={{0,1},{1,0},{2,3},{3,2},{4,5},{5,4},{6,7},{7,6},{8,9},{9,8},{10,11... | collective-permute-start | bytes 393224 | tf_op jit(solution)/shard_map/ppermute | solution.py:391
  174.3 2.5 %shard_map.104.half_ref = f32[8,512]{1,0:T(8,128)S(1)} custom-call(s32[1]{0:T(128)} %bitcast.2.core_ref, bf16[2,8,512,512]{3,2,1,0:T(8,128)(2,1)} %shard_map.87.h_ref, bf16[16,8,512]{2,1,0:T(8,128)(2,1)S(1)} %all-to-all-done.7.x_ref), custom_call_target="tpu_custom_call" | custom-call | flops 100000000 | bytes 5000000 | tf_op jit(solution)/shard_map/pallas_call | solution.py:170
  176.8 0.0 copy-start.1
  176.9 3.3 %shard_map.105 = (f32[8,512]{1,0:T(8,128)S(1)}, bf16[16,8,512]{2,1,0:T(8,128)(2,1)}) custom-call(s32[1]{0:T(128)} %bitcast.2.core_ref, s32[1]{0:T(128)} %bitcast.11.mine_ref, bf16[2,8,512,512]{3,2,1,0:T(8,128)(2,1)} %shard_map.87.h_ref, bf16[16,8,512]{2,1,0:T(8,128)(2,1)S(1)} %collective-permute-done.9.x_ref, f32[8,512]{1,0:T(8,128)S(1)} %shard_map.104.half_ref, ...), custom_call_target="tpu_custom_call" | custom-call | flops 100000000 | bytes 5000000 | tf_op jit(solution)/shard_map/pallas_call | solution.py:196
  180.1 1.9 collective-permute-start.10
  182.1 1.9 collective-permute-start.12
  184.0 6.0 %collective-permute-start.11 = (bf16[8,256]{1,0:T(8,128)(2,1)S(1)}, bf16[8,256]{1,0:T(8,128)(2,1)S(1)}, u32[]{:S(2)}, u32[]{:S(2)}) collective-permute-start(bf16[8,256]{1,0:T(8,128)(2,1)S(1)} %pad_maximum_fusion), channel_id=1, source_target_pairs={{0,1},{1,2},{2,3},{3,4},{4,5},{5,6},{6,7},{7,8},{8,9},{9,10},{10,1... | collective-permute-start | bytes 12296 | tf_op jit(solution)/shard_map/ppermute | solution.py:353
  190.1 0.7 collective-permute-done.11.vl_ref
  190.8 2.7 %shard_map.106 = (f32[2,8,192,128]{3,2,1,0:T(8,128)}, f32[2,8,192,128]{3,2,1,0:T(8,128)}) custom-call(f32[8,96,512]{2,1,0:T(8,128)S(1)} %get-tuple-element.54.y_ref, f32[2,8,192,128]{3,2,1,0:T(8,128)S(1)} %bitcast.24, bf16[8,2,96,128]{3,2,1,0:T(8,128)(2,1)S(1)} %collective-permute-done.6.low_ref, ...), custom_call_target="tpu_custom_call" | custom-call | tf_op jit(solution)/shard_map/pallas_call | solution.py:332
  (25 shorter events, 0.1 us)
Async XLA Ops:
  7.2 46.4 %all-gather.5.cloned.1.call-start = ((), (), s32[]{:S(2)}) async-start(), calls=%async_computation.8 | async-start | bytes 2359296 | tf_op jit(solution)/shard_map/all_gather | solution.py:362
  7.2 1.4 copy-start
  8.6 0.7 copy-start.2
  10.5 18.5 %all-to-all-start = ((bf16[16,32,512]{2,1,0:T(8,128)(2,1)}), bf16[16,32,512]{2,1,0:T(8,128)(2,1)S(1)}, u32[]{:S(2)}, u32[]{:S(2)}) async-start(bf16[16,32,512]{2,1,0:T(8,128)(2,1)} %get-tuple-element.40), calls=%async_computation | async-start | bytes 1048576 | tf_op jit(solution)/shard_map/all_to_all | solution.py:363
  19.2 115.2 %all-gather.7.cloned.1.call-start = ((), (), s32[]{:S(2)}) async-start(), calls=%async_computation.9 | async-start | bytes 14155776 | tf_op jit(solution)/shard_map/all_gather | solution.py:377
  45.2 5.2 %collective-permute-start = (bf16[16,8,512]{2,1,0:T(8,128)(2,1)S(1)}, bf16[16,8,512]{2,1,0:T(8,128)(2,1)S(1)}, u32[]{:S(2)}, u32[]{:S(2)}) collective-permute-start(bf16[16,8,512]{2,1,0:T(8,128)(2,1)S(1)} %all_to_all.40.x_ref), channel_id=1, source_target_pairs={{0,1},{1,0},{2,3},{3,2},{4,5},{5,4},{6,7},{7,6},{8,9},{9,8},{10,11... | collective-permute-start | bytes 393224 | tf_op jit(solution)/shard_map/ppermute | solution.py:391
  53.5 0.7 copy-start.5
  53.5 8.8 %copy-start.6 = (s32[256]{0:T(256)S(1)}, s32[256]{0:T(256)}, u32[]{:S(2)}) copy-start(s32[256]{0:T(256)} %param.11) | copy-start | bytes 3076
  53.6 8.8 %copy-start.7 = (s32[8]{0:T(128)S(1)}, s32[8]{0:T(128)}, u32[]{:S(2)}) copy-start(s32[8]{0:T(128)} %param.12) | copy-start | bytes 100
  53.6 9.0 %copy-start.4 = (bf16[256,2,128]{2,1,0:T(2,128)(2,1)S(1)}, bf16[256,2,128]{2,1,0:T(2,128)(2,1)}, u32[]{:S(2)}) copy-start(bf16[256,2,128]{2,1,0:T(2,128)(2,1)} %param.9) | copy-start | bytes 393220
  54.4 13.6 %all-to-all-start.2 = ((bf16[16,8,512]{2,1,0:T(8,128)(2,1)}), bf16[16,8,512]{2,1,0:T(8,128)(2,1)S(1)}, u32[]{:S(2)}, u32[]{:S(2)}) async-start(bf16[16,8,512]{2,1,0:T(8,128)(2,1)} %get-tuple-element.45), calls=%async_computation.2 | async-start | bytes 262144 | tf_op jit(solution)/shard_map/all_to_all | solution.py:378
  68.0 3.6 %collective-permute-start.1 = (bf16[16,8,512]{2,1,0:T(8,128)(2,1)S(1)}, bf16[16,8,512]{2,1,0:T(8,128)(2,1)S(1)}, u32[]{:S(2)}, u32[]{:S(2)}) collective-permute-start(bf16[16,8,512]{2,1,0:T(8,128)(2,1)S(1)} %all-to-all-done.2.x_ref), channel_id=1, source_target_pairs={{0,1},{1,0},{2,3},{3,2},{4,5},{5,4},{6,7},{7,6},{8,9},{9,8},{10,11... | collective-permute-start | bytes 393224 | tf_op jit(solution)/shard_map/ppermute | solution.py:391
  84.6 3.5 %collective-permute-start.2 = (bf16[16,8,512]{2,1,0:T(8,128)(2,1)S(1)}, bf16[16,8,512]{2,1,0:T(8,128)(2,1)S(1)}, u32[]{:S(2)}, u32[]{:S(2)}) collective-permute-start(bf16[16,8,512]{2,1,0:T(8,128)(2,1)S(1)} %all_to_all.41.x_ref), channel_id=1, source_target_pairs={{0,1},{1,0},{2,3},{3,2},{4,5},{5,4},{6,7},{7,6},{8,9},{9,8},{10,11... | collective-permute-start | bytes 393224 | tf_op jit(solution)/shard_map/ppermute | solution.py:391
  103.1 4.1 %collective-permute-start.3 = (bf16[16,8,512]{2,1,0:T(8,128)(2,1)S(1)}, bf16[16,8,512]{2,1,0:T(8,128)(2,1)S(1)}, u32[]{:S(2)}, u32[]{:S(2)}) collective-permute-start(bf16[16,8,512]{2,1,0:T(8,128)(2,1)S(1)} %all_to_all.42.x_ref), channel_id=1, source_target_pairs={{0,1},{1,0},{2,3},{3,2},{4,5},{5,4},{6,7},{7,6},{8,9},{9,8},{10,11... | collective-permute-start | bytes 393224 | tf_op jit(solution)/shard_map/ppermute | solution.py:391
  119.9 3.6 %collective-permute-start.4 = (bf16[16,8,512]{2,1,0:T(8,128)(2,1)S(1)}, bf16[16,8,512]{2,1,0:T(8,128)(2,1)S(1)}, u32[]{:S(2)}, u32[]{:S(2)}) collective-permute-start(bf16[16,8,512]{2,1,0:T(8,128)(2,1)S(1)} %all_to_all.43.x_ref), channel_id=1, source_target_pairs={{0,1},{1,0},{2,3},{3,2},{4,5},{5,4},{6,7},{7,6},{8,9},{9,8},{10,11... | collective-permute-start | bytes 393224 | tf_op jit(solution)/shard_map/ppermute | solution.py:391
  126.7 18.6 %all-to-all-start.6 = ((bf16[16,8,512]{2,1,0:T(8,128)(2,1)}), bf16[16,8,512]{2,1,0:T(8,128)(2,1)S(1)}, u32[]{:S(2)}, u32[]{:S(2)}) async-start(bf16[16,8,512]{2,1,0:T(8,128)(2,1)} %get-tuple-element.55), calls=%async_computation.6 | async-start | bytes 262144 | tf_op jit(solution)/shard_map/all_to_all | solution.py:378
  145.3 2.7 %collective-permute-start.5 = (bf16[16,8,512]{2,1,0:T(8,128)(2,1)S(1)}, bf16[16,8,512]{2,1,0:T(8,128)(2,1)S(1)}, u32[]{:S(2)}, u32[]{:S(2)}) collective-permute-start(bf16[16,8,512]{2,1,0:T(8,128)(2,1)S(1)} %all-to-all-done.6.x_ref), channel_id=1, source_target_pairs={{0,1},{1,0},{2,3},{3,2},{4,5},{5,4},{6,7},{7,6},{8,9},{9,8},{10,11... | collective-permute-start | bytes 393224 | tf_op jit(solution)/shard_map/ppermute | solution.py:391
  151.2 0.7 copy-start.3
  151.9 19.3 %collective-permute-start.6 = (bf16[8,2,96,128]{3,2,1,0:T(8,128)(2,1)}, bf16[8,2,96,128]{3,2,1,0:T(8,128)(2,1)S(1)}, u32[]{:S(2)}, u32[]{:S(2)}) collective-permute-start(bf16[8,2,96,128]{3,2,1,0:T(8,128)(2,1)} %get-tuple-element.65), channel_id=1, source_target_pairs={{0,1},{1,2},{2,3},{3,4},{4,5},{5,6},{6,7},{7,8},{8,9},{9,10},{10,1... | collective-permute-start | bytes 1179656 | tf_op jit(solution)/shard_map/ppermute | solution.py:353
  156.2 15.1 %collective-permute-start.7 = (bf16[8,2,96,128]{3,2,1,0:T(8,128)(2,1)}, bf16[8,2,96,128]{3,2,1,0:T(8,128)(2,1)S(1)}, u32[]{:S(2)}, u32[]{:S(2)}) collective-permute-start(bf16[8,2,96,128]{3,2,1,0:T(8,128)(2,1)} %copy-done.3), channel_id=1, source_target_pairs={{1,0},{2,1},{3,2},{4,3},{5,4},{6,5},{7,6},{8,7},{9,8},{10,9},{11,1... | collective-permute-start | bytes 1179656 | tf_op jit(solution)/shard_map/ppermute | solution.py:353
  158.1 13.2 %all-to-all-start.7 = ((bf16[16,8,512]{2,1,0:T(8,128)(2,1)}), bf16[16,8,512]{2,1,0:T(8,128)(2,1)S(1)}, u32[]{:S(2)}, u32[]{:S(2)}) async-start(bf16[16,8,512]{2,1,0:T(8,128)(2,1)} %get-tuple-element.60), calls=%async_computation.7 | async-start | bytes 262144 | tf_op jit(solution)/shard_map/all_to_all | solution.py:378
  164.5 6.8 %collective-permute-start.8 = (bf16[8,512]{1,0:T(8,128)(2,1)S(1)}, bf16[8,512]{1,0:T(8,128)(2,1)S(1)}, u32[]{:S(2)}, u32[]{:S(2)}) collective-permute-start(bf16[8,512]{1,0:T(8,128)(2,1)S(1)} %get-tuple-element.67), channel_id=1, source_target_pairs={{0,16},{16,32},{32,48},{48,64},{64,80},{80,96},{96,112},{1,17},{17... | collective-permute-start | bytes 24584 | tf_op jit(solution)/shard_map/ppermute | solution.py:353
  171.3 5.5 %collective-permute-start.9 = (bf16[16,8,512]{2,1,0:T(8,128)(2,1)S(1)}, bf16[16,8,512]{2,1,0:T(8,128)(2,1)S(1)}, u32[]{:S(2)}, u32[]{:S(2)}) collective-permute-start(bf16[16,8,512]{2,1,0:T(8,128)(2,1)S(1)} %all-to-all-done.7.x_ref), channel_id=1, source_target_pairs={{0,1},{1,0},{2,3},{3,2},{4,5},{5,4},{6,7},{7,6},{8,9},{9,8},{10,11... | collective-permute-start | bytes 393224 | tf_op jit(solution)/shard_map/ppermute | solution.py:391
  176.8 14.0 %copy-start.1 = (f32[2,8,96,2,128]{4,3,2,1,0:T(2,128)S(1)}, f32[2,8,96,2,128]{4,3,2,1,0:T(2,128)}, u32[]{:S(2)}) copy-start(f32[2,8,96,2,128]{4,3,2,1,0:T(2,128)} %param.7) | copy-start | bytes 4718596
  180.1 10.7 %collective-permute-start.10 = (bf16[8,512]{1,0:T(8,128)(2,1)S(1)}, bf16[8,512]{1,0:T(8,128)(2,1)S(1)}, u32[]{:S(2)}, u32[]{:S(2)}) collective-permute-start(bf16[8,512]{1,0:T(8,128)(2,1)S(1)} %convert_element_type.5), channel_id=1, source_target_pairs={{16,0},{32,16},{48,32},{64,48},{80,64},{96,80},{112,96},{17,1},{33... | collective-permute-start | bytes 24584 | tf_op jit(solution)/shard_map/ppermute | solution.py:353
  182.1 8.0 %collective-permute-start.12 = (bf16[8,256]{1,0:T(8,128)(2,1)S(1)}, bf16[8,256]{1,0:T(8,128)(2,1)S(1)}, u32[]{:S(2)}, u32[]{:S(2)}) collective-permute-start(bf16[8,256]{1,0:T(8,128)(2,1)S(1)} %pad_maximum_fusion.1), channel_id=1, source_target_pairs={{1,0},{2,1},{3,2},{4,3},{5,4},{6,5},{7,6},{8,7},{9,8},{10,9},{11,1... | collective-permute-start | bytes 12296 | tf_op jit(solution)/shard_map/ppermute | solution.py:353
  184.0 6.8 %collective-permute-start.11 = (bf16[8,256]{1,0:T(8,128)(2,1)S(1)}, bf16[8,256]{1,0:T(8,128)(2,1)S(1)}, u32[]{:S(2)}, u32[]{:S(2)}) collective-permute-start(bf16[8,256]{1,0:T(8,128)(2,1)S(1)} %pad_maximum_fusion), channel_id=1, source_target_pairs={{0,1},{1,2},{2,3},{3,4},{4,5},{5,6},{6,7},{7,8},{8,9},{9,10},{10,1... | collective-permute-start | bytes 12296 | tf_op jit(solution)/shard_map/ppermute | solution.py:353
Sparse Core Ops, SparseCore 0:
  10.7 33.7 all-gather.4
  53.8 71.5 all-gather.6

commit v5 on v4

--- a/solution.py
+++ b/solution.py
@@ -18,6 +18,7 @@
 R = 8
 K = 512
 NY = 128
+KEEP = 4
 
 bf16 = jnp.bfloat16
 f32 = jnp.float32
@@ -37,24 +38,24 @@
 
 
 def prepare_kernel(rhs_ref, profile_ref, x_ref, chunk_ref):
-    chunk_ref[0] = jnp.zeros((32, K), bf16)
     for a in range(2):
         for x in range(2):
             cols = pl.ds(a * 256 + x * NY, NY)
             for r in range(R):
                 x_ref[pl.ds(r * LZ, LZ), cols] = rhs_ref[a, r, pl.ds(x, LZ, stride=2), :].astype(bf16)
     head = jnp.concatenate([rhs_ref[a, :, x, :] for a in range(2) for x in range(2)], axis=1)
-    profile = jnp.concatenate([profile_ref[...], jnp.zeros((16, K - LZ), bf16)], axis=1)
-    chunk = jnp.concatenate([head, jnp.zeros((8, K), f32)], axis=0).astype(bf16)
+    profile = profile_ref[...].astype(f32)
+    gap = jnp.zeros((8, NY - LZ), f32)
+    tail = jnp.concatenate([profile[:8], gap, profile[8:], gap, jnp.zeros((8, K - 2 * NY), f32)], axis=1)
+    chunk = jnp.concatenate([head, tail], axis=0).astype(bf16)
     for i in range(D):
-        chunk_ref[i, pl.ds(0, 16), :] = chunk
-        chunk_ref[i, pl.ds(16, 16), :] = profile
+        chunk_ref[i] = chunk
 
 
 def prepare(rhs, profile):
     return pl.pallas_call(
         prepare_kernel,
-        out_shape=(jax.ShapeDtypeStruct((R * LZ, K), bf16), jax.ShapeDtypeStruct((D, 32, K), bf16)),
+        out_shape=(jax.ShapeDtypeStruct((R * LZ, K), bf16), jax.ShapeDtypeStruct((D, 16, K), bf16)),
         in_specs=[whole(), whole()],
         out_specs=(whole(), whole()),
         compiler_params=params(8),
@@ -121,90 +122,115 @@
 COST = pl.CostEstimate(flops=10**8, bytes_accessed=5 * 10**6, transcendentals=0)
 
 
-def fetch(h_ref, buf, sem, core):
-    copies = [pltpu.make_async_copy(h_ref.at[core, k], buf.at[k], sem.at[k]) for k in range(C)]
+def fetch(h_ref, buf, sem, core, first=0):
+    copies = [pltpu.make_async_copy(h_ref.at[core, k], buf.at[k], sem.at[k]) for k in range(first, C)]
     for copy in copies:
         copy.start()
     return copies
 
 
-def first_kernel(h_ref, x_ref, v_ref, out_ref, even, odd, even_sem, odd_sem):
+def first_kernel(core_ref, h_ref, x_ref, v_ref, out_ref, keep_ref, even, odd, even_sem, odd_sem):
     bufs = (even, odd)
     copies = [fetch(h_ref, bufs[core], (even_sem, odd_sem)[core], core) for core in range(2)]
     acc = jnp.zeros((16, K), f32)
     for core in range(2):
         for k in range(C):
             copies[core][k].wait()
-            acc = acc + dot_t(x_ref[2 * k + core, pl.ds(0, 16), :], bufs[core][k])
+            acc = acc + dot_t(x_ref[2 * k + core], bufs[core][k])
     v = acc[:R]
     v_ref[...] = v
     for i in range(D):
         out_ref[i] = v.astype(bf16)
+    for core in range(2):
+
+        @pl.when(core_ref[0] == core)
+        def _():
+            for k in range(KEEP):
+                keep_ref[k] = bufs[core][k]
 
 
 HALF = [VMEM((C, K, K), bf16)]
 SEMS = [pltpu.SemaphoreType.DMA((C,))]
 
 
-def first_product(h, x):
+def first_product(core, h, x):
     return pl.pallas_call(
         first_kernel,
-        out_shape=MATVEC_OUT,
-        in_specs=[whole(pltpu.HBM), whole()],
-        out_specs=(whole(), whole()),
+        out_shape=MATVEC_OUT + (jax.ShapeDtypeStruct((KEEP, K, K), bf16),),
+        in_specs=[whole(pltpu.SMEM), whole(pltpu.HBM), whole()],
+        out_specs=(whole(),) * 3,
         scratch_shapes=HALF * 2 + SEMS * 2,
         compiler_params=params(50),
         cost_estimate=COST,
-    )(h, x)
-
-
-def own_kernel(core_ref, h_ref, x_ref, acc_ref, buf, sem):
+    )(core, h, x)
+
+
+def own_kernel(core_ref, h_ref, keep_ref, x_ref, acc_ref, buf, sem):
+    copies = fetch(h_ref, buf, sem, core_ref[0], KEEP)
     acc = jnp.zeros((R, K), f32)
-    for k, copy in enumerate(fetch(h_ref, buf, sem, core_ref[0])):
-        copy.wait()
+    for k in range(KEEP):
+        acc = acc + dot_t(x_ref[k], keep_ref[k])
+    for k in range(KEEP, C):
+        copies[k - KEEP].wait()
         acc = acc + dot_t(x_ref[k], buf[k])
     acc_ref[...] = acc
 
 
-def own_half(core, h, x):
+def own_half(core, h, keep, x):
     return pl.pallas_call(
         own_kernel,
         out_shape=jax.ShapeDtypeStruct((R, K), f32),
-        in_specs=[whole(pltpu.SMEM), whole(pltpu.HBM), whole()],
+        in_specs=[whole(pltpu.SMEM), whole(pltpu.HBM), whole(), whole()],
         out_specs=whole(),
         scratch_shapes=HALF + SEMS,
         compiler_params=params(50),
         cost_estimate=COST,
-    )(core, h, x)
-
-
-def other_kernel(core_ref, mine_ref, h_ref, x_ref, half_ref, base_ref, old_ref, v_ref, out_ref, buf, sem):
+    )(core, h, keep, x)
+
+
+def other_kernel(core_ref, mine_ref, h_ref, x_ref, half_ref, base_ref, old_ref, v_ref, out_ref, buf, sem, ends_ref=None):
     acc = half_ref[...]
     for k, copy in enumerate(fetch(h_ref, buf, sem, 1 - core_ref[0])):
         copy.wait()
         acc = acc + dot_t(x_ref[k], buf[k])
     v = jnp.where(mine_ref[0] > 0, base_ref[...] + COUPLING * acc, old_ref[...])
     v_ref[...] = v
-    for i in range(D):
-        out_ref[i] = v.astype(bf16)
+    rounded = v.astype(bf16)
+    if ends_ref is None:
+        for i in range(D):
+            out_ref[i] = rounded
+        return
+    out_ref[...] = rounded
+    low = jnp.concatenate([rounded[:, :NY], rounded[:, 2 * NY : 3 * NY]], axis=1)
+    high = jnp.concatenate([rounded[:, NY : 2 * NY], rounded[:, 3 * NY :]], axis=1)
+    odd = core_ref[0] > 0
+    ends_ref[0] = jnp.where(odd, high, low)
+    ends_ref[1] = jnp.where(odd, low, high)
+
+
+def final_kernel(core_ref, mine_ref, h_ref, x_ref, half_ref, base_ref, old_ref, v_ref, out_ref, ends_ref, buf, sem):
+    other_kernel(core_ref, mine_ref, h_ref, x_ref, half_ref, base_ref, old_ref, v_ref, out_ref, buf, sem, ends_ref)
 
 
 MATVEC_OUT = (jax.ShapeDtypeStruct((R, K), f32), jax.ShapeDtypeStruct((D, R, K), bf16))
 
 
-def other_half(core, mine, h, x, half, base, old):
-    return pl.pallas_call(
-        other_kernel,
-        out_shape=MATVEC_OUT,
+def other_half(core, mine, h, x, half, base, old, final):
+    out = MATVEC_OUT
+    if final:
+        out = (out[0], jax.ShapeDtypeStruct((R, K), bf16), jax.ShapeDtypeStruct((2, R, 256), bf16))
+    return pl.pallas_call(
+        final_kernel if final else other_kernel,
+        out_shape=out,
         in_specs=[whole(pltpu.SMEM)] * 2 + [whole(pltpu.HBM)] + [whole()] * 4,
-        out_specs=(whole(), whole()),
+        out_specs=(whole(),) * len(out),
         scratch_shapes=HALF + SEMS,
         compiler_params=params(50),
         cost_estimate=COST,
     )(core, mine, h, x, half, base, old)
 
 
-def fronts_kernel(x_ref, h_ref, behind_ref, y_ref, low_ref, high_ref, last_ref, x_buf, h_buf, x_sem, h_sem):
+def fronts_kernel(core_ref, x_ref, h_ref, behind_ref, y_ref, inner_ref, outer_ref, last_ref, x_buf, h_buf, x_sem, h_sem):
     def loads(i):
         core, chip = lax.rem(lax.div(i, 2), 2), lax.div(i, 4) * 2 + lax.rem(i, 2)
         return (
@@ -227,19 +253,22 @@
         total = dot_t(x_buf[2 * j], h_buf[2 * j]) + dot_t(x_buf[2 * j + 1], h_buf[2 * j + 1])
         y_ref[...] += total.reshape(R, LZ, K)
 
+    odd = core_ref[0] > 0
     for r in range(R):
         for a in range(2):
-            low_ref[r, a] = y_ref[r, :, a * 256 : a * 256 + NY].astype(bf16)
-            high_ref[r, a] = y_ref[r, :, a * 256 + NY : a * 256 + 256].astype(bf16)
+            low = y_ref[r, :, a * 256 : a * 256 + NY].astype(bf16)
+            high = y_ref[r, :, a * 256 + NY : a * 256 + 256].astype(bf16)
+            inner_ref[r, a] = jnp.where(odd, low, high)
+            outer_ref[r, a] = jnp.where(odd, high, low)
     last_ref[...] = jnp.concatenate([y_ref[r, LZ - 1 : LZ, :] for r in range(R)], axis=0).astype(bf16)
 
 
-def fronts_of(x, h, behind):
+def fronts_of(core, x, h, behind):
     halo = jax.ShapeDtypeStruct((R, 2, LZ, NY), bf16)
     return pl.pallas_call(
         fronts_kernel,
         out_shape=(jax.ShapeDtypeStruct((R, LZ, K), f32), halo, halo, jax.ShapeDtypeStruct((R, K), bf16)),
-        in_specs=[whole(pltpu.HBM), whole(pltpu.HBM), whole(pl.ANY)],
+        in_specs=[whole(pltpu.SMEM), whole(pltpu.HBM), whole(pltpu.HBM), whole(pl.ANY)],
         out_specs=(whole(),) * 4,
         scratch_shapes=[
             VMEM((D, R * LZ, K), bf16),
@@ -249,28 +278,12 @@
         ],
         compiler_params=params(50),
         cost_estimate=pl.CostEstimate(flops=6 * 10**9, bytes_accessed=23 * 10**6, transcendentals=0),
-    )(x, h, behind)
-
-
-def gate_kernel(*refs):
-    pass
-
-
-def gate(behind, *arrays):
-    n = len(arrays)
-    return pl.pallas_call(
-        gate_kernel,
-        out_shape=tuple(jax.ShapeDtypeStruct(x.shape, x.dtype) for x in arrays),
-        in_specs=[whole(pl.ANY)] * (n + 1),
-        out_specs=(whole(pl.ANY),) * n,
-        input_output_aliases={i: i for i in range(n)},
-        compiler_params=params(8),
-        cost_estimate=pl.CostEstimate(flops=6 * 10**9, bytes_accessed=10**6, transcendentals=0),
-    )(*arrays, behind)
+    )(core, x, h, behind)
 
 
 def wave_kernel(x_ref, coef_ref, panel_ref, behind_ref, out_ref):
-    profile = jnp.concatenate([x_ref[i, pl.ds(16, 16), :][:, :LZ] for i in range(D)], axis=0).astype(f32)
+    chunks = [x_ref[i].astype(f32)[8:] for i in range(D)]
+    profile = jnp.concatenate([x[:, k * NY : k * NY + LZ] for x in chunks for k in range(2)], axis=0)
     panel = panel_ref[...]
     for r in range(R):
         weights = profile * coef_ref[:, r : r + 1]
@@ -293,7 +306,8 @@
     )(x, coef, panel, behind)
 
 
-def residual_kernel(y_ref, rhs_ref, low_ref, high_ref, prev_ref, v_ref, nl_ref, vl_ref, vh_ref, wave_ref, sol_ref, res_ref):
+def residual_kernel(core_ref, y_ref, rhs_ref, inner_ref, outer_ref, prev_ref, v_ref, nl_ref, vi_ref, vo_ref, wave_ref, sol_ref, res_ref):
+    odd = core_ref[0] > 0
     row = lax.broadcasted_iota(jnp.int32, (LZ, NY), 0)
     lane = lax.broadcasted_iota(jnp.int32, (LZ, NY), 1)
     for r in range(R):
@@ -304,8 +318,10 @@
                 s[a, x] = jnp.where(row == 0, v_ref[r : r + 1, cols], y_ref[r, :, cols])
         lap = {}
         for a in range(2):
-            below = jnp.where(row == 0, vl_ref[r : r + 1, a * NY : (a + 1) * NY].astype(f32), low_ref[r, a].astype(f32))
-            above = jnp.where(row == 0, vh_ref[r : r + 1, a * NY : (a + 1) * NY].astype(f32), high_ref[r, a].astype(f32))
+            ends = slice(a * NY, (a + 1) * NY)
+            inner = jnp.where(row == 0, vi_ref[r : r + 1, ends].astype(f32), inner_ref[r, a].astype(f32))
+            outer = jnp.where(row == 0, vo_ref[r : r + 1, ends].astype(f32), outer_ref[r, a].astype(f32))
+            below, above = jnp.where(odd, inner, outer), jnp.where(odd, outer, inner)
             for x in range(2):
                 cols = slice(a * 256 + x * NY, a * 256 + (x + 1) * NY)
                 own = s[a, x]
@@ -332,7 +348,7 @@
     return pl.pallas_call(
         residual_kernel,
         out_shape=(shape, shape),
-        in_specs=[whole()] * len(args),
+        in_specs=[whole(pltpu.SMEM)] + [whole()] * (len(args) - 1),
         out_specs=(whole(), whole()),
         compiler_params=params(24),
     )(*args)
@@ -361,15 +377,18 @@
     along_z = [[z * 4 + x * 2 + c for z in range(4) for c in range(2)] for x in range(2)]
     paired = lax.all_gather(own, "plane", axis=0, axis_index_groups=along_x)
     heads = lax.all_to_all(chunk, "plane", 0, 0)
-    h = arrange(inverse_blocks.reshape(K, 2, 32, NY))
+    blocks, _ = lax.optimization_barrier((inverse_blocks, chunk))
+    h = arrange(blocks.reshape(K, 2, 32, NY))
+    heads, _ = lax.optimization_barrier((heads, h))
 
     mixed = (lattice_index[None, :] * generator[:, None] + shift_index.T) % NPTS
     amplitude = 0.25 / jnp.sqrt(1.0 + jnp.arange(MODES, dtype=f32) / 8.0)
     coef = amplitude[:, None] * ((mixed.astype(f32) + 0.5) / NPTS - 0.5)
     core = lax.rem(lax.axis_index("plane"), 2).astype(jnp.int32).reshape(1)
     twin = [(i, i ^ 1) for i in range(D)]
-
-    base, out = first_product(h, heads)
+    next_chip = [(i, i + 1) for i in range(1, D - 1, 2)] + [(i + 1, i) for i in range(1, D - 1, 2)]
+
+    base, out, keep = first_product(core, h, heads)
     v = base
     for step in range(1, G):
         if step == 2:
@@ -380,24 +399,23 @@
             wavenum = wave(heads, coef, mode_panel.reshape(MODES, 256), v)
             got, wavenum = lax.optimization_barrier((got, wavenum))
         if step == 6:
-            y, low, high, last = fronts_of(gathered, h, v)
-            got, low, high, last = lax.optimization_barrier((got, low, high, last))
+            y, inner, outer, last = fronts_of(core, gathered, h, v)
+            got, inner, outer, last = lax.optimization_barrier((got, inner, outer, last))
         if step == 7:
-            low, high, last = gate(v, low, high, last)
-            before = shift(high, "plane", 1)
-            after = shift(low, "plane", -1)
-            below = shift(last, "layer", 1)
-            got, before, after, below = lax.optimization_barrier((got, before, after, below))
+            inner, outer, last, v = lax.optimization_barrier((inner, outer, last, v))
+            outer = lax.ppermute(outer, "plane", next_chip)
+            inner = lax.ppermute(inner, "plane", twin)
+            last = shift(last, "layer", 1)
+            got, inner, outer, last = lax.optimization_barrier((got, inner, outer, last))
         other = lax.ppermute(got, "plane", twin)
-        half = own_half(core, h, got)
+        half = own_half(core, h, keep, got)
         mine = (group == step).astype(jnp.int32).reshape(1)
-        v, out = other_half(core, mine, h, other, half, base, v)
-
-    vb = v.astype(bf16)
-    nl = shift(vb, "layer", -1)
-    vl = shift(jnp.concatenate([vb[:, NY : 2 * NY], vb[:, 3 * NY :]], axis=1), "plane", 1)
-    vh = shift(jnp.concatenate([vb[:, :NY], vb[:, 2 * NY : 3 * NY]], axis=1), "plane", -1)
-    sol, res = residual(y, flat, before, after, below, v, nl, vl, vh, wavenum)
+        v, out, *ends = other_half(core, mine, h, other, half, base, v, step == G - 1)
+
+    v_outer = lax.ppermute(ends[0][0], "plane", next_chip)
+    v_next = shift(out, "layer", -1)
+    v_inner = lax.ppermute(ends[0][1], "plane", twin)
+    sol, res = residual(core, y, flat, inner, outer, last, v, v_next, v_inner, v_outer, wavenum)
     return sol.reshape(rhs.shape), res.reshape(rhs.shape)
 
 

time: 203 us -> 194 us (0.956)
  starting transfers between devices: 60.6 us -> 51 us
  Pallas kernels: 65.8 us -> 62.1 us
  blocking collectives: 44.3 us -> 46.6 us
    ppermute x6 -> x2, starting transfers between devices: 19.1 us -> 6.01 us  [shift(): lax.ppermute(value, axis, [(i, i + by) for i in range(size) if 0 <= i + b...]
    ppermute x0 -> x4, starting transfers between devices: none -> 7 us  [the longest x1 4.11 us: shards(): outer = lax.ppermute(outer, 'plane', next_chip)]
    ppermute x0 -> x4, waiting for transfers between devices: none -> 5.06 us  [the longest x1 5.05 us: shards(): v_outer = lax.ppermute(ends[0][0], 'plane', next_chip)]
    pallas_call x7, Pallas kernels: 17.5 us -> 13 us  [own_half(): pl.pallas_call(own_kernel, out_shape=jax.ShapeDtypeStruct((R, K), f32), i...]
    ppermute x7, starting transfers between devices: 10.8 us -> 7.51 us  [shards(): other = lax.ppermute(got, 'plane', twin)]
    all_to_all x1, waiting for transfers between devices: 2.72 us -> 0.01 us  [shards(): heads = lax.all_to_all(chunk, 'plane', 0, 0)]
    all_to_all x4, blocking collectives: 44.3 us -> 46.6 us  [shards(): lax.all_to_all(out, ('layer', 'plane'), 0, 0, axis_index_groups=pair_grou...]
    unnamed x18 -> x28, local copies, waits for them, and re-layouts: 3.6 us -> 5.2 us
  transfers between devices with their start and end apart: 19 -> 19, of which waited for: 4 -> 4; matrix products, arithmetic and copies ran while one was open for 0% -> 0% of each run, Pallas kernels for 28% -> 27%
where the time goes in v5:
time: 194 us; the launch traced here: 193 us
  Pallas kernels  62.1 us (32%)
  starting transfers between devices  51 us (26%)
  blocking collectives  46.6 us (24%)
  between operations  14.5 us (7%)
  waiting for transfers between devices  13 us (7%)
  local copies, waits for them, and re-layouts  5.2 us (3%)
    all_to_all x4, blocking collectives, shards(): lax.all_to_all(out, ('layer', 'plane'), 0, 0, axis_index_groups=pair_grou...  46.6 us
    all_to_all x3, starting transfers between devices, shards(): lax.all_to_all(out, ('layer', 'plane'), 0, 0, axis_index_groups=pair_grou...  21.7 us
    pallas_call x7, Pallas kernels, other_half(): pl.pallas_call(final_kernel if final else other_kernel, out_shape=out, in...  19.9 us
    pallas_call x7, Pallas kernels, own_half(): pl.pallas_call(own_kernel, out_shape=jax.ShapeDtypeStruct((R, K), f32), i...  13 us
    pallas_call x1, Pallas kernels, fronts_of(): pl.pallas_call(fronts_kernel, out_shape=(jax.ShapeDtypeStruct((R, LZ, K),...  11.1 us
    all_to_all x1, starting transfers between devices, shards(): heads = lax.all_to_all(chunk, 'plane', 0, 0)  8.62 us
    ppermute x7, starting transfers between devices, shards(): other = lax.ppermute(got, 'plane', twin)  7.51 us
    pallas_call x1, Pallas kernels, arrange(): pl.pallas_call(arrange_kernel, out_shape=jax.ShapeDtypeStruct((2, C, K, K...  7.05 us
  transfers between devices with their start and end apart: 19, of which 4 were waited for; matrix products, arithmetic and copies ran while one was open for 0% of the time, Pallas kernels for 27%

profile of v5, /device:TPU:7, one launch (start us, length us, event | category | flops | bytes accessed | tf_op | source)
XLA Modules:
  0.0 192.5 jit_solution(15727530638172689647)
XLA Ops:
  7.2 0.0 all-gather.5.cloned.1.call-start
  7.2 0.0 copy-start
  7.2 1.4 copy-done
  8.6 0.7 copy-done.8
  9.3 1.1 shard_map.86
  10.4 0.0 all-gather.5.cloned.1.call-update
  10.4 8.6 %all-to-all-start = ((bf16[16,16,512]{2,1,0:T(8,128)(2,1)}), bf16[16,16,512]{2,1,0:T(8,128)(2,1)S(1)}, u32[]{:S(2)}, u32[]{:S(2)}) async-start(bf16[16,16,512]{2,1,0:T(8,128)(2,1)} %get-tuple-element.46), calls=%async_computation | async-start | bytes 524288 | tf_op jit(solution)/shard_map/all_to_all | solution.py:379
  19.1 0.0 all-gather.7.cloned.1.call-start
  19.1 7.0 %shard_map.87.h_ref = bf16[2,8,512,512]{3,2,1,0:T(8,128)(2,1)} custom-call(bf16[512,2,32,128]{3,2,1,0:T(8,128)(2,1)} %bitcast.30), custom_call_target="tpu_custom_call" | custom-call | flops 4000000000 | bytes 17000000 | tf_op jit(solution)/shard_map/pallas_call | solution.py:106
  26.2 4.9 %shard_map.88 = (f32[8,512]{1,0:T(8,128)S(1)}, bf16[16,8,512]{2,1,0:T(8,128)(2,1)S(1)}, bf16[4,512,512]{2,1,0:T(8,128)(2,1)S(1)}) custom-call(s32[1]{0:T(128)} %bitcast.core_ref, bf16[2,8,512,512]{3,2,1,0:T(8,128)(2,1)} %shard_map.87.h_ref, bf16[16,16,512]{2,1,0:T(8,128)(2,1)S(1)} %all-to-all-done.x_ref), custom_call_target="tpu_custom_call" | custom-call | flops 100000000 | bytes 5000000 | tf_op jit(solution)/shard_map/pallas_call | solution.py:157
  31.0 13.7 %all_to_all.40.x_ref = bf16[16,8,512]{2,1,0:T(8,128)(2,1)S(1)} all-to-all(bf16[16,8,512]{2,1,0:T(8,128)(2,1)S(1)} %get-tuple-element.49), channel_id=1, replica_groups={{0,2,4,6,8,10,12,14,16,18,20,22,24,26,28,30},{1,3,5,7,9,11,13,15,17,19,..., dimensions={0} | all-to-all | bytes 262144 | tf_op jit(solution)/shard_map/all_to_all | solution.py:397
  44.8 1.5 collective-permute-start
  46.2 1.8 shard_map.89.half_ref
  48.1 3.1 %shard_map.90 = (f32[8,512]{1,0:T(8,128)S(1)}, bf16[16,8,512]{2,1,0:T(8,128)(2,1)}) custom-call(s32[1]{0:T(128)} %bitcast.core_ref, s32[1]{0:T(128)} %bitcast.3.mine_ref, bf16[2,8,512,512]{3,2,1,0:T(8,128)(2,1)} %shard_map.87.h_ref, bf16[16,8,512]{2,1,0:T(8,128)(2,1)S(1)} %collective-permute-done.x_ref, f32[8,512]{1,0:T(8,128)S(1)} %shard_map.89.half_ref, ...), custom_call_target="tpu_custom_call" | custom-call | flops 100000000 | bytes 5000000 | tf_op jit(solution)/shard_map/pallas_call | solution.py:222
  51.2 0.0 copy-start.10
  51.2 0.0 copy-start.12
  51.3 0.0 copy-start.9
  51.3 0.0 all-gather.5.cloned.1.call-done
  51.3 0.0 all-gather.7.cloned.1.call-update
  51.3 0.6 copy-done.10
  51.9 0.1 copy.11
  52.1 7.9 %all-to-all-start.2 = ((bf16[16,8,512]{2,1,0:T(8,128)(2,1)}), bf16[16,8,512]{2,1,0:T(8,128)(2,1)S(1)}, u32[]{:S(2)}, u32[]{:S(2)}) async-start(bf16[16,8,512]{2,1,0:T(8,128)(2,1)} %get-tuple-element.54), calls=%async_computation.2 | async-start | bytes 262144 | tf_op jit(solution)/shard_map/all_to_all | solution.py:397
  60.0 0.2 fusion.5.coef_ref
  60.2 1.3 shard_map.91.wave_ref
  61.5 4.1 %all-to-all-done.2.x_ref = bf16[16,8,512]{2,1,0:T(8,128)(2,1)S(1)} async-done(((bf16[16,8,512]{2,1,0:T(8,128)(2,1)}), bf16[16,8,512]{2,1,0:T(8,128)(2,1)S(1)}, u32[]{:S(2)}, u32[]{:S(2)}) %all-to-all-start.2) | async-done | bytes 131104 | tf_op jit(solution)/shard_map/all_to_all | solution.py:397
  65.6 1.2 collective-permute-start.1
  66.8 1.8 shard_map.92.half_ref
  68.6 2.5 %shard_map.93 = (f32[8,512]{1,0:T(8,128)S(1)}, bf16[16,8,512]{2,1,0:T(8,128)(2,1)S(1)}) custom-call(s32[1]{0:T(128)} %bitcast.core_ref, s32[1]{0:T(128)} %bitcast.8.mine_ref, bf16[2,8,512,512]{3,2,1,0:T(8,128)(2,1)} %shard_map.87.h_ref, bf16[16,8,512]{2,1,0:T(8,128)(2,1)S(1)} %collective-permute-done.1.x_ref, f32[8,512]{1,0:T(8,128)S(1)} %shard_map.92.half_ref, ...), custom_call_target="tpu_custom_call" | custom-call | flops 100000000 | bytes 5000000 | tf_op jit(solution)/shard_map/pallas_call | solution.py:222
  71.1 10.2 %all_to_all.41.x_ref = bf16[16,8,512]{2,1,0:T(8,128)(2,1)S(1)} all-to-all(bf16[16,8,512]{2,1,0:T(8,128)(2,1)S(1)} %get-tuple-element.56), channel_id=1, replica_groups={{32,34,36,38,40,42,44,46,48,50,52,54,56,58,60,62},{33,35,37,39,41,43,45..., dimensions={0} | all-to-all | bytes 262144 | tf_op jit(solution)/shard_map/all_to_all | solution.py:397
  81.3 1.2 collective-permute-start.2
  82.5 1.8 shard_map.94.half_ref
  84.4 2.7 %shard_map.95 = (f32[8,512]{1,0:T(8,128)S(1)}, bf16[16,8,512]{2,1,0:T(8,128)(2,1)S(1)}) custom-call(s32[1]{0:T(128)} %bitcast.core_ref, s32[1]{0:T(128)} %bitcast.7.mine_ref, bf16[2,8,512,512]{3,2,1,0:T(8,128)(2,1)} %shard_map.87.h_ref, bf16[16,8,512]{2,1,0:T(8,128)(2,1)S(1)} %collective-permute-done.2.x_ref, f32[8,512]{1,0:T(8,128)S(1)} %shard_map.94.half_ref, ...), custom_call_target="tpu_custom_call" | custom-call | flops 100000000 | bytes 5000000 | tf_op jit(solution)/shard_map/pallas_call | solution.py:222
  87.1 12.3 %all_to_all.42.x_ref = bf16[16,8,512]{2,1,0:T(8,128)(2,1)S(1)} all-to-all(bf16[16,8,512]{2,1,0:T(8,128)(2,1)S(1)} %get-tuple-element.58), channel_id=1, replica_groups={{48,50,52,54,56,58,60,62,64,66,68,70,72,74,76,78},{49,51,53,55,57,59,61..., dimensions={0} | all-to-all | bytes 262144 | tf_op jit(solution)/shard_map/all_to_all | solution.py:397
  99.4 1.4 collective-permute-start.3
  100.8 1.8 shard_map.96.half_ref
  102.7 2.7 %shard_map.97 = (f32[8,512]{1,0:T(8,128)S(1)}, bf16[16,8,512]{2,1,0:T(8,128)(2,1)S(1)}) custom-call(s32[1]{0:T(128)} %bitcast.core_ref, s32[1]{0:T(128)} %bitcast.6.mine_ref, bf16[2,8,512,512]{3,2,1,0:T(8,128)(2,1)} %shard_map.87.h_ref, bf16[16,8,512]{2,1,0:T(8,128)(2,1)S(1)} %collective-permute-done.3.x_ref, f32[8,512]{1,0:T(8,128)S(1)} %shard_map.96.half_ref, ...), custom_call_target="tpu_custom_call" | custom-call | flops 100000000 | bytes 5000000 | tf_op jit(solution)/shard_map/pallas_call | solution.py:222
  105.4 10.4 %all_to_all.43.x_ref = bf16[16,8,512]{2,1,0:T(8,128)(2,1)S(1)} all-to-all(bf16[16,8,512]{2,1,0:T(8,128)(2,1)S(1)} %get-tuple-element.60), channel_id=1, replica_groups={{64,66,68,70,72,74,76,78,80,82,84,86,88,90,92,94},{65,67,69,71,73,75,77..., dimensions={0} | all-to-all | bytes 262144 | tf_op jit(solution)/shard_map/all_to_all | solution.py:397
  115.8 0.9 collective-permute-start.4
  116.7 2.0 %shard_map.98.half_ref = f32[8,512]{1,0:T(8,128)S(1)} custom-call(s32[1]{0:T(128)} %bitcast.core_ref, bf16[2,8,512,512]{3,2,1,0:T(8,128)(2,1)} %shard_map.87.h_ref, bf16[4,512,512]{2,1,0:T(8,128)(2,1)S(1)} %get-tuple-element.50.keep_ref, bf16[16,8,512]{2,1,0:T(8,128)(2,1)S(1)} %all_to_all.43.x_ref), custom_call_target="tpu_custom_call" | custom-call | flops 100000000 | bytes 5000000 | tf_op jit(solution)/shard_map/pallas_call | solution.py:180
  118.7 3.1 %shard_map.99 = (f32[8,512]{1,0:T(8,128)S(1)}, bf16[16,8,512]{2,1,0:T(8,128)(2,1)}) custom-call(s32[1]{0:T(128)} %bitcast.core_ref, s32[1]{0:T(128)} %bitcast.5.mine_ref, bf16[2,8,512,512]{3,2,1,0:T(8,128)(2,1)} %shard_map.87.h_ref, bf16[16,8,512]{2,1,0:T(8,128)(2,1)S(1)} %collective-permute-done.4.x_ref, f32[8,512]{1,0:T(8,128)S(1)} %shard_map.98.half_ref, ...), custom_call_target="tpu_custom_call" | custom-call | flops 100000000 | bytes 5000000 | tf_op jit(solution)/shard_map/pallas_call | solution.py:222
  121.8 7.4 %all-to-all-start.6 = ((bf16[16,8,512]{2,1,0:T(8,128)(2,1)}), bf16[16,8,512]{2,1,0:T(8,128)(2,1)S(1)}, u32[]{:S(2)}, u32[]{:S(2)}) async-start(bf16[16,8,512]{2,1,0:T(8,128)(2,1)} %get-tuple-element.64), calls=%async_computation.6 | async-start | bytes 262144 | tf_op jit(solution)/shard_map/all_to_all | solution.py:397
  129.2 0.0 all-gather.7.cloned.1.call-done.x_ref
  129.3 11.1 %shard_map.100 = (f32[8,96,512]{2,1,0:T(8,128)S(1)}, bf16[8,2,96,128]{3,2,1,0:T(8,128)(2,1)}, bf16[8,2,96,128]{3,2,1,0:T(8,128)(2,1)}, bf16[8,512]{1,0:T(8,128)(2,1)S(1)}) custom-call(s32[1]{0:T(128)} %bitcast.core_ref, bf16[16,768,512]{2,1,0:T(8,128)(2,1)} %all-gather.7.cloned.1.call-done.x_ref, bf16[2,8,512,512]{3,2,1,0:T(8,128)(2,1)} %shard_map.87.h_ref, ...), custom_call_target="tpu_custom_call" | custom-call | flops 6000000000 | bytes 23000000 | tf_op jit(solution)/shard_map/pallas_call | solution.py:268
  140.3 0.0 copy-start.2
  140.4 1.1 copy-done.2
  141.5 0.2 collective-permute-start.5
  141.7 1.8 shard_map.101.half_ref
  143.6 3.1 %shard_map.102 = (f32[8,512]{1,0:T(8,128)S(1)}, bf16[16,8,512]{2,1,0:T(8,128)(2,1)}) custom-call(s32[1]{0:T(128)} %bitcast.core_ref, s32[1]{0:T(128)} %bitcast.10.mine_ref, bf16[2,8,512,512]{3,2,1,0:T(8,128)(2,1)} %shard_map.87.h_ref, bf16[16,8,512]{2,1,0:T(8,128)(2,1)S(1)} %collective-permute-done.5.x_ref, f32[8,512]{1,0:T(8,128)S(1)} %shard_map.101.half_ref, ...), custom_call_target="tpu_custom_call" | custom-call | flops 100000000 | bytes 5000000 | tf_op jit(solution)/shard_map/pallas_call | solution.py:222
  146.7 0.6 copy-done.4
  147.3 0.3 collective-permute-start.6
  147.6 4.1 %collective-permute-start.7 = (bf16[8,2,96,128]{3,2,1,0:T(8,128)(2,1)}, bf16[8,2,96,128]{3,2,1,0:T(8,128)(2,1)}, u32[]{:S(2)}, u32[]{:S(2)}) collective-permute-start(bf16[8,2,96,128]{3,2,1,0:T(8,128)(2,1)} %get-tuple-element.75), channel_id=1, source_target_pairs={{1,2},{3,4},{5,6},{7,8},{9,10},{11,12},{13,14},{2,1},{4,3},{6,5},{... | collective-permute-start | bytes 1179656 | tf_op jit(solution)/shard_map/ppermute | solution.py:406
  151.7 6.4 %all-to-all-start.7 = ((bf16[16,8,512]{2,1,0:T(8,128)(2,1)}), bf16[16,8,512]{2,1,0:T(8,128)(2,1)S(1)}, u32[]{:S(2)}, u32[]{:S(2)}) async-start(bf16[16,8,512]{2,1,0:T(8,128)(2,1)} %get-tuple-element.69), calls=%async_computation.7 | async-start | bytes 262144 | tf_op jit(solution)/shard_map/all_to_all | solution.py:397
  158.1 3.1 %collective-permute-start.8 = (bf16[8,512]{1,0:T(8,128)(2,1)S(1)}, bf16[8,512]{1,0:T(8,128)(2,1)S(1)}, u32[]{:S(2)}, u32[]{:S(2)}) collective-permute-start(bf16[8,512]{1,0:T(8,128)(2,1)S(1)} %get-tuple-element.76), channel_id=1, source_target_pairs={{0,16},{16,32},{32,48},{48,64},{64,80},{80,96},{96,112},{1,17},{17... | collective-permute-start | bytes 24584 | tf_op jit(solution)/shard_map/ppermute | solution.py:369
  161.2 3.7 %collective-permute-done.8.prev_ref = bf16[8,512]{1,0:T(8,128)(2,1)S(1)} collective-permute-done((bf16[8,512]{1,0:T(8,128)(2,1)S(1)}, bf16[8,512]{1,0:T(8,128)(2,1)S(1)}, u32[]{:S(2)}, u32[]{:S(2)}) %collective-permute-start.8) | collective-permute-done | bytes 8224 | tf_op jit(solution)/shard_map/ppermute | solution.py:369
  164.9 0.6 copy-done.6
  165.5 0.1 all-to-all-done.7.x_ref
  165.6 1.1 collective-permute-start.9
  166.7 1.8 shard_map.103.half_ref
  168.6 2.6 %shard_map.104 = (f32[8,512]{1,0:T(8,128)S(1)}, bf16[8,512]{1,0:T(8,128)(2,1)S(1)}, bf16[2,8,256]{2,1,0:T(8,128)(2,1)S(1)}) custom-call(s32[1]{0:T(128)} %bitcast.core_ref, s32[1]{0:T(128)} %bitcast.11.mine_ref, bf16[2,8,512,512]{3,2,1,0:T(8,128)(2,1)} %shard_map.87.h_ref, bf16[16,8,512]{2,1,0:T(8,128)(2,1)S(1)} %collective-permute-done.9.x_ref, ...), custom_call_target="tpu_custom_call" | custom-call | flops 100000000 | bytes 5000000 | tf_op jit(solution)/shard_map/pallas_call | solution.py:222
  171.2 2.9 %collective-permute-start.10 = (bf16[8,512]{1,0:T(8,128)(2,1)S(1)}, bf16[8,512]{1,0:T(8,128)(2,1)S(1)}, u32[]{:S(2)}, u32[]{:S(2)}) collective-permute-start(bf16[8,512]{1,0:T(8,128)(2,1)S(1)} %get-tuple-element.83), channel_id=1, source_target_pairs={{16,0},{32,16},{48,32},{64,48},{80,64},{96,80},{112,96},{17,1},{33... | collective-permute-start | bytes 24584 | tf_op jit(solution)/shard_map/ppermute | solution.py:369
  174.2 0.4 collective-permute-start.11
  174.5 2.2 %collective-permute-start.12 = (bf16[8,256]{1,0:T(8,128)(2,1)S(1)}, bf16[8,256]{1,0:T(8,128)(2,1)S(1)}, u32[]{:S(2)}, u32[]{:S(2)}) collective-permute-start(bf16[8,256]{1,0:T(8,128)(2,1)S(1)} %get-tuple-element.88), channel_id=1, source_target_pairs={{1,2},{3,4},{5,6},{7,8},{9,10},{11,12},{13,14},{2,1},{4,3},{6,5},{... | collective-permute-start | bytes 12296 | tf_op jit(solution)/shard_map/ppermute | solution.py:415
  176.8 5.1 %collective-permute-done.12.vo_ref = bf16[8,256]{1,0:T(8,128)(2,1)S(1)} collective-permute-done((bf16[8,256]{1,0:T(8,128)(2,1)S(1)}, bf16[8,256]{1,0:T(8,128)(2,1)S(1)}, u32[]{:S(2)}, u32[]{:S(2)}) %collective-permute-start.12) | collective-permute-done | bytes 4128 | tf_op jit(solution)/shard_map/ppermute | solution.py:415
  181.9 3.8 %shard_map.105 = (f32[2,8,192,128]{3,2,1,0:T(8,128)}, f32[2,8,192,128]{3,2,1,0:T(8,128)}) custom-call(s32[1]{0:T(128)} %bitcast.core_ref, f32[8,96,512]{2,1,0:T(8,128)S(1)} %copy-done.3, f32[2,8,192,128]{3,2,1,0:T(8,128)S(1)} %bitcast.28, bf16[8,2,96,128]{3,2,1,0:T(8,128)(2,1)S(1)} %collective-permute-done.6.inner_ref, ...), custom_call_target="tpu_custom_call" | custom-call | tf_op jit(solution)/shard_map/pallas_call | solution.py:348
  (31 shorter events, 0.1 us)
Async XLA Ops:
  7.2 44.1 %all-gather.5.cloned.1.call-start = ((), (), s32[]{:S(2)}) async-start(), calls=%async_computation.8 | async-start | bytes 2359296 | tf_op jit(solution)/shard_map/all_gather | solution.py:378
  7.2 1.4 copy-start
  8.6 0.7 copy-start.8
  10.4 15.7 %all-to-all-start = ((bf16[16,16,512]{2,1,0:T(8,128)(2,1)}), bf16[16,16,512]{2,1,0:T(8,128)(2,1)S(1)}, u32[]{:S(2)}, u32[]{:S(2)}) async-start(bf16[16,16,512]{2,1,0:T(8,128)(2,1)} %get-tuple-element.46), calls=%async_computation | async-start | bytes 524288 | tf_op jit(solution)/shard_map/all_to_all | solution.py:379
  19.1 110.2 %all-gather.7.cloned.1.call-start = ((), (), s32[]{:S(2)}) async-start(), calls=%async_computation.9 | async-start | bytes 14155776 | tf_op jit(solution)/shard_map/all_gather | solution.py:396
  44.8 3.3 %collective-permute-start = (bf16[16,8,512]{2,1,0:T(8,128)(2,1)S(1)}, bf16[16,8,512]{2,1,0:T(8,128)(2,1)S(1)}, u32[]{:S(2)}, u32[]{:S(2)}) collective-permute-start(bf16[16,8,512]{2,1,0:T(8,128)(2,1)S(1)} %all_to_all.40.x_ref), channel_id=1, source_target_pairs={{0,1},{1,0},{2,3},{3,2},{4,5},{5,4},{6,7},{7,6},{8,9},{9,8},{10,11... | collective-permute-start | bytes 393224 | tf_op jit(solution)/shard_map/ppermute | solution.py:410
  51.2 0.7 copy-start.10
  51.2 8.8 %copy-start.11 = (s32[256]{0:T(256)S(1)}, s32[256]{0:T(256)}, u32[]{:S(2)}) copy-start(s32[256]{0:T(256)} %param.11) | copy-start | bytes 3076
  51.2 8.8 %copy-start.12 = (s32[8]{0:T(128)S(1)}, s32[8]{0:T(128)}, u32[]{:S(2)}) copy-start(s32[8]{0:T(128)} %param.12) | copy-start | bytes 100
  51.3 8.9 %copy-start.9 = (bf16[256,2,128]{2,1,0:T(2,128)(2,1)S(1)}, bf16[256,2,128]{2,1,0:T(2,128)(2,1)}, u32[]{:S(2)}) copy-start(bf16[256,2,128]{2,1,0:T(2,128)(2,1)} %param.9) | copy-start | bytes 393220
  52.1 13.6 %all-to-all-start.2 = ((bf16[16,8,512]{2,1,0:T(8,128)(2,1)}), bf16[16,8,512]{2,1,0:T(8,128)(2,1)S(1)}, u32[]{:S(2)}, u32[]{:S(2)}) async-start(bf16[16,8,512]{2,1,0:T(8,128)(2,1)} %get-tuple-element.54), calls=%async_computation.2 | async-start | bytes 262144 | tf_op jit(solution)/shard_map/all_to_all | solution.py:397
  65.6 3.0 %collective-permute-start.1 = (bf16[16,8,512]{2,1,0:T(8,128)(2,1)S(1)}, bf16[16,8,512]{2,1,0:T(8,128)(2,1)S(1)}, u32[]{:S(2)}, u32[]{:S(2)}) collective-permute-start(bf16[16,8,512]{2,1,0:T(8,128)(2,1)S(1)} %all-to-all-done.2.x_ref), channel_id=1, source_target_pairs={{0,1},{1,0},{2,3},{3,2},{4,5},{5,4},{6,7},{7,6},{8,9},{9,8},{10,11... | collective-permute-start | bytes 393224 | tf_op jit(solution)/shard_map/ppermute | solution.py:410
  81.3 3.1 %collective-permute-start.2 = (bf16[16,8,512]{2,1,0:T(8,128)(2,1)S(1)}, bf16[16,8,512]{2,1,0:T(8,128)(2,1)S(1)}, u32[]{:S(2)}, u32[]{:S(2)}) collective-permute-start(bf16[16,8,512]{2,1,0:T(8,128)(2,1)S(1)} %all_to_all.41.x_ref), channel_id=1, source_target_pairs={{0,1},{1,0},{2,3},{3,2},{4,5},{5,4},{6,7},{7,6},{8,9},{9,8},{10,11... | collective-permute-start | bytes 393224 | tf_op jit(solution)/shard_map/ppermute | solution.py:410
  99.4 3.3 %collective-permute-start.3 = (bf16[16,8,512]{2,1,0:T(8,128)(2,1)S(1)}, bf16[16,8,512]{2,1,0:T(8,128)(2,1)S(1)}, u32[]{:S(2)}, u32[]{:S(2)}) collective-permute-start(bf16[16,8,512]{2,1,0:T(8,128)(2,1)S(1)} %all_to_all.42.x_ref), channel_id=1, source_target_pairs={{0,1},{1,0},{2,3},{3,2},{4,5},{5,4},{6,7},{7,6},{8,9},{9,8},{10,11... | collective-permute-start | bytes 393224 | tf_op jit(solution)/shard_map/ppermute | solution.py:410
  115.8 2.9 %collective-permute-start.4 = (bf16[16,8,512]{2,1,0:T(8,128)(2,1)S(1)}, bf16[16,8,512]{2,1,0:T(8,128)(2,1)S(1)}, u32[]{:S(2)}, u32[]{:S(2)}) collective-permute-start(bf16[16,8,512]{2,1,0:T(8,128)(2,1)S(1)} %all_to_all.43.x_ref), channel_id=1, source_target_pairs={{0,1},{1,0},{2,3},{3,2},{4,5},{5,4},{6,7},{7,6},{8,9},{9,8},{10,11... | collective-permute-start | bytes 393224 | tf_op jit(solution)/shard_map/ppermute | solution.py:410
  121.8 19.6 %all-to-all-start.6 = ((bf16[16,8,512]{2,1,0:T(8,128)(2,1)}), bf16[16,8,512]{2,1,0:T(8,128)(2,1)S(1)}, u32[]{:S(2)}, u32[]{:S(2)}) async-start(bf16[16,8,512]{2,1,0:T(8,128)(2,1)} %get-tuple-element.64), calls=%async_computation.6 | async-start | bytes 262144 | tf_op jit(solution)/shard_map/all_to_all | solution.py:397
  140.3 1.1 copy-start.2
  141.5 2.1 %collective-permute-start.5 = (bf16[16,8,512]{2,1,0:T(8,128)(2,1)S(1)}, bf16[16,8,512]{2,1,0:T(8,128)(2,1)S(1)}, u32[]{:S(2)}, u32[]{:S(2)}) collective-permute-start(bf16[16,8,512]{2,1,0:T(8,128)(2,1)S(1)} %all-to-all-done.6.x_ref), channel_id=1, source_target_pairs={{0,1},{1,0},{2,3},{3,2},{4,5},{5,4},{6,7},{7,6},{8,9},{9,8},{10,11... | collective-permute-start | bytes 393224 | tf_op jit(solution)/shard_map/ppermute | solution.py:410
  146.7 0.6 copy-start.4
  147.3 18.3 %collective-permute-start.6 = (bf16[8,2,96,128]{3,2,1,0:T(8,128)(2,1)}, bf16[8,2,96,128]{3,2,1,0:T(8,128)(2,1)S(1)}, u32[]{:S(2)}, u32[]{:S(2)}) collective-permute-start(bf16[8,2,96,128]{3,2,1,0:T(8,128)(2,1)} %get-tuple-element.74), channel_id=1, source_target_pairs={{0,1},{1,0},{2,3},{3,2},{4,5},{5,4},{6,7},{7,6},{8,9},{9,8},{10,11... | collective-permute-start | bytes 1179656 | tf_op jit(solution)/shard_map/ppermute | solution.py:407
  147.6 18.0 %collective-permute-start.7 = (bf16[8,2,96,128]{3,2,1,0:T(8,128)(2,1)}, bf16[8,2,96,128]{3,2,1,0:T(8,128)(2,1)}, u32[]{:S(2)}, u32[]{:S(2)}) collective-permute-start(bf16[8,2,96,128]{3,2,1,0:T(8,128)(2,1)} %get-tuple-element.75), channel_id=1, source_target_pairs={{1,2},{3,4},{5,6},{7,8},{9,10},{11,12},{13,14},{2,1},{4,3},{6,5},{... | collective-permute-start | bytes 1179656 | tf_op jit(solution)/shard_map/ppermute | solution.py:406
  151.7 13.9 %all-to-all-start.7 = ((bf16[16,8,512]{2,1,0:T(8,128)(2,1)}), bf16[16,8,512]{2,1,0:T(8,128)(2,1)S(1)}, u32[]{:S(2)}, u32[]{:S(2)}) async-start(bf16[16,8,512]{2,1,0:T(8,128)(2,1)} %get-tuple-element.69), calls=%async_computation.7 | async-start | bytes 262144 | tf_op jit(solution)/shard_map/all_to_all | solution.py:397
  158.1 6.8 %collective-permute-start.8 = (bf16[8,512]{1,0:T(8,128)(2,1)S(1)}, bf16[8,512]{1,0:T(8,128)(2,1)S(1)}, u32[]{:S(2)}, u32[]{:S(2)}) collective-permute-start(bf16[8,512]{1,0:T(8,128)(2,1)S(1)} %get-tuple-element.76), channel_id=1, source_target_pairs={{0,16},{16,32},{32,48},{48,64},{64,80},{80,96},{96,112},{1,17},{17... | collective-permute-start | bytes 24584 | tf_op jit(solution)/shard_map/ppermute | solution.py:369
  164.9 0.6 copy-start.6
  165.6 2.9 %collective-permute-start.9 = (bf16[16,8,512]{2,1,0:T(8,128)(2,1)S(1)}, bf16[16,8,512]{2,1,0:T(8,128)(2,1)S(1)}, u32[]{:S(2)}, u32[]{:S(2)}) collective-permute-start(bf16[16,8,512]{2,1,0:T(8,128)(2,1)S(1)} %all-to-all-done.7.x_ref), channel_id=1, source_target_pairs={{0,1},{1,0},{2,3},{3,2},{4,5},{5,4},{6,7},{7,6},{8,9},{9,8},{10,11... | collective-permute-start | bytes 393224 | tf_op jit(solution)/shard_map/ppermute | solution.py:410
  166.7 1.9 copy-start.5
  168.5 13.3 %copy-start.1 = (f32[2,8,96,2,128]{4,3,2,1,0:T(2,128)S(1)}, f32[2,8,96,2,128]{4,3,2,1,0:T(2,128)}, u32[]{:S(2)}) copy-start(f32[2,8,96,2,128]{4,3,2,1,0:T(2,128)} %param.7) | copy-start | bytes 4718596
  168.6 13.3 %copy-start.3 = (f32[8,96,512]{2,1,0:T(8,128)S(1)}, f32[8,96,512]{2,1,0:T(8,128)}, u32[]{:S(2)}) copy-start(f32[8,96,512]{2,1,0:T(8,128)} %copy-done.2) | copy-start | bytes 4718596
  168.6 13.3 %copy-start.7 = (bf16[8,512]{1,0:T(8,128)(2,1)S(1)}, bf16[8,512]{1,0:T(8,128)(2,1)}, u32[]{:S(2)}) copy-start(bf16[8,512]{1,0:T(8,128)(2,1)} %copy-done.6) | copy-start | bytes 24580
  171.2 10.6 %collective-permute-start.10 = (bf16[8,512]{1,0:T(8,128)(2,1)S(1)}, bf16[8,512]{1,0:T(8,128)(2,1)S(1)}, u32[]{:S(2)}, u32[]{:S(2)}) collective-permute-start(bf16[8,512]{1,0:T(8,128)(2,1)S(1)} %get-tuple-element.83), channel_id=1, source_target_pairs={{16,0},{32,16},{48,32},{64,48},{80,64},{96,80},{112,96},{17,1},{33... | collective-permute-start | bytes 24584 | tf_op jit(solution)/shard_map/ppermute | solution.py:369
  174.2 2.6 %collective-permute-start.11 = (bf16[8,256]{1,0:T(8,128)(2,1)S(1)}, bf16[8,256]{1,0:T(8,128)(2,1)S(1)}, u32[]{:S(2)}, u32[]{:S(2)}) collective-permute-start(bf16[8,256]{1,0:T(8,128)(2,1)S(1)} %get-tuple-element.89), channel_id=1, source_target_pairs={{0,1},{1,0},{2,3},{3,2},{4,5},{5,4},{6,7},{7,6},{8,9},{9,8},{10,11... | collective-permute-start | bytes 12296 | tf_op jit(solution)/shard_map/ppermute | solution.py:417
  174.5 7.3 %collective-permute-start.12 = (bf16[8,256]{1,0:T(8,128)(2,1)S(1)}, bf16[8,256]{1,0:T(8,128)(2,1)S(1)}, u32[]{:S(2)}, u32[]{:S(2)}) collective-permute-start(bf16[8,256]{1,0:T(8,128)(2,1)S(1)} %get-tuple-element.88), channel_id=1, source_target_pairs={{1,2},{3,4},{5,6},{7,8},{9,10},{11,12},{13,14},{2,1},{4,3},{6,5},{... | collective-permute-start | bytes 12296 | tf_op jit(solution)/shard_map/ppermute | solution.py:415
Sparse Core Ops, SparseCore 0:
  10.6 33.4 all-gather.4
  51.4 71.5 all-gather.6

commit v6 on v5

--- a/solution.py
+++ b/solution.py
@@ -230,7 +230,9 @@
     )(core, mine, h, x, half, base, old)
 
 
-def fronts_kernel(core_ref, x_ref, h_ref, behind_ref, y_ref, inner_ref, outer_ref, last_ref, x_buf, h_buf, x_sem, h_sem):
+def fronts_kernel(
+    core_ref, x_ref, h_ref, behind_ref, y_out, inner_out, outer_out, last_ref, y_ref, inner_ref, outer_ref, x_buf, h_buf, x_sem, h_sem, out_sem
+):
     def loads(i):
         core, chip = lax.rem(lax.div(i, 2), 2), lax.div(i, 4) * 2 + lax.rem(i, 2)
         return (
@@ -253,6 +255,12 @@
         total = dot_t(x_buf[2 * j], h_buf[2 * j]) + dot_t(x_buf[2 * j + 1], h_buf[2 * j + 1])
         y_ref[...] += total.reshape(R, LZ, K)
 
+    stores = [
+        pltpu.make_async_copy(y_ref, y_out, out_sem.at[0]),
+        pltpu.make_async_copy(inner_ref, inner_out, out_sem.at[1]),
+        pltpu.make_async_copy(outer_ref, outer_out, out_sem.at[2]),
+    ]
+    stores[0].start()
     odd = core_ref[0] > 0
     for r in range(R):
         for a in range(2):
@@ -260,7 +268,11 @@
             high = y_ref[r, :, a * 256 + NY : a * 256 + 256].astype(bf16)
             inner_ref[r, a] = jnp.where(odd, low, high)
             outer_ref[r, a] = jnp.where(odd, high, low)
+    for store in stores[1:]:
+        store.start()
     last_ref[...] = jnp.concatenate([y_ref[r, LZ - 1 : LZ, :] for r in range(R)], axis=0).astype(bf16)
+    for store in stores:
+        store.wait()
 
 
 def fronts_of(core, x, h, behind):
@@ -269,14 +281,18 @@
         fronts_kernel,
         out_shape=(jax.ShapeDtypeStruct((R, LZ, K), f32), halo, halo, jax.ShapeDtypeStruct((R, K), bf16)),
         in_specs=[whole(pltpu.SMEM), whole(pltpu.HBM), whole(pltpu.HBM), whole(pl.ANY)],
-        out_specs=(whole(),) * 4,
+        out_specs=(whole(pltpu.HBM),) * 3 + (whole(),),
         scratch_shapes=[
+            VMEM((R, LZ, K), f32),
+            VMEM((R, 2, LZ, NY), bf16),
+            VMEM((R, 2, LZ, NY), bf16),
             VMEM((D, R * LZ, K), bf16),
             VMEM((D, K, K), bf16),
             pltpu.SemaphoreType.DMA((D,)),
             pltpu.SemaphoreType.DMA((D,)),
+            pltpu.SemaphoreType.DMA((3,)),
         ],
-        compiler_params=params(50),
+        compiler_params=params(52),
         cost_estimate=pl.CostEstimate(flops=6 * 10**9, bytes_accessed=23 * 10**6, transcendentals=0),
     )(core, x, h, behind)
 
@@ -402,11 +418,11 @@
             y, inner, outer, last = fronts_of(core, gathered, h, v)
             got, inner, outer, last = lax.optimization_barrier((got, inner, outer, last))
         if step == 7:
-            inner, outer, last, v = lax.optimization_barrier((inner, outer, last, v))
+            last, v = lax.optimization_barrier((last, v))
+            last = shift(last, "layer", 1)
+            got, inner, outer, last = lax.optimization_barrier((got, inner, outer, last))
             outer = lax.ppermute(outer, "plane", next_chip)
             inner = lax.ppermute(inner, "plane", twin)
-            last = shift(last, "layer", 1)
-            got, inner, outer, last = lax.optimization_barrier((got, inner, outer, last))
         other = lax.ppermute(got, "plane", twin)
         half = own_half(core, h, keep, got)
         mine = (group == step).astype(jnp.int32).reshape(1)

time: 194 us -> 193 us (level)
  waiting for transfers between devices: 13 us -> 10.1 us
    ppermute x1, waiting for transfers between devices: 5.05 us -> 2.48 us  [shards(): v_outer = lax.ppermute(ends[0][0], 'plane', next_chip)]
    ppermute x1, starting transfers between devices: 2.25 us -> 4.82 us  [shards(): v_outer = lax.ppermute(ends[0][0], 'plane', next_chip)]
    unnamed x28 -> x30, local copies, waits for them, and re-layouts: 5.2 us -> 5.56 us
  transfers between devices with their start and end apart: 19 -> 19, of which waited for: 4 -> 3; matrix products, arithmetic and copies ran while one was open for 0% -> 0% of each run, Pallas kernels for 27% -> 28%
where the time goes in v6:
time: 193 us; the launch traced here: 192 us
  Pallas kernels  62.3 us (32%)
  starting transfers between devices  52.8 us (27%)
  blocking collectives  46.6 us (24%)
  between operations  14.5 us (8%)
  waiting for transfers between devices  10.1 us (5%)
  local copies, waits for them, and re-layouts  5.56 us (3%)
    all_to_all x4, blocking collectives, shards(): lax.all_to_all(out, ('layer', 'plane'), 0, 0, axis_index_groups=pair_grou...  46.6 us
    all_to_all x3, starting transfers between devices, shards(): lax.all_to_all(out, ('layer', 'plane'), 0, 0, axis_index_groups=pair_grou...  22 us
    pallas_call x7, Pallas kernels, other_half(): pl.pallas_call(final_kernel if final else other_kernel, out_shape=out, in...  19.9 us
    pallas_call x7, Pallas kernels, own_half(): pl.pallas_call(own_kernel, out_shape=jax.ShapeDtypeStruct((R, K), f32), i...  13 us
    pallas_call x1, Pallas kernels, fronts_of(): pl.pallas_call(fronts_kernel, out_shape=(jax.ShapeDtypeStruct((R, LZ, K),...  11.2 us
    all_to_all x1, starting transfers between devices, shards(): heads = lax.all_to_all(chunk, 'plane', 0, 0)  8.62 us
    pallas_call x1, Pallas kernels, arrange(): pl.pallas_call(arrange_kernel, out_shape=jax.ShapeDtypeStruct((2, C, K, K...  7.09 us
    ppermute x7, starting transfers between devices, shards(): other = lax.ppermute(got, 'plane', twin)  6.51 us
  transfers between devices with their start and end apart: 19, of which 3 were waited for; matrix products, arithmetic and copies ran while one was open for 0% of the time, Pallas kernels for 28%

profile of v6, /device:TPU:7, one launch (start us, length us, event | category | flops | bytes accessed | tf_op | source)
XLA Modules:
  0.0 192.0 jit_solution(4972487796424453544)
XLA Ops:
  7.2 0.0 all-gather.5.cloned.1.call-start
  7.2 0.0 copy-start
  7.2 1.4 copy-done
  8.6 0.7 copy-done.7
  9.3 1.1 shard_map.86
  10.4 0.0 all-gather.5.cloned.1.call-update
  10.4 8.6 %all-to-all-start = ((bf16[16,16,512]{2,1,0:T(8,128)(2,1)}), bf16[16,16,512]{2,1,0:T(8,128)(2,1)S(1)}, u32[]{:S(2)}, u32[]{:S(2)}) async-start(bf16[16,16,512]{2,1,0:T(8,128)(2,1)} %get-tuple-element.44), calls=%async_computation | async-start | bytes 524288 | tf_op jit(solution)/shard_map/all_to_all | solution.py:395
  19.1 0.0 all-gather.7.cloned.1.call-start
  19.1 7.1 %shard_map.87.h_ref = bf16[2,8,512,512]{3,2,1,0:T(8,128)(2,1)} custom-call(bf16[512,2,32,128]{3,2,1,0:T(8,128)(2,1)} %bitcast.30), custom_call_target="tpu_custom_call" | custom-call | flops 4000000000 | bytes 17000000 | tf_op jit(solution)/shard_map/pallas_call | solution.py:106
  26.2 4.9 %shard_map.88 = (f32[8,512]{1,0:T(8,128)S(1)}, bf16[16,8,512]{2,1,0:T(8,128)(2,1)S(1)}, bf16[4,512,512]{2,1,0:T(8,128)(2,1)S(1)}) custom-call(s32[1]{0:T(128)} %bitcast.core_ref, bf16[2,8,512,512]{3,2,1,0:T(8,128)(2,1)} %shard_map.87.h_ref, bf16[16,16,512]{2,1,0:T(8,128)(2,1)S(1)} %all-to-all-done.x_ref), custom_call_target="tpu_custom_call" | custom-call | flops 100000000 | bytes 5000000 | tf_op jit(solution)/shard_map/pallas_call | solution.py:157
  31.1 13.7 %all_to_all.40.x_ref = bf16[16,8,512]{2,1,0:T(8,128)(2,1)S(1)} all-to-all(bf16[16,8,512]{2,1,0:T(8,128)(2,1)S(1)} %get-tuple-element.47), channel_id=1, replica_groups={{0,2,4,6,8,10,12,14,16,18,20,22,24,26,28,30},{1,3,5,7,9,11,13,15,17,19,..., dimensions={0} | all-to-all | bytes 262144 | tf_op jit(solution)/shard_map/all_to_all | solution.py:413
  44.8 1.5 collective-permute-start
  46.3 1.8 shard_map.89.half_ref
  48.1 3.1 %shard_map.90 = (f32[8,512]{1,0:T(8,128)S(1)}, bf16[16,8,512]{2,1,0:T(8,128)(2,1)}) custom-call(s32[1]{0:T(128)} %bitcast.core_ref, s32[1]{0:T(128)} %bitcast.3.mine_ref, bf16[2,8,512,512]{3,2,1,0:T(8,128)(2,1)} %shard_map.87.h_ref, bf16[16,8,512]{2,1,0:T(8,128)(2,1)S(1)} %collective-permute-done.x_ref, f32[8,512]{1,0:T(8,128)S(1)} %shard_map.89.half_ref, ...), custom_call_target="tpu_custom_call" | custom-call | flops 100000000 | bytes 5000000 | tf_op jit(solution)/shard_map/pallas_call | solution.py:222
  51.3 0.0 copy-start.11
  51.3 0.0 copy-start.12
  51.3 0.0 copy-start.13
  51.3 0.0 all-gather.5.cloned.1.call-done
  51.3 0.0 all-gather.7.cloned.1.call-update
  51.4 0.6 copy-done.11
  52.0 0.1 copy.11
  52.1 7.9 %all-to-all-start.2 = ((bf16[16,8,512]{2,1,0:T(8,128)(2,1)}), bf16[16,8,512]{2,1,0:T(8,128)(2,1)S(1)}, u32[]{:S(2)}, u32[]{:S(2)}) async-start(bf16[16,8,512]{2,1,0:T(8,128)(2,1)} %get-tuple-element.52), calls=%async_computation.2 | async-start | bytes 262144 | tf_op jit(solution)/shard_map/all_to_all | solution.py:413
  60.0 0.2 fusion.5.coef_ref
  60.2 1.3 shard_map.91.wave_ref
  61.6 4.1 %all-to-all-done.2.x_ref = bf16[16,8,512]{2,1,0:T(8,128)(2,1)S(1)} async-done(((bf16[16,8,512]{2,1,0:T(8,128)(2,1)}), bf16[16,8,512]{2,1,0:T(8,128)(2,1)S(1)}, u32[]{:S(2)}, u32[]{:S(2)}) %all-to-all-start.2) | async-done | bytes 131104 | tf_op jit(solution)/shard_map/all_to_all | solution.py:413
  65.6 1.1 collective-permute-start.1
  66.8 1.8 shard_map.92.half_ref
  68.6 2.5 %shard_map.93 = (f32[8,512]{1,0:T(8,128)S(1)}, bf16[16,8,512]{2,1,0:T(8,128)(2,1)S(1)}) custom-call(s32[1]{0:T(128)} %bitcast.core_ref, s32[1]{0:T(128)} %bitcast.8.mine_ref, bf16[2,8,512,512]{3,2,1,0:T(8,128)(2,1)} %shard_map.87.h_ref, bf16[16,8,512]{2,1,0:T(8,128)(2,1)S(1)} %collective-permute-done.1.x_ref, f32[8,512]{1,0:T(8,128)S(1)} %shard_map.92.half_ref, ...), custom_call_target="tpu_custom_call" | custom-call | flops 100000000 | bytes 5000000 | tf_op jit(solution)/shard_map/pallas_call | solution.py:222
  71.1 10.2 %all_to_all.41.x_ref = bf16[16,8,512]{2,1,0:T(8,128)(2,1)S(1)} all-to-all(bf16[16,8,512]{2,1,0:T(8,128)(2,1)S(1)} %get-tuple-element.54), channel_id=1, replica_groups={{32,34,36,38,40,42,44,46,48,50,52,54,56,58,60,62},{33,35,37,39,41,43,45..., dimensions={0} | all-to-all | bytes 262144 | tf_op jit(solution)/shard_map/all_to_all | solution.py:413
  81.3 1.2 collective-permute-start.2
  82.6 1.8 shard_map.94.half_ref
  84.4 2.7 %shard_map.95 = (f32[8,512]{1,0:T(8,128)S(1)}, bf16[16,8,512]{2,1,0:T(8,128)(2,1)S(1)}) custom-call(s32[1]{0:T(128)} %bitcast.core_ref, s32[1]{0:T(128)} %bitcast.7.mine_ref, bf16[2,8,512,512]{3,2,1,0:T(8,128)(2,1)} %shard_map.87.h_ref, bf16[16,8,512]{2,1,0:T(8,128)(2,1)S(1)} %collective-permute-done.2.x_ref, f32[8,512]{1,0:T(8,128)S(1)} %shard_map.94.half_ref, ...), custom_call_target="tpu_custom_call" | custom-call | flops 100000000 | bytes 5000000 | tf_op jit(solution)/shard_map/pallas_call | solution.py:222
  87.1 12.3 %all_to_all.42.x_ref = bf16[16,8,512]{2,1,0:T(8,128)(2,1)S(1)} all-to-all(bf16[16,8,512]{2,1,0:T(8,128)(2,1)S(1)} %get-tuple-element.56), channel_id=1, replica_groups={{48,50,52,54,56,58,60,62,64,66,68,70,72,74,76,78},{49,51,53,55,57,59,61..., dimensions={0} | all-to-all | bytes 262144 | tf_op jit(solution)/shard_map/all_to_all | solution.py:413
  99.4 1.4 collective-permute-start.3
  100.8 1.8 shard_map.96.half_ref
  102.7 2.7 %shard_map.97 = (f32[8,512]{1,0:T(8,128)S(1)}, bf16[16,8,512]{2,1,0:T(8,128)(2,1)S(1)}) custom-call(s32[1]{0:T(128)} %bitcast.core_ref, s32[1]{0:T(128)} %bitcast.6.mine_ref, bf16[2,8,512,512]{3,2,1,0:T(8,128)(2,1)} %shard_map.87.h_ref, bf16[16,8,512]{2,1,0:T(8,128)(2,1)S(1)} %collective-permute-done.3.x_ref, f32[8,512]{1,0:T(8,128)S(1)} %shard_map.96.half_ref, ...), custom_call_target="tpu_custom_call" | custom-call | flops 100000000 | bytes 5000000 | tf_op jit(solution)/shard_map/pallas_call | solution.py:222
  105.4 10.4 %all_to_all.43.x_ref = bf16[16,8,512]{2,1,0:T(8,128)(2,1)S(1)} all-to-all(bf16[16,8,512]{2,1,0:T(8,128)(2,1)S(1)} %get-tuple-element.58), channel_id=1, replica_groups={{64,66,68,70,72,74,76,78,80,82,84,86,88,90,92,94},{65,67,69,71,73,75,77..., dimensions={0} | all-to-all | bytes 262144 | tf_op jit(solution)/shard_map/all_to_all | solution.py:413
  115.8 1.0 collective-permute-start.4
  116.7 2.0 %shard_map.98.half_ref = f32[8,512]{1,0:T(8,128)S(1)} custom-call(s32[1]{0:T(128)} %bitcast.core_ref, bf16[2,8,512,512]{3,2,1,0:T(8,128)(2,1)} %shard_map.87.h_ref, bf16[4,512,512]{2,1,0:T(8,128)(2,1)S(1)} %get-tuple-element.48.keep_ref, bf16[16,8,512]{2,1,0:T(8,128)(2,1)S(1)} %all_to_all.43.x_ref), custom_call_target="tpu_custom_call" | custom-call | flops 100000000 | bytes 5000000 | tf_op jit(solution)/shard_map/pallas_call | solution.py:180
  118.7 3.1 %shard_map.99 = (f32[8,512]{1,0:T(8,128)S(1)}, bf16[16,8,512]{2,1,0:T(8,128)(2,1)}) custom-call(s32[1]{0:T(128)} %bitcast.core_ref, s32[1]{0:T(128)} %bitcast.5.mine_ref, bf16[2,8,512,512]{3,2,1,0:T(8,128)(2,1)} %shard_map.87.h_ref, bf16[16,8,512]{2,1,0:T(8,128)(2,1)S(1)} %collective-permute-done.4.x_ref, f32[8,512]{1,0:T(8,128)S(1)} %shard_map.98.half_ref, ...), custom_call_target="tpu_custom_call" | custom-call | flops 100000000 | bytes 5000000 | tf_op jit(solution)/shard_map/pallas_call | solution.py:222
  121.9 7.4 %all-to-all-start.6 = ((bf16[16,8,512]{2,1,0:T(8,128)(2,1)}), bf16[16,8,512]{2,1,0:T(8,128)(2,1)S(1)}, u32[]{:S(2)}, u32[]{:S(2)}) async-start(bf16[16,8,512]{2,1,0:T(8,128)(2,1)} %get-tuple-element.62), calls=%async_computation.6 | async-start | bytes 262144 | tf_op jit(solution)/shard_map/all_to_all | solution.py:413
  129.3 0.0 all-gather.7.cloned.1.call-done.x_ref
  129.3 11.2 %shard_map.100 = (f32[8,96,512]{2,1,0:T(8,128)}, bf16[8,2,96,128]{3,2,1,0:T(8,128)(2,1)S(1)}, bf16[8,2,96,128]{3,2,1,0:T(8,128)(2,1)S(1)}, bf16[8,512]{1,0:T(8,128)(2,1)S(1)}) custom-call(s32[1]{0:T(128)} %bitcast.core_ref, bf16[16,768,512]{2,1,0:T(8,128)(2,1)} %all-gather.7.cloned.1.call-done.x_ref, bf16[2,8,512,512]{3,2,1,0:T(8,128)(2,1)} %shard_map.87.h_ref, ...), custom_call_target="tpu_custom_call" | custom-call | flops 6000000000 | bytes 23000000 | tf_op jit(solution)/shard_map/pallas_call | solution.py:280
  140.6 0.7 copy-done.8
  141.3 0.7 copy-done.9
  142.1 0.2 collective-permute-start.5
  142.3 1.8 shard_map.101.half_ref
  144.2 3.1 %shard_map.102 = (f32[8,512]{1,0:T(8,128)S(1)}, bf16[16,8,512]{2,1,0:T(8,128)(2,1)}) custom-call(s32[1]{0:T(128)} %bitcast.core_ref, s32[1]{0:T(128)} %bitcast.10.mine_ref, bf16[2,8,512,512]{3,2,1,0:T(8,128)(2,1)} %shard_map.87.h_ref, bf16[16,8,512]{2,1,0:T(8,128)(2,1)S(1)} %collective-permute-done.5.x_ref, f32[8,512]{1,0:T(8,128)S(1)} %shard_map.101.half_ref, ...), custom_call_target="tpu_custom_call" | custom-call | flops 100000000 | bytes 5000000 | tf_op jit(solution)/shard_map/pallas_call | solution.py:222
  147.3 0.6 copy-done.3
  147.9 6.7 %all-to-all-start.7 = ((bf16[16,8,512]{2,1,0:T(8,128)(2,1)}), bf16[16,8,512]{2,1,0:T(8,128)(2,1)S(1)}, u32[]{:S(2)}, u32[]{:S(2)}) async-start(bf16[16,8,512]{2,1,0:T(8,128)(2,1)} %get-tuple-element.67), calls=%async_computation.7 | async-start | bytes 262144 | tf_op jit(solution)/shard_map/all_to_all | solution.py:413
  154.6 3.1 %collective-permute-start.6 = (bf16[8,512]{1,0:T(8,128)(2,1)S(1)}, bf16[8,512]{1,0:T(8,128)(2,1)S(1)}, u32[]{:S(2)}, u32[]{:S(2)}) collective-permute-start(bf16[8,512]{1,0:T(8,128)(2,1)S(1)} %get-tuple-element.72), channel_id=1, source_target_pairs={{0,16},{16,32},{32,48},{48,64},{64,80},{80,96},{96,112},{1,17},{17... | collective-permute-start | bytes 24584 | tf_op jit(solution)/shard_map/ppermute | solution.py:385
  157.7 3.4 %collective-permute-done.6.prev_ref = bf16[8,512]{1,0:T(8,128)(2,1)S(1)} collective-permute-done((bf16[8,512]{1,0:T(8,128)(2,1)S(1)}, bf16[8,512]{1,0:T(8,128)(2,1)S(1)}, u32[]{:S(2)}, u32[]{:S(2)}) %collective-permute-start.6) | collective-permute-done | bytes 8224 | tf_op jit(solution)/shard_map/ppermute | solution.py:385
  161.1 0.6 copy-done.5
  161.7 2.0 %collective-permute-start.7 = (bf16[8,2,96,128]{3,2,1,0:T(8,128)(2,1)}, bf16[8,2,96,128]{3,2,1,0:T(8,128)(2,1)S(1)}, u32[]{:S(2)}, u32[]{:S(2)}) collective-permute-start(bf16[8,2,96,128]{3,2,1,0:T(8,128)(2,1)} %copy-done.9), channel_id=1, source_target_pairs={{0,1},{1,0},{2,3},{3,2},{4,5},{5,4},{6,7},{7,6},{8,9},{9,8},{10,11... | collective-permute-start | bytes 1179656 | tf_op jit(solution)/shard_map/ppermute | solution.py:425
  163.7 3.0 %collective-permute-start.8 = (bf16[8,2,96,128]{3,2,1,0:T(8,128)(2,1)}, bf16[8,2,96,128]{3,2,1,0:T(8,128)(2,1)}, u32[]{:S(2)}, u32[]{:S(2)}) collective-permute-start(bf16[8,2,96,128]{3,2,1,0:T(8,128)(2,1)} %copy-done.8), channel_id=1, source_target_pairs={{1,2},{3,4},{5,6},{7,8},{9,10},{11,12},{13,14},{2,1},{4,3},{6,5},{... | collective-permute-start | bytes 1179656 | tf_op jit(solution)/shard_map/ppermute | solution.py:424
  166.7 0.1 collective-permute-start.9
  166.8 1.8 shard_map.103.half_ref
  168.6 0.0 copy-start.2
  168.7 2.6 %shard_map.104 = (f32[8,512]{1,0:T(8,128)S(1)}, bf16[8,512]{1,0:T(8,128)(2,1)S(1)}, bf16[2,8,256]{2,1,0:T(8,128)(2,1)S(1)}) custom-call(s32[1]{0:T(128)} %bitcast.core_ref, s32[1]{0:T(128)} %bitcast.11.mine_ref, bf16[2,8,512,512]{3,2,1,0:T(8,128)(2,1)} %shard_map.87.h_ref, bf16[16,8,512]{2,1,0:T(8,128)(2,1)S(1)} %collective-permute-done.9.x_ref, ...), custom_call_target="tpu_custom_call" | custom-call | flops 100000000 | bytes 5000000 | tf_op jit(solution)/shard_map/pallas_call | solution.py:222
  171.3 2.3 %collective-permute-start.10 = (bf16[8,512]{1,0:T(8,128)(2,1)S(1)}, bf16[8,512]{1,0:T(8,128)(2,1)S(1)}, u32[]{:S(2)}, u32[]{:S(2)}) collective-permute-start(bf16[8,512]{1,0:T(8,128)(2,1)S(1)} %get-tuple-element.79), channel_id=1, source_target_pairs={{16,0},{32,16},{48,32},{64,48},{80,64},{96,80},{112,96},{17,1},{33... | collective-permute-start | bytes 24584 | tf_op jit(solution)/shard_map/ppermute | solution.py:385
  173.6 0.4 collective-permute-start.11
  174.0 4.8 %collective-permute-start.12 = (bf16[8,256]{1,0:T(8,128)(2,1)S(1)}, bf16[8,256]{1,0:T(8,128)(2,1)S(1)}, u32[]{:S(2)}, u32[]{:S(2)}) collective-permute-start(bf16[8,256]{1,0:T(8,128)(2,1)S(1)} %get-tuple-element.84), channel_id=1, source_target_pairs={{1,2},{3,4},{5,6},{7,8},{9,10},{11,12},{13,14},{2,1},{4,3},{6,5},{... | collective-permute-start | bytes 12296 | tf_op jit(solution)/shard_map/ppermute | solution.py:431
  178.9 2.5 %collective-permute-done.12.vo_ref = bf16[8,256]{1,0:T(8,128)(2,1)S(1)} collective-permute-done((bf16[8,256]{1,0:T(8,128)(2,1)S(1)}, bf16[8,256]{1,0:T(8,128)(2,1)S(1)}, u32[]{:S(2)}, u32[]{:S(2)}) %collective-permute-start.12) | collective-permute-done | bytes 4128 | tf_op jit(solution)/shard_map/ppermute | solution.py:431
  181.4 3.8 %shard_map.105 = (f32[2,8,192,128]{3,2,1,0:T(8,128)}, f32[2,8,192,128]{3,2,1,0:T(8,128)}) custom-call(s32[1]{0:T(128)} %bitcast.core_ref, f32[8,96,512]{2,1,0:T(8,128)S(1)} %copy-done.2, f32[2,8,192,128]{3,2,1,0:T(8,128)S(1)} %bitcast.28, bf16[8,2,96,128]{3,2,1,0:T(8,128)(2,1)S(1)} %collective-permute-done.7.inner_ref, ...), custom_call_target="tpu_custom_call" | custom-call | tf_op jit(solution)/shard_map/pallas_call | solution.py:364
  (33 shorter events, 0.1 us)
Async XLA Ops:
  7.2 44.2 %all-gather.5.cloned.1.call-start = ((), (), s32[]{:S(2)}) async-start(), calls=%async_computation.8 | async-start | bytes 2359296 | tf_op jit(solution)/shard_map/all_gather | solution.py:394
  7.2 1.4 copy-start
  8.6 0.7 copy-start.7
  10.4 15.8 %all-to-all-start = ((bf16[16,16,512]{2,1,0:T(8,128)(2,1)}), bf16[16,16,512]{2,1,0:T(8,128)(2,1)S(1)}, u32[]{:S(2)}, u32[]{:S(2)}) async-start(bf16[16,16,512]{2,1,0:T(8,128)(2,1)} %get-tuple-element.44), calls=%async_computation | async-start | bytes 524288 | tf_op jit(solution)/shard_map/all_to_all | solution.py:395
  19.1 110.2 %all-gather.7.cloned.1.call-start = ((), (), s32[]{:S(2)}) async-start(), calls=%async_computation.9 | async-start | bytes 14155776 | tf_op jit(solution)/shard_map/all_gather | solution.py:412
  44.8 3.3 %collective-permute-start = (bf16[16,8,512]{2,1,0:T(8,128)(2,1)S(1)}, bf16[16,8,512]{2,1,0:T(8,128)(2,1)S(1)}, u32[]{:S(2)}, u32[]{:S(2)}) collective-permute-start(bf16[16,8,512]{2,1,0:T(8,128)(2,1)S(1)} %all_to_all.40.x_ref), channel_id=1, source_target_pairs={{0,1},{1,0},{2,3},{3,2},{4,5},{5,4},{6,7},{7,6},{8,9},{9,8},{10,11... | collective-permute-start | bytes 393224 | tf_op jit(solution)/shard_map/ppermute | solution.py:426
  51.3 0.7 copy-start.11
  51.3 8.7 %copy-start.12 = (s32[256]{0:T(256)S(1)}, s32[256]{0:T(256)}, u32[]{:S(2)}) copy-start(s32[256]{0:T(256)} %param.11) | copy-start | bytes 3076
  51.3 8.7 %copy-start.13 = (s32[8]{0:T(128)S(1)}, s32[8]{0:T(128)}, u32[]{:S(2)}) copy-start(s32[8]{0:T(128)} %param.12) | copy-start | bytes 100
  51.3 8.9 %copy-start.10 = (bf16[256,2,128]{2,1,0:T(2,128)(2,1)S(1)}, bf16[256,2,128]{2,1,0:T(2,128)(2,1)}, u32[]{:S(2)}) copy-start(bf16[256,2,128]{2,1,0:T(2,128)(2,1)} %param.9) | copy-start | bytes 393220
  52.1 13.5 %all-to-all-start.2 = ((bf16[16,8,512]{2,1,0:T(8,128)(2,1)}), bf16[16,8,512]{2,1,0:T(8,128)(2,1)S(1)}, u32[]{:S(2)}, u32[]{:S(2)}) async-start(bf16[16,8,512]{2,1,0:T(8,128)(2,1)} %get-tuple-element.52), calls=%async_computation.2 | async-start | bytes 262144 | tf_op jit(solution)/shard_map/all_to_all | solution.py:413
  65.6 3.0 %collective-permute-start.1 = (bf16[16,8,512]{2,1,0:T(8,128)(2,1)S(1)}, bf16[16,8,512]{2,1,0:T(8,128)(2,1)S(1)}, u32[]{:S(2)}, u32[]{:S(2)}) collective-permute-start(bf16[16,8,512]{2,1,0:T(8,128)(2,1)S(1)} %all-to-all-done.2.x_ref), channel_id=1, source_target_pairs={{0,1},{1,0},{2,3},{3,2},{4,5},{5,4},{6,7},{7,6},{8,9},{9,8},{10,11... | collective-permute-start | bytes 393224 | tf_op jit(solution)/shard_map/ppermute | solution.py:426
  81.3 3.1 %collective-permute-start.2 = (bf16[16,8,512]{2,1,0:T(8,128)(2,1)S(1)}, bf16[16,8,512]{2,1,0:T(8,128)(2,1)S(1)}, u32[]{:S(2)}, u32[]{:S(2)}) collective-permute-start(bf16[16,8,512]{2,1,0:T(8,128)(2,1)S(1)} %all_to_all.41.x_ref), channel_id=1, source_target_pairs={{0,1},{1,0},{2,3},{3,2},{4,5},{5,4},{6,7},{7,6},{8,9},{9,8},{10,11... | collective-permute-start | bytes 393224 | tf_op jit(solution)/shard_map/ppermute | solution.py:426
  99.4 3.3 %collective-permute-start.3 = (bf16[16,8,512]{2,1,0:T(8,128)(2,1)S(1)}, bf16[16,8,512]{2,1,0:T(8,128)(2,1)S(1)}, u32[]{:S(2)}, u32[]{:S(2)}) collective-permute-start(bf16[16,8,512]{2,1,0:T(8,128)(2,1)S(1)} %all_to_all.42.x_ref), channel_id=1, source_target_pairs={{0,1},{1,0},{2,3},{3,2},{4,5},{5,4},{6,7},{7,6},{8,9},{9,8},{10,11... | collective-permute-start | bytes 393224 | tf_op jit(solution)/shard_map/ppermute | solution.py:426
  115.8 2.9 %collective-permute-start.4 = (bf16[16,8,512]{2,1,0:T(8,128)(2,1)S(1)}, bf16[16,8,512]{2,1,0:T(8,128)(2,1)S(1)}, u32[]{:S(2)}, u32[]{:S(2)}) collective-permute-start(bf16[16,8,512]{2,1,0:T(8,128)(2,1)S(1)} %all_to_all.43.x_ref), channel_id=1, source_target_pairs={{0,1},{1,0},{2,3},{3,2},{4,5},{5,4},{6,7},{7,6},{8,9},{9,8},{10,11... | collective-permute-start | bytes 393224 | tf_op jit(solution)/shard_map/ppermute | solution.py:426
  121.9 20.2 %all-to-all-start.6 = ((bf16[16,8,512]{2,1,0:T(8,128)(2,1)}), bf16[16,8,512]{2,1,0:T(8,128)(2,1)S(1)}, u32[]{:S(2)}, u32[]{:S(2)}) async-start(bf16[16,8,512]{2,1,0:T(8,128)(2,1)} %get-tuple-element.62), calls=%async_computation.6 | async-start | bytes 262144 | tf_op jit(solution)/shard_map/all_to_all | solution.py:413
  140.6 0.8 copy-start.8
  141.3 0.7 copy-start.9
  142.1 2.1 %collective-permute-start.5 = (bf16[16,8,512]{2,1,0:T(8,128)(2,1)S(1)}, bf16[16,8,512]{2,1,0:T(8,128)(2,1)S(1)}, u32[]{:S(2)}, u32[]{:S(2)}) collective-permute-start(bf16[16,8,512]{2,1,0:T(8,128)(2,1)S(1)} %all-to-all-done.6.x_ref), channel_id=1, source_target_pairs={{0,1},{1,0},{2,3},{3,2},{4,5},{5,4},{6,7},{7,6},{8,9},{9,8},{10,11... | collective-permute-start | bytes 393224 | tf_op jit(solution)/shard_map/ppermute | solution.py:426
  147.3 0.6 copy-start.3
  147.9 13.8 %all-to-all-start.7 = ((bf16[16,8,512]{2,1,0:T(8,128)(2,1)}), bf16[16,8,512]{2,1,0:T(8,128)(2,1)S(1)}, u32[]{:S(2)}, u32[]{:S(2)}) async-start(bf16[16,8,512]{2,1,0:T(8,128)(2,1)} %get-tuple-element.67), calls=%async_computation.7 | async-start | bytes 262144 | tf_op jit(solution)/shard_map/all_to_all | solution.py:413
  154.6 6.5 %collective-permute-start.6 = (bf16[8,512]{1,0:T(8,128)(2,1)S(1)}, bf16[8,512]{1,0:T(8,128)(2,1)S(1)}, u32[]{:S(2)}, u32[]{:S(2)}) collective-permute-start(bf16[8,512]{1,0:T(8,128)(2,1)S(1)} %get-tuple-element.72), channel_id=1, source_target_pairs={{0,16},{16,32},{32,48},{48,64},{64,80},{80,96},{96,112},{1,17},{17... | collective-permute-start | bytes 24584 | tf_op jit(solution)/shard_map/ppermute | solution.py:385
  161.1 0.6 copy-start.5
  161.7 19.7 %collective-permute-start.7 = (bf16[8,2,96,128]{3,2,1,0:T(8,128)(2,1)}, bf16[8,2,96,128]{3,2,1,0:T(8,128)(2,1)S(1)}, u32[]{:S(2)}, u32[]{:S(2)}) collective-permute-start(bf16[8,2,96,128]{3,2,1,0:T(8,128)(2,1)} %copy-done.9), channel_id=1, source_target_pairs={{0,1},{1,0},{2,3},{3,2},{4,5},{5,4},{6,7},{7,6},{8,9},{9,8},{10,11... | collective-permute-start | bytes 1179656 | tf_op jit(solution)/shard_map/ppermute | solution.py:425
  163.7 17.7 %collective-permute-start.8 = (bf16[8,2,96,128]{3,2,1,0:T(8,128)(2,1)}, bf16[8,2,96,128]{3,2,1,0:T(8,128)(2,1)}, u32[]{:S(2)}, u32[]{:S(2)}) collective-permute-start(bf16[8,2,96,128]{3,2,1,0:T(8,128)(2,1)} %copy-done.8), channel_id=1, source_target_pairs={{1,2},{3,4},{5,6},{7,8},{9,10},{11,12},{13,14},{2,1},{4,3},{6,5},{... | collective-permute-start | bytes 1179656 | tf_op jit(solution)/shard_map/ppermute | solution.py:424
  166.7 2.0 %collective-permute-start.9 = (bf16[16,8,512]{2,1,0:T(8,128)(2,1)S(1)}, bf16[16,8,512]{2,1,0:T(8,128)(2,1)S(1)}, u32[]{:S(2)}, u32[]{:S(2)}) collective-permute-start(bf16[16,8,512]{2,1,0:T(8,128)(2,1)S(1)} %all-to-all-done.7.x_ref), channel_id=1, source_target_pairs={{0,1},{1,0},{2,3},{3,2},{4,5},{5,4},{6,7},{7,6},{8,9},{9,8},{10,11... | collective-permute-start | bytes 393224 | tf_op jit(solution)/shard_map/ppermute | solution.py:426
  166.8 1.9 copy-start.4
  168.6 12.7 %copy-start.1 = (f32[2,8,96,2,128]{4,3,2,1,0:T(2,128)S(1)}, f32[2,8,96,2,128]{4,3,2,1,0:T(2,128)}, u32[]{:S(2)}) copy-start(f32[2,8,96,2,128]{4,3,2,1,0:T(2,128)} %param.7) | copy-start | bytes 4718596
  168.6 12.7 %copy-start.2 = (f32[8,96,512]{2,1,0:T(8,128)S(1)}, f32[8,96,512]{2,1,0:T(8,128)}, u32[]{:S(2)}) copy-start(f32[8,96,512]{2,1,0:T(8,128)} %get-tuple-element.61.y_ref) | copy-start | bytes 4718596
  168.7 12.7 %copy-start.6 = (bf16[8,512]{1,0:T(8,128)(2,1)S(1)}, bf16[8,512]{1,0:T(8,128)(2,1)}, u32[]{:S(2)}) copy-start(bf16[8,512]{1,0:T(8,128)(2,1)} %copy-done.5) | copy-start | bytes 24580
  171.3 10.0 %collective-permute-start.10 = (bf16[8,512]{1,0:T(8,128)(2,1)S(1)}, bf16[8,512]{1,0:T(8,128)(2,1)S(1)}, u32[]{:S(2)}, u32[]{:S(2)}) collective-permute-start(bf16[8,512]{1,0:T(8,128)(2,1)S(1)} %get-tuple-element.79), channel_id=1, source_target_pairs={{16,0},{32,16},{48,32},{64,48},{80,64},{96,80},{112,96},{17,1},{33... | collective-permute-start | bytes 24584 | tf_op jit(solution)/shard_map/ppermute | solution.py:385
  173.6 5.2 %collective-permute-start.11 = (bf16[8,256]{1,0:T(8,128)(2,1)S(1)}, bf16[8,256]{1,0:T(8,128)(2,1)S(1)}, u32[]{:S(2)}, u32[]{:S(2)}) collective-permute-start(bf16[8,256]{1,0:T(8,128)(2,1)S(1)} %get-tuple-element.85), channel_id=1, source_target_pairs={{0,1},{1,0},{2,3},{3,2},{4,5},{5,4},{6,7},{7,6},{8,9},{9,8},{10,11... | collective-permute-start | bytes 12296 | tf_op jit(solution)/shard_map/ppermute | solution.py:433
  174.0 7.3 %collective-permute-start.12 = (bf16[8,256]{1,0:T(8,128)(2,1)S(1)}, bf16[8,256]{1,0:T(8,128)(2,1)S(1)}, u32[]{:S(2)}, u32[]{:S(2)}) collective-permute-start(bf16[8,256]{1,0:T(8,128)(2,1)S(1)} %get-tuple-element.84), channel_id=1, source_target_pairs={{1,2},{3,4},{5,6},{7,8},{9,10},{11,12},{13,14},{2,1},{4,3},{6,5},{... | collective-permute-start | bytes 12296 | tf_op jit(solution)/shard_map/ppermute | solution.py:431
Sparse Core Ops, SparseCore 0:
  10.6 33.4 all-gather.4
  51.5 71.5 all-gather.6

commit v7 on v5

--- a/solution.py
+++ b/solution.py
@@ -18,7 +18,7 @@
 R = 8
 K = 512
 NY = 128
-KEEP = 4
+KEEP = 3
 
 bf16 = jnp.bfloat16
 f32 = jnp.float32
@@ -402,11 +402,11 @@
             y, inner, outer, last = fronts_of(core, gathered, h, v)
             got, inner, outer, last = lax.optimization_barrier((got, inner, outer, last))
         if step == 7:
-            inner, outer, last, v = lax.optimization_barrier((inner, outer, last, v))
+            last, v = lax.optimization_barrier((last, v))
+            last = shift(last, "layer", 1)
+            got, inner, outer, last = lax.optimization_barrier((got, inner, outer, last))
             outer = lax.ppermute(outer, "plane", next_chip)
             inner = lax.ppermute(inner, "plane", twin)
-            last = shift(last, "layer", 1)
-            got, inner, outer, last = lax.optimization_barrier((got, inner, outer, last))
         other = lax.ppermute(got, "plane", twin)
         half = own_half(core, h, keep, got)
         mine = (group == step).astype(jnp.int32).reshape(1)

time: 194 us -> 193 us (level)
  starting transfers between devices: 51 us -> 53.5 us
  waiting for transfers between devices: 13 us -> 10.7 us
    ppermute x1, waiting for transfers between devices: 5.05 us -> 3.08 us  [shards(): v_outer = lax.ppermute(ends[0][0], 'plane', next_chip)]
    ppermute x1, starting transfers between devices: 2.25 us -> 4.22 us  [shards(): v_outer = lax.ppermute(ends[0][0], 'plane', next_chip)]
    unnamed x28 -> x22, local copies, waits for them, and re-layouts: 5.2 us -> 4.74 us
  transfers between devices with their start and end apart: 19 -> 19, of which waited for: 4 -> 3; matrix products, arithmetic and copies ran while one was open for 0% -> 0% of each run, Pallas kernels for 27% -> 28%
where the time goes in v7:
time: 193 us; the launch traced here: 192 us
  Pallas kernels  61.7 us (32%)
  starting transfers between devices  53.5 us (28%)
  blocking collectives  46.6 us (24%)
  between operations  14.5 us (8%)
  waiting for transfers between devices  10.7 us (6%)
  local copies, waits for them, and re-layouts  4.74 us (2%)
    all_to_all x4, blocking collectives, shards(): lax.all_to_all(out, ('layer', 'plane'), 0, 0, axis_index_groups=pair_grou...  46.6 us
    all_to_all x3, starting transfers between devices, shards(): lax.all_to_all(out, ('layer', 'plane'), 0, 0, axis_index_groups=pair_grou...  22.5 us
    pallas_call x7, Pallas kernels, other_half(): pl.pallas_call(final_kernel if final else other_kernel, out_shape=out, in...  19.7 us
    pallas_call x7, Pallas kernels, own_half(): pl.pallas_call(own_kernel, out_shape=jax.ShapeDtypeStruct((R, K), f32), i...  14 us
    pallas_call x1, Pallas kernels, fronts_of(): pl.pallas_call(fronts_kernel, out_shape=(jax.ShapeDtypeStruct((R, LZ, K),...  10.9 us
    all_to_all x1, starting transfers between devices, shards(): heads = lax.all_to_all(chunk, 'plane', 0, 0)  8.62 us
    pallas_call x1, Pallas kernels, arrange(): pl.pallas_call(arrange_kernel, out_shape=jax.ShapeDtypeStruct((2, C, K, K...  7.12 us
    ppermute x7, starting transfers between devices, shards(): other = lax.ppermute(got, 'plane', twin)  7 us
  transfers between devices with their start and end apart: 19, of which 3 were waited for; matrix products, arithmetic and copies ran while one was open for 0% of the time, Pallas kernels for 28%

profile of v7, /device:TPU:7, one launch (start us, length us, event | category | flops | bytes accessed | tf_op | source)
XLA Modules:
  0.0 191.9 jit_solution(1186867717709061039)
XLA Ops:
  7.2 0.0 all-gather.5.cloned.1.call-start
  7.2 0.0 copy-start
  7.2 1.4 copy-done
  8.6 0.7 copy-done.4
  9.3 1.1 shard_map.86
  10.4 0.0 all-gather.5.cloned.1.call-update
  10.4 8.6 %all-to-all-start = ((bf16[16,16,512]{2,1,0:T(8,128)(2,1)}), bf16[16,16,512]{2,1,0:T(8,128)(2,1)S(1)}, u32[]{:S(2)}, u32[]{:S(2)}) async-start(bf16[16,16,512]{2,1,0:T(8,128)(2,1)} %get-tuple-element.44), calls=%async_computation | async-start | bytes 524288 | tf_op jit(solution)/shard_map/all_to_all | solution.py:379
  19.1 0.0 all-gather.7.cloned.1.call-start
  19.1 7.1 %shard_map.87.h_ref = bf16[2,8,512,512]{3,2,1,0:T(8,128)(2,1)} custom-call(bf16[512,2,32,128]{3,2,1,0:T(8,128)(2,1)} %bitcast.30), custom_call_target="tpu_custom_call" | custom-call | flops 4000000000 | bytes 17000000 | tf_op jit(solution)/shard_map/pallas_call | solution.py:106
  26.2 4.8 %shard_map.88 = (f32[8,512]{1,0:T(8,128)S(1)}, bf16[16,8,512]{2,1,0:T(8,128)(2,1)S(1)}, bf16[3,512,512]{2,1,0:T(8,128)(2,1)S(1)}) custom-call(s32[1]{0:T(128)} %bitcast.core_ref, bf16[2,8,512,512]{3,2,1,0:T(8,128)(2,1)} %shard_map.87.h_ref, bf16[16,16,512]{2,1,0:T(8,128)(2,1)S(1)} %all-to-all-done.x_ref), custom_call_target="tpu_custom_call" | custom-call | flops 100000000 | bytes 5000000 | tf_op jit(solution)/shard_map/pallas_call | solution.py:157
  31.1 13.7 %all_to_all.40.x_ref = bf16[16,8,512]{2,1,0:T(8,128)(2,1)S(1)} all-to-all(bf16[16,8,512]{2,1,0:T(8,128)(2,1)S(1)} %get-tuple-element.47), channel_id=1, replica_groups={{0,2,4,6,8,10,12,14,16,18,20,22,24,26,28,30},{1,3,5,7,9,11,13,15,17,19,..., dimensions={0} | all-to-all | bytes 262144 | tf_op jit(solution)/shard_map/all_to_all | solution.py:397
  44.8 1.5 collective-permute-start
  46.3 2.0 %shard_map.89.half_ref = f32[8,512]{1,0:T(8,128)S(1)} custom-call(s32[1]{0:T(128)} %bitcast.core_ref, bf16[2,8,512,512]{3,2,1,0:T(8,128)(2,1)} %shard_map.87.h_ref, bf16[3,512,512]{2,1,0:T(8,128)(2,1)S(1)} %get-tuple-element.48.keep_ref, bf16[16,8,512]{2,1,0:T(8,128)(2,1)S(1)} %all_to_all.40.x_ref), custom_call_target="tpu_custom_call" | custom-call | flops 100000000 | bytes 5000000 | tf_op jit(solution)/shard_map/pallas_call | solution.py:180
  48.3 3.1 %shard_map.90 = (f32[8,512]{1,0:T(8,128)S(1)}, bf16[16,8,512]{2,1,0:T(8,128)(2,1)}) custom-call(s32[1]{0:T(128)} %bitcast.core_ref, s32[1]{0:T(128)} %bitcast.3.mine_ref, bf16[2,8,512,512]{3,2,1,0:T(8,128)(2,1)} %shard_map.87.h_ref, bf16[16,8,512]{2,1,0:T(8,128)(2,1)S(1)} %collective-permute-done.x_ref, f32[8,512]{1,0:T(8,128)S(1)} %shard_map.89.half_ref, ...), custom_call_target="tpu_custom_call" | custom-call | flops 100000000 | bytes 5000000 | tf_op jit(solution)/shard_map/pallas_call | solution.py:222
  51.4 0.0 copy-start.7
  51.4 0.0 copy-start.8
  51.5 0.0 copy-start.9
  51.5 0.0 copy-start.6
  51.5 0.0 all-gather.5.cloned.1.call-done
  51.5 0.0 all-gather.7.cloned.1.call-update
  51.5 0.6 copy-done.7
  52.1 0.1 copy.11
  52.3 7.9 %all-to-all-start.2 = ((bf16[16,8,512]{2,1,0:T(8,128)(2,1)}), bf16[16,8,512]{2,1,0:T(8,128)(2,1)S(1)}, u32[]{:S(2)}, u32[]{:S(2)}) async-start(bf16[16,8,512]{2,1,0:T(8,128)(2,1)} %get-tuple-element.52), calls=%async_computation.2 | async-start | bytes 262144 | tf_op jit(solution)/shard_map/all_to_all | solution.py:397
  60.2 0.2 fusion.5.coef_ref
  60.4 1.3 shard_map.91.wave_ref
  61.7 4.1 %all-to-all-done.2.x_ref = bf16[16,8,512]{2,1,0:T(8,128)(2,1)S(1)} async-done(((bf16[16,8,512]{2,1,0:T(8,128)(2,1)}), bf16[16,8,512]{2,1,0:T(8,128)(2,1)S(1)}, u32[]{:S(2)}, u32[]{:S(2)}) %all-to-all-start.2) | async-done | bytes 131104 | tf_op jit(solution)/shard_map/all_to_all | solution.py:397
  65.8 1.1 collective-permute-start.1
  67.0 2.0 %shard_map.92.half_ref = f32[8,512]{1,0:T(8,128)S(1)} custom-call(s32[1]{0:T(128)} %bitcast.core_ref, bf16[2,8,512,512]{3,2,1,0:T(8,128)(2,1)} %shard_map.87.h_ref, bf16[3,512,512]{2,1,0:T(8,128)(2,1)S(1)} %get-tuple-element.48.keep_ref, bf16[16,8,512]{2,1,0:T(8,128)(2,1)S(1)} %all-to-all-done.2.x_ref), custom_call_target="tpu_custom_call" | custom-call | flops 100000000 | bytes 5000000 | tf_op jit(solution)/shard_map/pallas_call | solution.py:180
  69.0 2.5 %shard_map.93 = (f32[8,512]{1,0:T(8,128)S(1)}, bf16[16,8,512]{2,1,0:T(8,128)(2,1)S(1)}) custom-call(s32[1]{0:T(128)} %bitcast.core_ref, s32[1]{0:T(128)} %bitcast.8.mine_ref, bf16[2,8,512,512]{3,2,1,0:T(8,128)(2,1)} %shard_map.87.h_ref, bf16[16,8,512]{2,1,0:T(8,128)(2,1)S(1)} %collective-permute-done.1.x_ref, f32[8,512]{1,0:T(8,128)S(1)} %shard_map.92.half_ref, ...), custom_call_target="tpu_custom_call" | custom-call | flops 100000000 | bytes 5000000 | tf_op jit(solution)/shard_map/pallas_call | solution.py:222
  71.5 10.2 %all_to_all.41.x_ref = bf16[16,8,512]{2,1,0:T(8,128)(2,1)S(1)} all-to-all(bf16[16,8,512]{2,1,0:T(8,128)(2,1)S(1)} %get-tuple-element.54), channel_id=1, replica_groups={{32,34,36,38,40,42,44,46,48,50,52,54,56,58,60,62},{33,35,37,39,41,43,45..., dimensions={0} | all-to-all | bytes 262144 | tf_op jit(solution)/shard_map/all_to_all | solution.py:397
  81.7 1.4 collective-permute-start.2
  83.1 2.0 %shard_map.94.half_ref = f32[8,512]{1,0:T(8,128)S(1)} custom-call(s32[1]{0:T(128)} %bitcast.core_ref, bf16[2,8,512,512]{3,2,1,0:T(8,128)(2,1)} %shard_map.87.h_ref, bf16[3,512,512]{2,1,0:T(8,128)(2,1)S(1)} %get-tuple-element.48.keep_ref, bf16[16,8,512]{2,1,0:T(8,128)(2,1)S(1)} %all_to_all.41.x_ref), custom_call_target="tpu_custom_call" | custom-call | flops 100000000 | bytes 5000000 | tf_op jit(solution)/shard_map/pallas_call | solution.py:180
  85.1 2.6 %shard_map.95 = (f32[8,512]{1,0:T(8,128)S(1)}, bf16[16,8,512]{2,1,0:T(8,128)(2,1)S(1)}) custom-call(s32[1]{0:T(128)} %bitcast.core_ref, s32[1]{0:T(128)} %bitcast.7.mine_ref, bf16[2,8,512,512]{3,2,1,0:T(8,128)(2,1)} %shard_map.87.h_ref, bf16[16,8,512]{2,1,0:T(8,128)(2,1)S(1)} %collective-permute-done.2.x_ref, f32[8,512]{1,0:T(8,128)S(1)} %shard_map.94.half_ref, ...), custom_call_target="tpu_custom_call" | custom-call | flops 100000000 | bytes 5000000 | tf_op jit(solution)/shard_map/pallas_call | solution.py:222
  87.7 12.4 %all_to_all.42.x_ref = bf16[16,8,512]{2,1,0:T(8,128)(2,1)S(1)} all-to-all(bf16[16,8,512]{2,1,0:T(8,128)(2,1)S(1)} %get-tuple-element.56), channel_id=1, replica_groups={{48,50,52,54,56,58,60,62,64,66,68,70,72,74,76,78},{49,51,53,55,57,59,61..., dimensions={0} | all-to-all | bytes 262144 | tf_op jit(solution)/shard_map/all_to_all | solution.py:397
  100.1 1.3 collective-permute-start.3
  101.4 2.0 %shard_map.96.half_ref = f32[8,512]{1,0:T(8,128)S(1)} custom-call(s32[1]{0:T(128)} %bitcast.core_ref, bf16[2,8,512,512]{3,2,1,0:T(8,128)(2,1)} %shard_map.87.h_ref, bf16[3,512,512]{2,1,0:T(8,128)(2,1)S(1)} %get-tuple-element.48.keep_ref, bf16[16,8,512]{2,1,0:T(8,128)(2,1)S(1)} %all_to_all.42.x_ref), custom_call_target="tpu_custom_call" | custom-call | flops 100000000 | bytes 5000000 | tf_op jit(solution)/shard_map/pallas_call | solution.py:180
  103.4 2.6 %shard_map.97 = (f32[8,512]{1,0:T(8,128)S(1)}, bf16[16,8,512]{2,1,0:T(8,128)(2,1)S(1)}) custom-call(s32[1]{0:T(128)} %bitcast.core_ref, s32[1]{0:T(128)} %bitcast.6.mine_ref, bf16[2,8,512,512]{3,2,1,0:T(8,128)(2,1)} %shard_map.87.h_ref, bf16[16,8,512]{2,1,0:T(8,128)(2,1)S(1)} %collective-permute-done.3.x_ref, f32[8,512]{1,0:T(8,128)S(1)} %shard_map.96.half_ref, ...), custom_call_target="tpu_custom_call" | custom-call | flops 100000000 | bytes 5000000 | tf_op jit(solution)/shard_map/pallas_call | solution.py:222
  105.9 10.3 %all_to_all.43.x_ref = bf16[16,8,512]{2,1,0:T(8,128)(2,1)S(1)} all-to-all(bf16[16,8,512]{2,1,0:T(8,128)(2,1)S(1)} %get-tuple-element.58), channel_id=1, replica_groups={{64,66,68,70,72,74,76,78,80,82,84,86,88,90,92,94},{65,67,69,71,73,75,77..., dimensions={0} | all-to-all | bytes 262144 | tf_op jit(solution)/shard_map/all_to_all | solution.py:397
  116.2 1.1 collective-permute-start.4
  117.4 2.0 %shard_map.98.half_ref = f32[8,512]{1,0:T(8,128)S(1)} custom-call(s32[1]{0:T(128)} %bitcast.core_ref, bf16[2,8,512,512]{3,2,1,0:T(8,128)(2,1)} %shard_map.87.h_ref, bf16[3,512,512]{2,1,0:T(8,128)(2,1)S(1)} %get-tuple-element.48.keep_ref, bf16[16,8,512]{2,1,0:T(8,128)(2,1)S(1)} %all_to_all.43.x_ref), custom_call_target="tpu_custom_call" | custom-call | flops 100000000 | bytes 5000000 | tf_op jit(solution)/shard_map/pallas_call | solution.py:180
  119.4 3.1 %shard_map.99 = (f32[8,512]{1,0:T(8,128)S(1)}, bf16[16,8,512]{2,1,0:T(8,128)(2,1)}) custom-call(s32[1]{0:T(128)} %bitcast.core_ref, s32[1]{0:T(128)} %bitcast.5.mine_ref, bf16[2,8,512,512]{3,2,1,0:T(8,128)(2,1)} %shard_map.87.h_ref, bf16[16,8,512]{2,1,0:T(8,128)(2,1)S(1)} %collective-permute-done.4.x_ref, f32[8,512]{1,0:T(8,128)S(1)} %shard_map.98.half_ref, ...), custom_call_target="tpu_custom_call" | custom-call | flops 100000000 | bytes 5000000 | tf_op jit(solution)/shard_map/pallas_call | solution.py:222
  122.5 7.9 %all-to-all-start.6 = ((bf16[16,8,512]{2,1,0:T(8,128)(2,1)}), bf16[16,8,512]{2,1,0:T(8,128)(2,1)S(1)}, u32[]{:S(2)}, u32[]{:S(2)}) async-start(bf16[16,8,512]{2,1,0:T(8,128)(2,1)} %get-tuple-element.62), calls=%async_computation.6 | async-start | bytes 262144 | tf_op jit(solution)/shard_map/all_to_all | solution.py:397
  130.4 0.0 all-gather.7.cloned.1.call-done.x_ref
  130.4 10.9 %shard_map.100 = (f32[8,96,512]{2,1,0:T(8,128)S(1)}, bf16[8,2,96,128]{3,2,1,0:T(8,128)(2,1)}, bf16[8,2,96,128]{3,2,1,0:T(8,128)(2,1)S(1)}, bf16[8,512]{1,0:T(8,128)(2,1)S(1)}) custom-call(s32[1]{0:T(128)} %bitcast.core_ref, bf16[16,768,512]{2,1,0:T(8,128)(2,1)} %all-gather.7.cloned.1.call-done.x_ref, bf16[2,8,512,512]{3,2,1,0:T(8,128)(2,1)} %shard_map.87.h_ref, ...), custom_call_target="tpu_custom_call" | custom-call | flops 6000000000 | bytes 23000000 | tf_op jit(solution)/shard_map/pallas_call | solution.py:268
  141.4 1.1 copy-done.2
  142.5 0.7 copy-done.5
  143.2 0.3 collective-permute-start.5
  143.5 2.0 %shard_map.101.half_ref = f32[8,512]{1,0:T(8,128)S(1)} custom-call(s32[1]{0:T(128)} %bitcast.core_ref, bf16[2,8,512,512]{3,2,1,0:T(8,128)(2,1)} %shard_map.87.h_ref, bf16[3,512,512]{2,1,0:T(8,128)(2,1)S(1)} %get-tuple-element.48.keep_ref, bf16[16,8,512]{2,1,0:T(8,128)(2,1)S(1)} %all-to-all-done.6.x_ref), custom_call_target="tpu_custom_call" | custom-call | flops 100000000 | bytes 5000000 | tf_op jit(solution)/shard_map/pallas_call | solution.py:180
  145.5 3.1 %shard_map.102 = (f32[8,512]{1,0:T(8,128)S(1)}, bf16[16,8,512]{2,1,0:T(8,128)(2,1)}) custom-call(s32[1]{0:T(128)} %bitcast.core_ref, s32[1]{0:T(128)} %bitcast.10.mine_ref, bf16[2,8,512,512]{3,2,1,0:T(8,128)(2,1)} %shard_map.87.h_ref, bf16[16,8,512]{2,1,0:T(8,128)(2,1)S(1)} %collective-permute-done.5.x_ref, f32[8,512]{1,0:T(8,128)S(1)} %shard_map.101.half_ref, ...), custom_call_target="tpu_custom_call" | custom-call | flops 100000000 | bytes 5000000 | tf_op jit(solution)/shard_map/pallas_call | solution.py:222
  148.7 6.7 %all-to-all-start.7 = ((bf16[16,8,512]{2,1,0:T(8,128)(2,1)}), bf16[16,8,512]{2,1,0:T(8,128)(2,1)S(1)}, u32[]{:S(2)}, u32[]{:S(2)}) async-start(bf16[16,8,512]{2,1,0:T(8,128)(2,1)} %get-tuple-element.67), calls=%async_computation.7 | async-start | bytes 262144 | tf_op jit(solution)/shard_map/all_to_all | solution.py:397
  155.4 3.1 %collective-permute-start.6 = (bf16[8,512]{1,0:T(8,128)(2,1)S(1)}, bf16[8,512]{1,0:T(8,128)(2,1)S(1)}, u32[]{:S(2)}, u32[]{:S(2)}) collective-permute-start(bf16[8,512]{1,0:T(8,128)(2,1)S(1)} %get-tuple-element.72), channel_id=1, source_target_pairs={{0,16},{16,32},{32,48},{48,64},{64,80},{80,96},{96,112},{1,17},{17... | collective-permute-start | bytes 24584 | tf_op jit(solution)/shard_map/ppermute | solution.py:369
  158.5 3.4 %collective-permute-done.6.prev_ref = bf16[8,512]{1,0:T(8,128)(2,1)S(1)} collective-permute-done((bf16[8,512]{1,0:T(8,128)(2,1)S(1)}, bf16[8,512]{1,0:T(8,128)(2,1)S(1)}, u32[]{:S(2)}, u32[]{:S(2)}) %collective-permute-start.6) | collective-permute-done | bytes 8224 | tf_op jit(solution)/shard_map/ppermute | solution.py:369
  161.9 1.9 %collective-permute-start.7 = (bf16[8,2,96,128]{3,2,1,0:T(8,128)(2,1)}, bf16[8,2,96,128]{3,2,1,0:T(8,128)(2,1)S(1)}, u32[]{:S(2)}, u32[]{:S(2)}) collective-permute-start(bf16[8,2,96,128]{3,2,1,0:T(8,128)(2,1)} %get-tuple-element.73), channel_id=1, source_target_pairs={{0,1},{1,0},{2,3},{3,2},{4,5},{5,4},{6,7},{7,6},{8,9},{9,8},{10,11... | collective-permute-start | bytes 1179656 | tf_op jit(solution)/shard_map/ppermute | solution.py:409
  163.8 3.0 %collective-permute-start.8 = (bf16[8,2,96,128]{3,2,1,0:T(8,128)(2,1)}, bf16[8,2,96,128]{3,2,1,0:T(8,128)(2,1)S(1)}, u32[]{:S(2)}, u32[]{:S(2)}) collective-permute-start(bf16[8,2,96,128]{3,2,1,0:T(8,128)(2,1)} %copy-done.5), channel_id=1, source_target_pairs={{1,2},{3,4},{5,6},{7,8},{9,10},{11,12},{13,14},{2,1},{4,3},{6,5},{... | collective-permute-start | bytes 1179656 | tf_op jit(solution)/shard_map/ppermute | solution.py:408
  166.8 0.2 collective-permute-start.9
  167.0 2.0 %shard_map.103.half_ref = f32[8,512]{1,0:T(8,128)S(1)} custom-call(s32[1]{0:T(128)} %bitcast.core_ref, bf16[2,8,512,512]{3,2,1,0:T(8,128)(2,1)} %shard_map.87.h_ref, bf16[3,512,512]{2,1,0:T(8,128)(2,1)S(1)} %get-tuple-element.48.keep_ref, bf16[16,8,512]{2,1,0:T(8,128)(2,1)S(1)} %all-to-all-done.7.x_ref), custom_call_target="tpu_custom_call" | custom-call | flops 100000000 | bytes 5000000 | tf_op jit(solution)/shard_map/pallas_call | solution.py:180
  169.0 0.0 copy-start.1
  169.1 0.0 copy-start.3
  169.1 2.6 %shard_map.104 = (f32[8,512]{1,0:T(8,128)S(1)}, bf16[8,512]{1,0:T(8,128)(2,1)S(1)}, bf16[2,8,256]{2,1,0:T(8,128)(2,1)S(1)}) custom-call(s32[1]{0:T(128)} %bitcast.core_ref, s32[1]{0:T(128)} %bitcast.11.mine_ref, bf16[2,8,512,512]{3,2,1,0:T(8,128)(2,1)} %shard_map.87.h_ref, bf16[16,8,512]{2,1,0:T(8,128)(2,1)S(1)} %collective-permute-done.9.x_ref, ...), custom_call_target="tpu_custom_call" | custom-call | flops 100000000 | bytes 5000000 | tf_op jit(solution)/shard_map/pallas_call | solution.py:222
  171.7 2.8 %collective-permute-start.10 = (bf16[8,512]{1,0:T(8,128)(2,1)S(1)}, bf16[8,512]{1,0:T(8,128)(2,1)S(1)}, u32[]{:S(2)}, u32[]{:S(2)}) collective-permute-start(bf16[8,512]{1,0:T(8,128)(2,1)S(1)} %get-tuple-element.79), channel_id=1, source_target_pairs={{16,0},{32,16},{48,32},{64,48},{80,64},{96,80},{112,96},{17,1},{33... | collective-permute-start | bytes 24584 | tf_op jit(solution)/shard_map/ppermute | solution.py:369
  174.5 0.4 collective-permute-start.11
  174.9 4.2 %collective-permute-start.12 = (bf16[8,256]{1,0:T(8,128)(2,1)S(1)}, bf16[8,256]{1,0:T(8,128)(2,1)S(1)}, u32[]{:S(2)}, u32[]{:S(2)}) collective-permute-start(bf16[8,256]{1,0:T(8,128)(2,1)S(1)} %get-tuple-element.84), channel_id=1, source_target_pairs={{1,2},{3,4},{5,6},{7,8},{9,10},{11,12},{13,14},{2,1},{4,3},{6,5},{... | collective-permute-start | bytes 12296 | tf_op jit(solution)/shard_map/ppermute | solution.py:415
  179.1 3.1 %collective-permute-done.12.vo_ref = bf16[8,256]{1,0:T(8,128)(2,1)S(1)} collective-permute-done((bf16[8,256]{1,0:T(8,128)(2,1)S(1)}, bf16[8,256]{1,0:T(8,128)(2,1)S(1)}, u32[]{:S(2)}, u32[]{:S(2)}) %collective-permute-start.12) | collective-permute-done | bytes 4128 | tf_op jit(solution)/shard_map/ppermute | solution.py:415
  182.2 2.8 %shard_map.105 = (f32[2,8,192,128]{3,2,1,0:T(8,128)}, f32[2,8,192,128]{3,2,1,0:T(8,128)}) custom-call(s32[1]{0:T(128)} %bitcast.core_ref, f32[8,96,512]{2,1,0:T(8,128)S(1)} %copy-done.3, f32[2,8,192,128]{3,2,1,0:T(8,128)S(1)} %bitcast.28, bf16[8,2,96,128]{3,2,1,0:T(8,128)(2,1)S(1)} %collective-permute-done.7.inner_ref, ...), custom_call_target="tpu_custom_call" | custom-call | tf_op jit(solution)/shard_map/pallas_call | solution.py:348
  (25 shorter events, 0.1 us)
Async XLA Ops:
  7.2 44.3 %all-gather.5.cloned.1.call-start = ((), (), s32[]{:S(2)}) async-start(), calls=%async_computation.8 | async-start | bytes 2359296 | tf_op jit(solution)/shard_map/all_gather | solution.py:378
  7.2 1.4 copy-start
  8.6 0.7 copy-start.4
  10.4 15.8 %all-to-all-start = ((bf16[16,16,512]{2,1,0:T(8,128)(2,1)}), bf16[16,16,512]{2,1,0:T(8,128)(2,1)S(1)}, u32[]{:S(2)}, u32[]{:S(2)}) async-start(bf16[16,16,512]{2,1,0:T(8,128)(2,1)} %get-tuple-element.44), calls=%async_computation | async-start | bytes 524288 | tf_op jit(solution)/shard_map/all_to_all | solution.py:379
  19.1 111.4 %all-gather.7.cloned.1.call-start = ((), (), s32[]{:S(2)}) async-start(), calls=%async_computation.9 | async-start | bytes 14155776 | tf_op jit(solution)/shard_map/all_gather | solution.py:396
  44.8 3.5 %collective-permute-start = (bf16[16,8,512]{2,1,0:T(8,128)(2,1)S(1)}, bf16[16,8,512]{2,1,0:T(8,128)(2,1)S(1)}, u32[]{:S(2)}, u32[]{:S(2)}) collective-permute-start(bf16[16,8,512]{2,1,0:T(8,128)(2,1)S(1)} %all_to_all.40.x_ref), channel_id=1, source_target_pairs={{0,1},{1,0},{2,3},{3,2},{4,5},{5,4},{6,7},{7,6},{8,9},{9,8},{10,11... | collective-permute-start | bytes 393224 | tf_op jit(solution)/shard_map/ppermute | solution.py:410
  51.4 0.7 copy-start.7
  51.4 8.7 %copy-start.8 = (s32[256]{0:T(256)S(1)}, s32[256]{0:T(256)}, u32[]{:S(2)}) copy-start(s32[256]{0:T(256)} %param.11) | copy-start | bytes 3076
  51.5 8.7 %copy-start.9 = (s32[8]{0:T(128)S(1)}, s32[8]{0:T(128)}, u32[]{:S(2)}) copy-start(s32[8]{0:T(128)} %param.12) | copy-start | bytes 100
  51.5 8.9 %copy-start.6 = (bf16[256,2,128]{2,1,0:T(2,128)(2,1)S(1)}, bf16[256,2,128]{2,1,0:T(2,128)(2,1)}, u32[]{:S(2)}) copy-start(bf16[256,2,128]{2,1,0:T(2,128)(2,1)} %param.9) | copy-start | bytes 393220
  52.3 13.5 %all-to-all-start.2 = ((bf16[16,8,512]{2,1,0:T(8,128)(2,1)}), bf16[16,8,512]{2,1,0:T(8,128)(2,1)S(1)}, u32[]{:S(2)}, u32[]{:S(2)}) async-start(bf16[16,8,512]{2,1,0:T(8,128)(2,1)} %get-tuple-element.52), calls=%async_computation.2 | async-start | bytes 262144 | tf_op jit(solution)/shard_map/all_to_all | solution.py:397
  65.8 3.1 %collective-permute-start.1 = (bf16[16,8,512]{2,1,0:T(8,128)(2,1)S(1)}, bf16[16,8,512]{2,1,0:T(8,128)(2,1)S(1)}, u32[]{:S(2)}, u32[]{:S(2)}) collective-permute-start(bf16[16,8,512]{2,1,0:T(8,128)(2,1)S(1)} %all-to-all-done.2.x_ref), channel_id=1, source_target_pairs={{0,1},{1,0},{2,3},{3,2},{4,5},{5,4},{6,7},{7,6},{8,9},{9,8},{10,11... | collective-permute-start | bytes 393224 | tf_op jit(solution)/shard_map/ppermute | solution.py:410
  81.7 3.4 %collective-permute-start.2 = (bf16[16,8,512]{2,1,0:T(8,128)(2,1)S(1)}, bf16[16,8,512]{2,1,0:T(8,128)(2,1)S(1)}, u32[]{:S(2)}, u32[]{:S(2)}) collective-permute-start(bf16[16,8,512]{2,1,0:T(8,128)(2,1)S(1)} %all_to_all.41.x_ref), channel_id=1, source_target_pairs={{0,1},{1,0},{2,3},{3,2},{4,5},{5,4},{6,7},{7,6},{8,9},{9,8},{10,11... | collective-permute-start | bytes 393224 | tf_op jit(solution)/shard_map/ppermute | solution.py:410
  100.1 3.3 %collective-permute-start.3 = (bf16[16,8,512]{2,1,0:T(8,128)(2,1)S(1)}, bf16[16,8,512]{2,1,0:T(8,128)(2,1)S(1)}, u32[]{:S(2)}, u32[]{:S(2)}) collective-permute-start(bf16[16,8,512]{2,1,0:T(8,128)(2,1)S(1)} %all_to_all.42.x_ref), channel_id=1, source_target_pairs={{0,1},{1,0},{2,3},{3,2},{4,5},{5,4},{6,7},{7,6},{8,9},{9,8},{10,11... | collective-permute-start | bytes 393224 | tf_op jit(solution)/shard_map/ppermute | solution.py:410
  116.2 3.1 %collective-permute-start.4 = (bf16[16,8,512]{2,1,0:T(8,128)(2,1)S(1)}, bf16[16,8,512]{2,1,0:T(8,128)(2,1)S(1)}, u32[]{:S(2)}, u32[]{:S(2)}) collective-permute-start(bf16[16,8,512]{2,1,0:T(8,128)(2,1)S(1)} %all_to_all.43.x_ref), channel_id=1, source_target_pairs={{0,1},{1,0},{2,3},{3,2},{4,5},{5,4},{6,7},{7,6},{8,9},{9,8},{10,11... | collective-permute-start | bytes 393224 | tf_op jit(solution)/shard_map/ppermute | solution.py:410
  122.5 20.7 %all-to-all-start.6 = ((bf16[16,8,512]{2,1,0:T(8,128)(2,1)}), bf16[16,8,512]{2,1,0:T(8,128)(2,1)S(1)}, u32[]{:S(2)}, u32[]{:S(2)}) async-start(bf16[16,8,512]{2,1,0:T(8,128)(2,1)} %get-tuple-element.62), calls=%async_computation.6 | async-start | bytes 262144 | tf_op jit(solution)/shard_map/all_to_all | solution.py:397
  141.3 1.1 copy-start.2
  142.5 0.7 copy-start.5
  143.2 2.3 %collective-permute-start.5 = (bf16[16,8,512]{2,1,0:T(8,128)(2,1)S(1)}, bf16[16,8,512]{2,1,0:T(8,128)(2,1)S(1)}, u32[]{:S(2)}, u32[]{:S(2)}) collective-permute-start(bf16[16,8,512]{2,1,0:T(8,128)(2,1)S(1)} %all-to-all-done.6.x_ref), channel_id=1, source_target_pairs={{0,1},{1,0},{2,3},{3,2},{4,5},{5,4},{6,7},{7,6},{8,9},{9,8},{10,11... | collective-permute-start | bytes 393224 | tf_op jit(solution)/shard_map/ppermute | solution.py:410
  148.7 13.2 %all-to-all-start.7 = ((bf16[16,8,512]{2,1,0:T(8,128)(2,1)}), bf16[16,8,512]{2,1,0:T(8,128)(2,1)S(1)}, u32[]{:S(2)}, u32[]{:S(2)}) async-start(bf16[16,8,512]{2,1,0:T(8,128)(2,1)} %get-tuple-element.67), calls=%async_computation.7 | async-start | bytes 262144 | tf_op jit(solution)/shard_map/all_to_all | solution.py:397
  155.4 6.5 %collective-permute-start.6 = (bf16[8,512]{1,0:T(8,128)(2,1)S(1)}, bf16[8,512]{1,0:T(8,128)(2,1)S(1)}, u32[]{:S(2)}, u32[]{:S(2)}) collective-permute-start(bf16[8,512]{1,0:T(8,128)(2,1)S(1)} %get-tuple-element.72), channel_id=1, source_target_pairs={{0,16},{16,32},{32,48},{48,64},{64,80},{80,96},{96,112},{1,17},{17... | collective-permute-start | bytes 24584 | tf_op jit(solution)/shard_map/ppermute | solution.py:369
  161.9 20.3 %collective-permute-start.7 = (bf16[8,2,96,128]{3,2,1,0:T(8,128)(2,1)}, bf16[8,2,96,128]{3,2,1,0:T(8,128)(2,1)S(1)}, u32[]{:S(2)}, u32[]{:S(2)}) collective-permute-start(bf16[8,2,96,128]{3,2,1,0:T(8,128)(2,1)} %get-tuple-element.73), channel_id=1, source_target_pairs={{0,1},{1,0},{2,3},{3,2},{4,5},{5,4},{6,7},{7,6},{8,9},{9,8},{10,11... | collective-permute-start | bytes 1179656 | tf_op jit(solution)/shard_map/ppermute | solution.py:409
  163.8 18.4 %collective-permute-start.8 = (bf16[8,2,96,128]{3,2,1,0:T(8,128)(2,1)}, bf16[8,2,96,128]{3,2,1,0:T(8,128)(2,1)S(1)}, u32[]{:S(2)}, u32[]{:S(2)}) collective-permute-start(bf16[8,2,96,128]{3,2,1,0:T(8,128)(2,1)} %copy-done.5), channel_id=1, source_target_pairs={{1,2},{3,4},{5,6},{7,8},{9,10},{11,12},{13,14},{2,1},{4,3},{6,5},{... | collective-permute-start | bytes 1179656 | tf_op jit(solution)/shard_map/ppermute | solution.py:408
  166.8 2.2 %collective-permute-start.9 = (bf16[16,8,512]{2,1,0:T(8,128)(2,1)S(1)}, bf16[16,8,512]{2,1,0:T(8,128)(2,1)S(1)}, u32[]{:S(2)}, u32[]{:S(2)}) collective-permute-start(bf16[16,8,512]{2,1,0:T(8,128)(2,1)S(1)} %all-to-all-done.7.x_ref), channel_id=1, source_target_pairs={{0,1},{1,0},{2,3},{3,2},{4,5},{5,4},{6,7},{7,6},{8,9},{9,8},{10,11... | collective-permute-start | bytes 393224 | tf_op jit(solution)/shard_map/ppermute | solution.py:410
  169.0 13.2 %copy-start.1 = (f32[2,8,96,2,128]{4,3,2,1,0:T(2,128)S(1)}, f32[2,8,96,2,128]{4,3,2,1,0:T(2,128)}, u32[]{:S(2)}) copy-start(f32[2,8,96,2,128]{4,3,2,1,0:T(2,128)} %param.7) | copy-start | bytes 4718596
  169.1 13.2 %copy-start.3 = (f32[8,96,512]{2,1,0:T(8,128)S(1)}, f32[8,96,512]{2,1,0:T(8,128)}, u32[]{:S(2)}) copy-start(f32[8,96,512]{2,1,0:T(8,128)} %copy-done.2) | copy-start | bytes 4718596
  171.7 10.5 %collective-permute-start.10 = (bf16[8,512]{1,0:T(8,128)(2,1)S(1)}, bf16[8,512]{1,0:T(8,128)(2,1)S(1)}, u32[]{:S(2)}, u32[]{:S(2)}) collective-permute-start(bf16[8,512]{1,0:T(8,128)(2,1)S(1)} %get-tuple-element.79), channel_id=1, source_target_pairs={{16,0},{32,16},{48,32},{64,48},{80,64},{96,80},{112,96},{17,1},{33... | collective-permute-start | bytes 24584 | tf_op jit(solution)/shard_map/ppermute | solution.py:369
  174.5 4.6 %collective-permute-start.11 = (bf16[8,256]{1,0:T(8,128)(2,1)S(1)}, bf16[8,256]{1,0:T(8,128)(2,1)S(1)}, u32[]{:S(2)}, u32[]{:S(2)}) collective-permute-start(bf16[8,256]{1,0:T(8,128)(2,1)S(1)} %get-tuple-element.85), channel_id=1, source_target_pairs={{0,1},{1,0},{2,3},{3,2},{4,5},{5,4},{6,7},{7,6},{8,9},{9,8},{10,11... | collective-permute-start | bytes 12296 | tf_op jit(solution)/shard_map/ppermute | solution.py:417
  174.9 7.3 %collective-permute-start.12 = (bf16[8,256]{1,0:T(8,128)(2,1)S(1)}, bf16[8,256]{1,0:T(8,128)(2,1)S(1)}, u32[]{:S(2)}, u32[]{:S(2)}) collective-permute-start(bf16[8,256]{1,0:T(8,128)(2,1)S(1)} %get-tuple-element.84), channel_id=1, source_target_pairs={{1,2},{3,4},{5,6},{7,8},{9,10},{11,12},{13,14},{2,1},{4,3},{6,5},{... | collective-permute-start | bytes 12296 | tf_op jit(solution)/shard_map/ppermute | solution.py:415
Sparse Core Ops, SparseCore 0:
  10.6 33.4 all-gather.4
  51.7 71.5 all-gather.6

commit v8 on v6

--- a/solution.py
+++ b/solution.py
@@ -18,7 +18,7 @@
 R = 8
 K = 512
 NY = 128
-KEEP = 4
+KEEP = 3
 
 bf16 = jnp.bfloat16
 f32 = jnp.float32

time: 193 us -> 192 us (level)
  local copies, waits for them, and re-layouts: 5.56 us -> 3.6 us
    unnamed x30 -> x20, local copies, waits for them, and re-layouts: 5.56 us -> 3.6 us
  transfers between devices with their start and end apart: 19 -> 19, of which waited for: 3 -> 3; matrix products, arithmetic and copies ran while one was open for 0% -> 0% of each run, Pallas kernels for 28% -> 29%
where the time goes in v8:
time: 192 us; the launch traced here: 191 us
  Pallas kernels  62.1 us (32%)
  starting transfers between devices  53.5 us (28%)
  blocking collectives  46.6 us (24%)
  between operations  14.5 us (8%)
  waiting for transfers between devices  10.7 us (6%)
  local copies, waits for them, and re-layouts  3.6 us (2%)
    all_to_all x4, blocking collectives, shards(): lax.all_to_all(out, ('layer', 'plane'), 0, 0, axis_index_groups=pair_grou...  46.6 us
    all_to_all x3, starting transfers between devices, shards(): lax.all_to_all(out, ('layer', 'plane'), 0, 0, axis_index_groups=pair_grou...  22.5 us
    pallas_call x7, Pallas kernels, other_half(): pl.pallas_call(final_kernel if final else other_kernel, out_shape=out, in...  19.7 us
    pallas_call x7, Pallas kernels, own_half(): pl.pallas_call(own_kernel, out_shape=jax.ShapeDtypeStruct((R, K), f32), i...  14 us
    pallas_call x1, Pallas kernels, fronts_of(): pl.pallas_call(fronts_kernel, out_shape=(jax.ShapeDtypeStruct((R, LZ, K),...  11.4 us
    all_to_all x1, starting transfers between devices, shards(): heads = lax.all_to_all(chunk, 'plane', 0, 0)  8.62 us
    pallas_call x1, Pallas kernels, arrange(): pl.pallas_call(arrange_kernel, out_shape=jax.ShapeDtypeStruct((2, C, K, K...  7.08 us
    ppermute x7, starting transfers between devices, shards(): other = lax.ppermute(got, 'plane', twin)  7.01 us
  transfers between devices with their start and end apart: 19, of which 3 were waited for; matrix products, arithmetic and copies ran while one was open for 0% of the time, Pallas kernels for 29%

profile of v8, /device:TPU:7, one launch (start us, length us, event | category | flops | bytes accessed | tf_op | source)
XLA Modules:
  0.0 191.1 jit_solution(17088467943064943119)
XLA Ops:
  7.2 0.0 all-gather.5.cloned.1.call-start
  7.2 0.0 copy-start
  7.2 1.4 copy-done
  8.6 0.7 copy-done.3
  9.3 1.1 shard_map.86
  10.4 0.0 all-gather.5.cloned.1.call-update
  10.4 8.6 %all-to-all-start = ((bf16[16,16,512]{2,1,0:T(8,128)(2,1)}), bf16[16,16,512]{2,1,0:T(8,128)(2,1)S(1)}, u32[]{:S(2)}, u32[]{:S(2)}) async-start(bf16[16,16,512]{2,1,0:T(8,128)(2,1)} %get-tuple-element.44), calls=%async_computation | async-start | bytes 524288 | tf_op jit(solution)/shard_map/all_to_all | solution.py:395
  19.1 0.0 all-gather.7.cloned.1.call-start
  19.1 7.1 %shard_map.87.h_ref = bf16[2,8,512,512]{3,2,1,0:T(8,128)(2,1)} custom-call(bf16[512,2,32,128]{3,2,1,0:T(8,128)(2,1)} %bitcast.30), custom_call_target="tpu_custom_call" | custom-call | flops 4000000000 | bytes 17000000 | tf_op jit(solution)/shard_map/pallas_call | solution.py:106
  26.2 4.8 %shard_map.88 = (f32[8,512]{1,0:T(8,128)S(1)}, bf16[16,8,512]{2,1,0:T(8,128)(2,1)S(1)}, bf16[3,512,512]{2,1,0:T(8,128)(2,1)S(1)}) custom-call(s32[1]{0:T(128)} %bitcast.core_ref, bf16[2,8,512,512]{3,2,1,0:T(8,128)(2,1)} %shard_map.87.h_ref, bf16[16,16,512]{2,1,0:T(8,128)(2,1)S(1)} %all-to-all-done.x_ref), custom_call_target="tpu_custom_call" | custom-call | flops 100000000 | bytes 5000000 | tf_op jit(solution)/shard_map/pallas_call | solution.py:157
  31.0 13.7 %all_to_all.40.x_ref = bf16[16,8,512]{2,1,0:T(8,128)(2,1)S(1)} all-to-all(bf16[16,8,512]{2,1,0:T(8,128)(2,1)S(1)} %get-tuple-element.47), channel_id=1, replica_groups={{0,2,4,6,8,10,12,14,16,18,20,22,24,26,28,30},{1,3,5,7,9,11,13,15,17,19,..., dimensions={0} | all-to-all | bytes 262144 | tf_op jit(solution)/shard_map/all_to_all | solution.py:413
  44.7 1.5 collective-permute-start
  46.2 2.0 %shard_map.89.half_ref = f32[8,512]{1,0:T(8,128)S(1)} custom-call(s32[1]{0:T(128)} %bitcast.core_ref, bf16[2,8,512,512]{3,2,1,0:T(8,128)(2,1)} %shard_map.87.h_ref, bf16[3,512,512]{2,1,0:T(8,128)(2,1)S(1)} %get-tuple-element.48.keep_ref, bf16[16,8,512]{2,1,0:T(8,128)(2,1)S(1)} %all_to_all.40.x_ref), custom_call_target="tpu_custom_call" | custom-call | flops 100000000 | bytes 5000000 | tf_op jit(solution)/shard_map/pallas_call | solution.py:180
  48.2 0.0 collective-permute-done.x_ref
  48.2 3.1 %shard_map.90 = (f32[8,512]{1,0:T(8,128)S(1)}, bf16[16,8,512]{2,1,0:T(8,128)(2,1)}) custom-call(s32[1]{0:T(128)} %bitcast.core_ref, s32[1]{0:T(128)} %bitcast.3.mine_ref, bf16[2,8,512,512]{3,2,1,0:T(8,128)(2,1)} %shard_map.87.h_ref, bf16[16,8,512]{2,1,0:T(8,128)(2,1)S(1)} %collective-permute-done.x_ref, f32[8,512]{1,0:T(8,128)S(1)} %shard_map.89.half_ref, ...), custom_call_target="tpu_custom_call" | custom-call | flops 100000000 | bytes 5000000 | tf_op jit(solution)/shard_map/pallas_call | solution.py:222
  51.4 0.0 copy-start.6
  51.4 0.0 copy-start.7
  51.4 0.0 copy-start.8
  51.4 0.0 copy-start.5
  51.4 0.0 all-gather.5.cloned.1.call-done
  51.5 0.0 all-gather.7.cloned.1.call-update
  51.5 0.6 copy-done.6
  52.1 0.1 copy.11
  52.2 7.9 %all-to-all-start.2 = ((bf16[16,8,512]{2,1,0:T(8,128)(2,1)}), bf16[16,8,512]{2,1,0:T(8,128)(2,1)S(1)}, u32[]{:S(2)}, u32[]{:S(2)}) async-start(bf16[16,8,512]{2,1,0:T(8,128)(2,1)} %get-tuple-element.52), calls=%async_computation.2 | async-start | bytes 262144 | tf_op jit(solution)/shard_map/all_to_all | solution.py:413
  60.2 0.2 fusion.5.coef_ref
  60.4 1.3 shard_map.91.wave_ref
  61.7 4.1 %all-to-all-done.2.x_ref = bf16[16,8,512]{2,1,0:T(8,128)(2,1)S(1)} async-done(((bf16[16,8,512]{2,1,0:T(8,128)(2,1)}), bf16[16,8,512]{2,1,0:T(8,128)(2,1)S(1)}, u32[]{:S(2)}, u32[]{:S(2)}) %all-to-all-start.2) | async-done | bytes 131104 | tf_op jit(solution)/shard_map/all_to_all | solution.py:413
  65.8 1.2 collective-permute-start.1
  66.9 2.0 %shard_map.92.half_ref = f32[8,512]{1,0:T(8,128)S(1)} custom-call(s32[1]{0:T(128)} %bitcast.core_ref, bf16[2,8,512,512]{3,2,1,0:T(8,128)(2,1)} %shard_map.87.h_ref, bf16[3,512,512]{2,1,0:T(8,128)(2,1)S(1)} %get-tuple-element.48.keep_ref, bf16[16,8,512]{2,1,0:T(8,128)(2,1)S(1)} %all-to-all-done.2.x_ref), custom_call_target="tpu_custom_call" | custom-call | flops 100000000 | bytes 5000000 | tf_op jit(solution)/shard_map/pallas_call | solution.py:180
  69.0 2.5 %shard_map.93 = (f32[8,512]{1,0:T(8,128)S(1)}, bf16[16,8,512]{2,1,0:T(8,128)(2,1)S(1)}) custom-call(s32[1]{0:T(128)} %bitcast.core_ref, s32[1]{0:T(128)} %bitcast.8.mine_ref, bf16[2,8,512,512]{3,2,1,0:T(8,128)(2,1)} %shard_map.87.h_ref, bf16[16,8,512]{2,1,0:T(8,128)(2,1)S(1)} %collective-permute-done.1.x_ref, f32[8,512]{1,0:T(8,128)S(1)} %shard_map.92.half_ref, ...), custom_call_target="tpu_custom_call" | custom-call | flops 100000000 | bytes 5000000 | tf_op jit(solution)/shard_map/pallas_call | solution.py:222
  71.4 10.2 %all_to_all.41.x_ref = bf16[16,8,512]{2,1,0:T(8,128)(2,1)S(1)} all-to-all(bf16[16,8,512]{2,1,0:T(8,128)(2,1)S(1)} %get-tuple-element.54), channel_id=1, replica_groups={{32,34,36,38,40,42,44,46,48,50,52,54,56,58,60,62},{33,35,37,39,41,43,45..., dimensions={0} | all-to-all | bytes 262144 | tf_op jit(solution)/shard_map/all_to_all | solution.py:413
  81.7 1.4 collective-permute-start.2
  83.0 2.0 %shard_map.94.half_ref = f32[8,512]{1,0:T(8,128)S(1)} custom-call(s32[1]{0:T(128)} %bitcast.core_ref, bf16[2,8,512,512]{3,2,1,0:T(8,128)(2,1)} %shard_map.87.h_ref, bf16[3,512,512]{2,1,0:T(8,128)(2,1)S(1)} %get-tuple-element.48.keep_ref, bf16[16,8,512]{2,1,0:T(8,128)(2,1)S(1)} %all_to_all.41.x_ref), custom_call_target="tpu_custom_call" | custom-call | flops 100000000 | bytes 5000000 | tf_op jit(solution)/shard_map/pallas_call | solution.py:180
  85.1 2.6 %shard_map.95 = (f32[8,512]{1,0:T(8,128)S(1)}, bf16[16,8,512]{2,1,0:T(8,128)(2,1)S(1)}) custom-call(s32[1]{0:T(128)} %bitcast.core_ref, s32[1]{0:T(128)} %bitcast.7.mine_ref, bf16[2,8,512,512]{3,2,1,0:T(8,128)(2,1)} %shard_map.87.h_ref, bf16[16,8,512]{2,1,0:T(8,128)(2,1)S(1)} %collective-permute-done.2.x_ref, f32[8,512]{1,0:T(8,128)S(1)} %shard_map.94.half_ref, ...), custom_call_target="tpu_custom_call" | custom-call | flops 100000000 | bytes 5000000 | tf_op jit(solution)/shard_map/pallas_call | solution.py:222
  87.6 12.4 %all_to_all.42.x_ref = bf16[16,8,512]{2,1,0:T(8,128)(2,1)S(1)} all-to-all(bf16[16,8,512]{2,1,0:T(8,128)(2,1)S(1)} %get-tuple-element.56), channel_id=1, replica_groups={{48,50,52,54,56,58,60,62,64,66,68,70,72,74,76,78},{49,51,53,55,57,59,61..., dimensions={0} | all-to-all | bytes 262144 | tf_op jit(solution)/shard_map/all_to_all | solution.py:413
  100.0 1.3 collective-permute-start.3
  101.3 2.0 %shard_map.96.half_ref = f32[8,512]{1,0:T(8,128)S(1)} custom-call(s32[1]{0:T(128)} %bitcast.core_ref, bf16[2,8,512,512]{3,2,1,0:T(8,128)(2,1)} %shard_map.87.h_ref, bf16[3,512,512]{2,1,0:T(8,128)(2,1)S(1)} %get-tuple-element.48.keep_ref, bf16[16,8,512]{2,1,0:T(8,128)(2,1)S(1)} %all_to_all.42.x_ref), custom_call_target="tpu_custom_call" | custom-call | flops 100000000 | bytes 5000000 | tf_op jit(solution)/shard_map/pallas_call | solution.py:180
  103.3 2.6 %shard_map.97 = (f32[8,512]{1,0:T(8,128)S(1)}, bf16[16,8,512]{2,1,0:T(8,128)(2,1)S(1)}) custom-call(s32[1]{0:T(128)} %bitcast.core_ref, s32[1]{0:T(128)} %bitcast.6.mine_ref, bf16[2,8,512,512]{3,2,1,0:T(8,128)(2,1)} %shard_map.87.h_ref, bf16[16,8,512]{2,1,0:T(8,128)(2,1)S(1)} %collective-permute-done.3.x_ref, f32[8,512]{1,0:T(8,128)S(1)} %shard_map.96.half_ref, ...), custom_call_target="tpu_custom_call" | custom-call | flops 100000000 | bytes 5000000 | tf_op jit(solution)/shard_map/pallas_call | solution.py:222
  105.9 10.3 %all_to_all.43.x_ref = bf16[16,8,512]{2,1,0:T(8,128)(2,1)S(1)} all-to-all(bf16[16,8,512]{2,1,0:T(8,128)(2,1)S(1)} %get-tuple-element.58), channel_id=1, replica_groups={{64,66,68,70,72,74,76,78,80,82,84,86,88,90,92,94},{65,67,69,71,73,75,77..., dimensions={0} | all-to-all | bytes 262144 | tf_op jit(solution)/shard_map/all_to_all | solution.py:413
  116.2 1.1 collective-permute-start.4
  117.4 2.0 %shard_map.98.half_ref = f32[8,512]{1,0:T(8,128)S(1)} custom-call(s32[1]{0:T(128)} %bitcast.core_ref, bf16[2,8,512,512]{3,2,1,0:T(8,128)(2,1)} %shard_map.87.h_ref, bf16[3,512,512]{2,1,0:T(8,128)(2,1)S(1)} %get-tuple-element.48.keep_ref, bf16[16,8,512]{2,1,0:T(8,128)(2,1)S(1)} %all_to_all.43.x_ref), custom_call_target="tpu_custom_call" | custom-call | flops 100000000 | bytes 5000000 | tf_op jit(solution)/shard_map/pallas_call | solution.py:180
  119.4 3.1 %shard_map.99 = (f32[8,512]{1,0:T(8,128)S(1)}, bf16[16,8,512]{2,1,0:T(8,128)(2,1)}) custom-call(s32[1]{0:T(128)} %bitcast.core_ref, s32[1]{0:T(128)} %bitcast.5.mine_ref, bf16[2,8,512,512]{3,2,1,0:T(8,128)(2,1)} %shard_map.87.h_ref, bf16[16,8,512]{2,1,0:T(8,128)(2,1)S(1)} %collective-permute-done.4.x_ref, f32[8,512]{1,0:T(8,128)S(1)} %shard_map.98.half_ref, ...), custom_call_target="tpu_custom_call" | custom-call | flops 100000000 | bytes 5000000 | tf_op jit(solution)/shard_map/pallas_call | solution.py:222
  122.5 7.8 %all-to-all-start.6 = ((bf16[16,8,512]{2,1,0:T(8,128)(2,1)}), bf16[16,8,512]{2,1,0:T(8,128)(2,1)S(1)}, u32[]{:S(2)}, u32[]{:S(2)}) async-start(bf16[16,8,512]{2,1,0:T(8,128)(2,1)} %get-tuple-element.62), calls=%async_computation.6 | async-start | bytes 262144 | tf_op jit(solution)/shard_map/all_to_all | solution.py:413
  130.4 0.0 all-gather.7.cloned.1.call-done.x_ref
  130.4 11.4 %shard_map.100 = (f32[8,96,512]{2,1,0:T(8,128)}, bf16[8,2,96,128]{3,2,1,0:T(8,128)(2,1)}, bf16[8,2,96,128]{3,2,1,0:T(8,128)(2,1)S(1)}, bf16[8,512]{1,0:T(8,128)(2,1)S(1)}) custom-call(s32[1]{0:T(128)} %bitcast.core_ref, bf16[16,768,512]{2,1,0:T(8,128)(2,1)} %all-gather.7.cloned.1.call-done.x_ref, bf16[2,8,512,512]{3,2,1,0:T(8,128)(2,1)} %shard_map.87.h_ref, ...), custom_call_target="tpu_custom_call" | custom-call | flops 6000000000 | bytes 23000000 | tf_op jit(solution)/shard_map/pallas_call | solution.py:280
  141.8 0.7 copy-done.4
  142.5 0.3 collective-permute-start.5
  142.8 2.0 %shard_map.101.half_ref = f32[8,512]{1,0:T(8,128)S(1)} custom-call(s32[1]{0:T(128)} %bitcast.core_ref, bf16[2,8,512,512]{3,2,1,0:T(8,128)(2,1)} %shard_map.87.h_ref, bf16[3,512,512]{2,1,0:T(8,128)(2,1)S(1)} %get-tuple-element.48.keep_ref, bf16[16,8,512]{2,1,0:T(8,128)(2,1)S(1)} %all-to-all-done.6.x_ref), custom_call_target="tpu_custom_call" | custom-call | flops 100000000 | bytes 5000000 | tf_op jit(solution)/shard_map/pallas_call | solution.py:180
  144.8 3.1 %shard_map.102 = (f32[8,512]{1,0:T(8,128)S(1)}, bf16[16,8,512]{2,1,0:T(8,128)(2,1)}) custom-call(s32[1]{0:T(128)} %bitcast.core_ref, s32[1]{0:T(128)} %bitcast.10.mine_ref, bf16[2,8,512,512]{3,2,1,0:T(8,128)(2,1)} %shard_map.87.h_ref, bf16[16,8,512]{2,1,0:T(8,128)(2,1)S(1)} %collective-permute-done.5.x_ref, f32[8,512]{1,0:T(8,128)S(1)} %shard_map.101.half_ref, ...), custom_call_target="tpu_custom_call" | custom-call | flops 100000000 | bytes 5000000 | tf_op jit(solution)/shard_map/pallas_call | solution.py:222
  147.9 6.7 %all-to-all-start.7 = ((bf16[16,8,512]{2,1,0:T(8,128)(2,1)}), bf16[16,8,512]{2,1,0:T(8,128)(2,1)S(1)}, u32[]{:S(2)}, u32[]{:S(2)}) async-start(bf16[16,8,512]{2,1,0:T(8,128)(2,1)} %get-tuple-element.67), calls=%async_computation.7 | async-start | bytes 262144 | tf_op jit(solution)/shard_map/all_to_all | solution.py:413
  154.6 3.1 %collective-permute-start.6 = (bf16[8,512]{1,0:T(8,128)(2,1)S(1)}, bf16[8,512]{1,0:T(8,128)(2,1)S(1)}, u32[]{:S(2)}, u32[]{:S(2)}) collective-permute-start(bf16[8,512]{1,0:T(8,128)(2,1)S(1)} %get-tuple-element.72), channel_id=1, source_target_pairs={{0,16},{16,32},{32,48},{48,64},{64,80},{80,96},{96,112},{1,17},{17... | collective-permute-start | bytes 24584 | tf_op jit(solution)/shard_map/ppermute | solution.py:385
  157.7 3.4 %collective-permute-done.6.prev_ref = bf16[8,512]{1,0:T(8,128)(2,1)S(1)} collective-permute-done((bf16[8,512]{1,0:T(8,128)(2,1)S(1)}, bf16[8,512]{1,0:T(8,128)(2,1)S(1)}, u32[]{:S(2)}, u32[]{:S(2)}) %collective-permute-start.6) | collective-permute-done | bytes 8224 | tf_op jit(solution)/shard_map/ppermute | solution.py:385
  161.1 1.9 %collective-permute-start.7 = (bf16[8,2,96,128]{3,2,1,0:T(8,128)(2,1)}, bf16[8,2,96,128]{3,2,1,0:T(8,128)(2,1)S(1)}, u32[]{:S(2)}, u32[]{:S(2)}) collective-permute-start(bf16[8,2,96,128]{3,2,1,0:T(8,128)(2,1)} %get-tuple-element.73), channel_id=1, source_target_pairs={{0,1},{1,0},{2,3},{3,2},{4,5},{5,4},{6,7},{7,6},{8,9},{9,8},{10,11... | collective-permute-start | bytes 1179656 | tf_op jit(solution)/shard_map/ppermute | solution.py:425
  163.1 3.0 %collective-permute-start.8 = (bf16[8,2,96,128]{3,2,1,0:T(8,128)(2,1)}, bf16[8,2,96,128]{3,2,1,0:T(8,128)(2,1)S(1)}, u32[]{:S(2)}, u32[]{:S(2)}) collective-permute-start(bf16[8,2,96,128]{3,2,1,0:T(8,128)(2,1)} %copy-done.4), channel_id=1, source_target_pairs={{1,2},{3,4},{5,6},{7,8},{9,10},{11,12},{13,14},{2,1},{4,3},{6,5},{... | collective-permute-start | bytes 1179656 | tf_op jit(solution)/shard_map/ppermute | solution.py:424
  166.0 0.2 collective-permute-start.9
  166.3 2.0 %shard_map.103.half_ref = f32[8,512]{1,0:T(8,128)S(1)} custom-call(s32[1]{0:T(128)} %bitcast.core_ref, bf16[2,8,512,512]{3,2,1,0:T(8,128)(2,1)} %shard_map.87.h_ref, bf16[3,512,512]{2,1,0:T(8,128)(2,1)S(1)} %get-tuple-element.48.keep_ref, bf16[16,8,512]{2,1,0:T(8,128)(2,1)S(1)} %all-to-all-done.7.x_ref), custom_call_target="tpu_custom_call" | custom-call | flops 100000000 | bytes 5000000 | tf_op jit(solution)/shard_map/pallas_call | solution.py:180
  168.3 0.0 copy-start.1
  168.3 0.0 copy-start.2
  168.3 2.6 %shard_map.104 = (f32[8,512]{1,0:T(8,128)S(1)}, bf16[8,512]{1,0:T(8,128)(2,1)S(1)}, bf16[2,8,256]{2,1,0:T(8,128)(2,1)S(1)}) custom-call(s32[1]{0:T(128)} %bitcast.core_ref, s32[1]{0:T(128)} %bitcast.11.mine_ref, bf16[2,8,512,512]{3,2,1,0:T(8,128)(2,1)} %shard_map.87.h_ref, bf16[16,8,512]{2,1,0:T(8,128)(2,1)S(1)} %collective-permute-done.9.x_ref, ...), custom_call_target="tpu_custom_call" | custom-call | flops 100000000 | bytes 5000000 | tf_op jit(solution)/shard_map/pallas_call | solution.py:222
  171.0 2.8 %collective-permute-start.10 = (bf16[8,512]{1,0:T(8,128)(2,1)S(1)}, bf16[8,512]{1,0:T(8,128)(2,1)S(1)}, u32[]{:S(2)}, u32[]{:S(2)}) collective-permute-start(bf16[8,512]{1,0:T(8,128)(2,1)S(1)} %get-tuple-element.79), channel_id=1, source_target_pairs={{16,0},{32,16},{48,32},{64,48},{80,64},{96,80},{112,96},{17,1},{33... | collective-permute-start | bytes 24584 | tf_op jit(solution)/shard_map/ppermute | solution.py:385
  173.8 0.4 collective-permute-start.11
  174.1 4.2 %collective-permute-start.12 = (bf16[8,256]{1,0:T(8,128)(2,1)S(1)}, bf16[8,256]{1,0:T(8,128)(2,1)S(1)}, u32[]{:S(2)}, u32[]{:S(2)}) collective-permute-start(bf16[8,256]{1,0:T(8,128)(2,1)S(1)} %get-tuple-element.84), channel_id=1, source_target_pairs={{1,2},{3,4},{5,6},{7,8},{9,10},{11,12},{13,14},{2,1},{4,3},{6,5},{... | collective-permute-start | bytes 12296 | tf_op jit(solution)/shard_map/ppermute | solution.py:431
  178.4 3.1 %collective-permute-done.12.vo_ref = bf16[8,256]{1,0:T(8,128)(2,1)S(1)} collective-permute-done((bf16[8,256]{1,0:T(8,128)(2,1)S(1)}, bf16[8,256]{1,0:T(8,128)(2,1)S(1)}, u32[]{:S(2)}, u32[]{:S(2)}) %collective-permute-start.12) | collective-permute-done | bytes 4128 | tf_op jit(solution)/shard_map/ppermute | solution.py:431
  181.5 2.8 %shard_map.105 = (f32[2,8,192,128]{3,2,1,0:T(8,128)}, f32[2,8,192,128]{3,2,1,0:T(8,128)}) custom-call(s32[1]{0:T(128)} %bitcast.core_ref, f32[8,96,512]{2,1,0:T(8,128)S(1)} %copy-done.2, f32[2,8,192,128]{3,2,1,0:T(8,128)S(1)} %bitcast.28, bf16[8,2,96,128]{3,2,1,0:T(8,128)(2,1)S(1)} %collective-permute-done.7.inner_ref, ...), custom_call_target="tpu_custom_call" | custom-call | tf_op jit(solution)/shard_map/pallas_call | solution.py:364
  (23 shorter events, 0.1 us)
Async XLA Ops:
  7.2 44.3 %all-gather.5.cloned.1.call-start = ((), (), s32[]{:S(2)}) async-start(), calls=%async_computation.8 | async-start | bytes 2359296 | tf_op jit(solution)/shard_map/all_gather | solution.py:394
  7.2 1.4 copy-start
  8.6 0.7 copy-start.3
  10.4 15.8 %all-to-all-start = ((bf16[16,16,512]{2,1,0:T(8,128)(2,1)}), bf16[16,16,512]{2,1,0:T(8,128)(2,1)S(1)}, u32[]{:S(2)}, u32[]{:S(2)}) async-start(bf16[16,16,512]{2,1,0:T(8,128)(2,1)} %get-tuple-element.44), calls=%async_computation | async-start | bytes 524288 | tf_op jit(solution)/shard_map/all_to_all | solution.py:395
  19.1 111.3 %all-gather.7.cloned.1.call-start = ((), (), s32[]{:S(2)}) async-start(), calls=%async_computation.9 | async-start | bytes 14155776 | tf_op jit(solution)/shard_map/all_gather | solution.py:412
  44.7 3.5 %collective-permute-start = (bf16[16,8,512]{2,1,0:T(8,128)(2,1)S(1)}, bf16[16,8,512]{2,1,0:T(8,128)(2,1)S(1)}, u32[]{:S(2)}, u32[]{:S(2)}) collective-permute-start(bf16[16,8,512]{2,1,0:T(8,128)(2,1)S(1)} %all_to_all.40.x_ref), channel_id=1, source_target_pairs={{0,1},{1,0},{2,3},{3,2},{4,5},{5,4},{6,7},{7,6},{8,9},{9,8},{10,11... | collective-permute-start | bytes 393224 | tf_op jit(solution)/shard_map/ppermute | solution.py:426
  51.4 0.7 copy-start.6
  51.4 8.8 %copy-start.7 = (s32[256]{0:T(256)S(1)}, s32[256]{0:T(256)}, u32[]{:S(2)}) copy-start(s32[256]{0:T(256)} %param.11) | copy-start | bytes 3076
  51.4 8.7 %copy-start.8 = (s32[8]{0:T(128)S(1)}, s32[8]{0:T(128)}, u32[]{:S(2)}) copy-start(s32[8]{0:T(128)} %param.12) | copy-start | bytes 100
  51.4 8.9 %copy-start.5 = (bf16[256,2,128]{2,1,0:T(2,128)(2,1)S(1)}, bf16[256,2,128]{2,1,0:T(2,128)(2,1)}, u32[]{:S(2)}) copy-start(bf16[256,2,128]{2,1,0:T(2,128)(2,1)} %param.9) | copy-start | bytes 393220
  52.2 13.6 %all-to-all-start.2 = ((bf16[16,8,512]{2,1,0:T(8,128)(2,1)}), bf16[16,8,512]{2,1,0:T(8,128)(2,1)S(1)}, u32[]{:S(2)}, u32[]{:S(2)}) async-start(bf16[16,8,512]{2,1,0:T(8,128)(2,1)} %get-tuple-element.52), calls=%async_computation.2 | async-start | bytes 262144 | tf_op jit(solution)/shard_map/all_to_all | solution.py:413
  65.8 3.2 %collective-permute-start.1 = (bf16[16,8,512]{2,1,0:T(8,128)(2,1)S(1)}, bf16[16,8,512]{2,1,0:T(8,128)(2,1)S(1)}, u32[]{:S(2)}, u32[]{:S(2)}) collective-permute-start(bf16[16,8,512]{2,1,0:T(8,128)(2,1)S(1)} %all-to-all-done.2.x_ref), channel_id=1, source_target_pairs={{0,1},{1,0},{2,3},{3,2},{4,5},{5,4},{6,7},{7,6},{8,9},{9,8},{10,11... | collective-permute-start | bytes 393224 | tf_op jit(solution)/shard_map/ppermute | solution.py:426
  81.7 3.4 %collective-permute-start.2 = (bf16[16,8,512]{2,1,0:T(8,128)(2,1)S(1)}, bf16[16,8,512]{2,1,0:T(8,128)(2,1)S(1)}, u32[]{:S(2)}, u32[]{:S(2)}) collective-permute-start(bf16[16,8,512]{2,1,0:T(8,128)(2,1)S(1)} %all_to_all.41.x_ref), channel_id=1, source_target_pairs={{0,1},{1,0},{2,3},{3,2},{4,5},{5,4},{6,7},{7,6},{8,9},{9,8},{10,11... | collective-permute-start | bytes 393224 | tf_op jit(solution)/shard_map/ppermute | solution.py:426
  100.0 3.3 %collective-permute-start.3 = (bf16[16,8,512]{2,1,0:T(8,128)(2,1)S(1)}, bf16[16,8,512]{2,1,0:T(8,128)(2,1)S(1)}, u32[]{:S(2)}, u32[]{:S(2)}) collective-permute-start(bf16[16,8,512]{2,1,0:T(8,128)(2,1)S(1)} %all_to_all.42.x_ref), channel_id=1, source_target_pairs={{0,1},{1,0},{2,3},{3,2},{4,5},{5,4},{6,7},{7,6},{8,9},{9,8},{10,11... | collective-permute-start | bytes 393224 | tf_op jit(solution)/shard_map/ppermute | solution.py:426
  116.2 3.1 %collective-permute-start.4 = (bf16[16,8,512]{2,1,0:T(8,128)(2,1)S(1)}, bf16[16,8,512]{2,1,0:T(8,128)(2,1)S(1)}, u32[]{:S(2)}, u32[]{:S(2)}) collective-permute-start(bf16[16,8,512]{2,1,0:T(8,128)(2,1)S(1)} %all_to_all.43.x_ref), channel_id=1, source_target_pairs={{0,1},{1,0},{2,3},{3,2},{4,5},{5,4},{6,7},{7,6},{8,9},{9,8},{10,11... | collective-permute-start | bytes 393224 | tf_op jit(solution)/shard_map/ppermute | solution.py:426
  122.5 20.0 %all-to-all-start.6 = ((bf16[16,8,512]{2,1,0:T(8,128)(2,1)}), bf16[16,8,512]{2,1,0:T(8,128)(2,1)S(1)}, u32[]{:S(2)}, u32[]{:S(2)}) async-start(bf16[16,8,512]{2,1,0:T(8,128)(2,1)} %get-tuple-element.62), calls=%async_computation.6 | async-start | bytes 262144 | tf_op jit(solution)/shard_map/all_to_all | solution.py:413
  141.7 0.7 copy-start.4
  142.5 2.3 %collective-permute-start.5 = (bf16[16,8,512]{2,1,0:T(8,128)(2,1)S(1)}, bf16[16,8,512]{2,1,0:T(8,128)(2,1)S(1)}, u32[]{:S(2)}, u32[]{:S(2)}) collective-permute-start(bf16[16,8,512]{2,1,0:T(8,128)(2,1)S(1)} %all-to-all-done.6.x_ref), channel_id=1, source_target_pairs={{0,1},{1,0},{2,3},{3,2},{4,5},{5,4},{6,7},{7,6},{8,9},{9,8},{10,11... | collective-permute-start | bytes 393224 | tf_op jit(solution)/shard_map/ppermute | solution.py:426
  147.9 13.2 %all-to-all-start.7 = ((bf16[16,8,512]{2,1,0:T(8,128)(2,1)}), bf16[16,8,512]{2,1,0:T(8,128)(2,1)S(1)}, u32[]{:S(2)}, u32[]{:S(2)}) async-start(bf16[16,8,512]{2,1,0:T(8,128)(2,1)} %get-tuple-element.67), calls=%async_computation.7 | async-start | bytes 262144 | tf_op jit(solution)/shard_map/all_to_all | solution.py:413
  154.6 6.5 %collective-permute-start.6 = (bf16[8,512]{1,0:T(8,128)(2,1)S(1)}, bf16[8,512]{1,0:T(8,128)(2,1)S(1)}, u32[]{:S(2)}, u32[]{:S(2)}) collective-permute-start(bf16[8,512]{1,0:T(8,128)(2,1)S(1)} %get-tuple-element.72), channel_id=1, source_target_pairs={{0,16},{16,32},{32,48},{48,64},{64,80},{80,96},{96,112},{1,17},{17... | collective-permute-start | bytes 24584 | tf_op jit(solution)/shard_map/ppermute | solution.py:385
  161.1 20.3 %collective-permute-start.7 = (bf16[8,2,96,128]{3,2,1,0:T(8,128)(2,1)}, bf16[8,2,96,128]{3,2,1,0:T(8,128)(2,1)S(1)}, u32[]{:S(2)}, u32[]{:S(2)}) collective-permute-start(bf16[8,2,96,128]{3,2,1,0:T(8,128)(2,1)} %get-tuple-element.73), channel_id=1, source_target_pairs={{0,1},{1,0},{2,3},{3,2},{4,5},{5,4},{6,7},{7,6},{8,9},{9,8},{10,11... | collective-permute-start | bytes 1179656 | tf_op jit(solution)/shard_map/ppermute | solution.py:425
  163.1 18.4 %collective-permute-start.8 = (bf16[8,2,96,128]{3,2,1,0:T(8,128)(2,1)}, bf16[8,2,96,128]{3,2,1,0:T(8,128)(2,1)S(1)}, u32[]{:S(2)}, u32[]{:S(2)}) collective-permute-start(bf16[8,2,96,128]{3,2,1,0:T(8,128)(2,1)} %copy-done.4), channel_id=1, source_target_pairs={{1,2},{3,4},{5,6},{7,8},{9,10},{11,12},{13,14},{2,1},{4,3},{6,5},{... | collective-permute-start | bytes 1179656 | tf_op jit(solution)/shard_map/ppermute | solution.py:424
  166.0 2.2 %collective-permute-start.9 = (bf16[16,8,512]{2,1,0:T(8,128)(2,1)S(1)}, bf16[16,8,512]{2,1,0:T(8,128)(2,1)S(1)}, u32[]{:S(2)}, u32[]{:S(2)}) collective-permute-start(bf16[16,8,512]{2,1,0:T(8,128)(2,1)S(1)} %all-to-all-done.7.x_ref), channel_id=1, source_target_pairs={{0,1},{1,0},{2,3},{3,2},{4,5},{5,4},{6,7},{7,6},{8,9},{9,8},{10,11... | collective-permute-start | bytes 393224 | tf_op jit(solution)/shard_map/ppermute | solution.py:426
  168.3 13.2 %copy-start.1 = (f32[2,8,96,2,128]{4,3,2,1,0:T(2,128)S(1)}, f32[2,8,96,2,128]{4,3,2,1,0:T(2,128)}, u32[]{:S(2)}) copy-start(f32[2,8,96,2,128]{4,3,2,1,0:T(2,128)} %param.7) | copy-start | bytes 4718596
  168.3 13.2 %copy-start.2 = (f32[8,96,512]{2,1,0:T(8,128)S(1)}, f32[8,96,512]{2,1,0:T(8,128)}, u32[]{:S(2)}) copy-start(f32[8,96,512]{2,1,0:T(8,128)} %get-tuple-element.61.y_ref) | copy-start | bytes 4718596
  171.0 10.5 %collective-permute-start.10 = (bf16[8,512]{1,0:T(8,128)(2,1)S(1)}, bf16[8,512]{1,0:T(8,128)(2,1)S(1)}, u32[]{:S(2)}, u32[]{:S(2)}) collective-permute-start(bf16[8,512]{1,0:T(8,128)(2,1)S(1)} %get-tuple-element.79), channel_id=1, source_target_pairs={{16,0},{32,16},{48,32},{64,48},{80,64},{96,80},{112,96},{17,1},{33... | collective-permute-start | bytes 24584 | tf_op jit(solution)/shard_map/ppermute | solution.py:385
  173.8 4.6 %collective-permute-start.11 = (bf16[8,256]{1,0:T(8,128)(2,1)S(1)}, bf16[8,256]{1,0:T(8,128)(2,1)S(1)}, u32[]{:S(2)}, u32[]{:S(2)}) collective-permute-start(bf16[8,256]{1,0:T(8,128)(2,1)S(1)} %get-tuple-element.85), channel_id=1, source_target_pairs={{0,1},{1,0},{2,3},{3,2},{4,5},{5,4},{6,7},{7,6},{8,9},{9,8},{10,11... | collective-permute-start | bytes 12296 | tf_op jit(solution)/shard_map/ppermute | solution.py:433
  174.1 7.3 %collective-permute-start.12 = (bf16[8,256]{1,0:T(8,128)(2,1)S(1)}, bf16[8,256]{1,0:T(8,128)(2,1)S(1)}, u32[]{:S(2)}, u32[]{:S(2)}) collective-permute-start(bf16[8,256]{1,0:T(8,128)(2,1)S(1)} %get-tuple-element.84), channel_id=1, source_target_pairs={{1,2},{3,4},{5,6},{7,8},{9,10},{11,12},{13,14},{2,1},{4,3},{6,5},{... | collective-permute-start | bytes 12296 | tf_op jit(solution)/shard_map/ppermute | solution.py:431
Sparse Core Ops, SparseCore 0:
  10.6 33.4 all-gather.4
  51.6 71.5 all-gather.6
